TPU v7x, 32 devices: a whole 2x2x4 slice. The times are simulated.
32 devices in a mesh: patch: 8 (over y, x, core), frame: 4 (over z).
Axes of the slice: x: 2, y: 2, z: 4, core: 2. Of those that a mesh axis runs over, the one named last changes fastest.
Arguments:
- block_input: float32 [20, 512, 1152], P('frame', 'patch'), may hold values from -6 to 6
- out_cotangent: float32 [20, 512, 1152], P('frame', 'patch'), may hold values from -6 to 6
- caption: float32 [4, 120, 1152], replicated, may hold values from -6 to 6
- cond: float32 [4, 1152], replicated, may hold values from -6 to 6
- ada_weight: float32 [1152, 6912], P('patch'), may hold values from -0.1875 to 0.1875
- ada_bias: float32 [6912], P('patch'), may hold values from -3 to 3
- qkv_weight: float32 [1152, 3456], P('patch'), may hold values from -0.1875 to 0.1875
- q_bias: float32 [1152], P('patch'), may hold values from -3 to 3
- v_bias: float32 [1152], P('patch'), may hold values from -3 to 3
- attn_out_weight: float32 [1152, 1152], P('patch'), may hold values from -0.5 to 0.5
- attn_out_bias: float32 [1152], P('patch'), may hold values from -3 to 3
- cross_q_weight: float32 [1152, 1152], P('patch'), may hold values from -0.1875 to 0.1875
- cross_q_bias: float32 [1152], P('patch'), may hold values from -3 to 3
- cross_kv_weight: float32 [1152, 2304], P('patch'), may hold values from -0.1875 to 0.1875
- cross_v_bias: float32 [1152], P('patch'), may hold values from -3 to 3
- cross_out_weight: float32 [1152, 1152], P('patch'), may hold values from -0.5 to 0.5
- cross_out_bias: float32 [1152], P('patch'), may hold values from -3 to 3
- fc1_weight: float32 [1152, 4608], P('patch'), may hold values from -0.1875 to 0.1875
- fc1_bias: float32 [4608], P('patch'), may hold values from -3 to 3
- fc2_weight: float32 [4608, 1152], P('patch'), may hold values from -0.09375 to 0.09375
- fc2_bias: float32 [1152], P('patch'), may hold values from -3 to 3
- frame_slot: int32 [20], P('frame'), may hold values from 0 to 17, as said below
- clip_id: int32 [512], P('patch'), may hold values from 0 to 3, never falling along the last dimension, each value on 1 to 256 neighbouring positions
- patch_mask: int32 [512], P('patch'), may hold values 0 or 1
- caption_mask: int32 [4, 120], replicated, may hold values from 0 to 1, as said below
Outputs:
- block_out: float32 [20, 512, 1152], P('frame', 'patch')
- input_grad: float32 [20, 512, 1152], P('frame', 'patch')
- caption_grad: float32 [4, 120, 1152], replicated
- cond_grad: float32 [4, 1152], replicated
- ada_weight_grad: float32 [1152, 6912], P('patch')
- ada_bias_grad: float32 [6912], P('patch')
- qkv_weight_grad: float32 [1152, 3456], P('patch')
- q_bias_grad: float32 [1152], P('patch')
- v_bias_grad: float32 [1152], P('patch')
- attn_out_weight_grad: float32 [1152, 1152], P('patch')
- attn_out_bias_grad: float32 [1152], P('patch')
- cross_q_weight_grad: float32 [1152, 1152], P('patch')
- cross_q_bias_grad: float32 [1152], P('patch')
- cross_kv_weight_grad: float32 [1152, 2304], P('patch')
- cross_v_bias_grad: float32 [1152], P('patch')
- cross_out_weight_grad: float32 [1152, 1152], P('patch')
- cross_out_bias_grad: float32 [1152], P('patch')
- fc1_weight_grad: float32 [1152, 4608], P('patch')
- fc1_bias_grad: float32 [4608], P('patch')
- fc2_weight_grad: float32 [4608, 1152], P('patch')
- fc2_bias_grad: float32 [1152], P('patch')
Inputs may be any that keep to these rules, and one draw needn't show every extreme that they name: `frame_slot`: each of the 17 frames is named by exactly one slot, in increasing order along the slots; the other slots hold 17 and are empty; every index of frame holds at least one frame. `clip_id`: clip numbers never fall along the columns. `caption_mask`: each row is ones followed by zeros, with at least 30 ones.
All inputs are finite; a program needn't handle non-finite values. No bound on the sum of `patch_mask` on one device may be relied on, other than what follows from the above.
Results may differ from a plain program's by a relative error of at most 0.0003.
Values sent between devices are 32-bit elements; how exact they have to be, the bound alone decides.
A program may use at most 448 MiB of HBM per device.

v0:
```python
from functools import partial

import jax
import jax.numpy as jnp
from jax import lax
from jax.sharding import PartitionSpec as P

H = 16
CAP = 120
FRAMES = 17
CLIPS = 4


EPSILON = 1e-06
BEST = lax.Precision.HIGHEST


def matmul(left, right):
    return jnp.dot(left, right, precision=BEST)


def contract(form, left, right):
    return jnp.einsum(form, left, right, precision=BEST)


def normalize(rows):
    average = jnp.mean(rows, axis=-1, keepdims=True)
    centred = rows - average
    spread = jnp.mean(centred * centred, axis=-1, keepdims=True)
    inverse = lax.rsqrt(spread + EPSILON)
    return (centred * inverse, inverse)


def normalize_back(grad_normed, normed, inverse):
    first_mean = jnp.mean(grad_normed, axis=-1, keepdims=True)
    second_mean = jnp.mean(grad_normed * normed, axis=-1, keepdims=True)
    return inverse * (grad_normed - first_mean - normed * second_mean)


def softmax_rows(scores, allowed):
    masked = jnp.where(allowed, scores, -1e30)
    highest = jnp.max(masked, axis=-1, keepdims=True)
    exponent = jnp.exp(masked - highest)
    return exponent / jnp.sum(exponent, axis=-1, keepdims=True)


def plan_rows(
    block_input,
    out_cotangent,
    caption,
    cond,
    ada_weight,
    ada_bias,
    qkv_weight,
    q_bias,
    v_bias,
    attn_out_weight,
    attn_out_bias,
    cross_q_weight,
    cross_q_bias,
    cross_kv_weight,
    cross_v_bias,
    cross_out_weight,
    cross_out_bias,
    fc1_weight,
    fc1_bias,
    fc2_weight,
    fc2_bias,
    frame_slot,
    clip_id,
    patch_mask,
    caption_mask,
):
    (
        w_ada,
        b_ada,
        w_qkv,
        b_query,
        b_value,
        w_attn,
        b_attn,
        w_cross_q,
        b_cross_q,
        w_cross_kv,
        b_cross_v,
        w_cross_o,
        b_cross_o,
        w_first,
        b_first,
        w_second,
        b_second,
    ) = (
        lax.all_gather(ada_weight, "patch", axis=0, tiled=True),
        lax.all_gather(ada_bias, "patch", axis=0, tiled=True),
        lax.all_gather(qkv_weight, "patch", axis=0, tiled=True),
        lax.all_gather(q_bias, "patch", axis=0, tiled=True),
        lax.all_gather(v_bias, "patch", axis=0, tiled=True),
        lax.all_gather(attn_out_weight, "patch", axis=0, tiled=True),
        lax.all_gather(attn_out_bias, "patch", axis=0, tiled=True),
        lax.all_gather(cross_q_weight, "patch", axis=0, tiled=True),
        lax.all_gather(cross_q_bias, "patch", axis=0, tiled=True),
        lax.all_gather(cross_kv_weight, "patch", axis=0, tiled=True),
        lax.all_gather(cross_v_bias, "patch", axis=0, tiled=True),
        lax.all_gather(cross_out_weight, "patch", axis=0, tiled=True),
        lax.all_gather(cross_out_bias, "patch", axis=0, tiled=True),
        lax.all_gather(fc1_weight, "patch", axis=0, tiled=True),
        lax.all_gather(fc1_bias, "patch", axis=0, tiled=True),
        lax.all_gather(fc2_weight, "patch", axis=0, tiled=True),
        lax.all_gather(fc2_bias, "patch", axis=0, tiled=True),
    )
    slots_dev, cols_dev, width = block_input.shape
    tokens_dev = slots_dev * cols_dev
    head_dim = width // H
    scaling = head_dim ** (-0.5)
    slopes = 2.0 ** (-8.0 * (jnp.arange(H).astype(jnp.float32) + 1.0) / H)
    clip_onehot = (clip_id[:, None] == jnp.arange(CLIPS, dtype=jnp.int32)[None, :]).astype(
        jnp.float32
    )
    column_mask = patch_mask.astype(jnp.float32)[:, None]
    cond_act, silu_pull = jax.vjp(jax.nn.silu, cond)
    modulation = matmul(cond_act, w_ada) + b_ada
    per_column = matmul(clip_onehot, modulation)
    shift_one = per_column[:, 0:width]
    scale_one = per_column[:, width : 2 * width]
    gate_one = per_column[:, 2 * width : 3 * width]
    shift_two = per_column[:, 3 * width : 4 * width]
    scale_two = per_column[:, 4 * width : 5 * width]
    gate_two = per_column[:, 5 * width : 6 * width]
    normed_one, inverse_one = normalize(block_input)
    hidden_one = normed_one * (1.0 + scale_one) + shift_one
    hidden_one_rows = hidden_one.reshape(tokens_dev, width)
    qkv_rows = matmul(hidden_one_rows, w_qkv)
    queries = (qkv_rows[:, :width] + b_query).reshape(slots_dev, cols_dev, H, head_dim)
    key_rows = qkv_rows[:, width : 2 * width].reshape(slots_dev, cols_dev, width)
    value_rows = (qkv_rows[:, 2 * width :] + b_value).reshape(slots_dev, cols_dev, width)
    frame_pos = frame_slot.astype(jnp.float32)
    all_keys, all_values, all_pos = (
        lax.all_gather(key_rows, "frame", axis=0, tiled=True),
        lax.all_gather(value_rows, "frame", axis=0, tiled=True),
        lax.all_gather(frame_pos, "frame", axis=0, tiled=True),
    )
    total_slots = all_keys.shape[0]
    all_keys = all_keys.reshape(total_slots, cols_dev, H, head_dim)
    all_values = all_values.reshape(total_slots, cols_dev, H, head_dim)
    distance = jnp.abs(frame_pos[:, None] - all_pos[None, :])
    bias_table = -slopes[:, None, None] * distance[None]
    key_valid = (all_pos < FRAMES - 0.5)[None, None, None, :]
    scores = contract("fchd,schd->chfs", queries, all_keys) * scaling + bias_table[None]
    probs = softmax_rows(scores, key_valid)
    attended = contract("chfs,schd->fchd", probs, all_values)
    attended_rows = attended.reshape(tokens_dev, width)
    attn_branch = (matmul(attended_rows, w_attn) + b_attn).reshape(slots_dev, cols_dev, width)
    after_attn = block_input + column_mask * gate_one * attn_branch
    after_attn_rows = after_attn.reshape(tokens_dev, width)
    cross_queries = (matmul(after_attn_rows, w_cross_q) + b_cross_q).reshape(
        slots_dev, cols_dev, H, head_dim
    )
    caption_rows = caption.reshape(CLIPS * CAP, width)
    caption_kv = matmul(caption_rows, w_cross_kv)
    cross_keys = caption_kv[:, :width].reshape(CLIPS * CAP, H, head_dim)
    cross_values = (caption_kv[:, width:] + b_cross_v).reshape(CLIPS * CAP, H, head_dim)
    key_clip = jnp.arange(CLIPS * CAP, dtype=jnp.int32) // CAP
    caption_ok = (
        (clip_id[:, None] == key_clip[None, :]) & (caption_mask.reshape(CLIPS * CAP)[None, :] > 0)
    )[None, :, None, :]
    cross_scores = contract("fchd,khd->fchk", cross_queries, cross_keys) * scaling
    cross_probs = softmax_rows(cross_scores, caption_ok)
    cross_att = contract("fchk,khd->fchd", cross_probs, cross_values)
    cross_rows = cross_att.reshape(tokens_dev, width)
    cross_branch = (matmul(cross_rows, w_cross_o) + b_cross_o).reshape(slots_dev, cols_dev, width)
    after_cross = after_attn + column_mask * cross_branch
    normed_two, inverse_two = normalize(after_cross)
    hidden_two = normed_two * (1.0 + scale_two) + shift_two
    hidden_two_rows = hidden_two.reshape(tokens_dev, width)
    pre_act = matmul(hidden_two_rows, w_first) + b_first
    activated, gelu_pull = jax.vjp(partial(jax.nn.gelu, approximate=True), pre_act)
    mlp_branch = (matmul(activated, w_second) + b_second).reshape(slots_dev, cols_dev, width)
    block_out = after_cross + column_mask * gate_two * mlp_branch
    grad_mlp = (column_mask * gate_two * out_cotangent).reshape(tokens_dev, width)
    grad_gate_two = jnp.sum(column_mask * mlp_branch * out_cotangent, axis=0)
    grad_w_second = matmul(activated.T, grad_mlp)
    grad_b_second = jnp.sum(grad_mlp, axis=0)
    grad_pre = gelu_pull(matmul(grad_mlp, w_second.T))[0]
    grad_w_first = matmul(hidden_two_rows.T, grad_pre)
    grad_b_first = jnp.sum(grad_pre, axis=0)
    grad_hidden_two = matmul(grad_pre, w_first.T).reshape(slots_dev, cols_dev, width)
    grad_shift_two = jnp.sum(grad_hidden_two, axis=0)
    grad_scale_two = jnp.sum(grad_hidden_two * normed_two, axis=0)
    grad_after_cross = out_cotangent + normalize_back(
        grad_hidden_two * (1.0 + scale_two), normed_two, inverse_two
    )
    grad_cross_branch = (column_mask * grad_after_cross).reshape(tokens_dev, width)
    grad_w_cross_o = matmul(cross_rows.T, grad_cross_branch)
    grad_b_cross_o = jnp.sum(grad_cross_branch, axis=0)
    grad_cross_att = matmul(grad_cross_branch, w_cross_o.T).reshape(
        slots_dev, cols_dev, H, head_dim
    )
    cross_row_terms = jnp.sum(grad_cross_att * cross_att, axis=-1)[..., None]
    grad_cross_probs = contract("fchd,khd->fchk", grad_cross_att, cross_values)
    grad_cross_scores = cross_probs * (grad_cross_probs - cross_row_terms) * scaling
    grad_cross_queries = contract("fchk,khd->fchd", grad_cross_scores, cross_keys).reshape(
        tokens_dev, width
    )
    grad_cross_keys = contract("fchk,fchd->khd", grad_cross_scores, cross_queries).reshape(
        CLIPS * CAP, width
    )
    grad_cross_values = contract("fchk,fchd->khd", cross_probs, grad_cross_att).reshape(
        CLIPS * CAP, width
    )
    grad_caption_kv = jnp.concatenate([grad_cross_keys, grad_cross_values], axis=1)
    grad_w_cross_kv = matmul(caption_rows.T, grad_caption_kv)
    grad_b_cross_v = jnp.sum(grad_cross_values, axis=0)
    grad_caption_part = matmul(grad_caption_kv, w_cross_kv.T).reshape(CLIPS, CAP, width)
    grad_w_cross_q = matmul(after_attn_rows.T, grad_cross_queries)
    grad_b_cross_q = jnp.sum(grad_cross_queries, axis=0)
    grad_after_attn = grad_after_cross + matmul(grad_cross_queries, w_cross_q.T).reshape(
        slots_dev, cols_dev, width
    )
    grad_attn_rows = (column_mask * gate_one * grad_after_attn).reshape(tokens_dev, width)
    grad_gate_one = jnp.sum(column_mask * attn_branch * grad_after_attn, axis=0)
    grad_w_attn = matmul(attended_rows.T, grad_attn_rows)
    grad_b_attn = jnp.sum(grad_attn_rows, axis=0)
    grad_attended = matmul(grad_attn_rows, w_attn.T).reshape(slots_dev, cols_dev, H, head_dim)
    row_terms = jnp.transpose(jnp.sum(grad_attended * attended, axis=-1), (1, 2, 0))[..., None]
    grad_probs = contract("fchd,schd->chfs", grad_attended, all_values)
    grad_scores = probs * (grad_probs - row_terms)
    grad_queries = (contract("chfs,schd->fchd", grad_scores, all_keys) * scaling).reshape(
        tokens_dev, width
    )
    grad_all_keys = (contract("chfs,fchd->schd", grad_scores, queries) * scaling).reshape(
        total_slots, cols_dev, width
    )
    grad_all_values = contract("chfs,fchd->schd", probs, grad_attended).reshape(
        total_slots, cols_dev, width
    )
    grad_keys, grad_values = (
        lax.psum_scatter(grad_all_keys, "frame", scatter_dimension=0, tiled=True),
        lax.psum_scatter(grad_all_values, "frame", scatter_dimension=0, tiled=True),
    )
    grad_key_rows = grad_keys.reshape(tokens_dev, width)
    grad_value_rows = grad_values.reshape(tokens_dev, width)
    grad_qkv = jnp.concatenate([grad_queries, grad_key_rows, grad_value_rows], axis=1)
    grad_w_qkv = matmul(hidden_one_rows.T, grad_qkv)
    grad_b_query = jnp.sum(grad_queries, axis=0)
    grad_b_value = jnp.sum(grad_value_rows, axis=0)
    grad_hidden_one = matmul(grad_qkv, w_qkv.T).reshape(slots_dev, cols_dev, width)
    grad_shift_one = jnp.sum(grad_hidden_one, axis=0)
    grad_scale_one = jnp.sum(grad_hidden_one * normed_one, axis=0)
    input_grad = grad_after_attn + normalize_back(
        grad_hidden_one * (1.0 + scale_one), normed_one, inverse_one
    )
    grad_per_column = jnp.concatenate(
        [
            grad_shift_one,
            grad_scale_one,
            grad_gate_one,
            grad_shift_two,
            grad_scale_two,
            grad_gate_two,
        ],
        axis=1,
    )
    grad_modulation = matmul(clip_onehot.T, grad_per_column)
    grad_w_ada = matmul(cond_act.T, grad_modulation)
    grad_b_ada = jnp.sum(grad_modulation, axis=0)
    grad_cond_part = silu_pull(matmul(grad_modulation, w_ada.T))[0]
    shares = (
        lax.psum_scatter(grad_w_ada, "patch", scatter_dimension=0, tiled=True),
        lax.psum_scatter(grad_w_qkv, "patch", scatter_dimension=0, tiled=True),
        lax.psum_scatter(grad_w_attn, "patch", scatter_dimension=0, tiled=True),
        lax.psum_scatter(grad_w_cross_q, "patch", scatter_dimension=0, tiled=True),
        lax.psum_scatter(grad_w_cross_kv, "patch", scatter_dimension=0, tiled=True),
        lax.psum_scatter(grad_w_cross_o, "patch", scatter_dimension=0, tiled=True),
        lax.psum_scatter(grad_w_first, "patch", scatter_dimension=0, tiled=True),
        lax.psum_scatter(grad_w_second, "patch", scatter_dimension=0, tiled=True),
    )
    summed = lax.psum(
        (shares[0], shares[1], shares[2], shares[3], shares[4], shares[5], shares[6], shares[7]),
        "frame",
    )
    biases = (
        grad_b_ada,
        grad_b_query,
        grad_b_value,
        grad_b_attn,
        grad_b_cross_q,
        grad_b_cross_v,
        grad_b_cross_o,
        grad_b_first,
        grad_b_second,
    )
    return (block_out, input_grad, grad_caption_part, grad_cond_part, biases, summed)


def on_device(
    block_input,
    out_cotangent,
    caption,
    cond,
    ada_weight,
    ada_bias,
    qkv_weight,
    q_bias,
    v_bias,
    attn_out_weight,
    attn_out_bias,
    cross_q_weight,
    cross_q_bias,
    cross_kv_weight,
    cross_v_bias,
    cross_out_weight,
    cross_out_bias,
    fc1_weight,
    fc1_bias,
    fc2_weight,
    fc2_bias,
    frame_slot,
    clip_id,
    patch_mask,
    caption_mask,
):
    outcome = plan_rows(
        block_input,
        out_cotangent,
        caption,
        cond,
        ada_weight,
        ada_bias,
        qkv_weight,
        q_bias,
        v_bias,
        attn_out_weight,
        attn_out_bias,
        cross_q_weight,
        cross_q_bias,
        cross_kv_weight,
        cross_v_bias,
        cross_out_weight,
        cross_out_bias,
        fc1_weight,
        fc1_bias,
        fc2_weight,
        fc2_bias,
        frame_slot,
        clip_id,
        patch_mask,
        caption_mask,
    )
    block_out, input_grad, caption_part, cond_part, biases, weights = outcome
    summed = lax.psum(
        (
            caption_part,
            cond_part,
            biases[0],
            biases[1],
            biases[2],
            biases[3],
            biases[4],
            biases[5],
            biases[6],
            biases[7],
            biases[8],
        ),
        ("patch", "frame"),
    )
    patch_index = lax.axis_index("patch")
    patch_count = lax.axis_size("patch")

    def own_slice(vector):
        length = vector.shape[0] // patch_count
        return lax.dynamic_slice_in_dim(vector, patch_index * length, length)

    return (
        block_out,
        input_grad,
        summed[0],
        summed[1],
        weights[0],
        own_slice(summed[2]),
        weights[1],
        own_slice(summed[3]),
        own_slice(summed[4]),
        weights[2],
        own_slice(summed[5]),
        weights[3],
        own_slice(summed[6]),
        weights[4],
        own_slice(summed[7]),
        weights[5],
        own_slice(summed[8]),
        weights[6],
        own_slice(summed[9]),
        weights[7],
        own_slice(summed[10]),
    )


def solution(mesh):
    in_specs = (
        P("frame", "patch", None),
        P("frame", "patch", None),
        P(),
        P(),
        P("patch", None),
        P("patch"),
        P("patch", None),
        P("patch"),
        P("patch"),
        P("patch", None),
        P("patch"),
        P("patch", None),
        P("patch"),
        P("patch", None),
        P("patch"),
        P("patch", None),
        P("patch"),
        P("patch", None),
        P("patch"),
        P("patch", None),
        P("patch"),
        P("frame"),
        P("patch"),
        P("patch"),
        P(),
    )
    out_specs = (
        P("frame", "patch", None),
        P("frame", "patch", None),
        P(),
        P(),
        P("patch", None),
        P("patch"),
        P("patch", None),
        P("patch"),
        P("patch"),
        P("patch", None),
        P("patch"),
        P("patch", None),
        P("patch"),
        P("patch", None),
        P("patch"),
        P("patch", None),
        P("patch"),
        P("patch", None),
        P("patch"),
        P("patch", None),
        P("patch"),
    )
    return jax.shard_map(
        on_device, mesh=mesh, in_specs=in_specs, out_specs=out_specs, check_vma=False
    )
```

profile of v0, /device:TPU:0, one launch (start us, length us, event | category | flops | bytes accessed | tf_op | source)
XLA Modules:
  0.0 3064.2 jit_solution(12596796376718076856)
XLA Ops:
  25.2 51.2 %all-reduce.22.cloned.1.call-done = (f32[6912]{0:T(1024)}, f32[1152]{0:T(1024)}, f32[1152]{0:T(1024)}, f32[1152]{0:T(1024)}, f32[1152]{0:T(1024)}, /*index=5*/f3...) async-done(((f32[6912]{0:T(1024)}, f32[1152]{0:T(1024)}, f32[1152]{0:T(1024)}, f32[1152]{0:T(1024)}, f32[1152]{0:T(1024)}, /*index=5*/f32[1152]{0:T(1024)}, ...) | async-done | bytes 78352
  76.4 156.2 %all-gather.11.cloned.1.call-done = f32[1152,6912]{1,0:T(8,128)} async-done(((f32[144,6912]{1,0:T(8,128)}), f32[1152,6912]{1,0:T(8,128)}) %all-gather.11.cloned.1.call-update) | async-done | bytes 31850512 | tf_op jit(solution)/shard_map/all_gather | solution.py:93
  258.0 63.0 %all-gather.13.cloned.1.call-done = f32[1152,3456]{1,0:T(8,128)} async-done(((f32[144,3456]{1,0:T(8,128)}), f32[1152,3456]{1,0:T(8,128)}) %all-gather.13.cloned.1.call-update) | async-done | bytes 15925264 | tf_op jit(solution)/shard_map/all_gather | solution.py:95
  321.0 24.1 fusion.99
  423.4 74.0 %all-gather.29.cloned.1.call-done = f32[4608,1152]{1,0:T(8,128)} async-done(((f32[576,1152]{1,0:T(8,128)}), f32[4608,1152]{1,0:T(8,128)}) %all-gather.29.cloned.1.call-update) | async-done | bytes 21233680 | tf_op jit(solution)/shard_map/all_gather | solution.py:108
  497.4 29.2 fusion.103
  526.5 81.8 %all-gather.15.cloned.1.call-done = f32[20,64,1152]{2,1,0:T(8,128)} async-done(((f32[5,64,1152]{2,1,0:T(8,128)}), f32[20,64,1152]{2,1,0:T(8,128)}) %all-gather.15.cloned.1.call-update) | async-done | bytes 5898256 | tf_op jit(solution)/shard_map/all_gather | solution.py:139
  620.8 97.0 %all-gather.17.cloned.1.call-done = f32[20,64,1152]{2,1,0:T(8,128)} async-done(((f32[5,64,1152]{2,1,0:T(8,128)}), f32[20,64,1152]{2,1,0:T(8,128)}) %all-gather.17.cloned.1.call-update) | async-done | bytes 5898256 | tf_op jit(solution)/shard_map/all_gather | solution.py:138
  730.1 31.2 %fusion.44 = (f32[64,16,5]{2,1,0:T(8,128)S(1)}, f32[64,16,5,20]{3,2,1,0:T(8,128)S(1)}) fusion(f32[16,5,20]{2,1,0:T(8,128)S(1)} %broadcast_multiply_fusion.3, pred[20]{0:T(512)(128)(4,1)S(1)} %broadcast_compare_fusion.1, f32[20,64,16,72]{3,2,1,0:T(8,128)} %reshape.332, f32[5,64,16,72]{3,2,1,0:T(8,128)} %reshape.330), kind=kOutput, calls=%fused_computation.60 | convolution fusion | flops 88878080 | bytes 7809300 | tf_op jit(solution)/shard_map/fchd,schd->chfs/dot_general | solution.py:23
  889.8 67.3 %all-gather.27.cloned.1.call-done = f32[1152,4608]{1,0:T(8,128)} async-done(((f32[144,4608]{1,0:T(8,128)}), f32[1152,4608]{1,0:T(8,128)}) %all-gather.27.cloned.1.call-update) | async-done | bytes 21233680 | tf_op jit(solution)/shard_map/all_gather | solution.py:106
  957.1 33.7 %fusion.90 = (f32[4608]{0:T(1024)}, f32[320,4608]{1,0:T(8,128)}, f32[320,4608]{1,0:T(8,128)}) fusion(f32[320,4608]{1,0:T(8,128)} %fusion.103, f32[4608]{0:T(1024)S(1)} %copy-done.83, f32[320,1152]{1,0:T(8,128)} %bitcast.210, f32[1152,4608]{1,0:T(8,128)} %all-gather.27.cloned.1.call-done), kind=kOutput, calls=%fused_computation.153 | convolution fusion | flops 20415279104 | bytes 40439808 | tf_op jit(solution)/shard_map/dot_general | solution.py:19
  992.0 28.1 multiply_reduce_fusion.8
  1106.2 26.6 fusion.31
  1159.4 30.8 %subtract_multiply_fusion = f32[64,16,5,20]{3,2,1,0:T(8,128)S(1)} fusion(f32[64,16,5]{2,1,0:T(8,128)S(1)} %bitcast.226, f32[20,64,16,72]{3,2,1,0:T(8,128)} %reshape.329, f32[5,64,16,72]{3,1,2,0:T(8,128)S(1)} %copy-done.43, f32[64,16,5]{2,1,0:T(8,128)} %copy-done.54, f32[64,16,5]{2,1,0:T(8,128)S(1)} %copy-done.46, ...), kind=kOutput, calls=%fused_computation.46 | convolution fusion | flops 89190400 | bytes 8259860 | tf_op jit(solution)/shard_map/fchd,schd->chfs/dot_general | solution.py:23
  1192.2 22.9 multiply_bitcast_fusion
  1263.1 22.3 convolution_bitcast_fusion
  1338.8 39.2 %fusion.109 = f32[1152,4608]{1,0:T(8,128)} fusion(f32[320,1152]{1,0:T(8,128)} %bitcast.211, f32[320,4608]{1,0:T(8,128)} %get-tuple-element.122), kind=kOutput, calls=%fused_computation.171 | convolution fusion | flops 20384317440 | bytes 28606464 | tf_op jit(solution)/shard_map/dot_general | solution.py:19
  1378.1 42.0 %fusion.43 = f32[4608,1152]{1,0:T(8,128)} fusion(f32[320,1152]{1,0:T(8,128)} %bitcast.191, f32[320,4608]{1,0:T(8,128)} %get-tuple-element.149), kind=kOutput, calls=%fused_computation.59 | convolution fusion | flops 20396113920 | bytes 28606464 | tf_op jit(solution)/shard_map/dot_general | solution.py:19
  1420.2 22.7 fusion.98
  1448.4 32.4 %fusion.38 = f32[1152,3456]{1,0:T(8,128)} fusion(f32[320,1152]{1,0:T(8,128)} %bitcast.193, f32[320,1152]{1,0:T(8,128)} %bitcast.198, f32[320,1152]{1,0:T(8,128)} %bitcast.217, f32[320,1152]{1,0:T(8,128)} %reshape.346), kind=kOutput, calls=%fused_computation.52 | convolution fusion | flops 15290449920 | bytes 21823488 | tf_op jit(solution)/shard_map/dot_general | solution.py:19
  1481.4 30.7 %convolution_add_fusion.5 = f32[320,1152]{1,0:T(8,128)} fusion(f32[4608,1152]{1,0:T(8,128)} %all-gather.29.cloned.1.call-done, f32[320,4608]{1,0:T(8,128)} %get-tuple-element.149, f32[1152]{0:T(1024)S(1)} %copy-done.84), kind=kOutput, calls=%fused_computation.58 | convolution fusion | flops 20396482560 | bytes 28611072 | tf_op jit(solution)/shard_map/dot_general | solution.py:19
  1513.6 22.6 multiply_reduce_fusion.6
  1546.4 29.5 fusion.82
  1582.2 32.0 %fusion.61 = f32[4,1152]{1,0:T(4,128)} fusion(f32[4,1152]{1,0:T(4,128)S(1)} %copy-done.57, f32[4,6912]{1,0:T(4,128)S(1)} %get-tuple-element.156, f32[1152,6912]{1,0:T(8,128)} %all-gather.11.cloned.1.call-done), kind=kOutput, calls=%fused_computation.104 | convolution fusion | flops 382247424 | bytes 31997952 | tf_op jit(solution)/shard_map/dot_general | solution.py:19
  1633.4 140.7 %reduce-scatter.27.cloned.1.call-done = f32[144,4608]{1,0:T(8,128)} async-done(((f32[1152,4608]{1,0:T(8,128)}), f32[144,4608]{1,0:T(8,128)}) %reduce-scatter.27.cloned.1.call-update) | async-done | bytes 2654224 | tf_op jit(solution)/shard_map/reduce_scatter | solution.py:274
  1774.1 140.8 %reduce-scatter.29.cloned.1.call-done = f32[576,1152]{1,0:T(8,128)} async-done(((f32[4608,1152]{1,0:T(8,128)}), f32[576,1152]{1,0:T(8,128)}) %reduce-scatter.29.cloned.1.call-update) | async-done | bytes 2654224 | tf_op jit(solution)/shard_map/reduce_scatter | solution.py:275
  1914.9 116.4 %reduce-scatter.19.cloned.1.call-done = f32[144,3456]{1,0:T(8,128)} async-done(((f32[1152,3456]{1,0:T(8,128)}), f32[144,3456]{1,0:T(8,128)}) %reduce-scatter.19.cloned.1.call-update) | async-done | bytes 1990672 | tf_op jit(solution)/shard_map/reduce_scatter | solution.py:269
  2031.3 202.7 %reduce-scatter.17.cloned.1.call-done = f32[144,6912]{1,0:T(8,128)} async-done(((f32[1152,6912]{1,0:T(8,128)}), f32[144,6912]{1,0:T(8,128)}) %reduce-scatter.17.cloned.1.call-update) | async-done | bytes 3981328 | tf_op jit(solution)/shard_map/reduce_scatter | solution.py:268
  2234.1 41.3 %fusion.35 = f32[480,1152]{1,0:T(8,128)} fusion(f32[1152,2304]{1,0:T(8,128)} %all-gather.21.cloned.1.call-done, f32[480,1152]{0,1:T(8,128)} %bitcast.206, f32[480,1152]{0,1:T(8,128)} %bitcast.208), kind=kOutput, calls=%fused_computation.49 | convolution fusion | flops 15289344000 | bytes 17252352 | tf_op jit(solution)/shard_map/dot_general | solution.py:19
  2275.5 93.6 %all-reduce.20.cloned.1.call-done = (f32[4,1152]{1,0:T(4,128)}, f32[6912]{0:T(1024)}, f32[1152]{0:T(1024)}, f32[1152]{0:T(1024)}, f32[1152]{0:T(1024)}, /*index=...) async-done(((f32[4,1152]{1,0:T(4,128)}, f32[6912]{0:T(1024)}, f32[1152]{0:T(1024)}, f32[1152]{0:T(1024)}, f32[1152]{0:T(1024)}, ...) | async-done | bytes 96784 | tf_op jit(solution)/shard_map/psum | solution.py:350
  2381.1 521.3 %all-reduce.24.cloned.1.call-done = (f32[144,6912]{1,0:T(8,128)}, f32[144,3456]{1,0:T(8,128)}, f32[144,1152]{1,0:T(8,128)}, f32[144,1152]{1,0:T(8,128)}, f32[144...) async-done(((f32[144,6912]{1,0:T(8,128)}, f32[144,3456]{1,0:T(8,128)}, f32[144,1152]{1,0:T(8,128)}, f32[144,1152]{1,0:T(8,128)}, ...) | async-done | bytes 14598160 | tf_op jit(solution)/shard_map/psum | solution.py:277
  2905.2 136.8 %all-reduce.18.cloned.1.call-done = f32[4,120,1152]{2,1,0:T(8,128)} async-done(((f32[4,120,1152]{2,1,0:T(8,128)}), f32[4,120,1152]{2,1,0:T(8,128)}) %all-reduce.18.cloned.1.call-update) | async-done | bytes 2211856 | tf_op jit(solution)/shard_map/psum | solution.py:350
  (397 shorter events, 561.7 us)
Async XLA Ops:
  7.2 379.5 %copy-start = (f32[4,120,1152]{2,1,0:T(8,128)S(1)}, f32[4,120,1152]{2,1,0:T(8,128)}, u32[]{:S(2)}) copy-start(f32[4,120,1152]{2,1,0:T(8,128)} %param.27) | copy-start | bytes 6635524
  7.2 69.2 %all-reduce.22.cloned.1.call-start = ((), (), s32[]{:S(2)}) async-start(), calls=%async_computation.32 | async-start | bytes 212992
  19.2 213.4 %all-gather.11.cloned.1.call-start = ((), (), s32[]{:S(2)}) async-start(), calls=%async_computation.10 | async-start | bytes 35831808 | tf_op jit(solution)/shard_map/all_gather | solution.py:93
  20.0 301.0 %all-gather.13.cloned.1.call-start = ((), (), s32[]{:S(2)}) async-start(), calls=%async_computation.11 | async-start | bytes 17915904 | tf_op jit(solution)/shard_map/all_gather | solution.py:95
  20.7 366.0 %all-gather.21.cloned.1.call-start = ((), (), s32[]{:S(2)}) async-start(), calls=%async_computation.15 | async-start | bytes 11943936 | tf_op jit(solution)/shard_map/all_gather | solution.py:102
  21.3 211.3 %copy-start.56 = (f32[4,1152]{1,0:T(4,128)S(1)}, f32[4,1152]{1,0:T(4,128)}, u32[]{:S(2)}) copy-start(f32[4,1152]{1,0:T(4,128)} %param.28) | copy-start | bytes 55300
  21.3 476.0 %all-gather.29.cloned.1.call-start = ((), (), s32[]{:S(2)}) async-start(), calls=%async_computation.19 | async-start | bytes 23887872 | tf_op jit(solution)/shard_map/all_gather | solution.py:108
  21.9 586.4 %all-gather.15.cloned.1.call-start = ((), (), s32[]{:S(2)}) async-start(), calls=%async_computation.12 | async-start | bytes 7372800 | tf_op jit(solution)/shard_map/all_gather | solution.py:139
  22.0 1001.0 %copy-start.72 = (f32[64]{0:T(128)}, f32[64]{0:T(128)S(1)}, u32[]{:S(2)}) copy-start(f32[64]{0:T(128)S(1)} %convert_element_type.14) | copy-start | bytes 772
  23.5 232.4 %copy-start.59 = (f32[5,64]{1,0:T(8,128)}, f32[5,64]{1,0:T(8,128)S(1)}, u32[]{:S(2)}) copy-start(f32[5,64]{1,0:T(8,128)S(1)} %broadcast_multiply_fusion.7) | copy-start | bytes 3844
  25.2 230.7 %copy-start.62 = (f32[5,64]{1,0:T(8,128)}, f32[5,64]{1,0:T(8,128)S(1)}, u32[]{:S(2)}) copy-start(f32[5,64]{1,0:T(8,128)S(1)} %add_rsqrt_fusion.1) | copy-start | bytes 3844
  255.9 164.3 %copy-start.40 = (f32[64,1152]{1,0:T(8,128)}, f32[64,1152]{1,0:T(8,128)S(1)}, u32[]{:S(2)}) copy-start(f32[64,1152]{1,0:T(8,128)S(1)} %get-tuple-element.137) | copy-start | bytes 884740
  255.9 544.3 %copy-start.37 = (f32[64,1152]{1,0:T(8,128)}, f32[64,1152]{1,0:T(8,128)S(1)}, u32[]{:S(2)}) copy-start(f32[64,1152]{1,0:T(8,128)S(1)} %get-tuple-element.138) | copy-start | bytes 884740
  347.3 370.4 %all-gather.17.cloned.1.call-start = ((), (), s32[]{:S(2)}) async-start(), calls=%async_computation.13 | async-start | bytes 7372800 | tf_op jit(solution)/shard_map/all_gather | solution.py:138
  348.1 442.2 %all-gather.19.cloned.1.call-start = ((), (), s32[]{:S(2)}) async-start(), calls=%async_computation.14 | async-start | bytes 5971968 | tf_op jit(solution)/shard_map/all_gather | solution.py:98
  348.9 454.1 %all-gather.23.cloned.1.call-start = ((), (), s32[]{:S(2)}) async-start(), calls=%async_computation.16 | async-start | bytes 5971968 | tf_op jit(solution)/shard_map/all_gather | solution.py:100
  349.6 527.5 %all-gather.25.cloned.1.call-start = ((), (), s32[]{:S(2)}) async-start(), calls=%async_computation.17 | async-start | bytes 5971968 | tf_op jit(solution)/shard_map/all_gather | solution.py:104
  350.2 606.9 %all-gather.27.cloned.1.call-start = ((), (), s32[]{:S(2)}) async-start(), calls=%async_computation.18 | async-start | bytes 23887872 | tf_op jit(solution)/shard_map/all_gather | solution.py:106
  350.9 1097.4 %reduce-scatter.15.cloned.1.call-start = ((), (), s32[]{:S(2)}) async-start(), calls=%async_computation.21 | async-start | bytes 7372800 | tf_op jit(solution)/shard_map/reduce_scatter | solution.py:238
  1153.6 294.7 %reduce-scatter.13.cloned.1.call-start = ((), (), s32[]{:S(2)}) async-start(), calls=%async_computation.20 | async-start | bytes 7372800 | tf_op jit(solution)/shard_map/reduce_scatter | solution.py:237
  1236.0 378.3 %reduce-scatter.31.cloned.1.call-start = ((), (), s32[]{:S(2)}) async-start(), calls=%async_computation.30 | async-start | bytes 11943936
  1298.3 318.8 %reduce-scatter.21.cloned.1.call-start = ((), (), s32[]{:S(2)}) async-start(), calls=%async_computation.25 | async-start | bytes 5971968 | tf_op jit(solution)/shard_map/reduce_scatter | solution.py:270
  1310.7 306.4 %reduce-scatter.23.cloned.1.call-start = ((), (), s32[]{:S(2)}) async-start(), calls=%async_computation.26 | async-start | bytes 5971968 | tf_op jit(solution)/shard_map/reduce_scatter | solution.py:271
  1326.5 307.0 %reduce-scatter.25.cloned.1.call-start = ((), (), s32[]{:S(2)}) async-start(), calls=%async_computation.27 | async-start | bytes 5971968 | tf_op jit(solution)/shard_map/reduce_scatter | solution.py:273
  1338.7 435.4 %reduce-scatter.27.cloned.1.call-start = ((), (), s32[]{:S(2)}) async-start(), calls=%async_computation.28 | async-start | bytes 23887872 | tf_op jit(solution)/shard_map/reduce_scatter | solution.py:274
  1378.0 536.9 %reduce-scatter.29.cloned.1.call-start = ((), (), s32[]{:S(2)}) async-start(), calls=%async_computation.29 | async-start | bytes 23887872 | tf_op jit(solution)/shard_map/reduce_scatter | solution.py:275
  1420.1 611.2 %reduce-scatter.19.cloned.1.call-start = ((), (), s32[]{:S(2)}) async-start(), calls=%async_computation.24 | async-start | bytes 17915904 | tf_op jit(solution)/shard_map/reduce_scatter | solution.py:269
  1480.8 753.3 %reduce-scatter.17.cloned.1.call-start = ((), (), s32[]{:S(2)}) async-start(), calls=%async_computation.23 | async-start | bytes 35831808 | tf_op jit(solution)/shard_map/reduce_scatter | solution.py:268
  1576.0 793.0 %all-reduce.20.cloned.1.call-start = ((), (), s32[]{:S(2)}) async-start(), calls=%async_computation.31 | async-start | bytes 249856 | tf_op jit(solution)/shard_map/psum | solution.py:350
  1614.2 1288.3 %all-reduce.24.cloned.1.call-start = ((), (), s32[]{:S(2)}) async-start(), calls=%async_computation.33 | async-start | bytes 31260672 | tf_op jit(solution)/shard_map/psum | solution.py:277
  2234.1 807.9 %all-reduce.18.cloned.1.call-start = ((), (), s32[]{:S(2)}) async-start(), calls=%async_computation.22 | async-start | bytes 4423680 | tf_op jit(solution)/shard_map/psum | solution.py:350
  2905.2 140.0 %copy-start.71 = (f32[4,1152]{1,0:T(4,128)S(1)}, f32[4,1152]{1,0:T(4,128)}, u32[]{:S(2)}) copy-start(f32[4,1152]{1,0:T(4,128)} %get-tuple-element.164) | copy-start | bytes 55300
  (91 other events, 991.7 us)
Sparse Core Ops, SparseCore 0:
  19.4 56.9 all-reduce.21
  78.4 154.1 all-gather.10
  234.7 86.2 all-gather.12
  322.9 63.8 all-gather.20
  388.6 108.6 all-gather.28
  499.4 108.8 all-gather.14
  610.6 107.1 all-gather.16
  719.8 39.6 all-gather.18
  761.5 41.3 all-gather.22
  804.9 41.3 all-gather.24
  848.3 108.6 all-gather.26
  1153.7 104.3 reduce-scatter.14
  1260.6 104.8 reduce-scatter.12
  1369.3 82.6 reduce-scatter.30
  1455.6 56.9 reduce-scatter.20
  1515.9 56.9 reduce-scatter.22
  1576.5 56.9 reduce-scatter.24
  1636.9 137.1 reduce-scatter.26
  1777.7 137.1 reduce-scatter.28
  1918.4 112.8 reduce-scatter.18
  2035.4 198.5 reduce-scatter.16
  2241.6 127.3 all-reduce.19
  2373.5 528.8 all-reduce.23
  2908.4 133.5 all-reduce.17
where the time goes:
time: 3070 us; the launch traced here: 3060 us
  waiting for transfers between devices  1990 us (65%)
  matrix products  781 us (25%)
  local copies, waits for them, and re-layouts  189 us (6%)
  other arithmetic  75.4 us (2%)
    dot_general x26, matrix products, matmul(): return jnp.dot(left, right, precision=BEST)  559 us
    psum x1, waiting for transfers between devices, plan_rows(): lax.psum((shares[0], shares[1], shares[2], shares[3], shares[4], shares[5...  521 us
    psum x2, waiting for transfers between devices, on_device(): lax.psum((caption_part, cond_part, biases[0], biases[1], biases[2], biase...  230 us
    reduce_scatter x1, waiting for transfers between devices, plan_rows(): lax.psum_scatter(grad_w_ada, 'patch', scatter_dimension=0, tiled=True)  203 us
    dot_general x8, matrix products, contract(): return jnp.einsum(form, left, right, precision=BEST)  178 us
    all_gather x1, waiting for transfers between devices, plan_rows(): lax.all_gather(ada_weight, 'patch', axis=0, tiled=True)  156 us
    reduce_scatter x1, waiting for transfers between devices, plan_rows(): lax.psum_scatter(grad_w_second, 'patch', scatter_dimension=0, tiled=True)  141 us
    reduce_scatter x1, waiting for transfers between devices, plan_rows(): lax.psum_scatter(grad_w_first, 'patch', scatter_dimension=0, tiled=True)  141 us
  transfers between devices with their start and end apart: 24, of which 17 were waited for; matrix products, arithmetic and copies ran while one was open for 26% of the time, Pallas kernels for 0%

commit v1 on v0

v1 whole, which is shorter than its diff:
```python
from functools import partial

import jax
import jax.numpy as jnp
from jax import lax
from jax.sharding import PartitionSpec as P

H = 16
CAP = 120
FRAMES = 17
CLIPS = 4


EPSILON = 1e-06
BEST = lax.Precision.HIGH


def matmul(left, right):
    return jnp.dot(left, right, precision=BEST)


def contract(form, left, right):
    return jnp.einsum(form, left, right, precision=BEST)


def matmul_nt(left, right):
    return lax.dot_general(left, right, (((1,), (1,)), ((), ())), precision=BEST)


def matmul_tn(left, right):
    return lax.dot_general(left, right, (((0,), (0,)), ((), ())), precision=BEST)


def normalize(rows):
    average = jnp.mean(rows, axis=-1, keepdims=True)
    centred = rows - average
    spread = jnp.mean(centred * centred, axis=-1, keepdims=True)
    inverse = lax.rsqrt(spread + EPSILON)
    return (centred * inverse, inverse)


def normalize_back(grad_normed, normed, inverse):
    first_mean = jnp.mean(grad_normed, axis=-1, keepdims=True)
    second_mean = jnp.mean(grad_normed * normed, axis=-1, keepdims=True)
    return inverse * (grad_normed - first_mean - normed * second_mean)


def softmax_rows(scores, allowed):
    masked = jnp.where(allowed, scores, -1e30)
    highest = jnp.max(masked, axis=-1, keepdims=True)
    exponent = jnp.exp(masked - highest)
    return exponent / jnp.sum(exponent, axis=-1, keepdims=True)


def swap(value, axis, bit):
    size = lax.axis_size(axis)
    return lax.ppermute(value, axis, [(i, i ^ bit) for i in range(size)])


def all_sum(value, axis):
    bit = 1
    while bit < lax.axis_size(axis):
        value = value + swap(value, axis, bit)
        bit *= 2
    return value


def placed(vector, axis):
    length = vector.shape[-1]
    whole = jnp.zeros(vector.shape[:-1] + (length * lax.axis_size(axis),), vector.dtype)
    return lax.dynamic_update_slice_in_dim(
        whole, vector, lax.axis_index(axis) * length, axis=vector.ndim - 1
    )


def own_part(array, axis, dim):
    length = array.shape[dim] // lax.axis_size(axis)
    return lax.dynamic_slice_in_dim(array, lax.axis_index(axis) * length, length, axis=dim)


def gather_rows(shard):
    return lax.all_gather(shard, "patch", axis=0, tiled=True)


def scatter_rows(whole):
    return lax.psum_scatter(whole, "patch", scatter_dimension=0, tiled=True)


def on_device(
    block_input,
    out_cotangent,
    caption,
    cond,
    ada_weight,
    ada_bias,
    qkv_weight,
    q_bias,
    v_bias,
    attn_out_weight,
    attn_out_bias,
    cross_q_weight,
    cross_q_bias,
    cross_kv_weight,
    cross_v_bias,
    cross_out_weight,
    cross_out_bias,
    fc1_weight,
    fc1_bias,
    fc2_weight,
    fc2_bias,
    frame_slot,
    clip_id,
    patch_mask,
    caption_mask,
):
    width = block_input.shape[-1]
    head_dim = width // H
    scaling = head_dim ** (-0.5)
    to_columns = partial(
        lax.all_to_all, axis_name="frame", split_axis=1, concat_axis=0, tiled=True
    )
    to_slots = partial(
        lax.all_to_all, axis_name="frame", split_axis=0, concat_axis=1, tiled=True
    )
    tokens_in = to_columns(block_input)
    cotangent = to_columns(out_cotangent)
    slots, cols, _ = tokens_in.shape
    rows = slots * cols
    clip_own = own_part(clip_id, "frame", 0)
    column_mask = own_part(patch_mask, "frame", 0).astype(jnp.float32)[:, None]
    frame_pos = all_sum(placed(frame_slot.astype(jnp.float32), "frame"), "frame")

    cond_act, silu_pull = jax.vjp(jax.nn.silu, cond)
    cond_own = own_part(cond_act, "patch", 1)
    modulation_part = matmul(cond_own, ada_weight)
    biases = (ada_bias, q_bias, v_bias, attn_out_bias, cross_q_bias, cross_v_bias, cross_out_bias, fc2_bias)
    small = all_sum(
        jnp.concatenate(
            [modulation_part.reshape(-1)] + [placed(b, "patch") for b in biases]
        ),
        "patch",
    )
    place = modulation_part.size
    modulation = small[:place].reshape(modulation_part.shape)
    whole = []
    for b in biases:
        length = b.shape[0] * lax.axis_size("patch")
        whole.append(small[place : place + length])
        place += length
    b_ada, b_query, b_value, b_attn, b_cross_q, b_cross_v, b_cross_o, b_second = whole
    modulation = modulation + b_ada
    clip_onehot = (clip_own[:, None] == jnp.arange(CLIPS, dtype=jnp.int32)[None, :]).astype(
        jnp.float32
    )
    per_column = jnp.dot(clip_onehot, modulation, precision=lax.Precision.HIGHEST)
    shift_one, scale_one, gate_one, shift_two, scale_two, gate_two = jnp.split(
        per_column, 6, axis=1
    )

    caption_rows = caption.reshape(CLIPS * CAP, width)
    caption_share = own_part(own_part(caption_rows, "frame", 0), "patch", 1)
    caption_kv_share = lax.psum(matmul(caption_share, cross_kv_weight), "patch")
    caption_kv = lax.all_gather(caption_kv_share, "frame", axis=0, tiled=True)
    cross_keys = caption_kv[:, :width].reshape(CLIPS * CAP, H, head_dim)
    cross_values = (caption_kv[:, width:] + b_cross_v).reshape(CLIPS * CAP, H, head_dim)

    w_qkv = gather_rows(qkv_weight)
    w_attn = gather_rows(attn_out_weight)
    w_cross_q = gather_rows(cross_q_weight)
    w_cross_o = gather_rows(cross_out_weight)
    w_first = lax.all_to_all(fc1_weight, "patch", 1, 0, tiled=True)
    grad_mlp = (column_mask * gate_two * cotangent).reshape(rows, width)
    grad_mlp_all = gather_rows(grad_mlp)

    normed_one, inverse_one = normalize(tokens_in)
    hidden_one = (normed_one * (1.0 + scale_one) + shift_one).reshape(rows, width)
    qkv_rows = matmul(hidden_one, w_qkv)
    queries = (qkv_rows[:, :width] + b_query).reshape(slots, cols, H, head_dim)
    keys = qkv_rows[:, width : 2 * width].reshape(slots, cols, H, head_dim)
    values = (qkv_rows[:, 2 * width :] + b_value).reshape(slots, cols, H, head_dim)
    slopes = 2.0 ** (-8.0 * (jnp.arange(H).astype(jnp.float32) + 1.0) / H)
    distance = jnp.abs(frame_pos[:, None] - frame_pos[None, :])
    bias_table = -slopes[:, None, None] * distance[None]
    key_valid = (frame_pos < FRAMES - 0.5)[None, None, None, :]
    scores = contract("fchd,schd->chfs", queries, keys) * scaling + bias_table[None]
    probs = softmax_rows(scores, key_valid)
    attended = contract("chfs,schd->fchd", probs, values)
    attended_rows = attended.reshape(rows, width)
    attn_branch = (matmul(attended_rows, w_attn) + b_attn).reshape(slots, cols, width)
    after_attn = tokens_in + column_mask * gate_one * attn_branch
    after_attn_rows = after_attn.reshape(rows, width)
    cross_queries = (matmul(after_attn_rows, w_cross_q) + b_cross_q).reshape(
        slots, cols, H, head_dim
    )
    key_clip = jnp.arange(CLIPS * CAP, dtype=jnp.int32) // CAP
    caption_ok = (
        (clip_own[:, None] == key_clip[None, :]) & (caption_mask.reshape(CLIPS * CAP)[None, :] > 0)
    )[None, :, None, :]
    cross_scores = contract("fchd,khd->fchk", cross_queries, cross_keys) * scaling
    cross_probs = softmax_rows(cross_scores, caption_ok)
    cross_att = contract("fchk,khd->fchd", cross_probs, cross_values)
    cross_rows = cross_att.reshape(rows, width)
    cross_branch = (matmul(cross_rows, w_cross_o) + b_cross_o).reshape(slots, cols, width)
    after_cross = after_attn + column_mask * cross_branch
    normed_two, inverse_two = normalize(after_cross)
    hidden_two = (normed_two * (1.0 + scale_two) + shift_two).reshape(rows, width)

    hidden_all = gather_rows(hidden_two)
    pre_act = matmul(hidden_all, w_first) + fc1_bias
    activated, gelu_pull = jax.vjp(partial(jax.nn.gelu, approximate=True), pre_act)
    grad_pre = gelu_pull(matmul_nt(grad_mlp_all, fc2_weight))[0]
    grad_hidden_two = scatter_rows(matmul_nt(grad_pre, w_first)).reshape(slots, cols, width)
    mlp_sum = scatter_rows(matmul(activated, fc2_weight))
    grad_w_second = lax.psum(matmul_tn(activated, grad_mlp_all), "frame")
    grad_w_first = lax.psum(
        lax.all_to_all(matmul_tn(hidden_all, grad_pre), "patch", 0, 1, tiled=True), "frame"
    )
    grad_b_first = all_sum(jnp.sum(grad_pre, axis=0), "frame")
    mlp_branch = (mlp_sum + b_second).reshape(slots, cols, width)
    block_out = to_slots(after_cross + column_mask * gate_two * mlp_branch)
    grad_gate_two = jnp.sum(column_mask * mlp_branch * cotangent, axis=0)
    grad_b_second = jnp.sum(grad_mlp, axis=0)

    grad_shift_two = jnp.sum(grad_hidden_two, axis=0)
    grad_scale_two = jnp.sum(grad_hidden_two * normed_two, axis=0)
    grad_after_cross = cotangent + normalize_back(
        grad_hidden_two * (1.0 + scale_two), normed_two, inverse_two
    )
    grad_cross_branch = (column_mask * grad_after_cross).reshape(rows, width)
    grad_w_cross_o = matmul_tn(cross_rows, grad_cross_branch)
    grad_b_cross_o = jnp.sum(grad_cross_branch, axis=0)
    grad_cross_att = matmul_nt(grad_cross_branch, w_cross_o).reshape(slots, cols, H, head_dim)
    cross_row_terms = jnp.sum(grad_cross_att * cross_att, axis=-1)[..., None]
    grad_cross_probs = contract("fchd,khd->fchk", grad_cross_att, cross_values)
    grad_cross_scores = cross_probs * (grad_cross_probs - cross_row_terms) * scaling
    grad_cross_queries = contract("fchk,khd->fchd", grad_cross_scores, cross_keys).reshape(
        rows, width
    )
    grad_cross_keys = contract("fchk,fchd->khd", grad_cross_scores, cross_queries).reshape(
        CLIPS * CAP, width
    )
    grad_cross_values = contract("fchk,fchd->khd", cross_probs, grad_cross_att).reshape(
        CLIPS * CAP, width
    )
    grad_kv = jnp.concatenate([grad_cross_keys, grad_cross_values], axis=1)
    grad_kv_share = lax.psum(
        lax.psum_scatter(grad_kv, "frame", scatter_dimension=0, tiled=True), "patch"
    )
    grad_w_cross_kv = lax.psum(matmul_tn(caption_share, grad_kv_share), "frame")
    grad_b_cross_v = jnp.sum(grad_kv_share[:, width:], axis=0)
    grad_caption_share = lax.all_gather(
        matmul_nt(grad_kv_share, cross_kv_weight), "patch", axis=1, tiled=True
    )
    grad_caption = lax.all_gather(grad_caption_share, "frame", axis=0, tiled=True).reshape(
        caption.shape
    )
    grad_w_cross_q = matmul_tn(after_attn_rows, grad_cross_queries)
    grad_b_cross_q = jnp.sum(grad_cross_queries, axis=0)
    grad_after_attn = grad_after_cross + matmul_nt(grad_cross_queries, w_cross_q).reshape(
        slots, cols, width
    )
    grad_attn_rows = (column_mask * gate_one * grad_after_attn).reshape(rows, width)
    grad_gate_one = jnp.sum(column_mask * attn_branch * grad_after_attn, axis=0)
    grad_w_attn = matmul_tn(attended_rows, grad_attn_rows)
    grad_b_attn = jnp.sum(grad_attn_rows, axis=0)
    grad_attended = matmul_nt(grad_attn_rows, w_attn).reshape(slots, cols, H, head_dim)
    row_terms = jnp.transpose(jnp.sum(grad_attended * attended, axis=-1), (1, 2, 0))[..., None]
    grad_probs = contract("fchd,schd->chfs", grad_attended, values)
    grad_scores = probs * (grad_probs - row_terms)
    grad_queries = (contract("chfs,schd->fchd", grad_scores, keys) * scaling).reshape(rows, width)
    grad_keys = (contract("chfs,fchd->schd", grad_scores, queries) * scaling).reshape(rows, width)
    grad_values = contract("chfs,fchd->schd", probs, grad_attended).reshape(rows, width)
    grad_qkv = jnp.concatenate([grad_queries, grad_keys, grad_values], axis=1)
    grad_w_qkv = matmul_tn(hidden_one, grad_qkv)
    grad_b_query = jnp.sum(grad_queries, axis=0)
    grad_b_value = jnp.sum(grad_values, axis=0)
    grad_hidden_one = matmul_nt(grad_qkv, w_qkv).reshape(slots, cols, width)
    grad_shift_one = jnp.sum(grad_hidden_one, axis=0)
    grad_scale_one = jnp.sum(grad_hidden_one * normed_one, axis=0)
    input_grad = to_slots(
        grad_after_attn
        + normalize_back(grad_hidden_one * (1.0 + scale_one), normed_one, inverse_one)
    )
    grad_per_column = jnp.concatenate(
        [
            grad_shift_one,
            grad_scale_one,
            grad_gate_one,
            grad_shift_two,
            grad_scale_two,
            grad_gate_two,
        ],
        axis=1,
    )
    grad_modulation_part = jnp.dot(
        clip_onehot.T, grad_per_column, precision=lax.Precision.HIGHEST
    )
    first = (lax.axis_index("patch") == 0).astype(jnp.float32)
    bias_grads = (
        grad_b_query,
        grad_b_value,
        grad_b_attn,
        grad_b_cross_q,
        grad_b_cross_v * first,
        grad_b_cross_o,
        grad_b_second,
    )
    small_grads = all_sum(
        all_sum(
            jnp.concatenate([grad_modulation_part.reshape(-1)] + list(bias_grads)), "patch"
        ),
        "frame",
    )
    place = grad_modulation_part.size
    grad_modulation = small_grads[:place].reshape(grad_modulation_part.shape)
    own_biases = []
    for b in bias_grads:
        own_biases.append(own_part(small_grads[place : place + b.shape[0]], "patch", 0))
        place += b.shape[0]
    g_query, g_value, g_attn, g_cross_q, g_cross_v, g_cross_o, g_second = own_biases
    grad_w_ada = matmul_tn(cond_own, grad_modulation)
    grad_b_ada = own_part(jnp.sum(grad_modulation, axis=0), "patch", 0)
    grad_cond_act = all_sum(placed(matmul_nt(grad_modulation, ada_weight), "patch"), "patch")
    grad_cond = silu_pull(grad_cond_act)[0]

    def finish(whole_grad):
        return lax.psum(scatter_rows(whole_grad), "frame")

    return (
        block_out,
        input_grad,
        grad_caption,
        grad_cond,
        grad_w_ada,
        grad_b_ada,
        finish(grad_w_qkv),
        g_query,
        g_value,
        finish(grad_w_attn),
        g_attn,
        finish(grad_w_cross_q),
        g_cross_q,
        grad_w_cross_kv,
        g_cross_v,
        finish(grad_w_cross_o),
        g_cross_o,
        grad_w_first,
        grad_b_first,
        grad_w_second,
        g_second,
    )


def solution(mesh):
    tokens = P("frame", "patch", None)
    weight = P("patch", None)
    vector = P("patch")
    parameters = (
        weight, vector, weight, vector, vector, weight, vector, weight, vector,
        weight, vector, weight, vector, weight, vector, weight, vector,
    )
    in_specs = (tokens, tokens, P(), P()) + parameters + (P("frame"), vector, vector, P())
    out_specs = (tokens, tokens, P(), P()) + parameters
    return jax.shard_map(
        on_device, mesh=mesh, in_specs=in_specs, out_specs=out_specs, check_vma=False
    )
```

time: 3070 us -> 1880 us (0.61)
  waiting for transfers between devices: 1990 us -> 1180 us
  matrix products: 781 us -> 367 us
  blocking collectives: 11.8 us -> 62.8 us
  local copies, waits for them, and re-layouts: 189 us -> 147 us
  starting transfers between devices: 0.96 us -> 41.8 us
    dot_general x26 -> x8, matrix products: 559 us -> 79.3 us  [matmul(): return jnp.dot(left, right, precision=BEST)]
    psum x3, waiting for transfers between devices: 752 us -> 346 us  [the longest x1 285 us: finish(): return lax.psum(scatter_rows(whole_grad), 'frame')]
    all_gather x10 -> x8, waiting for transfers between devices: 562 us -> 192 us  [the longest x6 192 us: gather_rows(): return lax.all_gather(shard, 'patch', axis=0, tiled=True)]
    reduce_scatter x9 -> x6, waiting for transfers between devices: 617 us -> 300 us  [scatter_rows(): return lax.psum_scatter(whole, 'patch', scatter_dimension=0, tiled=True)]
    dot_general x0 -> x18, matrix products: none -> 197 us  [the longest x8 104 us: matmul_tn(): lax.dot_general(left, right, (((0,), (0,)), ((), ())), precision=BEST)]
    ppermute x0 -> x15, waiting for transfers between devices: none -> 192 us  [swap(): return lax.ppermute(value, axis, [(i, i ^ bit) for i in range(size)])]
    dot_general x8 -> x12, matrix products: 178 us -> 90.5 us  [contract(): return jnp.einsum(form, left, right, precision=BEST)]
    all_to_all x0 -> x5, waiting for transfers between devices: none -> 64.8 us  [the longest x1 46.2 us: on_device(): block_out = to_slots(after_cross + column_mask * gate_two * mlp_branch)]
  transfers between devices with their start and end apart: 24 -> 38, of which waited for: 17 -> 23; matrix products, arithmetic and copies ran while one was open for 26% -> 20% of each run, Pallas kernels for 0% -> 0%
where the time goes in v1:
time: 1880 us
  waiting for transfers between devices  1180 us (63%)
  matrix products  367 us (20%)
  local copies, waits for them, and re-layouts  147 us (8%)
  other arithmetic  65.3 us (3%)
  blocking collectives  62.8 us (3%)
  starting transfers between devices  41.8 us (2%)
    reduce_scatter x6, waiting for transfers between devices, scatter_rows(): return lax.psum_scatter(whole, 'patch', scatter_dimension=0, tiled=True)  300 us
    psum x1, waiting for transfers between devices, finish(): return lax.psum(scatter_rows(whole_grad), 'frame')  285 us
    all_gather x6, waiting for transfers between devices, gather_rows(): return lax.all_gather(shard, 'patch', axis=0, tiled=True)  192 us
    ppermute x15, waiting for transfers between devices, swap(): return lax.ppermute(value, axis, [(i, i ^ bit) for i in range(size)])  192 us
    dot_general x8, matrix products, matmul_tn(): lax.dot_general(left, right, (((0,), (0,)), ((), ())), precision=BEST)  104 us
    dot_general x8, matrix products, matmul_nt(): lax.dot_general(left, right, (((1,), (1,)), ((), ())), precision=BEST)  92.4 us
    dot_general x12, matrix products, contract(): return jnp.einsum(form, left, right, precision=BEST)  90.5 us
    unnamed x19, waiting for transfers between devices  83 us
  transfers between devices with their start and end apart: 38, of which 23 were waited for; matrix products, arithmetic and copies ran while one was open for 20% of the time, Pallas kernels for 0%

profile of v1, /device:TPU:0, one launch (start us, length us, event | category | flops | bytes accessed | tf_op | source)
XLA Modules:
  0.0 1877.3 jit_solution(9502814746011153830)
XLA Ops:
  10.6 60.9 %all-reduce.5.cloned.1.call-done = f32[120,2304]{1,0:T(8,128)} async-done(((f32[120,2304]{1,0:T(8,128)}), f32[120,2304]{1,0:T(8,128)}) %all-reduce.5.cloned.1.call-update) | async-done | bytes 1105936 | tf_op jit(solution)/shard_map/psum | solution.py:162
  94.9 105.1 %collective-permute-done.4 = f32[20]{0:T(128)S(1)} collective-permute-done((f32[20]{0:T(128)S(1)}, f32[20]{0:T(128)S(1)}, u32[]{:S(2)}, u32[]{:S(2)}) %collective-permute-start.4) | collective-permute-done | bytes 112 | tf_op jit(solution)/shard_map/ppermute | solution.py:57
  233.2 60.3 %all-gather.9.cloned.1.call-done = f32[1152,3456]{1,0:T(8,128)} async-done(((f32[144,3456]{1,0:T(8,128)}), f32[1152,3456]{1,0:T(8,128)}) %all-gather.9.cloned.1.call-update) | async-done | bytes 15925264 | tf_op jit(solution)/shard_map/all_gather | solution.py:82
  293.5 14.3 fusion.104
  356.2 23.7 %all-gather.15.cloned.1.call-done = f32[1152,1152]{1,0:T(8,128)} async-done(((f32[144,1152]{1,0:T(8,128)}), f32[1152,1152]{1,0:T(8,128)}) %all-gather.15.cloned.1.call-update) | async-done | bytes 5308432 | tf_op jit(solution)/shard_map/all_gather | solution.py:82
  391.9 9.7 fusion.6
  452.6 52.9 %all_to_all.116 = f32[144,8,576]{2,0,1:T(8,128)} all-to-all(f32[144,8,576]{2,0,1:T(8,128)S(1)} %copy.187), channel_id=1, replica_groups=mesh['patch'=8,'frame'=4] {'patch'}, dimensions={1} | all-to-all | bytes 5308416 | tf_op jit(solution)/shard_map/all_to_all | solution.py:171
  505.5 39.5 %all-gather.19.cloned.1.call-done = f32[2560,1152]{1,0:T(8,128)} async-done(((f32[320,1152]{1,0:T(8,128)}), f32[2560,1152]{1,0:T(8,128)}) %all-gather.19.cloned.1.call-update) | async-done | bytes 11796496 | tf_op jit(solution)/shard_map/all_gather | solution.py:82
  545.0 16.7 fusion.105
  564.2 19.1 %fusion.60 = f32[2560,1152]{1,0:T(8,128)} fusion(f32[576,1152]{1,0:T(8,128)S(1)} %copy-done, f32[2560,576]{0,1:T(8,128)S(1)} %fusion.105, f32[576]{0:T(1024)S(1)} %copy-done.85), kind=kOutput, calls=%fused_computation.99 | convolution fusion | flops 10205429760 | bytes 20351232 | tf_op jit(solution)/shard_map/dot_general | solution.py:19
  591.6 80.0 %reduce-scatter.10.cloned.1.call-done = f32[320,1152]{1,0:T(8,128)} async-done(((f32[2560,1152]{1,0:T(8,128)}), f32[320,1152]{1,0:T(8,128)}) %reduce-scatter.10.cloned.1.call-update) | async-done | bytes 1474576 | tf_op jit(solution)/shard_map/reduce_scatter | solution.py:86
  679.9 68.9 %all-gather.21.cloned.1.call-done = f32[2560,1152]{1,0:T(8,128)} async-done(((f32[320,1152]{1,0:T(8,128)}), f32[2560,1152]{1,0:T(8,128)}) %all-gather.21.cloned.1.call-update) | async-done | bytes 11796496 | tf_op jit(solution)/shard_map/all_gather | solution.py:82
  748.8 18.6 fusion.89
  769.9 29.6 %fusion.106 = f32[2560,1152]{1,0:T(8,128)} fusion(f32[2560,576]{0,1:T(8,128)S(1)} %get-tuple-element.60, f32[1152,576]{1,0:T(8,128)S(1)} %bitcast.252), kind=kOutput, calls=%fused_computation.196 | convolution fusion | flops 10192158720 | bytes 20348928 | tf_op jit(solution)/shard_map/dot_general | solution.py:27
  799.6 88.3 %reduce-scatter.12.cloned.1.call-done = f32[320,1152]{1,0:T(8,128)} async-done(((f32[2560,1152]{1,0:T(8,128)}), f32[320,1152]{1,0:T(8,128)}) %reduce-scatter.12.cloned.1.call-update) | async-done | bytes 1474576 | tf_op jit(solution)/shard_map/reduce_scatter | solution.py:86
  902.6 11.0 fusion.4
  913.6 11.7 fusion.1
  925.3 9.5 fusion.16
  943.5 80.6 %reduce-scatter.22.cloned.1.call-done = f32[120,2304]{1,0:T(8,128)} async-done(((f32[480,2304]{1,0:T(8,128)}), f32[120,2304]{1,0:T(8,128)}) %reduce-scatter.22.cloned.1.call-update) | async-done | bytes 1105936
  1081.7 10.2 multiply_reduce_fusion
  1134.7 17.1 fusion.110
  1154.3 9.9 all_gather.34
  1165.2 33.2 %fusion.114 = f32[1152,576]{1,0:T(8,128)} fusion(f32[2560,1152]{1,0:T(8,128)} %all-gather.19.cloned.1.call-done, f32[2560,576]{0,1:T(8,128)} %copy-done.89), kind=kOutput, calls=%fused_computation.204 | convolution fusion | flops 10192158720 | bytes 20348928 | tf_op jit(solution)/shard_map/dot_general | solution.py:31
  1203.0 20.9 %fusion.59 = f32[576,1152]{1,0:T(8,128)} fusion(f32[2560,1152]{1,0:T(8,128)} %all-gather.21.cloned.1.call-done, f32[2560,576]{0,1:T(8,128)} %copy-done.90, f32[576]{0:T(1024)S(1)} %copy-done.86), kind=kOutput, calls=%fused_computation.98 | convolution fusion | flops 10205429760 | bytes 20351232 | tf_op jit(solution)/shard_map/dot_general | solution.py:31
  1223.9 18.6 all-to-all-done.5
  1254.4 14.8 reduce-scatter.20.cloned.1.call-done
  1269.2 116.8 %reduce-scatter.14.cloned.1.call-done = f32[144,3456]{1,0:T(8,128)} async-done(((f32[1152,3456]{1,0:T(8,128)}), f32[144,3456]{1,0:T(8,128)}) %reduce-scatter.14.cloned.1.call-update) | async-done | bytes 1990672 | tf_op jit(solution)/shard_map/reduce_scatter | solution.py:86
  1392.9 15.9 multiply_reduce_fusion.7
  1413.9 46.2 %all-to-all-done.2 = f32[20,16,1152]{2,1,0:T(8,128)} async-done(((f32[20,16,1152]{2,1,0:T(8,128)}), f32[20,16,1152]{2,1,0:T(8,128)}, u32[]{:S(2)}, u32[]{:S(2)}) %all-to-all-start.2) | async-done | bytes 1474592 | tf_op jit(solution)/shard_map/all_to_all | solution.py:220
  1479.1 30.8 %collective-permute-done.8 = f32[35712]{0:T(1024)S(1)} collective-permute-done((f32[35712]{0:T(1024)S(1)}, f32[35712]{0:T(1024)S(1)}, u32[]{:S(2)}, u32[]{:S(2)}) %collective-permute-start.8) | collective-permute-done | bytes 142880 | tf_op jit(solution)/shard_map/ppermute | solution.py:57
  1514.8 27.2 %collective-permute-done.9 = f32[35712]{0:T(1024)S(1)} collective-permute-done((f32[35712]{0:T(1024)S(1)}, f32[35712]{0:T(1024)S(1)}, u32[]{:S(2)}, u32[]{:S(2)}) %collective-permute-start.9) | collective-permute-done | bytes 142880 | tf_op jit(solution)/shard_map/ppermute | solution.py:57
  1572.9 284.7 %all-reduce.9.cloned.1.call-done = (f32[144,3456]{1,0:T(8,128)}, f32[144,1152]{1,0:T(8,128)}, f32[144,1152]{1,0:T(8,128)}, f32[144,2304]{1,0:T(8,128)}, f32[144,...) async-done(((f32[144,3456]{1,0:T(8,128)}, f32[144,1152]{1,0:T(8,128)}, f32[144,1152]{1,0:T(8,128)}, f32[144,2304]{1,0:T(8,128)}, f32[144,1152]{1,0:T(8,128)}, ...) | async-done | bytes 10616848 | tf_op jit(solution)/shard_map/psum | solution.py:327
  (473 shorter events, 414.6 us)
Async XLA Ops:
  7.2 64.2 %all-reduce.5.cloned.1.call-start = ((), (), s32[]{:S(2)}) async-start(), calls=%async_computation.15 | async-start | bytes 2211840 | tf_op jit(solution)/shard_map/psum | solution.py:162
  10.5 211.8 %all-gather.13.cloned.1.call-start = ((), (), s32[]{:S(2)}) async-start(), calls=%async_computation.16 | async-start | bytes 5529600 | tf_op jit(solution)/shard_map/all_gather | solution.py:163
  71.5 222.0 %all-gather.9.cloned.1.call-start = ((), (), s32[]{:S(2)}) async-start(), calls=%async_computation.13 | async-start | bytes 17915904 | tf_op jit(solution)/shard_map/all_gather | solution.py:82
  72.2 275.4 %all-gather.11.cloned.1.call-start = ((), (), s32[]{:S(2)}) async-start(), calls=%async_computation.14 | async-start | bytes 5971968 | tf_op jit(solution)/shard_map/all_gather | solution.py:82
  72.9 307.0 %all-gather.15.cloned.1.call-start = ((), (), s32[]{:S(2)}) async-start(), calls=%async_computation.17 | async-start | bytes 5971968 | tf_op jit(solution)/shard_map/all_gather | solution.py:82
  73.6 17.4 collective-permute-start.3
  81.4 119.1 %collective-permute-start = (f32[42624]{0:T(1024)S(1)}, f32[42624]{0:T(1024)S(1)}, u32[]{:S(2)}, u32[]{:S(2)}) collective-permute-start(f32[42624]{0:T(1024)S(1)} %constant_dynamic-update-slice_fusion.15), channel_id=1, source_target_pairs={{0,4},{4,0},{8,12},{12,8},{16,20},{20,16},{24,28},{28,24},{1,5},{5... | collective-permute-start | bytes 511496 | tf_op jit(solution)/shard_map/ppermute | solution.py:57
  85.3 128.1 %all-to-all-start = ((f32[5,64,1152]{2,0,1:T(8,128)}), f32[5,64,1152]{2,0,1:T(8,128)}, u32[]{:S(2)}, u32[]{:S(2)}) async-start(f32[5,64,1152]{2,0,1:T(8,128)} %copy.176), calls=%async_computation | async-start | bytes 4718592 | tf_op jit(solution)/shard_map/all_to_all | solution.py:125
  90.0 341.8 %all-gather.17.cloned.1.call-start = ((), (), s32[]{:S(2)}) async-start(), calls=%async_computation.18 | async-start | bytes 5971968 | tf_op jit(solution)/shard_map/all_gather | solution.py:82
  90.6 454.4 %all-gather.19.cloned.1.call-start = ((), (), s32[]{:S(2)}) async-start(), calls=%async_computation.19 | async-start | bytes 13271040 | tf_op jit(solution)/shard_map/all_gather | solution.py:82
  91.3 108.7 %collective-permute-start.4 = (f32[20]{0:T(128)S(1)}, f32[20]{0:T(128)S(1)}, u32[]{:S(2)}, u32[]{:S(2)}) collective-permute-start(f32[20]{0:T(128)S(1)} %add_dynamic-update-slice_fusion), channel_id=1, source_target_pairs={{0,2},{1,3},{2,0},{3,1},{4,6},{5,7},{6,4},{7,5},{8,10},{9,11},{10,... | collective-permute-start | bytes 248 | tf_op jit(solution)/shard_map/ppermute | solution.py:57
  200.6 6.1 collective-permute-start.1
  446.0 225.7 %reduce-scatter.10.cloned.1.call-start = ((), (), s32[]{:S(2)}) async-start(), calls=%async_computation.20 | async-start | bytes 13271040 | tf_op jit(solution)/shard_map/reduce_scatter | solution.py:86
  587.0 87.2 %all-to-all-start.3 = ((f32[5,64,1152]{2,0,1:T(8,128)}), f32[5,64,1152]{2,0,1:T(8,128)}, u32[]{:S(2)}, u32[]{:S(2)}) async-start(f32[5,64,1152]{2,0,1:T(8,128)} %copy.189), calls=%async_computation.4 | async-start | bytes 4718592 | tf_op jit(solution)/shard_map/all_to_all | solution.py:126
  591.6 157.2 %all-gather.21.cloned.1.call-start = ((), (), s32[]{:S(2)}) async-start(), calls=%async_computation.21 | async-start | bytes 13271040 | tf_op jit(solution)/shard_map/all_gather | solution.py:82
  679.8 208.1 %reduce-scatter.12.cloned.1.call-start = ((), (), s32[]{:S(2)}) async-start(), calls=%async_computation.22 | async-start | bytes 13271040 | tf_op jit(solution)/shard_map/reduce_scatter | solution.py:86
  799.5 224.6 %reduce-scatter.22.cloned.1.call-start = ((), (), s32[]{:S(2)}) async-start(), calls=%async_computation.29 | async-start | bytes 5529600
  943.5 208.4 %all-reduce.7.cloned.1.call-start = ((), (), s32[]{:S(2)}) async-start(), calls=%async_computation.23 | async-start | bytes 2359296 | tf_op jit(solution)/shard_map/psum | solution.py:246
  1026.8 227.6 %reduce-scatter.18.cloned.1.call-start = ((), (), s32[]{:S(2)}) async-start(), calls=%async_computation.27 | async-start | bytes 5971968 | tf_op jit(solution)/shard_map/reduce_scatter | solution.py:86
  1048.1 206.3 %reduce-scatter.16.cloned.1.call-start = ((), (), s32[]{:S(2)}) async-start(), calls=%async_computation.26 | async-start | bytes 5971968 | tf_op jit(solution)/shard_map/reduce_scatter | solution.py:86
  1072.1 197.0 %reduce-scatter.20.cloned.1.call-start = ((), (), s32[]{:S(2)}) async-start(), calls=%async_computation.28 | async-start | bytes 5971968 | tf_op jit(solution)/shard_map/reduce_scatter | solution.py:86
  1081.5 304.4 %reduce-scatter.14.cloned.1.call-start = ((), (), s32[]{:S(2)}) async-start(), calls=%async_computation.25 | async-start | bytes 17915904 | tf_op jit(solution)/shard_map/reduce_scatter | solution.py:86
  1151.8 421.1 %all-gather.23.cloned.1.call-start = ((), (), s32[]{:S(2)}) async-start(), calls=%async_computation.24 | async-start | bytes 2764800 | tf_op jit(solution)/shard_map/all_gather | solution.py:254
  1198.4 44.1 %all-to-all-start.5 = ((f32[8,144,576]{2,1,0:T(8,128)}), f32[8,144,576]{2,1,0:T(8,128)}, u32[]{:S(2)}, u32[]{:S(2)}) async-start(f32[8,144,576]{2,1,0:T(8,128)} %bitcast.253), calls=%async_computation.11 | async-start | bytes 5898240 | tf_op jit(solution)/shard_map/all_to_all | solution.py:216
  1203.0 654.6 %all-reduce.9.cloned.1.call-start = ((), (), s32[]{:S(2)}) async-start(), calls=%async_computation.30 | async-start | bytes 21233664 | tf_op jit(solution)/shard_map/psum | solution.py:327
  1386.7 73.4 %all-to-all-start.2 = ((f32[20,16,1152]{2,1,0:T(8,128)}), f32[20,16,1152]{2,1,0:T(8,128)}, u32[]{:S(2)}, u32[]{:S(2)}) async-start(f32[20,16,1152]{2,1,0:T(8,128)} %get-tuple-element.88), calls=%async_computation.3 | async-start | bytes 2949120 | tf_op jit(solution)/shard_map/all_to_all | solution.py:220
  1460.1 99.8 %all-to-all-start.4 = ((f32[20,16,1152]{2,1,0:T(8,128)}), f32[20,16,1152]{2,1,0:T(8,128)S(1)}, u32[]{:S(2)}, u32[]{:S(2)}) async-start(f32[20,16,1152]{2,1,0:T(8,128)} %get-tuple-element.85), calls=%async_computation.6 | async-start | bytes 2949120 | tf_op jit(solution)/shard_map/all_to_all | solution.py:280
  1466.0 5.9 collective-permute-start.6
  1477.1 32.9 %collective-permute-start.8 = (f32[35712]{0:T(1024)S(1)}, f32[35712]{0:T(1024)S(1)}, u32[]{:S(2)}, u32[]{:S(2)}) collective-permute-start(f32[35712]{0:T(1024)S(1)} %add.366), channel_id=1, source_target_pairs={{0,1},{1,0},{2,3},{3,2},{4,5},{5,4},{6,7},{7,6},{8,9},{9,8},{10,11... | collective-permute-start | bytes 428552 | tf_op jit(solution)/shard_map/ppermute | solution.py:57
  1510.0 32.0 %collective-permute-start.9 = (f32[35712]{0:T(1024)S(1)}, f32[35712]{0:T(1024)S(1)}, u32[]{:S(2)}, u32[]{:S(2)}) collective-permute-start(f32[35712]{0:T(1024)S(1)} %add.367), channel_id=1, source_target_pairs={{0,2},{1,3},{2,0},{3,1},{4,6},{5,7},{6,4},{7,5},{8,10},{9,11},{10,... | collective-permute-start | bytes 428552 | tf_op jit(solution)/shard_map/ppermute | solution.py:57
  1546.1 15.0 collective-permute-start.10
  1566.4 5.9 collective-permute-start.12
  (102 other events, 1707.8 us)
Sparse Core Ops, SparseCore 0:
  11.8 59.5 all-reduce.4
  73.0 133.9 all-gather.12
  208.9 84.5 all-gather.8
  295.3 41.3 all-gather.10
  338.4 41.3 all-gather.14
  381.6 41.3 all-gather.16
  446.1 98.8 all-gather.18
  583.4 88.1 reduce-scatter.9
  679.9 68.7 all-gather.20
  799.7 88.1 reduce-scatter.11
  943.6 80.4 reduce-scatter.21
  1028.0 57.5 all-reduce.6
  1089.1 56.0 reduce-scatter.17
  1148.8 56.8 reduce-scatter.15
  1209.0 60.0 reduce-scatter.19
  1273.1 112.8 reduce-scatter.13
  1388.0 74.3 all-gather.22
  1466.7 390.7 all-reduce.8

commit v2 on v1

--- a/solution.py
+++ b/solution.py
@@ -3,6 +3,8 @@
 import jax
 import jax.numpy as jnp
 from jax import lax
+from jax.experimental import pallas as pl
+from jax.experimental.pallas import tpu as pltpu
 from jax.sharding import PartitionSpec as P
 
 H = 16
@@ -78,12 +80,214 @@
     return lax.dynamic_slice_in_dim(array, lax.axis_index(axis) * length, length, axis=dim)
 
 
-def gather_rows(shard):
-    return lax.all_gather(shard, "patch", axis=0, tiled=True)
+def after(value, done):
+    return lax.optimization_barrier((value, done))[0]
+
+
+def small_patch():
+    return lax.axis_size("patch") == 8
+
+
+def gather_blocks(shard, done):
+    half = shard.shape[0] // 2
+    sent = after(shard, done)
+    along_x = swap(sent, "patch", 2)
+    along_y = swap(sent, "patch", 4)
+    x_half, y_half = lax.optimization_barrier((along_x[:half], along_y[half:]))
+    across_y, across_x = swap(x_half, "patch", 4), swap(y_half, "patch", 2)
+    across = jnp.concatenate([across_y, across_x], axis=0)
+    blocks = []
+    for block in (shard, along_x, along_y, across):
+        blocks += [block, swap(block, "patch", 1)]
+    return blocks, (across_y, across_x)
+
+
+def assemble_kernel(*refs):
+    blocks, whole, semaphores = refs[:-2], refs[-2], refs[-1]
+    own = lax.axis_index("patch")
+    copies = []
+    for k, block in enumerate(blocks):
+        length = block.shape[0]
+        row = pl.multiple_of((own ^ k) * length, 8)
+        copies.append(
+            pltpu.make_async_copy(block, whole.at[pl.ds(row, length)], semaphores.at[k])
+        )
+    for copy in copies:
+        copy.start()
+    for copy in copies:
+        copy.wait()
+
+
+def assemble(blocks):
+    length, width = blocks[0].shape
+    return pl.pallas_call(
+        assemble_kernel,
+        out_shape=jax.ShapeDtypeStruct((length * len(blocks), width), jnp.float32),
+        in_specs=[pl.BlockSpec(memory_space=pl.ANY)] * len(blocks),
+        out_specs=pl.BlockSpec(memory_space=pl.ANY),
+        scratch_shapes=[pltpu.SemaphoreType.DMA((len(blocks),))],
+        cost_estimate=pl.CostEstimate(
+            flops=0, bytes_accessed=8 * length * len(blocks) * width, transcendentals=0
+        ),
+    )(*blocks)
+
+
+def gather_rows(shard, done):
+    if not small_patch():
+        return lax.all_gather(shard, "patch", axis=0, tiled=True), done
+    blocks, done = gather_blocks(shard, done)
+    return assemble(blocks), done
+
+
+def scatter_chips(chips):
+    half = chips[0].shape[0] // 2
+    second = swap(chips[3][:half], "patch", 2)
+    first = swap(chips[3][half:], "patch", 4)
+    for_y = jnp.concatenate([chips[2][:half] + second, chips[2][half:]], axis=0)
+    for_x = jnp.concatenate([chips[1][:half], chips[1][half:] + first], axis=0)
+    return chips[0] + swap(for_x, "patch", 2) + swap(for_y, "patch", 4)
 
 
 def scatter_rows(whole):
-    return lax.psum_scatter(whole, "patch", scatter_dimension=0, tiled=True)
+    if not small_patch():
+        return lax.psum_scatter(whole, "patch", scatter_dimension=0, tiled=True)
+    own = lax.axis_index("patch")
+    core, chip = own % 2, own // 2
+    length = whole.shape[0] // 8
+    parts = whole.reshape(4, 2, length, whole.shape[1])
+    sent = lax.dynamic_index_in_dim(parts, 1 - core, axis=1, keepdims=False)
+    kept = lax.dynamic_index_in_dim(parts, core, axis=1, keepdims=False)
+    kept = kept + swap(sent, "patch", 1)
+    return scatter_chips(
+        [lax.dynamic_index_in_dim(kept, chip ^ j, axis=0, keepdims=False) for j in range(4)]
+    )
+
+
+def gather_tokens(rows, done):
+    if not small_patch():
+        return [lax.all_gather(rows, "patch", axis=0, tiled=True)], done
+    blocks, done = gather_blocks(rows, done)
+    return [jnp.concatenate(blocks[2 * j : 2 * j + 2], axis=0) for j in range(4)], done
+
+
+def scatter_tokens(groups):
+    if not small_patch():
+        return lax.psum_scatter(groups[0], "patch", scatter_dimension=0, tiled=True)
+    half = groups[0].shape[0] // 2
+    return scatter_chips([g[:half] + swap(g[half:], "patch", 1) for g in groups])
+
+
+def sum_chips(value, done):
+    if not small_patch():
+        bit = 2
+        while bit < lax.axis_size("patch"):
+            value = value + swap(value, "patch", bit)
+            bit *= 2
+        return value, done
+    half = value.shape[0] // 2
+    upper, lower = after((value[:half], value[half:]), done)
+    upper = upper + swap(upper, "patch", 2)
+    lower = lower + swap(lower, "patch", 4)
+    from_y, from_x = swap(upper, "patch", 4), swap(lower, "patch", 2)
+    return jnp.concatenate([upper + from_y, lower + from_x], axis=0), (from_y, from_x)
+
+
+def exchange(parts, axis):
+    return [parts[0]] + [swap(parts[k], axis, k) for k in range(1, len(parts))]
+
+
+def frame_sum(value):
+    if lax.axis_size("frame") != 4:
+        return lax.psum(value, "frame")
+    place = lax.axis_index("frame")
+    inner = (place == 1) | (place == 2)
+    value = value + lax.ppermute(value, "frame", [(0, 1), (3, 2)])
+    value = value + lax.ppermute(value, "frame", [(1, 2), (2, 1)])
+    return jnp.where(inner, value, lax.ppermute(value, "frame", [(1, 0), (2, 3)]))
+
+
+def half_over_cores(value, core):
+    width = value.shape[1] // 2
+    sent = lax.dynamic_slice_in_dim(value, (1 - core) * width, width, axis=1)
+    kept = lax.dynamic_slice_in_dim(value, core * width, width, axis=1)
+    return kept + swap(sent, "patch", 1)
+
+
+def both_halves(half, core):
+    other = swap(half, "patch", 1)
+    return jnp.concatenate(
+        [jnp.where(core == 0, half, other), jnp.where(core == 0, other, half)], axis=1
+    )
+
+
+def in_order(parts, axis):
+    length = parts[0].shape[0]
+    whole = jnp.zeros((length * len(parts),) + parts[0].shape[1:], parts[0].dtype)
+    for k, part in enumerate(parts):
+        start = (lax.axis_index(axis) ^ k) * length
+        whole = lax.dynamic_update_slice_in_dim(whole, part, start, axis=0)
+    return whole
+
+
+def block_of(array, axis_name, k, dim):
+    length = array.shape[dim] // lax.axis_size(axis_name)
+    start = (lax.axis_index(axis_name) ^ k) * length
+    return lax.dynamic_slice_in_dim(array, start, length, axis=dim)
+
+
+def to_own_columns(weight, done):
+    if not small_patch():
+        return lax.all_to_all(weight, "patch", 1, 0, tiled=True), done
+    blocks = [block_of(weight, "patch", k, 1) for k in range(8)]
+    pairs = []
+    for j in range(4):
+        kept, sent = blocks[2 * j], blocks[2 * j + 1]
+        pairs.append((kept, sent))
+    theirs = swap(jnp.concatenate([sent for _, sent in pairs], axis=0), "patch", 1)
+    length = weight.shape[0]
+    both = [
+        jnp.concatenate([kept, theirs[j * length : (j + 1) * length]], axis=0)
+        for j, (kept, _) in enumerate(pairs)
+    ]
+    sent_x, sent_y, sent_xy = after(tuple(both[1:]), done)
+    arrived = [
+        both[0],
+        swap(sent_x, "patch", 2),
+        swap(sent_y, "patch", 4),
+        swap(sent_xy, "patch", 6),
+    ]
+    halves = []
+    for block in arrived:
+        halves += [block[:length], block[length:]]
+    return assemble(halves), tuple(arrived[1:])
+
+
+def back_to_rows(grad):
+    count = lax.axis_size("patch")
+    if not small_patch():
+        return lax.all_to_all(grad, "patch", 0, 1, tiled=True)
+    parts = exchange([block_of(grad, "patch", k, 0) for k in range(count)], "patch")
+    length, width = parts[0].shape
+    whole = jnp.zeros((length, width * count), grad.dtype)
+    for k, part in enumerate(parts):
+        start = (lax.axis_index("patch") ^ k) * width
+        whole = lax.dynamic_update_slice_in_dim(whole, part, start, axis=1)
+    return whole
+
+
+def to_columns(x):
+    return lax.all_to_all(x, "frame", split_axis=1, concat_axis=0, tiled=True)
+
+
+def to_slots(x):
+    count = lax.axis_size("frame")
+    length = x.shape[0] // count
+    parts = exchange([block_of(x, "frame", k, 0) for k in range(count)], "frame")
+    whole = jnp.zeros((length, x.shape[1] * count, x.shape[2]), x.dtype)
+    for k, part in enumerate(parts):
+        start = (lax.axis_index("frame") ^ k) * x.shape[1]
+        whole = lax.dynamic_update_slice_in_dim(whole, part, start, axis=1)
+    return whole
 
 
 def on_device(
@@ -116,19 +320,15 @@
     width = block_input.shape[-1]
     head_dim = width // H
     scaling = head_dim ** (-0.5)
-    to_columns = partial(
-        lax.all_to_all, axis_name="frame", split_axis=1, concat_axis=0, tiled=True
-    )
-    to_slots = partial(
-        lax.all_to_all, axis_name="frame", split_axis=0, concat_axis=1, tiled=True
-    )
     tokens_in = to_columns(block_input)
     cotangent = to_columns(out_cotangent)
     slots, cols, _ = tokens_in.shape
     rows = slots * cols
     clip_own = own_part(clip_id, "frame", 0)
     column_mask = own_part(patch_mask, "frame", 0).astype(jnp.float32)[:, None]
+    frame_count = lax.axis_size("frame")
     frame_pos = all_sum(placed(frame_slot.astype(jnp.float32), "frame"), "frame")
+    w_qkv, done = gather_rows(qkv_weight, ())
 
     cond_act, silu_pull = jax.vjp(jax.nn.silu, cond)
     cond_own = own_part(cond_act, "patch", 1)
@@ -159,18 +359,21 @@
 
     caption_rows = caption.reshape(CLIPS * CAP, width)
     caption_share = own_part(own_part(caption_rows, "frame", 0), "patch", 1)
-    caption_kv_share = lax.psum(matmul(caption_share, cross_kv_weight), "patch")
-    caption_kv = lax.all_gather(caption_kv_share, "frame", axis=0, tiled=True)
+    core = lax.axis_index("patch") % 2
+    kv_part = matmul(caption_share, cross_kv_weight)
+    kv_half, done = sum_chips(half_over_cores(kv_part, core), done)
+    kv_halves = in_order(exchange([kv_half] * frame_count, "frame"), "frame")
+    caption_kv = both_halves(kv_halves, core)
     cross_keys = caption_kv[:, :width].reshape(CLIPS * CAP, H, head_dim)
     cross_values = (caption_kv[:, width:] + b_cross_v).reshape(CLIPS * CAP, H, head_dim)
 
-    w_qkv = gather_rows(qkv_weight)
-    w_attn = gather_rows(attn_out_weight)
-    w_cross_q = gather_rows(cross_q_weight)
-    w_cross_o = gather_rows(cross_out_weight)
-    w_first = lax.all_to_all(fc1_weight, "patch", 1, 0, tiled=True)
+    w_three, done = gather_rows(
+        jnp.concatenate([attn_out_weight, cross_q_weight, cross_out_weight], axis=1), done
+    )
+    w_attn, w_cross_q, w_cross_o = jnp.split(w_three, 3, axis=1)
+    w_first, done = to_own_columns(fc1_weight, done)
     grad_mlp = (column_mask * gate_two * cotangent).reshape(rows, width)
-    grad_mlp_all = gather_rows(grad_mlp)
+    grad_mlp_groups, done = gather_tokens(grad_mlp, done)
 
     normed_one, inverse_one = normalize(tokens_in)
     hidden_one = (normed_one * (1.0 + scale_one) + shift_one).reshape(rows, width)
@@ -205,17 +408,23 @@
     normed_two, inverse_two = normalize(after_cross)
     hidden_two = (normed_two * (1.0 + scale_two) + shift_two).reshape(rows, width)
 
-    hidden_all = gather_rows(hidden_two)
-    pre_act = matmul(hidden_all, w_first) + fc1_bias
-    activated, gelu_pull = jax.vjp(partial(jax.nn.gelu, approximate=True), pre_act)
-    grad_pre = gelu_pull(matmul_nt(grad_mlp_all, fc2_weight))[0]
-    grad_hidden_two = scatter_rows(matmul_nt(grad_pre, w_first)).reshape(slots, cols, width)
-    mlp_sum = scatter_rows(matmul(activated, fc2_weight))
-    grad_w_second = lax.psum(matmul_tn(activated, grad_mlp_all), "frame")
-    grad_w_first = lax.psum(
-        lax.all_to_all(matmul_tn(hidden_all, grad_pre), "patch", 0, 1, tiled=True), "frame"
-    )
-    grad_b_first = all_sum(jnp.sum(grad_pre, axis=0), "frame")
+    hidden_groups, done = gather_tokens(hidden_two, done)
+    mlp_parts, hidden_parts = [], []
+    grad_w_second, grad_w_first, grad_b_first = 0.0, 0.0, 0.0
+    for hidden, cotan in zip(hidden_groups, grad_mlp_groups):
+        pre_act = matmul(hidden, w_first) + fc1_bias
+        activated, gelu_pull = jax.vjp(partial(jax.nn.gelu, approximate=True), pre_act)
+        grad_pre = gelu_pull(matmul_nt(cotan, fc2_weight))[0]
+        hidden_parts.append(matmul_nt(grad_pre, w_first))
+        mlp_parts.append(matmul(activated, fc2_weight))
+        grad_w_second = grad_w_second + matmul_tn(activated, cotan)
+        grad_w_first = grad_w_first + matmul_tn(hidden, grad_pre)
+        grad_b_first = grad_b_first + jnp.sum(grad_pre, axis=0)
+    grad_hidden_two = scatter_tokens(hidden_parts).reshape(slots, cols, width)
+    mlp_sum = scatter_tokens(after(mlp_parts, grad_hidden_two))
+    grad_w_second = frame_sum(grad_w_second)
+    grad_w_first = frame_sum(back_to_rows(grad_w_first))
+    grad_b_first = all_sum(grad_b_first, "frame")
     mlp_branch = (mlp_sum + b_second).reshape(slots, cols, width)
     block_out = to_slots(after_cross + column_mask * gate_two * mlp_branch)
     grad_gate_two = jnp.sum(column_mask * mlp_branch * cotangent, axis=0)
@@ -243,17 +452,19 @@
         CLIPS * CAP, width
     )
     grad_kv = jnp.concatenate([grad_cross_keys, grad_cross_values], axis=1)
-    grad_kv_share = lax.psum(
-        lax.psum_scatter(grad_kv, "frame", scatter_dimension=0, tiled=True), "patch"
-    )
-    grad_w_cross_kv = lax.psum(matmul_tn(caption_share, grad_kv_share), "frame")
+    half_kv = half_over_cores(grad_kv, core)
+    half_share = sum(
+        exchange([block_of(half_kv, "frame", k, 0) for k in range(frame_count)], "frame")
+    )
+    grad_kv_share = both_halves(sum_chips(half_share, ())[0], core)
+    grad_w_cross_kv = frame_sum(matmul_tn(caption_share, grad_kv_share))
     grad_b_cross_v = jnp.sum(grad_kv_share[:, width:], axis=0)
-    grad_caption_share = lax.all_gather(
-        matmul_nt(grad_kv_share, cross_kv_weight), "patch", axis=1, tiled=True
-    )
-    grad_caption = lax.all_gather(grad_caption_share, "frame", axis=0, tiled=True).reshape(
-        caption.shape
-    )
+    grad_caption_share = all_sum(
+        placed(matmul_nt(grad_kv_share, cross_kv_weight), "patch"), "patch"
+    )
+    grad_caption = in_order(
+        exchange([grad_caption_share] * frame_count, "frame"), "frame"
+    ).reshape(caption.shape)
     grad_w_cross_q = matmul_tn(after_attn_rows, grad_cross_queries)
     grad_b_cross_q = jnp.sum(grad_cross_queries, axis=0)
     grad_after_attn = grad_after_cross + matmul_nt(grad_cross_queries, w_cross_q).reshape(
@@ -324,7 +535,7 @@
     grad_cond = silu_pull(grad_cond_act)[0]
 
     def finish(whole_grad):
-        return lax.psum(scatter_rows(whole_grad), "frame")
+        return frame_sum(scatter_rows(whole_grad))
 
     return (
         block_out,

time: 1880 us -> 2650 us (1.41)
  Pallas kernels: 0 us -> 1060 us
  waiting for transfers between devices: 1180 us -> 511 us
  local copies, waits for them, and re-layouts: 147 us -> 352 us
  starting transfers between devices: 41.8 us -> 203 us
  other arithmetic: 65.3 us -> 174 us
  blocking collectives: 62.8 us -> 0 us
  matrix products: 367 us -> 337 us
    pallas_call x0 -> x3, Pallas kernels: none -> 1060 us  [assemble(): pl.pallas_call(assemble_kernel, out_shape=jax.ShapeDtypeStruct((length *...]
    psum x3 -> x0, waiting for transfers between devices: 346 us -> none  [the longest x1 285 us: finish(): return lax.psum(scatter_rows(whole_grad), 'frame')]
    reduce_scatter x6 -> x0, waiting for transfers between devices: 300 us -> none  [scatter_rows(): return lax.psum_scatter(whole, 'patch', scatter_dimension=0, tiled=True)]
    ppermute x15 -> x124, waiting for transfers between devices: 192 us -> 406 us  [swap(): return lax.ppermute(value, axis, [(i, i ^ bit) for i in range(size)])]
    all_gather x8 -> x0, waiting for transfers between devices: 192 us -> none  [the longest x6 192 us: gather_rows(): return lax.all_gather(shard, 'patch', axis=0, tiled=True)]
    ppermute x15 -> x124, starting transfers between devices: 18.3 us -> 143 us  [swap(): return lax.ppermute(value, axis, [(i, i ^ bit) for i in range(size)])]
    ppermute x0 -> x21, waiting for transfers between devices: none -> 105 us  [the longest x7 54.4 us: frame_sum(): lax.ppermute(value, 'frame', [(1, 0), (2, 3)])]
    dynamic_update_slice x0 -> x24, local copies, waits for them, and re-layouts: none -> 88.4 us  [the longest x10 54 us: in_order(): whole = lax.dynamic_update_slice_in_dim(whole, part, start, axis=0)]
  transfers between devices with their start and end apart: 38 -> 147, of which waited for: 23 -> 44; matrix products, arithmetic and copies ran while one was open for 20% -> 30% of each run, Pallas kernels for 0% -> 40%
where the time goes in v2:
time: 2650 us; the launch traced here: 2640 us
  Pallas kernels  1060 us (40%)
  waiting for transfers between devices  511 us (19%)
  local copies, waits for them, and re-layouts  352 us (13%)
  matrix products  337 us (13%)
  starting transfers between devices  203 us (8%)
  other arithmetic  174 us (7%)
    pallas_call x3, Pallas kernels, assemble(): pl.pallas_call(assemble_kernel, out_shape=jax.ShapeDtypeStruct((length *...  1060 us
    ppermute x124, waiting for transfers between devices, swap(): return lax.ppermute(value, axis, [(i, i ^ bit) for i in range(size)])  406 us
    ppermute x124, starting transfers between devices, swap(): return lax.ppermute(value, axis, [(i, i ^ bit) for i in range(size)])  143 us
    dot_general x12, matrix products, contract(): return jnp.einsum(form, left, right, precision=BEST)  87.7 us
    dot_general x14, matrix products, matmul_nt(): lax.dot_general(left, right, (((1,), (1,)), ((), ())), precision=BEST)  84.8 us
    dot_general x14, matrix products, matmul_tn(): lax.dot_general(left, right, (((0,), (0,)), ((), ())), precision=BEST)  81.5 us
    dot_general x14, matrix products, matmul(): return jnp.dot(left, right, precision=BEST)  81.3 us
    unnamed x457, local copies, waits for them, and re-layouts  59.1 us
  transfers between devices with their start and end apart: 147, of which 44 were waited for; matrix products, arithmetic and copies ran while one was open for 30% of the time, Pallas kernels for 40%

profile of v2, /device:TPU:0, one launch (start us, length us, event | category | flops | bytes accessed | tf_op | source)
XLA Modules:
  0.0 2638.0 jit_solution(2182264010596753894)
XLA Ops:
  40.0 15.4 collective-permute-done.11
  60.1 11.1 collective-permute-done.12
  79.8 21.0 collective-permute-done.8
  130.2 17.5 collective-permute-done.26
  152.6 62.4 %collective-permute-done.27 = f32[120,1152]{1,0:T(8,128)S(1)} collective-permute-done((f32[120,1152]{1,0:T(8,128)S(1)}, f32[120,1152]{1,0:T(8,128)S(1)}, u32[]{:S(2)}, u32[]{:S(2)}) %collective-permute-start.27) | collective-permute-done | bytes 552992 | tf_op jit(solution)/shard_map/ppermute | solution.py:59
  264.6 483.6 %shard_map.400 = f32[1152,3456]{1,0:T(8,128)} custom-call(f32[144,3456]{1,0:T(8,128)} %refs_0_.1, f32[144,3456]{1,0:T(8,128)} %collective-permute-done.3.refs_1_, f32[144,3456]{1,0:T(8,128)} %collective-permute-done.4.refs_2_, f32[144,3456]{1,0:T(8,128)} %collective-permute-done.5.refs_3_, f32[144,3456]{1,0:T(8,128)} %collective-permute-done.6.refs_4_, ...), custom_call_target="tpu_custom_call" | custom-call | bytes 31850496 | tf_op jit(solution)/shard_map/pallas_call | solution.py:123
  748.2 14.3 fusion.215
  802.5 12.3 collective-permute-done.34
  840.0 12.7 collective-permute-done.32
  856.5 90.5 %shard_map.402 = f32[1152,576]{1,0:T(8,128)} custom-call(f32[144,576]{1,0:T(8,128)} %get-tuple-element.161.refs_0_, f32[144,576]{1,0:T(8,128)} %get-tuple-element.195.refs_1_, f32[144,576]{1,0:T(8,128)} %get-tuple-element.205.refs_2_, f32[144,576]{1,0:T(8,128)} %get-tuple-element.204.refs_3_, f32[144,576]{1,0:T(8,128)} %get-tuple-element.203.refs_4_, ...), custom_call_target="tpu_custom_call" | custom-call | bytes 5308416 | tf_op jit(solution)/shard_map/pallas_call | solution.py:123
  948.9 483.6 %shard_map.401 = f32[1152,3456]{1,0:T(8,128)} custom-call(f32[144,3456]{1,0:T(8,128)} %constant_dynamic-update-slice_fusion.3.refs_0_, f32[144,3456]{1,0:T(8,128)} %collective-permute-done.13.refs_1_, f32[144,3456]{1,0:T(8,128)} %collective-permute-done.19.refs_2_, f32[144,3456]{1,0:T(8,128)} %collective-permute-done.20.refs_3_, ...), custom_call_target="tpu_custom_call" | custom-call | bytes 31850496 | tf_op jit(solution)/shard_map/pallas_call | solution.py:123
  1574.2 14.8 collective-permute-done.43
  1762.0 16.9 collective-permute-done.56
  1779.5 14.3 collective-permute-done.141
  1823.3 26.7 %collective-permute-done.137 = f32[144,4608]{1,0:T(8,128)S(1)} collective-permute-done((f32[144,4608]{1,0:T(8,128)S(1)}, f32[144,4608]{1,0:T(8,128)S(1)}, u32[]{:S(2)}, u32[]{:S(2)}) %collective-permute-start.137) | collective-permute-done | bytes 2654240 | tf_op jit(solution)/shard_map/ppermute | solution.py:204
  1865.4 11.3 fusion.4
  1879.1 11.2 fusion.1
  1890.3 11.0 fusion.17
  1998.7 11.4 collective-permute-done.73
  2010.2 21.5 collective-permute-done.74
  2034.3 16.3 collective-permute-done.123
  2144.2 16.4 fusion.12
  2173.7 14.4 multiply_reduce_fusion.7
  2246.8 13.2 collective-permute-done.90
  2269.3 10.3 collective-permute-done.91
  2291.5 22.8 collective-permute-done.70
  2316.1 29.7 %collective-permute-done.67 = f32[5,16,1152]{2,1,0:T(8,128)S(1)} collective-permute-done((f32[5,16,1152]{2,1,0:T(8,128)S(1)}, f32[5,16,1152]{2,1,0:T(8,128)S(1)}, u32[]{:S(2)}, u32[]{:S(2)}) %collective-permute-start.67) | collective-permute-done | bytes 368672 | tf_op jit(solution)/shard_map/ppermute | solution.py:59
  2384.7 20.9 collective-permute-done.97
  2411.5 18.2 collective-permute-done.144
  2464.1 11.3 collective-permute-done.100
  2526.6 20.8 collective-permute-start.85
  2598.4 35.3 %collective-permute-done.110 = f32[144,1152]{1,0:T(8,128)S(1)} collective-permute-done((f32[144,1152]{1,0:T(8,128)S(1)}, f32[144,1152]{1,0:T(8,128)S(1)}, u32[]{:S(2)}, u32[]{:S(2)}) %collective-permute-start.110) | collective-permute-done | bytes 663584 | tf_op jit(solution)/shard_map/ppermute | solution.py:206
  (1101 shorter events, 1040.4 us)
Async XLA Ops:
  5.2 122.0 %collective-permute-start.3 = (f32[144,3456]{1,0:T(8,128)}, f32[144,3456]{1,0:T(8,128)}, u32[]{:S(2)}, u32[]{:S(2)}) collective-permute-start(f32[144,3456]{1,0:T(8,128)} %refs_0_.1), channel_id=1, source_target_pairs={{0,4},{4,0},{8,12},{12,8},{16,20},{20,16},{24,28},{28,24},{1,5},{5... | collective-permute-start | bytes 5971976 | tf_op jit(solution)/shard_map/ppermute | solution.py:59
  12.1 107.4 %all-to-all-start = ((f32[5,64,1152]{2,0,1:T(8,128)}), f32[5,64,1152]{2,0,1:T(8,128)}, u32[]{:S(2)}, u32[]{:S(2)}) async-start(f32[5,64,1152]{2,0,1:T(8,128)} %copy.416), calls=%async_computation | async-start | bytes 4718592 | tf_op jit(solution)/shard_map/all_to_all | solution.py:279
  106.7 157.4 %collective-permute-start.5 = (f32[144,3456]{1,0:T(8,128)}, f32[144,3456]{1,0:T(8,128)}, u32[]{:S(2)}, u32[]{:S(2)}) collective-permute-start(f32[144,3456]{1,0:T(8,128)} %collective-permute-done.4.refs_2_), channel_id=1, source_target_pairs={{0,4},{4,0},{8,12},{12,8},{16,20},{20,16},{24,28},{28,24},{1,5},{5... | collective-permute-start | bytes 5971976 | tf_op jit(solution)/shard_map/ppermute | solution.py:59
  117.3 146.7 %collective-permute-start.7 = (f32[144,3456]{1,0:T(8,128)}, f32[144,3456]{1,0:T(8,128)}, u32[]{:S(2)}, u32[]{:S(2)}) collective-permute-start(f32[144,3456]{1,0:T(8,128)} %collective-permute-done.6.refs_4_), channel_id=1, source_target_pairs={{0,4},{4,0},{8,12},{12,8},{16,20},{20,16},{24,28},{28,24},{1,5},{5... | collective-permute-start | bytes 5971976 | tf_op jit(solution)/shard_map/ppermute | solution.py:59
  119.5 104.4 %all-to-all-start.1 = ((f32[5,64,1152]{2,0,1:T(8,128)}), f32[5,64,1152]{2,0,1:T(8,128)}, u32[]{:S(2)}, u32[]{:S(2)}) async-start(f32[5,64,1152]{2,0,1:T(8,128)} %copy.432), calls=%async_computation.1 | async-start | bytes 4718592 | tf_op jit(solution)/shard_map/all_to_all | solution.py:279
  126.5 138.1 %collective-permute-start.10 = (f32[144,3456]{1,0:T(8,128)}, f32[144,3456]{1,0:T(8,128)}, u32[]{:S(2)}, u32[]{:S(2)}) collective-permute-start(f32[144,3456]{1,0:T(8,128)} %constant_dynamic-update-slice_fusion.1.refs_6_), channel_id=1, source_target_pairs={{0,4},{4,0},{8,12},{12,8},{16,20},{20,16},{24,28},{28,24},{1,5},{5... | collective-permute-start | bytes 5971976 | tf_op jit(solution)/shard_map/ppermute | solution.py:59
  127.2 87.8 %collective-permute-start.27 = (f32[120,1152]{1,0:T(8,128)S(1)}, f32[120,1152]{1,0:T(8,128)S(1)}, u32[]{:S(2)}, u32[]{:S(2)}) collective-permute-start(f32[120,1152]{1,0:T(8,128)S(1)} %pad_maximum_fusion.31), channel_id=1, source_target_pairs={{0,2},{1,3},{2,0},{3,1},{4,6},{5,7},{6,4},{7,5},{8,10},{9,11},{10,... | collective-permute-start | bytes 1658888 | tf_op jit(solution)/shard_map/ppermute | solution.py:59
  215.0 547.4 %collective-permute-start.19 = (f32[144,3456]{1,0:T(8,128)}, f32[144,3456]{1,0:T(8,128)}, u32[]{:S(2)}, u32[]{:S(2)}) collective-permute-start(f32[144,3456]{1,0:T(8,128)} %constant_dynamic-update-slice_fusion.3.refs_0_), channel_id=1, source_target_pairs={{0,8},{4,12},{8,0},{12,4},{16,24},{20,28},{24,16},{28,20},{1,9},{5... | collective-permute-start | bytes 5971976 | tf_op jit(solution)/shard_map/ppermute | solution.py:59
  216.2 548.5 %collective-permute-start.21 = (f32[144,3456]{1,0:T(8,128)}, f32[144,3456]{1,0:T(8,128)}, u32[]{:S(2)}, u32[]{:S(2)}) collective-permute-start(f32[144,3456]{1,0:T(8,128)} %constant_dynamic-update-slice_fusion.3.refs_0_), channel_id=1, source_target_pairs={{0,16},{4,20},{8,24},{12,28},{16,0},{20,4},{24,8},{28,12},{1,17},{... | collective-permute-start | bytes 5971976 | tf_op jit(solution)/shard_map/ppermute | solution.py:59
  264.0 683.0 %collective-permute-start.13 = (f32[144,3456]{1,0:T(8,128)}, f32[144,3456]{1,0:T(8,128)}, u32[]{:S(2)}, u32[]{:S(2)}) collective-permute-start(f32[144,3456]{1,0:T(8,128)} %constant_dynamic-update-slice_fusion.3.refs_0_), channel_id=1, source_target_pairs={{0,4},{4,0},{8,12},{12,8},{16,20},{20,16},{24,28},{28,24},{1,5},{5... | collective-permute-start | bytes 5971976 | tf_op jit(solution)/shard_map/ppermute | solution.py:59
  264.0 537.1 %collective-permute-start.29 = (f32[480,1152]{1,0:T(8,128)}, f32[480,1152]{1,0:T(8,128)}, u32[]{:S(2)}, u32[]{:S(2)}) collective-permute-start(f32[480,1152]{1,0:T(8,128)} %copy.427), channel_id=1, source_target_pairs={{0,4},{4,0},{8,12},{12,8},{16,20},{20,16},{24,28},{28,24},{1,5},{5... | collective-permute-start | bytes 6635528 | tf_op jit(solution)/shard_map/ppermute | solution.py:59
  794.8 153.5 %collective-permute-start.20 = (f32[144,3456]{1,0:T(8,128)}, f32[144,3456]{1,0:T(8,128)}, u32[]{:S(2)}, u32[]{:S(2)}) collective-permute-start(f32[144,3456]{1,0:T(8,128)} %collective-permute-done.19.refs_2_), channel_id=1, source_target_pairs={{0,4},{4,0},{8,12},{12,8},{16,20},{20,16},{24,28},{28,24},{1,5},{5... | collective-permute-start | bytes 5971976 | tf_op jit(solution)/shard_map/ppermute | solution.py:59
  794.9 154.1 %collective-permute-start.22 = (f32[144,3456]{1,0:T(8,128)}, f32[144,3456]{1,0:T(8,128)}, u32[]{:S(2)}, u32[]{:S(2)}) collective-permute-start(f32[144,3456]{1,0:T(8,128)} %collective-permute-done.21.refs_4_), channel_id=1, source_target_pairs={{0,4},{4,0},{8,12},{12,8},{16,20},{20,16},{24,28},{28,24},{1,5},{5... | collective-permute-start | bytes 5971976 | tf_op jit(solution)/shard_map/ppermute | solution.py:59
  815.7 133.2 %collective-permute-start.25 = (f32[144,3456]{1,0:T(8,128)}, f32[144,3456]{1,0:T(8,128)}, u32[]{:S(2)}, u32[]{:S(2)}) collective-permute-start(f32[144,3456]{1,0:T(8,128)} %constant_dynamic-update-slice_fusion.6.refs_6_), channel_id=1, source_target_pairs={{0,4},{4,0},{8,12},{12,8},{16,20},{20,16},{24,28},{28,24},{1,5},{5... | collective-permute-start | bytes 5971976 | tf_op jit(solution)/shard_map/ppermute | solution.py:59
  852.7 690.3 %collective-permute-start.46 = (f32[320,1152]{1,0:T(8,128)}, f32[320,1152]{1,0:T(8,128)}, u32[]{:S(2)}, u32[]{:S(2)}) collective-permute-start(f32[320,1152]{1,0:T(8,128)} %bitcast_multiply_fusion), channel_id=1, source_target_pairs={{0,4},{4,0},{8,12},{12,8},{16,20},{20,16},{24,28},{28,24},{1,5},{5... | collective-permute-start | bytes 4423688 | tf_op jit(solution)/shard_map/ppermute | solution.py:59
  947.1 559.8 %collective-permute-start.35 = (f32[320,1152]{1,0:T(8,128)}, f32[320,1152]{1,0:T(8,128)}, u32[]{:S(2)}, u32[]{:S(2)}) collective-permute-start(f32[320,1152]{1,0:T(8,128)} %bitcast_multiply_fusion), channel_id=1, source_target_pairs={{0,8},{4,12},{8,0},{12,4},{16,24},{20,28},{24,16},{28,20},{1,9},{5... | collective-permute-start | bytes 4423688 | tf_op jit(solution)/shard_map/ppermute | solution.py:59
  948.2 560.7 %collective-permute-start.36 = (f32[320,1152]{1,0:T(8,128)}, f32[320,1152]{1,0:T(8,128)}, u32[]{:S(2)}, u32[]{:S(2)}) collective-permute-start(f32[320,1152]{1,0:T(8,128)} %bitcast_multiply_fusion), channel_id=1, source_target_pairs={{0,16},{4,20},{8,24},{12,28},{16,0},{20,4},{24,8},{28,12},{1,17},{... | collective-permute-start | bytes 4423688 | tf_op jit(solution)/shard_map/ppermute | solution.py:59
  1724.2 129.9 %collective-permute-start.47 = (f32[320,1152]{1,0:T(8,128)}, f32[320,1152]{1,0:T(8,128)}, u32[]{:S(2)}, u32[]{:S(2)}) collective-permute-start(f32[320,1152]{1,0:T(8,128)} %slice.504), channel_id=1, source_target_pairs={{0,4},{4,0},{8,12},{12,8},{16,20},{20,16},{24,28},{28,24},{1,5},{5... | collective-permute-start | bytes 4423688 | tf_op jit(solution)/shard_map/ppermute | solution.py:59
  1732.7 84.8 %collective-permute-start.142 = (f32[576,1152]{1,0:T(8,128)}, f32[576,1152]{1,0:T(8,128)}, u32[]{:S(2)}, u32[]{:S(2)}) collective-permute-start(f32[576,1152]{1,0:T(8,128)} %fusion.15), channel_id=1, source_target_pairs={{0,1},{3,2},{4,5},{7,6},{8,9},{11,10},{12,13},{15,14},{16,17},{19,... | collective-permute-start | bytes 7962632 | tf_op jit(solution)/shard_map/ppermute | solution.py:204
  1745.8 104.1 %collective-permute-start.137 = (f32[144,4608]{1,0:T(8,128)S(1)}, f32[144,4608]{1,0:T(8,128)S(1)}, u32[]{:S(2)}, u32[]{:S(2)}) collective-permute-start(f32[144,4608]{1,0:T(8,128)S(1)} %copy-done.69), channel_id=1, source_target_pairs={{0,1},{3,2},{4,5},{7,6},{8,9},{11,10},{12,13},{15,14},{16,17},{19,... | collective-permute-start | bytes 7962632 | tf_op jit(solution)/shard_map/ppermute | solution.py:204
  1821.1 140.9 %collective-permute-start.143 = (f32[576,1152]{1,0:T(8,128)}, f32[576,1152]{1,0:T(8,128)}, u32[]{:S(2)}, u32[]{:S(2)}) collective-permute-start(f32[576,1152]{1,0:T(8,128)} %add.881), channel_id=1, source_target_pairs={{1,2},{2,1},{5,6},{6,5},{9,10},{10,9},{13,14},{14,13},{17,18},{18,... | collective-permute-start | bytes 7962632 | tf_op jit(solution)/shard_map/ppermute | solution.py:205
  1851.8 115.7 %collective-permute-start.138 = (f32[144,4608]{1,0:T(8,128)}, f32[144,4608]{1,0:T(8,128)}, u32[]{:S(2)}, u32[]{:S(2)}) collective-permute-start(f32[144,4608]{1,0:T(8,128)} %add.871), channel_id=1, source_target_pairs={{1,2},{2,1},{5,6},{6,5},{9,10},{10,9},{13,14},{14,13},{17,18},{18,... | collective-permute-start | bytes 7962632 | tf_op jit(solution)/shard_map/ppermute | solution.py:205
  1963.1 113.7 %collective-permute-start.58 = (f32[320,1152]{1,0:T(8,128)S(1)}, f32[320,1152]{1,0:T(8,128)S(1)}, u32[]{:S(2)}, u32[]{:S(2)}) collective-permute-start(f32[320,1152]{1,0:T(8,128)S(1)} %copy-done.107), channel_id=1, source_target_pairs={{0,4},{4,0},{8,12},{12,8},{16,20},{20,16},{24,28},{28,24},{1,5},{5... | collective-permute-start | bytes 4423688 | tf_op jit(solution)/shard_map/ppermute | solution.py:59
  2072.3 95.6 %collective-permute-start.124 = (f32[144,1152]{1,0:T(8,128)}, f32[144,1152]{1,0:T(8,128)}, u32[]{:S(2)}, u32[]{:S(2)}) collective-permute-start(f32[144,1152]{1,0:T(8,128)} %pad_maximum_fusion.29), channel_id=1, source_target_pairs={{0,8},{4,12},{8,0},{12,4},{16,24},{20,28},{24,16},{28,20},{1,9},{5... | collective-permute-start | bytes 1990664 | tf_op jit(solution)/shard_map/ppermute | solution.py:59
  2074.2 94.2 %collective-permute-start.126 = (f32[144,1152]{1,0:T(8,128)S(1)}, f32[144,1152]{1,0:T(8,128)}, u32[]{:S(2)}, u32[]{:S(2)}) collective-permute-start(f32[144,1152]{1,0:T(8,128)S(1)} %pad_maximum_fusion.30), channel_id=1, source_target_pairs={{0,16},{4,20},{8,24},{12,28},{16,0},{20,4},{24,8},{28,12},{1,17},{... | collective-permute-start | bytes 1990664 | tf_op jit(solution)/shard_map/ppermute | solution.py:59
  2076.8 93.1 %collective-permute-start.113 = (f32[144,1152]{1,0:T(8,128)}, f32[144,1152]{1,0:T(8,128)}, u32[]{:S(2)}, u32[]{:S(2)}) collective-permute-start(f32[144,1152]{1,0:T(8,128)} %pad_maximum_fusion.27), channel_id=1, source_target_pairs={{0,8},{4,12},{8,0},{12,4},{16,24},{20,28},{24,16},{28,20},{1,9},{5... | collective-permute-start | bytes 1990664 | tf_op jit(solution)/shard_map/ppermute | solution.py:59
  2076.9 93.0 %collective-permute-start.115 = (f32[144,1152]{1,0:T(8,128)}, f32[144,1152]{1,0:T(8,128)}, u32[]{:S(2)}, u32[]{:S(2)}) collective-permute-start(f32[144,1152]{1,0:T(8,128)} %pad_maximum_fusion.28), channel_id=1, source_target_pairs={{0,16},{4,20},{8,24},{12,28},{16,0},{20,4},{24,8},{28,12},{1,17},{... | collective-permute-start | bytes 1990664 | tf_op jit(solution)/shard_map/ppermute | solution.py:59
  2078.8 132.9 %collective-permute-start.80 = (f32[120,1152]{1,0:T(8,128)S(1)}, f32[120,1152]{1,0:T(8,128)}, u32[]{:S(2)}, u32[]{:S(2)}) collective-permute-start(f32[120,1152]{1,0:T(8,128)S(1)} %pad_maximum_fusion.32), channel_id=1, source_target_pairs={{0,4},{4,0},{8,12},{12,8},{16,20},{20,16},{24,28},{28,24},{1,5},{5... | collective-permute-start | bytes 1658888 | tf_op jit(solution)/shard_map/ppermute | solution.py:59
  2241.0 108.4 %collective-permute-start.127 = (f32[144,1152]{1,0:T(8,128)S(1)}, f32[144,1152]{1,0:T(8,128)}, u32[]{:S(2)}, u32[]{:S(2)}) collective-permute-start(f32[144,1152]{1,0:T(8,128)S(1)} %fusion.111), channel_id=1, source_target_pairs={{0,1},{3,2},{4,5},{7,6},{8,9},{11,10},{12,13},{15,14},{16,17},{19,... | collective-permute-start | bytes 1990664 | tf_op jit(solution)/shard_map/ppermute | solution.py:204
  2260.0 90.9 %collective-permute-start.116 = (f32[144,1152]{1,0:T(8,128)S(1)}, f32[144,1152]{1,0:T(8,128)}, u32[]{:S(2)}, u32[]{:S(2)}) collective-permute-start(f32[144,1152]{1,0:T(8,128)S(1)} %copy-done.91), channel_id=1, source_target_pairs={{0,1},{3,2},{4,5},{7,6},{8,9},{11,10},{12,13},{15,14},{16,17},{19,... | collective-permute-start | bytes 1990664 | tf_op jit(solution)/shard_map/ppermute | solution.py:204
  2279.6 100.9 %collective-permute-start.103 = (f32[4,144,1152]{2,1,0:T(8,128)}, f32[4,144,1152]{2,1,0:T(8,128)}, u32[]{:S(2)}, u32[]{:S(2)}) collective-permute-start(f32[4,144,1152]{2,1,0:T(8,128)} %dynamic-slice_bitcast_fusion.3), channel_id=1, source_target_pairs={{0,4},{4,0},{8,12},{12,8},{16,20},{20,16},{24,28},{28,24},{1,5},{5... | collective-permute-start | bytes 7962632 | tf_op jit(solution)/shard_map/ppermute | solution.py:59
  2376.2 110.4 %collective-permute-start.139 = (f32[144,4608]{1,0:T(8,128)S(1)}, f32[144,4608]{1,0:T(8,128)}, u32[]{:S(2)}, u32[]{:S(2)}) collective-permute-start(f32[144,4608]{1,0:T(8,128)S(1)} %copy-done.63), channel_id=1, source_target_pairs={{1,0},{2,3},{5,4},{6,7},{9,8},{10,11},{13,12},{14,15},{17,16},{18,... | collective-permute-start | bytes 7962632 | tf_op jit(solution)/shard_map/ppermute | solution.py:206
  (326 other events, 7820.2 us)

commit v3 on v1

--- a/solution.py
+++ b/solution.py
@@ -3,6 +3,8 @@
 import jax
 import jax.numpy as jnp
 from jax import lax
+from jax.experimental import pallas as pl
+from jax.experimental.pallas import tpu as pltpu
 from jax.sharding import PartitionSpec as P
 
 H = 16
@@ -78,12 +80,318 @@
     return lax.dynamic_slice_in_dim(array, lax.axis_index(axis) * length, length, axis=dim)
 
 
+def after(value, done):
+    return lax.optimization_barrier((value, done))[0]
+
+
+def small_patch():
+    return lax.axis_size("patch") == 8
+
+
+def greet(partners):
+    barrier = pltpu.get_barrier_semaphore()
+    for partner in partners:
+        pl.semaphore_signal(barrier, inc=1, device_id={"patch": partner}, device_id_type=pl.DeviceIdType.MESH)
+    pl.semaphore_wait(barrier, len(partners))
+
+
+def remote(source, target, send_sems, recv_sems, index, device):
+    return pltpu.make_async_remote_copy(
+        src_ref=source, dst_ref=target, send_sem=send_sems.at[index], recv_sem=recv_sems.at[index],
+        device_id={"patch": device}, device_id_type=pl.DeviceIdType.MESH)
+
+
+def token_gather_kernel(rows, whole, local_sem, send_sems, recv_sems):
+    own = lax.axis_index("patch")
+    core, along_x, along_y, across = own ^ 1, own ^ 2, own ^ 4, own ^ 6
+    greet((core, along_x, along_y))
+    length = rows.shape[0] // 4
+    sent = []
+
+    def piece(owner, q):
+        return whole.at[owner, pl.ds(q * length, length)]
+
+    def send(source, owner, q, index, device):
+        copy = remote(source, piece(owner, q), send_sems, recv_sems, index, device)
+        copy.start()
+        sent.append(copy)
+
+    def arrived(owner, q, index, device):
+        remote(piece(owner, q), piece(owner, q), send_sems, recv_sems, index, device).wait_recv()
+
+    mine = pltpu.make_async_copy(rows, whole.at[own], local_sem)
+    mine.start()
+    for q_x, q_y in ((0, 2), (1, 3), (2, 0), (3, 1)):
+        send(rows.at[pl.ds(q_x * length, length)], own, q_x, q_x, along_x)
+        send(rows.at[pl.ds(q_y * length, length)], own, q_y, 4 + q_y, along_y)
+    for q in range(4):
+        send(rows.at[pl.ds(q * length, length)], own, q, 12 + q, core)
+    for q_x, q_y in ((0, 2), (1, 3), (2, 0), (3, 1)):
+        arrived(along_x, q_x, q_x, along_x)
+        if q_x < 2:
+            send(piece(along_x, q_x), along_x, q_x, 8 + q_x, along_y)
+        send(piece(along_x, q_x), along_x, q_x, 16 + q_x, core)
+        arrived(along_y, q_y, 4 + q_y, along_y)
+        if q_y >= 2:
+            send(piece(along_y, q_y), along_y, q_y, 8 + q_y, along_x)
+        send(piece(along_y, q_y), along_y, q_y, 20 + q_y, core)
+    for q in (0, 2, 1, 3):
+        arrived(across, q, 8 + q, along_y if q < 2 else along_x)
+        send(piece(across, q), across, q, 24 + q, core)
+    for q in range(4):
+        arrived(core, q, 12 + q, core)
+        arrived(core ^ 2, q, 16 + q, core)
+        arrived(core ^ 4, q, 20 + q, core)
+        arrived(core ^ 6, q, 24 + q, core)
+    for copy in sent:
+        copy.wait_send()
+    mine.wait()
+
+
+def token_gather(rows):
+    length, width = rows.shape
+    return pl.pallas_call(
+        token_gather_kernel,
+        out_shape=jax.ShapeDtypeStruct((8, length, width), jnp.float32),
+        in_specs=[pl.BlockSpec(memory_space=pltpu.VMEM)],
+        out_specs=pl.BlockSpec(memory_space=pl.ANY),
+        scratch_shapes=[pltpu.SemaphoreType.DMA, pltpu.SemaphoreType.DMA((28,)), pltpu.SemaphoreType.DMA((28,))],
+        compiler_params=pltpu.CompilerParams(collective_id=0, has_side_effects=True, vmem_limit_bytes=16 << 20),
+        cost_estimate=pl.CostEstimate(flops=0, bytes_accessed=64 * length * width, transcendentals=0),
+    )(rows).reshape(8 * length, width)
+
+
+def token_scatter_kernel(parts, total, kept, theirs, by_x, by_y, from_x, from_y, local_sems, send_sems, recv_sems):
+    own = lax.axis_index("patch")
+    core, along_x, along_y = own ^ 1, own ^ 2, own ^ 4
+    greet((core, along_x, along_y))
+    half = total.shape[0] // 2
+    upper, lower = pl.ds(0, half), pl.ds(half, half)
+    order = (3, 2, 1, 0)
+    sent, loads = [], {}
+
+    def send(source, target, index, device):
+        copy = remote(source, target, send_sems, recv_sems, index, device)
+        copy.start()
+        sent.append(copy)
+
+    def arrived(target, index, device):
+        remote(target, target, send_sems, recv_sems, index, device).wait_recv()
+
+    for j in order:
+        send(parts.at[core ^ (2 * j)], theirs.at[j], j, core)
+        loads[j] = pltpu.make_async_copy(parts.at[own ^ (2 * j)], kept.at[j], local_sems.at[j])
+        loads[j].start()
+
+    def add_cores(j):
+        loads[j].wait()
+        arrived(theirs.at[j], j, core)
+        kept[j] = kept[j] + theirs[j]
+
+    add_cores(3)
+    send(kept.at[3, upper], by_x, 4, along_x)
+    send(kept.at[3, lower], by_y, 5, along_y)
+    add_cores(2)
+    send(kept.at[2, lower], from_y.at[lower], 6, along_y)
+    add_cores(1)
+    send(kept.at[1, upper], from_x.at[upper], 7, along_x)
+    add_cores(0)
+    arrived(by_x, 4, along_x)
+    kept[2, upper] = kept[2, upper] + by_x[...]
+    send(kept.at[2, upper], from_y.at[upper], 8, along_y)
+    arrived(by_y, 5, along_y)
+    kept[1, lower] = kept[1, lower] + by_y[...]
+    send(kept.at[1, lower], from_x.at[lower], 9, along_x)
+    arrived(from_y.at[lower], 6, along_y)
+    arrived(from_x.at[upper], 7, along_x)
+    arrived(from_y.at[upper], 8, along_y)
+    arrived(from_x.at[lower], 9, along_x)
+    total[...] = kept[0] + from_x[...] + from_y[...]
+    for copy in sent:
+        copy.wait_send()
+
+
+def token_scatter(parts):
+    length, width = parts.shape[0] // 8, parts.shape[1]
+    block = (length, width)
+    return pl.pallas_call(
+        token_scatter_kernel,
+        out_shape=jax.ShapeDtypeStruct(block, jnp.float32),
+        in_specs=[pl.BlockSpec(memory_space=pl.ANY)],
+        out_specs=pl.BlockSpec(memory_space=pltpu.VMEM),
+        scratch_shapes=[
+            pltpu.VMEM((4,) + block, jnp.float32), pltpu.VMEM((4,) + block, jnp.float32),
+            pltpu.VMEM((length // 2, width), jnp.float32), pltpu.VMEM((length // 2, width), jnp.float32),
+            pltpu.VMEM(block, jnp.float32), pltpu.VMEM(block, jnp.float32),
+            pltpu.SemaphoreType.DMA((4,)), pltpu.SemaphoreType.DMA((10,)), pltpu.SemaphoreType.DMA((10,)),
+        ],
+        compiler_params=pltpu.CompilerParams(collective_id=1, has_side_effects=True, vmem_limit_bytes=32 << 20),
+        cost_estimate=pl.CostEstimate(flops=0, bytes_accessed=48 * length * width, transcendentals=0),
+    )(parts.reshape((8,) + block))
+
+
+def assemble_kernel(axis, dim, *refs):
+    blocks, whole = refs[:-1], refs[-1]
+    own = lax.axis_index(axis)
+    for k, block in enumerate(blocks):
+        length = block.shape[dim]
+        start = pl.multiple_of((own ^ k) * length, length)
+        where = (slice(None),) * dim + (pl.ds(start, length),)
+        whole[where] = block[...]
+
+
+def assemble(blocks, axis, dim):
+    shape = list(blocks[0].shape)
+    shape[dim] *= len(blocks)
+    size = 4 * len(blocks) * blocks[0].size
+    return pl.pallas_call(
+        partial(assemble_kernel, axis, dim),
+        out_shape=jax.ShapeDtypeStruct(tuple(shape), jnp.float32),
+        in_specs=[pl.BlockSpec(memory_space=pltpu.VMEM)] * len(blocks),
+        out_specs=pl.BlockSpec(memory_space=pltpu.VMEM),
+        compiler_params=pltpu.CompilerParams(vmem_limit_bytes=24 << 20),
+        cost_estimate=pl.CostEstimate(flops=0, bytes_accessed=2 * size, transcendentals=0),
+    )(*blocks)
+
+
 def gather_rows(shard):
     return lax.all_gather(shard, "patch", axis=0, tiled=True)
 
 
 def scatter_rows(whole):
     return lax.psum_scatter(whole, "patch", scatter_dimension=0, tiled=True)
+
+
+def gather_tokens(rows):
+    return token_gather(rows) if small_patch() else gather_rows(rows)
+
+
+def scatter_tokens(parts):
+    return token_scatter(parts) if small_patch() else scatter_rows(parts)
+
+
+def sum_chips(value):
+    if not small_patch():
+        bit = 2
+        while bit < lax.axis_size("patch"):
+            value = value + swap(value, "patch", bit)
+            bit *= 2
+        return value
+    half = value.shape[0] // 2
+    upper, lower = value[:half], value[half:]
+    upper = upper + swap(upper, "patch", 2)
+    lower = lower + swap(lower, "patch", 4)
+    from_y, from_x = swap(upper, "patch", 4), swap(lower, "patch", 2)
+    return jnp.concatenate([upper + from_y, lower + from_x], axis=0)
+
+
+def exchange(parts, axis):
+    return [parts[0]] + [swap(parts[k], axis, k) for k in range(1, len(parts))]
+
+
+def frame_sum(value):
+    if lax.axis_size("frame") != 4:
+        return lax.psum(value, "frame")
+    place = lax.axis_index("frame")
+    inner = (place == 1) | (place == 2)
+    value = value + lax.ppermute(value, "frame", [(0, 1), (3, 2)])
+    value = value + lax.ppermute(value, "frame", [(1, 2), (2, 1)])
+    return jnp.where(inner, value, lax.ppermute(value, "frame", [(1, 0), (2, 3)]))
+
+
+def half_over_cores(value, core):
+    width = value.shape[1] // 2
+    sent = lax.dynamic_slice_in_dim(value, (1 - core) * width, width, axis=1)
+    kept = lax.dynamic_slice_in_dim(value, core * width, width, axis=1)
+    return kept + swap(sent, "patch", 1)
+
+
+def both_halves(half, core):
+    other = swap(half, "patch", 1)
+    return jnp.concatenate(
+        [jnp.where(core == 0, half, other), jnp.where(core == 0, other, half)], axis=1
+    )
+
+
+def block_of(array, axis_name, k, dim):
+    length = array.shape[dim] // lax.axis_size(axis_name)
+    start = (lax.axis_index(axis_name) ^ k) * length
+    return lax.dynamic_slice_in_dim(array, start, length, axis=dim)
+
+
+def pair_up(kept, theirs, core):
+    return jnp.where(
+        core == 0,
+        jnp.concatenate([kept, theirs], axis=-1),
+        jnp.concatenate([theirs, kept], axis=-1),
+    )
+
+
+def over_chips(blocks):
+    return [
+        blocks[0],
+        swap(blocks[1], "patch", 2),
+        swap(blocks[2], "patch", 4),
+        swap(blocks[3], "patch", 6),
+    ]
+
+
+def to_own_columns(weight):
+    if not small_patch():
+        return lax.all_to_all(weight, "patch", 1, 0, tiled=True)
+    length = weight.shape[0]
+    blocks = [block_of(weight, "patch", k, 1) for k in range(8)]
+    theirs = swap(jnp.concatenate(blocks[1::2], axis=0), "patch", 1)
+    both = [
+        jnp.concatenate([kept, theirs[j * length : (j + 1) * length]], axis=0)
+        for j, kept in enumerate(blocks[::2])
+    ]
+    halves = []
+    for block in over_chips(both):
+        halves += [block[:length], block[length:]]
+    return assemble(halves, "patch", 0)
+
+
+def back_to_rows(grad):
+    core = lax.axis_index("patch") % 2
+    blocks = [block_of(grad, "patch", k, 0) for k in range(8)]
+    length = blocks[0].shape[0]
+    theirs = swap(jnp.concatenate(blocks[1::2], axis=0), "patch", 1)
+    both = [
+        pair_up(kept, theirs[j * length : (j + 1) * length], core)
+        for j, kept in enumerate(blocks[::2])
+    ]
+    return jnp.concatenate(over_chips(both), axis=0)
+
+
+def side_by_side_kernel(stack, whole):
+    own = lax.axis_index("patch") // 2
+    length, width = whole.shape[0], stack.shape[1]
+    for j in range(4):
+        start = pl.multiple_of((own ^ j) * width, width)
+        whole[:, pl.ds(start, width)] = stack[j * length : (j + 1) * length, :]
+
+
+def side_by_side(stack):
+    length, width = stack.shape[0] // 4, stack.shape[1]
+    return pl.pallas_call(
+        side_by_side_kernel,
+        out_shape=jax.ShapeDtypeStruct((length, 4 * width), jnp.float32),
+        in_specs=[pl.BlockSpec(memory_space=pltpu.VMEM)],
+        out_specs=pl.BlockSpec(memory_space=pltpu.VMEM),
+        compiler_params=pltpu.CompilerParams(vmem_limit_bytes=24 << 20),
+        cost_estimate=pl.CostEstimate(flops=0, bytes_accessed=8 * stack.size, transcendentals=0),
+    )(stack)
+
+
+def to_columns(x):
+    return lax.all_to_all(x, "frame", split_axis=1, concat_axis=0, tiled=True)
+
+
+def to_slots(x):
+    count = lax.axis_size("frame")
+    parts = exchange([block_of(x, "frame", k, 0) for k in range(count)], "frame")
+    return assemble(parts, "frame", 1)
 
 
 def on_device(
@@ -116,19 +424,15 @@
     width = block_input.shape[-1]
     head_dim = width // H
     scaling = head_dim ** (-0.5)
-    to_columns = partial(
-        lax.all_to_all, axis_name="frame", split_axis=1, concat_axis=0, tiled=True
-    )
-    to_slots = partial(
-        lax.all_to_all, axis_name="frame", split_axis=0, concat_axis=1, tiled=True
-    )
     tokens_in = to_columns(block_input)
     cotangent = to_columns(out_cotangent)
     slots, cols, _ = tokens_in.shape
     rows = slots * cols
     clip_own = own_part(clip_id, "frame", 0)
     column_mask = own_part(patch_mask, "frame", 0).astype(jnp.float32)[:, None]
+    frame_count = lax.axis_size("frame")
     frame_pos = all_sum(placed(frame_slot.astype(jnp.float32), "frame"), "frame")
+    w_qkv = gather_rows(qkv_weight)
 
     cond_act, silu_pull = jax.vjp(jax.nn.silu, cond)
     cond_own = own_part(cond_act, "patch", 1)
@@ -159,18 +463,21 @@
 
     caption_rows = caption.reshape(CLIPS * CAP, width)
     caption_share = own_part(own_part(caption_rows, "frame", 0), "patch", 1)
-    caption_kv_share = lax.psum(matmul(caption_share, cross_kv_weight), "patch")
-    caption_kv = lax.all_gather(caption_kv_share, "frame", axis=0, tiled=True)
+    core = lax.axis_index("patch") % 2
+    kv_part = matmul(caption_share, cross_kv_weight)
+    kv_half = sum_chips(half_over_cores(kv_part, core))
+    kv_halves = assemble(exchange([kv_half] * frame_count, "frame"), "frame", 0)
+    caption_kv = both_halves(kv_halves, core)
     cross_keys = caption_kv[:, :width].reshape(CLIPS * CAP, H, head_dim)
     cross_values = (caption_kv[:, width:] + b_cross_v).reshape(CLIPS * CAP, H, head_dim)
 
-    w_qkv = gather_rows(qkv_weight)
-    w_attn = gather_rows(attn_out_weight)
-    w_cross_q = gather_rows(cross_q_weight)
-    w_cross_o = gather_rows(cross_out_weight)
-    w_first = lax.all_to_all(fc1_weight, "patch", 1, 0, tiled=True)
+    w_three = gather_rows(
+        jnp.concatenate([attn_out_weight, cross_q_weight, cross_out_weight], axis=1)
+    )
+    w_attn, w_cross_q, w_cross_o = jnp.split(w_three, 3, axis=1)
+    w_first = to_own_columns(after(fc1_weight, w_qkv))
     grad_mlp = (column_mask * gate_two * cotangent).reshape(rows, width)
-    grad_mlp_all = gather_rows(grad_mlp)
+    grad_mlp_all = gather_rows(after(grad_mlp, w_three))
 
     normed_one, inverse_one = normalize(tokens_in)
     hidden_one = (normed_one * (1.0 + scale_one) + shift_one).reshape(rows, width)
@@ -205,20 +512,12 @@
     normed_two, inverse_two = normalize(after_cross)
     hidden_two = (normed_two * (1.0 + scale_two) + shift_two).reshape(rows, width)
 
-    hidden_all = gather_rows(hidden_two)
+    hidden_all = gather_tokens(hidden_two)
     pre_act = matmul(hidden_all, w_first) + fc1_bias
     activated, gelu_pull = jax.vjp(partial(jax.nn.gelu, approximate=True), pre_act)
     grad_pre = gelu_pull(matmul_nt(grad_mlp_all, fc2_weight))[0]
-    grad_hidden_two = scatter_rows(matmul_nt(grad_pre, w_first)).reshape(slots, cols, width)
-    mlp_sum = scatter_rows(matmul(activated, fc2_weight))
-    grad_w_second = lax.psum(matmul_tn(activated, grad_mlp_all), "frame")
-    grad_w_first = lax.psum(
-        lax.all_to_all(matmul_tn(hidden_all, grad_pre), "patch", 0, 1, tiled=True), "frame"
-    )
-    grad_b_first = all_sum(jnp.sum(grad_pre, axis=0), "frame")
-    mlp_branch = (mlp_sum + b_second).reshape(slots, cols, width)
-    block_out = to_slots(after_cross + column_mask * gate_two * mlp_branch)
-    grad_gate_two = jnp.sum(column_mask * mlp_branch * cotangent, axis=0)
+    grad_hidden_two = scatter_tokens(matmul_nt(grad_pre, w_first))
+    grad_hidden_two = grad_hidden_two.reshape(slots, cols, width)
     grad_b_second = jnp.sum(grad_mlp, axis=0)
 
     grad_shift_two = jnp.sum(grad_hidden_two, axis=0)
@@ -229,6 +528,17 @@
     grad_cross_branch = (column_mask * grad_after_cross).reshape(rows, width)
     grad_w_cross_o = matmul_tn(cross_rows, grad_cross_branch)
     grad_b_cross_o = jnp.sum(grad_cross_branch, axis=0)
+    activated, grad_pre = after((activated, grad_pre), grad_w_cross_o)
+    grad_w_first = matmul_tn(hidden_all, grad_pre)
+    grad_w_second = matmul_tn(activated, grad_mlp_all)
+    grad_cross_branch = after(grad_cross_branch, (grad_w_first, grad_w_second))
+    grad_w_second = frame_sum(grad_w_second)
+    if small_patch():
+        grad_w_first = side_by_side(frame_sum(back_to_rows(grad_w_first)))
+    else:
+        grad_w_first = frame_sum(lax.all_to_all(grad_w_first, "patch", 0, 1, tiled=True))
+    grad_b_first = all_sum(jnp.sum(grad_pre, axis=0), "frame")
+    mlp_parts = matmul(activated, fc2_weight)
     grad_cross_att = matmul_nt(grad_cross_branch, w_cross_o).reshape(slots, cols, H, head_dim)
     cross_row_terms = jnp.sum(grad_cross_att * cross_att, axis=-1)[..., None]
     grad_cross_probs = contract("fchd,khd->fchk", grad_cross_att, cross_values)
@@ -243,19 +553,22 @@
         CLIPS * CAP, width
     )
     grad_kv = jnp.concatenate([grad_cross_keys, grad_cross_values], axis=1)
-    grad_kv_share = lax.psum(
-        lax.psum_scatter(grad_kv, "frame", scatter_dimension=0, tiled=True), "patch"
-    )
-    grad_w_cross_kv = lax.psum(matmul_tn(caption_share, grad_kv_share), "frame")
+    half_kv = half_over_cores(grad_kv, core)
+    half_share = sum(
+        exchange([block_of(half_kv, "frame", k, 0) for k in range(frame_count)], "frame")
+    )
+    grad_kv_share = both_halves(sum_chips(half_share), core)
+    grad_w_cross_kv = frame_sum(matmul_tn(caption_share, grad_kv_share))
     grad_b_cross_v = jnp.sum(grad_kv_share[:, width:], axis=0)
-    grad_caption_share = lax.all_gather(
-        matmul_nt(grad_kv_share, cross_kv_weight), "patch", axis=1, tiled=True
-    )
-    grad_caption = lax.all_gather(grad_caption_share, "frame", axis=0, tiled=True).reshape(
-        caption.shape
-    )
+    grad_caption_share = all_sum(
+        placed(matmul_nt(grad_kv_share, cross_kv_weight), "patch"), "patch"
+    )
+    grad_caption = assemble(
+        exchange([grad_caption_share] * frame_count, "frame"), "frame", 0
+    ).reshape(caption.shape)
     grad_w_cross_q = matmul_tn(after_attn_rows, grad_cross_queries)
     grad_b_cross_q = jnp.sum(grad_cross_queries, axis=0)
+    grad_cross_queries = after(grad_cross_queries, grad_w_cross_q)
     grad_after_attn = grad_after_cross + matmul_nt(grad_cross_queries, w_cross_q).reshape(
         slots, cols, width
     )
@@ -263,6 +576,11 @@
     grad_gate_one = jnp.sum(column_mask * attn_branch * grad_after_attn, axis=0)
     grad_w_attn = matmul_tn(attended_rows, grad_attn_rows)
     grad_b_attn = jnp.sum(grad_attn_rows, axis=0)
+    grad_attn_rows = after(grad_attn_rows, grad_w_attn)
+    mlp_sum = scatter_tokens(after(mlp_parts, grad_w_attn))
+    mlp_branch = (mlp_sum + b_second).reshape(slots, cols, width)
+    block_out = to_slots(after_cross + column_mask * gate_two * mlp_branch)
+    grad_gate_two = jnp.sum(column_mask * mlp_branch * cotangent, axis=0)
     grad_attended = matmul_nt(grad_attn_rows, w_attn).reshape(slots, cols, H, head_dim)
     row_terms = jnp.transpose(jnp.sum(grad_attended * attended, axis=-1), (1, 2, 0))[..., None]
     grad_probs = contract("fchd,schd->chfs", grad_attended, values)
@@ -324,7 +642,7 @@
     grad_cond = silu_pull(grad_cond_act)[0]
 
     def finish(whole_grad):
-        return lax.psum(scatter_rows(whole_grad), "frame")
+        return frame_sum(scatter_rows(whole_grad))
 
     return (
         block_out,

time: 1880 us -> 1670 us (0.89)
  waiting for transfers between devices: 1180 us -> 592 us
  Pallas kernels: 0 us -> 231 us
  starting transfers between devices: 41.8 us -> 145 us
  other arithmetic: 65.3 us -> 133 us
  blocking collectives: 62.8 us -> 0 us
  local copies, waits for them, and re-layouts: 147 us -> 182 us
    psum x3 -> x0, waiting for transfers between devices: 346 us -> none  [the longest x1 285 us: finish(): return lax.psum(scatter_rows(whole_grad), 'frame')]
    reduce_scatter x6 -> x4, waiting for transfers between devices: 300 us -> 0.01 us  [scatter_rows(): return lax.psum_scatter(whole, 'patch', scatter_dimension=0, tiled=True)]
    ppermute x15 -> x53, waiting for transfers between devices: 192 us -> 429 us  [swap(): return lax.ppermute(value, axis, [(i, i ^ bit) for i in range(size)])]
    pallas_call x0 -> x9, Pallas kernels: none -> 231 us  [the longest x2 149 us: token_scatter(): pl.pallas_call(token_scatter_kernel, out_shape=jax.ShapeDtypeStruct(block...]
    all_gather x6 -> x3, waiting for transfers between devices: 192 us -> 23.4 us  [gather_rows(): return lax.all_gather(shard, 'patch', axis=0, tiled=True)]
    ppermute x0 -> x21, waiting for transfers between devices: none -> 115 us  [the longest x7 94.8 us: frame_sum(): lax.ppermute(value, 'frame', [(1, 0), (2, 3)])]
    unnamed x19 -> x7, waiting for transfers between devices: 83 us -> 1.82 us
    ppermute x0 -> x21, starting transfers between devices: none -> 65.7 us  [the longest x7 46.3 us: frame_sum(): value = value + lax.ppermute(value, 'frame', [(0, 1), (3, 2)])]
  transfers between devices with their start and end apart: 38 -> 83, of which waited for: 23 -> 36; matrix products, arithmetic and copies ran while one was open for 20% -> 22% of each run, Pallas kernels for 0% -> 11%
where the time goes in v3:
time: 1670 us; the launch traced here: 1650 us
  waiting for transfers between devices  592 us (35%)
  matrix products  353 us (21%)
  Pallas kernels  231 us (14%)
  local copies, waits for them, and re-layouts  182 us (11%)
  starting transfers between devices  145 us (9%)
  other arithmetic  133 us (8%)
  between operations  17.1 us (1%)
    ppermute x53, waiting for transfers between devices, swap(): return lax.ppermute(value, axis, [(i, i ^ bit) for i in range(size)])  429 us
    pallas_call x2, Pallas kernels, token_scatter(): pl.pallas_call(token_scatter_kernel, out_shape=jax.ShapeDtypeStruct(block...  149 us
    dot_general x12, matrix products, contract(): return jnp.einsum(form, left, right, precision=BEST)  100 us
    ppermute x7, waiting for transfers between devices, frame_sum(): lax.ppermute(value, 'frame', [(1, 0), (2, 3)])  94.8 us
    dot_general x8, matrix products, matmul_nt(): lax.dot_general(left, right, (((1,), (1,)), ((), ())), precision=BEST)  84.8 us
    dot_general x8, matrix products, matmul(): return jnp.dot(left, right, precision=BEST)  83.7 us
    dot_general x8, matrix products, matmul_tn(): lax.dot_general(left, right, (((0,), (0,)), ((), ())), precision=BEST)  83.7 us
    pallas_call x1, Pallas kernels, token_gather(): pl.pallas_call(token_gather_kernel, out_shape=jax.ShapeDtypeStruct((8, le...  72.7 us
  transfers between devices with their start and end apart: 83, of which 36 were waited for; matrix products, arithmetic and copies ran while one was open for 22% of the time, Pallas kernels for 11%

profile of v3, /device:TPU:0, one launch (start us, length us, event | category | flops | bytes accessed | tf_op | source)
XLA Modules:
  0.0 1654.3 jit_solution(16846384446958306201)
XLA Ops:
  52.2 23.0 %all-to-all-done.1 = f32[5,64,1152]{2,0,1:T(8,128)} async-done(((f32[5,64,1152]{2,0,1:T(8,128)}), f32[5,64,1152]{2,0,1:T(8,128)}, u32[]{:S(2)}, u32[]{:S(2)}) %all-to-all-start.1) | async-done | bytes 1474592 | tf_op jit(solution)/shard_map/all_to_all | solution.py:388
  79.4 23.4 %all-gather.6.cloned.1.call-done = f32[1152,3456]{1,0:T(8,128)} async-done(((f32[144,3456]{1,0:T(8,128)}), f32[1152,3456]{1,0:T(8,128)}) %all-gather.6.cloned.1.call-update) | async-done | bytes 15925264 | tf_op jit(solution)/shard_map/all_gather | solution.py:258
  147.6 36.4 %collective-permute-done.10.refs_1_ = f32[120,1152]{1,0:T(8,128)} collective-permute-done((f32[120,1152]{1,0:T(8,128)S(1)}, f32[120,1152]{1,0:T(8,128)}, u32[]{:S(2)}, u32[]{:S(2)}) %collective-permute-start.10) | collective-permute-done | bytes 552992 | tf_op jit(solution)/shard_map/ppermute | solution.py:59
  184.0 37.3 %collective-permute-done.11.refs_2_ = f32[120,1152]{1,0:T(8,128)} collective-permute-done((f32[120,1152]{1,0:T(8,128)S(1)}, f32[120,1152]{1,0:T(8,128)}, u32[]{:S(2)}, u32[]{:S(2)}) %collective-permute-start.11) | collective-permute-done | bytes 552992 | tf_op jit(solution)/shard_map/ppermute | solution.py:59
  259.2 14.5 fusion.126
  392.9 72.7 %shard_map.401 = f32[8,320,1152]{2,1,0:T(8,128)S(1)} custom-call(f32[320,1152]{1,0:T(8,128)S(1)} %get-tuple-element.58.rows), custom_call_target="tpu_custom_call" | custom-call | bytes 23592960 | tf_op jit(solution)/shard_map/pallas_call | solution.py:153
  475.1 16.3 fusion.127
  491.5 22.2 %multiply_multiply_fusion.2 = (f32[2560,576]{0,1:T(8,128)}, f32[2560,576]{0,1:T(8,128)S(1)}) fusion(f32[576]{0:T(1024)S(1)} %copy-done.152, f32[2560,576]{0,1:T(8,128)} %fusion.127, f32[2560,1152]{1,0:T(8,128)} %bitcast.193, f32[1152,576]{1,0:T(8,128)S(1)} %copy-done.5), kind=kOutput, calls=%fused_computation.16 | convolution fusion | flops 10223124480 | bytes 32147712 | tf_op jit(solution)/shard_map/dot_general | solution.py:21
  513.7 26.3 %fusion.128 = f32[2560,1152]{1,0:T(8,128)S(1)} fusion(f32[2560,576]{0,1:T(8,128)S(1)} %get-tuple-element.32, f32[1152,576]{1,0:T(8,128)S(1)} %copy-done.5), kind=kOutput, calls=%fused_computation.275 | convolution fusion | flops 10192158720 | bytes 20348928 | tf_op jit(solution)/shard_map/dot_general | solution.py:29
  540.1 55.1 %shard_map.403 = f32[320,1152]{1,0:T(8,128)S(1)} custom-call(f32[8,320,1152]{2,1,0:T(8,128)S(1)} %bitcast.195), custom_call_target="tpu_custom_call" | custom-call | bytes 17694720 | tf_op jit(solution)/shard_map/pallas_call | solution.py:217
  607.5 17.3 %fusion.131 = f32[1152,576]{0,1:T(8,128)} fusion(f32[2560,1152]{1,0:T(8,128)} %bitcast.194, f32[2560,576]{0,1:T(8,128)} %copy-done.59), kind=kOutput, calls=%fused_computation.278 | convolution fusion | flops 10192158720 | bytes 20348928 | tf_op jit(solution)/shard_map/dot_general | solution.py:33
  624.8 17.5 %fusion.132 = f32[576,1152]{1,0:T(8,128)} fusion(f32[2560,576]{0,1:T(8,128)} %get-tuple-element.31, f32[2560,1152]{1,0:T(8,128)} %all-gather.8.cloned.1.call-done), kind=kOutput, calls=%fused_computation.279 | convolution fusion | flops 10192158720 | bytes 20348928 | tf_op jit(solution)/shard_map/dot_general | solution.py:33
  658.6 11.9 fusion.1
  778.6 18.3 %fusion.136 = f32[1152,3456]{1,0:T(8,128)} fusion(f32[320,1152]{1,0:T(8,128)S(1)} %copy-done.40, f32[320,3456]{1,0:T(8,128)} %constant_dynamic-update-slice_fusion.1), kind=kOutput, calls=%fused_computation.283 | convolution fusion | flops 7644119040 | bytes 21823488 | tf_op jit(solution)/shard_map/dot_general | solution.py:33
  805.1 19.4 %fusion.130 = f32[2560,1152]{1,0:T(8,128)S(1)} fusion(f32[2560,576]{0,1:T(8,128)} %get-tuple-element.31, f32[576,1152]{1,0:T(8,128)S(1)} %copy-done), kind=kOutput, calls=%fused_computation.277 | convolution fusion | flops 10192158720 | bytes 20348928 | tf_op jit(solution)/shard_map/dot_general | solution.py:21
  824.5 93.6 %shard_map.404 = f32[320,1152]{1,0:T(8,128)S(1)} custom-call(f32[8,320,1152]{2,1,0:T(8,128)S(1)} %bitcast.196), custom_call_target="tpu_custom_call" | custom-call | bytes 17694720 | tf_op jit(solution)/shard_map/pallas_call | solution.py:217
  928.5 14.6 multiply_reduce_fusion.6
  944.4 12.7 fusion.30
  960.1 14.3 fusion.27
  1024.1 12.0 collective-permute-done.27
  1036.9 33.5 %collective-permute-done.26 = f32[120,1152]{1,0:T(8,128)S(1)} collective-permute-done((f32[120,1152]{1,0:T(8,128)S(1)}, f32[120,1152]{1,0:T(8,128)S(1)}, u32[]{:S(2)}, u32[]{:S(2)}) %collective-permute-start.26) | collective-permute-done | bytes 552992 | tf_op jit(solution)/shard_map/ppermute | solution.py:59
  1074.2 19.7 %collective-permute-done.64 = f32[144,1152]{1,0:T(8,128)S(1)} collective-permute-done((f32[144,1152]{1,0:T(8,128)S(1)}, f32[144,1152]{1,0:T(8,128)S(1)}, u32[]{:S(2)}, u32[]{:S(2)}) %collective-permute-start.64) | collective-permute-done | bytes 663584 | tf_op jit(solution)/shard_map/ppermute | solution.py:59
  1123.5 36.6 %collective-permute-done.69 = f32[576]{0:T(1024)S(1)} collective-permute-done((f32[576]{0:T(1024)S(1)}, f32[576]{0:T(1024)S(1)}, u32[]{:S(2)}, u32[]{:S(2)}) %collective-permute-start.69) | collective-permute-done | bytes 2336 | tf_op jit(solution)/shard_map/ppermute | solution.py:59
  1173.7 14.2 collective-permute-done.70
  1209.7 17.1 %collective-permute-done.21.refs_1_ = f32[5,16,1152]{2,1,0:T(8,128)S(1)} collective-permute-done((f32[5,16,1152]{2,1,0:T(8,128)}, f32[5,16,1152]{2,1,0:T(8,128)S(1)}, u32[]{:S(2)}, u32[]{:S(2)}) %collective-permute-start.21) | collective-permute-done | bytes 368672 | tf_op jit(solution)/shard_map/ppermute | solution.py:59
  1241.1 92.2 %collective-permute-done.22.refs_2_ = f32[5,16,1152]{2,1,0:T(8,128)S(1)} collective-permute-done((f32[5,16,1152]{2,1,0:T(8,128)}, f32[5,16,1152]{2,1,0:T(8,128)S(1)}, u32[]{:S(2)}, u32[]{:S(2)}) %collective-permute-start.22) | collective-permute-done | bytes 368672 | tf_op jit(solution)/shard_map/ppermute | solution.py:59
  1336.5 15.2 collective-permute-start.47
  1397.8 62.1 %collective-permute-done.36.refs_1_ = f32[120,1152]{1,0:T(8,128)S(1)} collective-permute-done((f32[120,1152]{1,0:T(8,128)S(1)}, f32[120,1152]{1,0:T(8,128)S(1)}, u32[]{:S(2)}, u32[]{:S(2)}) %collective-permute-start.36) | collective-permute-done | bytes 552992 | tf_op jit(solution)/shard_map/ppermute | solution.py:59
  1558.1 16.3 collective-permute-done.52
  1577.0 11.6 collective-permute-done.55
  1589.5 14.9 collective-permute-done.61
  1605.3 40.2 %collective-permute-done.49 = f32[144,3456]{1,0:T(8,128)S(1)} collective-permute-done((f32[144,3456]{1,0:T(8,128)S(1)}, f32[144,3456]{1,0:T(8,128)S(1)}, u32[]{:S(2)}, u32[]{:S(2)}) %collective-permute-start.49) | collective-permute-done | bytes 1990688 | tf_op jit(solution)/shard_map/ppermute | solution.py:299
  (742 shorter events, 704.8 us)
Async XLA Ops:
  7.2 95.6 %all-gather.6.cloned.1.call-start = ((), (), s32[]{:S(2)}) async-start(), calls=%async_computation.7 | async-start | bytes 17915904 | tf_op jit(solution)/shard_map/all_gather | solution.py:258
  10.3 248.8 %all-gather.4.cloned.1.call-start = ((), (), s32[]{:S(2)}) async-start(), calls=%async_computation.6 | async-start | bytes 17915904 | tf_op jit(solution)/shard_map/all_gather | solution.py:258
  14.8 60.4 %all-to-all-start.1 = ((f32[5,64,1152]{2,0,1:T(8,128)}), f32[5,64,1152]{2,0,1:T(8,128)}, u32[]{:S(2)}, u32[]{:S(2)}) async-start(f32[5,64,1152]{2,0,1:T(8,128)} %copy.162), calls=%async_computation.1 | async-start | bytes 4718592 | tf_op jit(solution)/shard_map/all_to_all | solution.py:388
  21.3 453.8 %all-gather.8.cloned.1.call-start = ((), (), s32[]{:S(2)}) async-start(), calls=%async_computation.8 | async-start | bytes 13271040 | tf_op jit(solution)/shard_map/all_gather | solution.py:258
  128.4 111.7 %all-to-all-start = ((f32[5,64,1152]{2,0,1:T(8,128)}), f32[5,64,1152]{2,0,1:T(8,128)}, u32[]{:S(2)}, u32[]{:S(2)}) async-start(f32[5,64,1152]{2,0,1:T(8,128)} %copy.151), calls=%async_computation | async-start | bytes 4718592 | tf_op jit(solution)/shard_map/all_to_all | solution.py:388
  132.9 1203.6 %reduce-scatter.5.cloned.1.call-start = ((), (), s32[]{:S(2)}) async-start(), calls=%async_computation.9 | async-start | bytes 17915904 | tf_op jit(solution)/shard_map/reduce_scatter | solution.py:262
  143.9 77.5 %collective-permute-start.11 = (f32[120,1152]{1,0:T(8,128)S(1)}, f32[120,1152]{1,0:T(8,128)}, u32[]{:S(2)}, u32[]{:S(2)}) collective-permute-start(f32[120,1152]{1,0:T(8,128)S(1)} %pad_maximum_fusion.10.refs_0_), channel_id=1, source_target_pairs={{0,2},{1,3},{2,0},{3,1},{4,6},{5,7},{6,4},{7,5},{8,10},{9,11},{10,... | collective-permute-start | bytes 1658888 | tf_op jit(solution)/shard_map/ppermute | solution.py:59
  146.3 75.1 %collective-permute-start.12 = (f32[120,1152]{1,0:T(8,128)S(1)}, f32[120,1152]{1,0:T(8,128)}, u32[]{:S(2)}, u32[]{:S(2)}) collective-permute-start(f32[120,1152]{1,0:T(8,128)S(1)} %pad_maximum_fusion.10.refs_0_), channel_id=1, source_target_pairs={{0,3},{1,2},{2,1},{3,0},{4,7},{5,6},{6,5},{7,4},{8,11},{9,10},{10,... | collective-permute-start | bytes 1658888 | tf_op jit(solution)/shard_map/ppermute | solution.py:59
  146.9 78.2 %collective-permute-start.3 = (f32[20]{0:T(128)S(1)}, f32[20]{0:T(128)S(1)}, u32[]{:S(2)}, u32[]{:S(2)}) collective-permute-start(f32[20]{0:T(128)S(1)} %convert_dynamic-update-slice_fusion), channel_id=1, source_target_pairs={{0,1},{1,0},{2,3},{3,2},{4,5},{5,4},{6,7},{7,6},{8,9},{9,8},{10,11... | collective-permute-start | bytes 248 | tf_op jit(solution)/shard_map/ppermute | solution.py:59
  380.0 89.8 %collective-permute-start.15 = (f32[288,576]{1,0:T(8,128)}, f32[288,576]{1,0:T(8,128)}, u32[]{:S(2)}, u32[]{:S(2)}) collective-permute-start(f32[288,576]{1,0:T(8,128)} %pad_maximum_fusion.7), channel_id=1, source_target_pairs={{0,8},{4,12},{8,0},{12,4},{16,24},{20,28},{24,16},{28,20},{1,9},{5... | collective-permute-start | bytes 1990664 | tf_op jit(solution)/shard_map/ppermute | solution.py:59
  381.7 89.3 %collective-permute-start.16 = (f32[288,576]{1,0:T(8,128)}, f32[288,576]{1,0:T(8,128)}, u32[]{:S(2)}, u32[]{:S(2)}) collective-permute-start(f32[288,576]{1,0:T(8,128)} %pad_maximum_fusion.8), channel_id=1, source_target_pairs={{0,16},{4,20},{8,24},{12,28},{16,0},{20,4},{24,8},{28,12},{1,17},{... | collective-permute-start | bytes 1990664 | tf_op jit(solution)/shard_map/ppermute | solution.py:59
  387.3 84.9 %collective-permute-start.17 = (f32[288,576]{1,0:T(8,128)}, f32[288,576]{1,0:T(8,128)}, u32[]{:S(2)}, u32[]{:S(2)}) collective-permute-start(f32[288,576]{1,0:T(8,128)} %pad_maximum_fusion.9), channel_id=1, source_target_pairs={{0,24},{4,28},{8,16},{12,20},{16,8},{20,12},{24,0},{28,4},{1,25},{... | collective-permute-start | bytes 1990664 | tf_op jit(solution)/shard_map/ppermute | solution.py:59
  797.0 680.4 %reduce-scatter.7.cloned.1.call-start = ((), (), s32[]{:S(2)}) async-start(), calls=%async_computation.10 | async-start | bytes 5971968 | tf_op jit(solution)/shard_map/reduce_scatter | solution.py:262
  797.6 702.6 %reduce-scatter.9.cloned.1.call-start = ((), (), s32[]{:S(2)}) async-start(), calls=%async_computation.11 | async-start | bytes 5971968 | tf_op jit(solution)/shard_map/reduce_scatter | solution.py:262
  798.2 708.9 %reduce-scatter.11.cloned.1.call-start = ((), (), s32[]{:S(2)}) async-start(), calls=%async_computation.12 | async-start | bytes 5971968 | tf_op jit(solution)/shard_map/reduce_scatter | solution.py:262
  799.1 363.7 %collective-permute-start.71 = (f32[576,1152]{1,0:T(8,128)}, f32[576,1152]{1,0:T(8,128)}, u32[]{:S(2)}, u32[]{:S(2)}) collective-permute-start(f32[576,1152]{1,0:T(8,128)} %fusion.132), channel_id=1, source_target_pairs={{0,1},{3,2},{4,5},{7,6},{8,9},{11,10},{12,13},{15,14},{16,17},{19,... | collective-permute-start | bytes 7962632 | tf_op jit(solution)/shard_map/ppermute | solution.py:297
  927.2 269.4 %collective-permute-start.18 = (f32[5,16,1152]{2,1,0:T(8,128)}, f32[5,16,1152]{2,1,0:T(8,128)S(1)}, u32[]{:S(2)}, u32[]{:S(2)}) collective-permute-start(f32[5,16,1152]{2,1,0:T(8,128)} %get-tuple-element.108), channel_id=1, source_target_pairs={{0,1},{1,0},{2,3},{3,2},{4,5},{5,4},{6,7},{7,6},{8,9},{9,8},{10,11... | collective-permute-start | bytes 1105928 | tf_op jit(solution)/shard_map/ppermute | solution.py:59
  1097.3 92.8 %collective-permute-start.66 = (f32[576,1152]{1,0:T(8,128)}, f32[576,1152]{1,0:T(8,128)}, u32[]{:S(2)}, u32[]{:S(2)}) collective-permute-start(f32[576,1152]{1,0:T(8,128)} %pad_maximum_fusion), channel_id=1, source_target_pairs={{0,1},{3,2},{4,5},{7,6},{8,9},{11,10},{12,13},{15,14},{16,17},{19,... | collective-permute-start | bytes 7962632 | tf_op jit(solution)/shard_map/ppermute | solution.py:297
  1188.0 180.1 %collective-permute-start.72 = (f32[576,1152]{1,0:T(8,128)}, f32[576,1152]{1,0:T(8,128)}, u32[]{:S(2)}, u32[]{:S(2)}) collective-permute-start(f32[576,1152]{1,0:T(8,128)} %add.584), channel_id=1, source_target_pairs={{1,2},{2,1},{5,6},{6,5},{9,10},{10,9},{13,14},{14,13},{17,18},{18,... | collective-permute-start | bytes 7962632 | tf_op jit(solution)/shard_map/ppermute | solution.py:298
  1198.0 194.0 %collective-permute-start.67 = (f32[576,1152]{1,0:T(8,128)}, f32[576,1152]{1,0:T(8,128)}, u32[]{:S(2)}, u32[]{:S(2)}) collective-permute-start(f32[576,1152]{1,0:T(8,128)} %fusion.100), channel_id=1, source_target_pairs={{1,2},{2,1},{5,6},{6,5},{9,10},{10,9},{13,14},{14,13},{17,18},{18,... | collective-permute-start | bytes 7962632 | tf_op jit(solution)/shard_map/ppermute | solution.py:298
  1208.7 127.8 %collective-permute-start.33 = (f32[120,1152]{1,0:T(8,128)}, f32[120,1152]{1,0:T(8,128)}, u32[]{:S(2)}, u32[]{:S(2)}) collective-permute-start(f32[120,1152]{1,0:T(8,128)} %dynamic_update_slice.49), channel_id=1, source_target_pairs={{0,4},{4,0},{8,12},{12,8},{16,20},{20,16},{24,28},{28,24},{1,5},{5... | collective-permute-start | bytes 1658888 | tf_op jit(solution)/shard_map/ppermute | solution.py:59
  1233.3 100.0 %collective-permute-start.22 = (f32[5,16,1152]{2,1,0:T(8,128)}, f32[5,16,1152]{2,1,0:T(8,128)S(1)}, u32[]{:S(2)}, u32[]{:S(2)}) collective-permute-start(f32[5,16,1152]{2,1,0:T(8,128)} %get-tuple-element.102), channel_id=1, source_target_pairs={{0,2},{1,3},{2,0},{3,1},{4,6},{5,7},{6,4},{7,5},{8,10},{9,11},{10,... | collective-permute-start | bytes 1105928 | tf_op jit(solution)/shard_map/ppermute | solution.py:59
  1235.1 98.9 %collective-permute-start.23 = (f32[5,16,1152]{2,1,0:T(8,128)}, f32[5,16,1152]{2,1,0:T(8,128)S(1)}, u32[]{:S(2)}, u32[]{:S(2)}) collective-permute-start(f32[5,16,1152]{2,1,0:T(8,128)} %get-tuple-element.101), channel_id=1, source_target_pairs={{0,3},{1,2},{2,1},{3,0},{4,7},{5,6},{6,5},{7,4},{8,11},{9,10},{10,... | collective-permute-start | bytes 1105928 | tf_op jit(solution)/shard_map/ppermute | solution.py:59
  1336.5 140.9 %collective-permute-start.47 = (f32[144,3456]{1,0:T(8,128)}, f32[144,3456]{1,0:T(8,128)}, u32[]{:S(2)}, u32[]{:S(2)}) collective-permute-start(f32[144,3456]{1,0:T(8,128)} %reduce-scatter.5.cloned.1.call-done), channel_id=1, source_target_pairs={{0,1},{3,2},{4,5},{7,6},{8,9},{11,10},{12,13},{15,14},{16,17},{19,... | collective-permute-start | bytes 5971976 | tf_op jit(solution)/shard_map/ppermute | solution.py:297
  1373.6 162.0 %collective-permute-start.73 = (f32[576,1152]{1,0:T(8,128)}, f32[576,1152]{1,0:T(8,128)}, u32[]{:S(2)}, u32[]{:S(2)}) collective-permute-start(f32[576,1152]{1,0:T(8,128)} %add.585), channel_id=1, source_target_pairs={{1,0},{2,3},{5,4},{6,7},{9,8},{10,11},{13,12},{14,15},{17,16},{18,... | collective-permute-start | bytes 7962632 | tf_op jit(solution)/shard_map/ppermute | solution.py:299
  1385.9 73.9 %collective-permute-start.36 = (f32[120,1152]{1,0:T(8,128)S(1)}, f32[120,1152]{1,0:T(8,128)S(1)}, u32[]{:S(2)}, u32[]{:S(2)}) collective-permute-start(f32[120,1152]{1,0:T(8,128)S(1)} %add.554.refs_0_), channel_id=1, source_target_pairs={{0,1},{1,0},{2,3},{3,2},{4,5},{5,4},{6,7},{7,6},{8,9},{9,8},{10,11... | collective-permute-start | bytes 1658888 | tf_op jit(solution)/shard_map/ppermute | solution.py:59
  1385.9 84.4 %collective-permute-start.37 = (f32[120,1152]{1,0:T(8,128)S(1)}, f32[120,1152]{1,0:T(8,128)}, u32[]{:S(2)}, u32[]{:S(2)}) collective-permute-start(f32[120,1152]{1,0:T(8,128)S(1)} %add.554.refs_0_), channel_id=1, source_target_pairs={{0,2},{1,3},{2,0},{3,1},{4,6},{5,7},{6,4},{7,5},{8,10},{9,11},{10,... | collective-permute-start | bytes 1658888 | tf_op jit(solution)/shard_map/ppermute | solution.py:59
  1392.0 108.2 %collective-permute-start.58 = (f32[144,2304]{1,0:T(8,128)}, f32[144,2304]{1,0:T(8,128)}, u32[]{:S(2)}, u32[]{:S(2)}) collective-permute-start(f32[144,2304]{1,0:T(8,128)} %add.570), channel_id=1, source_target_pairs={{1,0},{2,3},{5,4},{6,7},{9,8},{10,11},{13,12},{14,15},{17,16},{18,... | collective-permute-start | bytes 3981320 | tf_op jit(solution)/shard_map/ppermute | solution.py:299
  1460.7 95.4 %collective-permute-start.68 = (f32[576,1152]{1,0:T(8,128)}, f32[576,1152]{1,0:T(8,128)}, u32[]{:S(2)}, u32[]{:S(2)}) collective-permute-start(f32[576,1152]{1,0:T(8,128)} %add.581), channel_id=1, source_target_pairs={{1,0},{2,3},{5,4},{6,7},{9,8},{10,11},{13,12},{14,15},{17,16},{18,... | collective-permute-start | bytes 7962632 | tf_op jit(solution)/shard_map/ppermute | solution.py:299
  1491.2 52.9 %collective-permute-start.48 = (f32[144,3456]{1,0:T(8,128)}, f32[144,3456]{1,0:T(8,128)}, u32[]{:S(2)}, u32[]{:S(2)}) collective-permute-start(f32[144,3456]{1,0:T(8,128)} %add.563), channel_id=1, source_target_pairs={{1,2},{2,1},{5,6},{6,5},{9,10},{10,9},{13,14},{14,13},{17,18},{18,... | collective-permute-start | bytes 5971976 | tf_op jit(solution)/shard_map/ppermute | solution.py:298
  1542.8 61.6 %collective-permute-start.61 = (f32[144,1152]{1,0:T(8,128)S(1)}, f32[144,1152]{1,0:T(8,128)S(1)}, u32[]{:S(2)}, u32[]{:S(2)}) collective-permute-start(f32[144,1152]{1,0:T(8,128)S(1)} %add.572), channel_id=1, source_target_pairs={{1,0},{2,3},{5,4},{6,7},{9,8},{10,11},{13,12},{14,15},{17,16},{18,... | collective-permute-start | bytes 1990664 | tf_op jit(solution)/shard_map/ppermute | solution.py:299
  1546.5 99.0 %collective-permute-start.49 = (f32[144,3456]{1,0:T(8,128)S(1)}, f32[144,3456]{1,0:T(8,128)S(1)}, u32[]{:S(2)}, u32[]{:S(2)}) collective-permute-start(f32[144,3456]{1,0:T(8,128)S(1)} %add.564), channel_id=1, source_target_pairs={{1,0},{2,3},{5,4},{6,7},{9,8},{10,11},{13,12},{14,15},{17,16},{18,... | collective-permute-start | bytes 5971976 | tf_op jit(solution)/shard_map/ppermute | solution.py:299
  (210 other events, 4956.4 us)
Sparse Core Ops, SparseCore 0:
  10.5 92.2 all-gather.5
  104.7 95.5 all-gather.3
  202.2 68.7 all-gather.7
  797.1 153.6 reduce-scatter.4
  954.5 56.9 reduce-scatter.6
  1014.7 74.3 reduce-scatter.8
  1092.9 57.0 reduce-scatter.10

commit v4 on v3

--- a/solution.py
+++ b/solution.py
@@ -85,7 +85,11 @@
 
 
 def small_patch():
-    return lax.axis_size("patch") == 8
+    return lax.axis_size("patch") == 8 and lax.axis_size("frame") == 4
+
+
+def padded(vector, rows):
+    return jnp.pad(vector, (0, rows * 128 - vector.shape[0])).reshape(rows, 128)
 
 
 def greet(partners):
@@ -230,6 +234,548 @@
     )(parts.reshape((8,) + block))
 
 
+class Links:
+    def __init__(self, send_sems, recv_sems):
+        self.send_sems, self.recv_sems = send_sems, recv_sems
+        self.count = 0
+        self.sent = []
+
+    def plan(self):
+        self.count += 1
+        return self.count - 1
+
+    def copy(self, source, target, index, device):
+        return pltpu.make_async_remote_copy(
+            src_ref=source, dst_ref=target, send_sem=self.send_sems.at[index],
+            recv_sem=self.recv_sems.at[index], device_id=device,
+            device_id_type=pl.DeviceIdType.MESH,
+        )
+
+    def send(self, source, target, index, device):
+        self.copy(source, target, index, device).start()
+        self.sent.append((source, index, device))
+
+    def wait(self, target, index, device):
+        self.copy(target, target, index, device).wait_recv()
+
+    def drain(self):
+        for source, index, device in self.sent:
+            self.copy(source, source, index, device).wait_send()
+
+
+def greet_all(devices):
+    barrier = pltpu.get_barrier_semaphore()
+    for device in devices:
+        pl.semaphore_signal(barrier, inc=1, device_id=device, device_id_type=pl.DeviceIdType.MESH)
+    pl.semaphore_wait(barrier, len(devices))
+
+
+def begin_kernel(
+    tokens, slots, small, kv,
+    tokens_out, slots_out, small_out, kv_out,
+    small_1, small_2, small_got, kv_1, kv_2, kv_got_core, kv_got_1, kv_got_2,
+    send_sems, recv_sems,
+):
+    me, z = lax.axis_index("patch"), lax.axis_index("frame")
+    core, x, y = ({"patch": me ^ k} for k in (1, 2, 4))
+    frames = [None] + [{"frame": z ^ k} for k in (1, 2, 3)]
+    greet_all([core, x, y] + frames[1:])
+    links = Links(send_sems, recv_sems)
+    count, part = tokens.shape[0], tokens.shape[1] // 4
+    rows, width = kv_1.shape
+
+    def columns(k):
+        return pl.ds(pl.multiple_of((z ^ k) * part, part), part)
+
+    def of_slots(k):
+        return pl.ds((z ^ k) * count, count)
+
+    half = pl.multiple_of((me % 2) * width, 128)
+    other = pl.multiple_of((1 - me % 2) * width, 128)
+    mine, theirs = pl.ds(half, width), pl.ds(other, width)
+
+    at = links.plan()
+    links.send(small, small_got.at[0], at, core)
+    at_kv = links.plan()
+    links.send(kv.at[:, theirs], kv_got_core, at_kv, core)
+    token_at = [None] + [links.plan() for _ in range(3)]
+    slot_at = [None] + [links.plan() for _ in range(3)]
+    for k in (1, 2, 3):
+        links.send(slots, slots_out.at[z], slot_at[k], frames[k])
+        links.send(tokens.at[:, columns(k)], tokens_out.at[of_slots(0)], token_at[k], frames[k])
+    slots_out[z] = slots[...]
+    tokens_out[of_slots(0)] = tokens[:, columns(0)]
+
+    links.wait(small_got.at[0], at, core)
+    small_1[...] = small[...] + small_got[0]
+    at = links.plan()
+    links.send(small_1, small_got.at[1], at, x)
+    links.wait(kv_got_core, at_kv, core)
+    kv_1[...] = kv[:, mine] + kv_got_core[...]
+    upper, lower = pl.ds(0, 64), pl.ds(64, rows - 64)
+    at_u, at_l = links.plan(), links.plan()
+    links.send(kv_1.at[upper], kv_got_1.at[upper], at_u, x)
+    links.send(kv_1.at[lower], kv_got_1.at[lower], at_l, y)
+    links.wait(small_got.at[1], at, x)
+    small_2[...] = small_1[...] + small_got[1]
+    at = links.plan()
+    links.send(small_2, small_got.at[2], at, y)
+    links.wait(kv_got_1.at[upper], at_u, x)
+    links.wait(kv_got_1.at[lower], at_l, y)
+    kv_2[...] = kv_1[...] + kv_got_1[...]
+    at_u, at_l = links.plan(), links.plan()
+    links.send(kv_2.at[upper], kv_got_2.at[upper], at_u, y)
+    links.send(kv_2.at[lower], kv_got_2.at[lower], at_l, x)
+    links.wait(small_got.at[2], at, y)
+    small_out[...] = small_2[...] + small_got[2]
+    links.wait(kv_got_2.at[upper], at_u, y)
+    links.wait(kv_got_2.at[lower], at_l, x)
+
+    def share(k, columns):
+        return kv_out.at[pl.ds(pl.multiple_of((z ^ k) * rows, rows), rows), columns]
+
+    kv_out[pl.ds(pl.multiple_of(z * rows, rows), rows), mine] = kv_2[...] + kv_got_2[...]
+    kv_at = [None] + [links.plan() for _ in range(3)]
+    core_at = [links.plan() for _ in range(4)]
+    for k in (1, 2, 3):
+        links.send(share(0, mine), share(0, mine), kv_at[k], frames[k])
+    links.send(share(0, mine), share(0, mine), core_at[0], core)
+    for k in (1, 2, 3):
+        links.wait(share(k, mine), kv_at[k], frames[k])
+        links.send(share(k, mine), share(k, mine), core_at[k], core)
+    for k in (1, 2, 3):
+        links.wait(slots_out.at[z ^ k], slot_at[k], frames[k])
+        links.wait(tokens_out.at[of_slots(k)], token_at[k], frames[k])
+    for k in range(4):
+        links.wait(share(k, theirs), core_at[k], core)
+    links.drain()
+
+
+def begin(tokens, slots, small, kv):
+    count, cols, width = tokens.shape
+    rows = kv.shape[0]
+    f32, vmem = jnp.float32, pl.BlockSpec(memory_space=pltpu.VMEM)
+    half = pltpu.VMEM((rows, width), f32)
+    return pl.pallas_call(
+        begin_kernel,
+        out_shape=(
+            jax.ShapeDtypeStruct((4 * count, cols // 4, width), f32),
+            jax.ShapeDtypeStruct((4,) + slots.shape, f32),
+            jax.ShapeDtypeStruct(small.shape, f32),
+            jax.ShapeDtypeStruct((4 * rows, 2 * width), f32),
+        ),
+        in_specs=[vmem] * 4,
+        out_specs=[vmem] * 4,
+        scratch_shapes=[
+            pltpu.VMEM(small.shape, f32), pltpu.VMEM(small.shape, f32),
+            pltpu.VMEM((3,) + small.shape, f32), half, half, half, half, half,
+            pltpu.SemaphoreType.DMA((24,)), pltpu.SemaphoreType.DMA((24,)),
+        ],
+        compiler_params=pltpu.CompilerParams(
+            collective_id=2, has_side_effects=True, vmem_limit_bytes=32 << 20
+        ),
+        cost_estimate=pl.CostEstimate(flops=0, bytes_accessed=32 << 20, transcendentals=0),
+    )(tokens, slots, small, kv)
+
+
+UNITS = 6
+
+
+def finish_kernel(
+    first, attn, cross_q, cross_o, kv, tokens, small, caption,
+    first_out, attn_out, cross_q_out, cross_o_out, kv_out, tokens_out, small_out, caption_out,
+    kept, theirs, by_x, by_y, from_x, from_y, along_z, across_z,
+    small_sums, small_got, small_z, load_sems, credit, send_sems, recv_sems,
+):
+    me, z = lax.axis_index("patch"), lax.axis_index("frame")
+    outer = (z == 0) | (z == 3)
+    inner = (z == 1) | (z == 2)
+    core, x, y = ({"patch": me ^ k} for k in (1, 2, 4))
+    frames = [None] + [{"frame": z ^ k} for k in (1, 2, 3)]
+    near, facing = frames[1], frames[3]
+    greet_all([core, x, y] + frames[1:])
+    links = Links(send_sems, recv_sems)
+    rows, width = by_x.shape[1] * 2, by_x.shape[2]
+    upper, lower = pl.ds(0, rows // 2), pl.ds(rows // 2, rows // 2)
+    count, part = tokens_out.shape[0], tokens_out.shape[1] // 4
+
+    token_at = [None] + [links.plan() for _ in range(3)]
+
+    def send_tokens():
+        for k in (1, 2, 3):
+            links.send(
+                tokens.at[pl.ds((z ^ k) * count, count)],
+                tokens_out.at[:, pl.ds(pl.multiple_of(z * part, part), part)],
+                token_at[k], frames[k],
+            )
+        tokens_out[:, pl.ds(pl.multiple_of(z * part, part), part)] = tokens[pl.ds(z * count, count)]
+
+    def frame_steps(value, result, near_got, facing_got):
+        up, over, down = links.plan(), links.plan(), links.plan()
+
+        def one():
+            @pl.when(outer)
+            def _():
+                links.copy(value, near_got, up, near).start()
+
+        def two():
+            @pl.when(inner)
+            def _():
+                links.wait(near_got, up, near)
+                near_got[...] = near_got[...] + value[...]
+                links.copy(near_got, facing_got, over, facing).start()
+
+        def three():
+            @pl.when(inner)
+            def _():
+                links.wait(facing_got, over, facing)
+                result[...] = near_got[...] + facing_got[...]
+                links.copy(result, near_got, down, near).start()
+
+        def four():
+            @pl.when(outer)
+            def _():
+                links.wait(near_got, down, near)
+                result[...] = near_got[...]
+                links.copy(value, value, up, near).wait_send()
+
+            @pl.when(inner)
+            def _():
+                links.copy(near_got, near_got, over, facing).wait_send()
+                links.copy(result, result, down, near).wait_send()
+
+        return one, two, three, four
+
+    def piece(ref, u):
+        return ref.at[:, pl.ds(u * width, width)]
+
+    outs = [piece(first_out, u) for u in range(3)] + [attn_out, cross_q_out, cross_o_out]
+    steps = [
+        frame_steps(kept.at[u, 0], outs[u], along_z.at[u], across_z.at[u]) for u in range(UNITS)
+    ] + [
+        frame_steps(piece(kv, u), piece(kv_out, u), along_z.at[UNITS + u], across_z.at[UNITS + u])
+        for u in range(2)
+    ]
+    small_steps = frame_steps(small_sums.at[2], small_out, small_z.at[0], small_z.at[1])
+
+    core_at = [[links.plan() for _ in range(4)] for _ in range(UNITS)]
+    link_at = [[links.plan() for _ in range(6)] for _ in range(UNITS)]
+
+    def source(u, device, j):
+        start = pl.multiple_of((device ^ (2 * j)) * rows, rows)
+        ref = first if u < 3 else (attn, cross_q, cross_o)[u - 3]
+        return ref.at[pl.ds(start, rows), pl.ds((u % 3) * width if u < 3 else 0, width)]
+
+    def load(u, j):
+        return pltpu.make_async_copy(source(u, me, j), kept.at[u, j], load_sems.at[u, j])
+
+    def to_core(u):
+        if u >= 3:
+            pl.semaphore_wait(credit.at[u - 3], 1)
+        for j in (3, 2, 1, 0):
+            links.send(source(u, me ^ 1, j), theirs.at[u % 3, j], core_at[u][j], core)
+
+    def add_cores(u, j):
+        load(u, j).wait()
+        links.wait(theirs.at[u % 3, j], core_at[u][j], core)
+        kept[u, j] = kept[u, j] + theirs[u % 3, j]
+
+    def stage_one(u):
+        at = link_at[u]
+        add_cores(u, 3)
+        links.send(kept.at[u, 3, upper], by_x.at[u], at[0], x)
+        links.send(kept.at[u, 3, lower], by_y.at[u], at[1], y)
+        add_cores(u, 2)
+        links.send(kept.at[u, 2, lower], from_y.at[u, lower], at[2], y)
+        add_cores(u, 1)
+        links.send(kept.at[u, 1, upper], from_x.at[u, upper], at[3], x)
+        add_cores(u, 0)
+        if u + 3 < UNITS:
+            pl.semaphore_signal(
+                credit.at[u], inc=1, device_id=core, device_id_type=pl.DeviceIdType.MESH
+            )
+            to_core(u + 3)
+
+    def stage_two(u):
+        at = link_at[u]
+        links.wait(by_x.at[u], at[0], x)
+        kept[u, 2, upper] = kept[u, 2, upper] + by_x[u]
+        links.send(kept.at[u, 2, upper], from_y.at[u, upper], at[4], y)
+        links.wait(by_y.at[u], at[1], y)
+        kept[u, 1, lower] = kept[u, 1, lower] + by_y[u]
+        links.send(kept.at[u, 1, lower], from_x.at[u, lower], at[5], x)
+
+    def stage_three(u):
+        at = link_at[u]
+        links.wait(from_y.at[u, lower], at[2], y)
+        links.wait(from_x.at[u, upper], at[3], x)
+        links.wait(from_y.at[u, upper], at[4], y)
+        links.wait(from_x.at[u, lower], at[5], x)
+        kept[u, 0] = kept[u, 0] + from_x[u] + from_y[u]
+        steps[u][0]()
+
+    caption_at = [links.plan() for _ in range(10)]
+
+    def caption_frames():
+        caption_out[me, z] = caption[...]
+        for k in (1, 2, 3):
+            links.send(caption, caption_out.at[me, z], caption_at[k - 1], frames[k])
+
+    def caption_x():
+        for k in (1, 2, 3):
+            links.wait(caption_out.at[me, z ^ k], caption_at[k - 1], frames[k])
+        links.send(caption_out.at[me], caption_out.at[me], caption_at[3], x)
+
+    def caption_y():
+        links.wait(caption_out.at[me ^ 2], caption_at[3], x)
+        for i, k in enumerate((0, 2)):
+            links.send(caption_out.at[me ^ k], caption_out.at[me ^ k], caption_at[4 + i], y)
+
+    def caption_core():
+        for i, k in enumerate((0, 2)):
+            links.wait(caption_out.at[me ^ 4 ^ k], caption_at[4 + i], y)
+        for i, k in enumerate((0, 2, 4, 6)):
+            links.send(caption_out.at[me ^ k], caption_out.at[me ^ k], caption_at[6 + i], core)
+
+    def caption_end():
+        for i, k in enumerate((0, 2, 4, 6)):
+            links.wait(caption_out.at[me ^ 1 ^ k], caption_at[6 + i], core)
+
+    small_at = [links.plan() for _ in range(3)]
+    links.send(small, small_got.at[0], small_at[0], core)
+    caption_frames()
+    for u in range(UNITS):
+        for j in (3, 2, 1, 0):
+            load(u, j).start()
+    steps[6][0]()
+    steps[7][0]()
+    for u in range(3):
+        to_core(u)
+    links.wait(small_got.at[0], small_at[0], core)
+    small_sums[0] = small[...] + small_got[0]
+    links.send(small_sums.at[0], small_got.at[1], small_at[1], x)
+    stage_one(0)
+    links.wait(small_got.at[1], small_at[1], x)
+    small_sums[1] = small_sums[0] + small_got[1]
+    links.send(small_sums.at[1], small_got.at[2], small_at[2], y)
+    stage_one(1)
+    steps[6][1]()
+    steps[7][1]()
+    links.wait(small_got.at[2], small_at[2], y)
+    small_sums[2] = small_sums[1] + small_got[2]
+    small_steps[0]()
+    stage_two(0)
+    caption_x()
+    stage_one(2)
+    send_tokens()
+    small_steps[1]()
+    steps[6][2]()
+    steps[7][2]()
+    small_steps[2]()
+    for u in range(1, UNITS):
+        stage_two(u)
+        if u + 2 < UNITS:
+            stage_one(u + 2)
+        stage_three(u - 1)
+        if u >= 2:
+            steps[u - 2][1]()
+        if u >= 3:
+            steps[u - 3][2]()
+        if u == 2:
+            caption_y()
+        if u == 4:
+            caption_core()
+    stage_three(UNITS - 1)
+    steps[UNITS - 2][1]()
+    steps[UNITS - 3][2]()
+    steps[UNITS - 1][1]()
+    steps[UNITS - 2][2]()
+    steps[UNITS - 1][2]()
+    for step in steps + [small_steps]:
+        step[3]()
+    caption_end()
+    for k in (1, 2, 3):
+        where = pl.ds(pl.multiple_of((z ^ k) * part, part), part)
+        links.wait(tokens_out.at[:, where], token_at[k], frames[k])
+    links.drain()
+
+
+def finish(first, attn, cross_q, cross_o, kv, tokens, small, caption):
+    rows, width = first.shape[0] // 8, first.shape[1] // 3
+    count, part = tokens.shape[0] // 4, tokens.shape[1]
+    f32, vmem = jnp.float32, pl.BlockSpec(memory_space=pltpu.VMEM)
+    hbm = pl.BlockSpec(memory_space=pl.ANY)
+
+    def shape(*sizes):
+        return jax.ShapeDtypeStruct(sizes, f32)
+
+    return pl.pallas_call(
+        finish_kernel,
+        out_shape=(
+            shape(rows, 3 * width), shape(rows, width), shape(rows, width), shape(rows, width),
+            shape(rows, 2 * width), shape(count, 4 * part, tokens.shape[2]), shape(*small.shape),
+            shape(8, 4, *caption.shape),
+        ),
+        in_specs=[hbm] * 4 + [vmem] * 4,
+        out_specs=[vmem] * 8,
+        scratch_shapes=[
+            pltpu.VMEM((UNITS, 4, rows, width), f32), pltpu.VMEM((3, 4, rows, width), f32),
+            pltpu.VMEM((UNITS, rows // 2, width), f32), pltpu.VMEM((UNITS, rows // 2, width), f32),
+            pltpu.VMEM((UNITS, rows, width), f32), pltpu.VMEM((UNITS, rows, width), f32),
+            pltpu.VMEM((UNITS + 2, rows, width), f32), pltpu.VMEM((UNITS + 2, rows, width), f32),
+            pltpu.VMEM((3,) + small.shape, f32), pltpu.VMEM((3,) + small.shape, f32),
+            pltpu.VMEM((2,) + small.shape, f32),
+            pltpu.SemaphoreType.DMA((UNITS, 4)), pltpu.SemaphoreType.REGULAR((3,)),
+            pltpu.SemaphoreType.DMA((112,)), pltpu.SemaphoreType.DMA((112,)),
+        ],
+        compiler_params=pltpu.CompilerParams(
+            collective_id=3, has_side_effects=True, vmem_limit_bytes=60 << 20
+        ),
+        cost_estimate=pl.CostEstimate(flops=0, bytes_accessed=256 << 20, transcendentals=0),
+    )(first, attn, cross_q, cross_o, kv, tokens, small, caption)
+
+
+def middle_kernel(
+    parts, kv,
+    total, kv_out,
+    kept, theirs, by_x, by_y, from_x, from_y,
+    kv_half, kv_core, kv_got, kv_1, kv_2, kv_got_1, kv_got_2,
+    load_sems, send_sems, recv_sems,
+):
+    me, z = lax.axis_index("patch"), lax.axis_index("frame")
+    core, x, y = ({"patch": me ^ k} for k in (1, 2, 4))
+    frames = [None] + [{"frame": z ^ k} for k in (1, 2, 3)]
+    greet_all([core, x, y] + frames[1:])
+    links = Links(send_sems, recv_sems)
+    rows, width = kv_1.shape
+    half = pl.multiple_of((me % 2) * width, 128)
+    other = pl.multiple_of((1 - me % 2) * width, 128)
+    mine, others = pl.ds(half, width), pl.ds(other, width)
+
+    def share(ref, k):
+        return ref.at[pl.ds(pl.multiple_of((z ^ k) * rows, rows), rows)]
+
+    at_kv = links.plan()
+    links.send(kv.at[:, others], kv_core, at_kv, core)
+    core_at = [links.plan() for _ in range(4)]
+    loads = [
+        pltpu.make_async_copy(parts.at[me ^ (2 * j)], kept.at[j], load_sems.at[j])
+        for j in range(4)
+    ]
+    for j in (3, 2, 1, 0):
+        links.send(parts.at[me ^ 1 ^ (2 * j)], theirs.at[j], core_at[j], core)
+        loads[j].start()
+    links.wait(kv_core, at_kv, core)
+    kv_half[...] = kv[:, mine] + kv_core[...]
+    kv_at = [None] + [links.plan() for _ in range(3)]
+    for k in (1, 2, 3):
+        links.send(share(kv_half, k), kv_got.at[k - 1], kv_at[k], frames[k])
+
+    count = total.shape[0] // 2
+    upper, lower = pl.ds(0, count), pl.ds(count, count)
+    at = [links.plan() for _ in range(6)]
+
+    def add_cores(j):
+        loads[j].wait()
+        links.wait(theirs.at[j], core_at[j], core)
+        kept[j] = kept[j] + theirs[j]
+
+    add_cores(3)
+    links.send(kept.at[3, upper], by_x, at[0], x)
+    links.send(kept.at[3, lower], by_y, at[1], y)
+    add_cores(2)
+    links.send(kept.at[2, lower], from_y.at[lower], at[2], y)
+    add_cores(1)
+    links.send(kept.at[1, upper], from_x.at[upper], at[3], x)
+    add_cores(0)
+    links.wait(by_x, at[0], x)
+    kept[2, upper] = kept[2, upper] + by_x[...]
+    links.send(kept.at[2, upper], from_y.at[upper], at[4], y)
+    links.wait(by_y, at[1], y)
+    kept[1, lower] = kept[1, lower] + by_y[...]
+    links.send(kept.at[1, lower], from_x.at[lower], at[5], x)
+
+    for k in (1, 2, 3):
+        links.wait(kv_got.at[k - 1], kv_at[k], frames[k])
+    kv_1[...] = share(kv_half, 0)[...] + kv_got[0] + (kv_got[1] + kv_got[2])
+    top, bottom = pl.ds(0, 64), pl.ds(64, rows - 64)
+    at_u, at_l = links.plan(), links.plan()
+    links.send(kv_1.at[top], kv_got_1.at[top], at_u, x)
+    links.send(kv_1.at[bottom], kv_got_1.at[bottom], at_l, y)
+    links.wait(from_y.at[lower], at[2], y)
+    links.wait(from_x.at[upper], at[3], x)
+    links.wait(from_y.at[upper], at[4], y)
+    links.wait(from_x.at[lower], at[5], x)
+    total[...] = kept[0] + from_x[...] + from_y[...]
+    links.wait(kv_got_1.at[top], at_u, x)
+    links.wait(kv_got_1.at[bottom], at_l, y)
+    kv_2[...] = kv_1[...] + kv_got_1[...]
+    at_u, at_l = links.plan(), links.plan()
+    links.send(kv_2.at[top], kv_got_2.at[top], at_u, y)
+    links.send(kv_2.at[bottom], kv_got_2.at[bottom], at_l, x)
+    links.wait(kv_got_2.at[top], at_u, y)
+    links.wait(kv_got_2.at[bottom], at_l, x)
+    kv_out[:, mine] = kv_2[...] + kv_got_2[...]
+    at_core = links.plan()
+    links.send(kv_out.at[:, mine], kv_out.at[:, mine], at_core, core)
+    links.wait(kv_out.at[:, others], at_core, core)
+    links.drain()
+
+
+def middle(parts, kv):
+    length, width = parts.shape[0] // 8, parts.shape[1]
+    rows = kv.shape[0] // 4
+    f32, vmem = jnp.float32, pl.BlockSpec(memory_space=pltpu.VMEM)
+    block, half = (length, width), pltpu.VMEM((rows, width), f32)
+    return pl.pallas_call(
+        middle_kernel,
+        out_shape=(
+            jax.ShapeDtypeStruct(block, f32), jax.ShapeDtypeStruct((rows, 2 * width), f32),
+        ),
+        in_specs=[pl.BlockSpec(memory_space=pl.ANY), vmem],
+        out_specs=[vmem] * 2,
+        scratch_shapes=[
+            pltpu.VMEM((4,) + block, f32), pltpu.VMEM((4,) + block, f32),
+            pltpu.VMEM((length // 2, width), f32), pltpu.VMEM((length // 2, width), f32),
+            pltpu.VMEM(block, f32), pltpu.VMEM(block, f32),
+            pltpu.VMEM((4 * rows, width), f32), pltpu.VMEM((4 * rows, width), f32),
+            pltpu.VMEM((3, rows, width), f32), half, half, half, half,
+            pltpu.SemaphoreType.DMA((4,)), pltpu.SemaphoreType.DMA((24,)),
+            pltpu.SemaphoreType.DMA((24,)),
+        ],
+        compiler_params=pltpu.CompilerParams(
+            collective_id=4, has_side_effects=True, vmem_limit_bytes=48 << 20
+        ),
+        cost_estimate=pl.CostEstimate(flops=0, bytes_accessed=64 << 20, transcendentals=0),
+    )(parts.reshape((8,) + block), kv)
+
+
+def spread_kernel(block, whole, send_sems, recv_sems):
+    me = lax.axis_index("patch")
+    peers = [None] + [{"patch": me ^ k} for k in range(1, 8)]
+    greet_all(peers[1:])
+    links = Links(send_sems, recv_sems)
+    at = [links.plan() for _ in range(8)]
+    for k in range(1, 8):
+        links.send(block, whole.at[me], at[k], peers[k])
+    whole[me] = block[...]
+    for k in range(1, 8):
+        links.wait(whole.at[me ^ k], at[k], peers[k])
+    links.drain()
+
+
+def spread(block):
+    vmem = pl.BlockSpec(memory_space=pltpu.VMEM)
+    return pl.pallas_call(
+        spread_kernel,
+        out_shape=jax.ShapeDtypeStruct((8,) + block.shape, jnp.float32),
+        in_specs=[vmem],
+        out_specs=vmem,
+        scratch_shapes=[pltpu.SemaphoreType.DMA((8,)), pltpu.SemaphoreType.DMA((8,))],
+        compiler_params=pltpu.CompilerParams(collective_id=5, has_side_effects=True),
+    )(block)
+
+
 def assemble_kernel(axis, dim, *refs):
     blocks, whole = refs[:-1], refs[-1]
     own = lax.axis_index(axis)
@@ -264,53 +810,6 @@
 
 def gather_tokens(rows):
     return token_gather(rows) if small_patch() else gather_rows(rows)
-
-
-def scatter_tokens(parts):
-    return token_scatter(parts) if small_patch() else scatter_rows(parts)
-
-
-def sum_chips(value):
-    if not small_patch():
-        bit = 2
-        while bit < lax.axis_size("patch"):
-            value = value + swap(value, "patch", bit)
-            bit *= 2
-        return value
-    half = value.shape[0] // 2
-    upper, lower = value[:half], value[half:]
-    upper = upper + swap(upper, "patch", 2)
-    lower = lower + swap(lower, "patch", 4)
-    from_y, from_x = swap(upper, "patch", 4), swap(lower, "patch", 2)
-    return jnp.concatenate([upper + from_y, lower + from_x], axis=0)
-
-
-def exchange(parts, axis):
-    return [parts[0]] + [swap(parts[k], axis, k) for k in range(1, len(parts))]
-
-
-def frame_sum(value):
-    if lax.axis_size("frame") != 4:
-        return lax.psum(value, "frame")
-    place = lax.axis_index("frame")
-    inner = (place == 1) | (place == 2)
-    value = value + lax.ppermute(value, "frame", [(0, 1), (3, 2)])
-    value = value + lax.ppermute(value, "frame", [(1, 2), (2, 1)])
-    return jnp.where(inner, value, lax.ppermute(value, "frame", [(1, 0), (2, 3)]))
-
-
-def half_over_cores(value, core):
-    width = value.shape[1] // 2
-    sent = lax.dynamic_slice_in_dim(value, (1 - core) * width, width, axis=1)
-    kept = lax.dynamic_slice_in_dim(value, core * width, width, axis=1)
-    return kept + swap(sent, "patch", 1)
-
-
-def both_halves(half, core):
-    other = swap(half, "patch", 1)
-    return jnp.concatenate(
-        [jnp.where(core == 0, half, other), jnp.where(core == 0, other, half)], axis=1
-    )
 
 
 def block_of(array, axis_name, k, dim):
@@ -389,9 +888,53 @@
 
 
 def to_slots(x):
-    count = lax.axis_size("frame")
-    parts = exchange([block_of(x, "frame", k, 0) for k in range(count)], "frame")
-    return assemble(parts, "frame", 1)
+    return lax.all_to_all(x, "frame", split_axis=0, concat_axis=1, tiled=True)
+
+
+def scatter_tokens(parts):
+    return token_scatter(parts) if small_patch() else scatter_rows(parts)
+
+
+def open_up(block_input, frame_slot, small, kv_part):
+    frame_number = frame_slot.astype(jnp.float32)
+    if not small_patch():
+        kv = all_sum(kv_part, "patch")
+        return (
+            to_columns(block_input),
+            all_sum(placed(frame_number, "frame"), "frame"),
+            all_sum(small, "patch"),
+            lax.all_gather(kv, "frame", axis=0, tiled=True),
+        )
+    count = frame_slot.shape[0]
+    rows = -(-small.shape[0] // 1024) * 8
+    tokens, slots, summed, kv = begin(
+        block_input, padded(frame_number, 8), padded(small, rows), kv_part
+    )
+    return tokens, slots[:, 0, :count].reshape(-1), summed.reshape(-1)[: small.shape[0]], kv
+
+
+def mid_way(parts, kv):
+    if not small_patch():
+        kv = lax.psum_scatter(all_sum(kv, "patch"), "frame", scatter_dimension=0, tiled=True)
+        return scatter_rows(parts), kv
+    return middle(parts, kv)
+
+
+def close_up(weights, kv, tokens, small, caption):
+    clips, length = lax.axis_size("frame"), caption.shape[1]
+    if not small_patch():
+        weights = [lax.psum(scatter_rows(w), "frame") for w in weights]
+        whole = lax.all_gather(caption, "patch", axis=0, tiled=True)
+        whole = lax.all_gather(whole, "frame", axis=0)
+        whole = jnp.transpose(whole, (0, 2, 1))
+        small = all_sum(all_sum(small, "patch"), "frame")
+        return weights, lax.psum(kv, "frame"), to_slots(tokens), small, whole
+    rows = -(-small.shape[0] // 1024) * 8
+    *weights, kv, tokens, summed, whole = finish(
+        *weights, kv, tokens, padded(small, rows), caption
+    )
+    whole = jnp.transpose(whole, (1, 3, 0, 2)).reshape(clips, length, -1)
+    return weights, kv, tokens, summed.reshape(-1)[: small.shape[0]], whole
 
 
 def on_device(
@@ -424,26 +967,30 @@
     width = block_input.shape[-1]
     head_dim = width // H
     scaling = head_dim ** (-0.5)
-    tokens_in = to_columns(block_input)
-    cotangent = to_columns(out_cotangent)
+    cond_act, silu_pull = jax.vjp(jax.nn.silu, cond)
+    cond_own = own_part(cond_act, "patch", 1)
+    modulation_part = matmul(cond_own, ada_weight)
+    biases = (
+        ada_bias, q_bias, v_bias, attn_out_bias, cross_q_bias, cross_v_bias, cross_out_bias,
+        fc2_bias,
+    )
+    small = jnp.concatenate(
+        [modulation_part.reshape(-1)] + [placed(b, "patch") for b in biases]
+    )
+    caption_rows = caption.reshape(CLIPS * CAP, width)
+    caption_share = own_part(own_part(caption_rows, "frame", 0), "patch", 1)
+    tokens_in, frame_pos, small, caption_kv = open_up(
+        block_input, frame_slot, small, matmul(caption_share, cross_kv_weight)
+    )
+    cotangent = to_columns(after(out_cotangent, tokens_in))
+    w_qkv = gather_rows(qkv_weight)
+    three = jnp.concatenate([attn_out_weight, cross_q_weight, cross_out_weight], axis=1)
+    w_three = gather_rows(after(three, tokens_in))
+    w_attn, w_cross_q, w_cross_o = jnp.split(w_three, 3, axis=1)
     slots, cols, _ = tokens_in.shape
     rows = slots * cols
     clip_own = own_part(clip_id, "frame", 0)
     column_mask = own_part(patch_mask, "frame", 0).astype(jnp.float32)[:, None]
-    frame_count = lax.axis_size("frame")
-    frame_pos = all_sum(placed(frame_slot.astype(jnp.float32), "frame"), "frame")
-    w_qkv = gather_rows(qkv_weight)
-
-    cond_act, silu_pull = jax.vjp(jax.nn.silu, cond)
-    cond_own = own_part(cond_act, "patch", 1)
-    modulation_part = matmul(cond_own, ada_weight)
-    biases = (ada_bias, q_bias, v_bias, attn_out_bias, cross_q_bias, cross_v_bias, cross_out_bias, fc2_bias)
-    small = all_sum(
-        jnp.concatenate(
-            [modulation_part.reshape(-1)] + [placed(b, "patch") for b in biases]
-        ),
-        "patch",
-    )
     place = modulation_part.size
     modulation = small[:place].reshape(modulation_part.shape)
     whole = []
@@ -461,27 +1008,15 @@
         per_column, 6, axis=1
     )
 
-    caption_rows = caption.reshape(CLIPS * CAP, width)
-    caption_share = own_part(own_part(caption_rows, "frame", 0), "patch", 1)
-    core = lax.axis_index("patch") % 2
-    kv_part = matmul(caption_share, cross_kv_weight)
-    kv_half = sum_chips(half_over_cores(kv_part, core))
-    kv_halves = assemble(exchange([kv_half] * frame_count, "frame"), "frame", 0)
-    caption_kv = both_halves(kv_halves, core)
     cross_keys = caption_kv[:, :width].reshape(CLIPS * CAP, H, head_dim)
     cross_values = (caption_kv[:, width:] + b_cross_v).reshape(CLIPS * CAP, H, head_dim)
 
-    w_three = gather_rows(
-        jnp.concatenate([attn_out_weight, cross_q_weight, cross_out_weight], axis=1)
-    )
-    w_attn, w_cross_q, w_cross_o = jnp.split(w_three, 3, axis=1)
-    w_first = to_own_columns(after(fc1_weight, w_qkv))
     grad_mlp = (column_mask * gate_two * cotangent).reshape(rows, width)
-    grad_mlp_all = gather_rows(after(grad_mlp, w_three))
-
     normed_one, inverse_one = normalize(tokens_in)
     hidden_one = (normed_one * (1.0 + scale_one) + shift_one).reshape(rows, width)
     qkv_rows = matmul(hidden_one, w_qkv)
+    w_first = to_own_columns(after(fc1_weight, qkv_rows))
+    grad_mlp_all = gather_rows(after(grad_mlp, qkv_rows))
     queries = (qkv_rows[:, :width] + b_query).reshape(slots, cols, H, head_dim)
     keys = qkv_rows[:, width : 2 * width].reshape(slots, cols, H, head_dim)
     values = (qkv_rows[:, 2 * width :] + b_value).reshape(slots, cols, H, head_dim)
@@ -531,13 +1066,15 @@
     activated, grad_pre = after((activated, grad_pre), grad_w_cross_o)
     grad_w_first = matmul_tn(hidden_all, grad_pre)
     grad_w_second = matmul_tn(activated, grad_mlp_all)
+    if small_patch():
+        grad_w_first = back_to_rows(grad_w_first)
+    else:
+        grad_w_first = lax.all_to_all(grad_w_first, "patch", 0, 1, tiled=True)
     grad_cross_branch = after(grad_cross_branch, (grad_w_first, grad_w_second))
-    grad_w_second = frame_sum(grad_w_second)
+    grad_w_first, grad_w_second = lax.psum((grad_w_first, grad_w_second), "frame")
     if small_patch():
-        grad_w_first = side_by_side(frame_sum(back_to_rows(grad_w_first)))
-    else:
-        grad_w_first = frame_sum(lax.all_to_all(grad_w_first, "patch", 0, 1, tiled=True))
-    grad_b_first = all_sum(jnp.sum(grad_pre, axis=0), "frame")
+        grad_w_first = side_by_side(grad_w_first)
+    grad_b_first = jnp.sum(grad_pre, axis=0)
     mlp_parts = matmul(activated, fc2_weight)
     grad_cross_att = matmul_nt(grad_cross_branch, w_cross_o).reshape(slots, cols, H, head_dim)
     cross_row_terms = jnp.sum(grad_cross_att * cross_att, axis=-1)[..., None]
@@ -553,19 +1090,6 @@
         CLIPS * CAP, width
     )
     grad_kv = jnp.concatenate([grad_cross_keys, grad_cross_values], axis=1)
-    half_kv = half_over_cores(grad_kv, core)
-    half_share = sum(
-        exchange([block_of(half_kv, "frame", k, 0) for k in range(frame_count)], "frame")
-    )
-    grad_kv_share = both_halves(sum_chips(half_share), core)
-    grad_w_cross_kv = frame_sum(matmul_tn(caption_share, grad_kv_share))
-    grad_b_cross_v = jnp.sum(grad_kv_share[:, width:], axis=0)
-    grad_caption_share = all_sum(
-        placed(matmul_nt(grad_kv_share, cross_kv_weight), "patch"), "patch"
-    )
-    grad_caption = assemble(
-        exchange([grad_caption_share] * frame_count, "frame"), "frame", 0
-    ).reshape(caption.shape)
     grad_w_cross_q = matmul_tn(after_attn_rows, grad_cross_queries)
     grad_b_cross_q = jnp.sum(grad_cross_queries, axis=0)
     grad_cross_queries = after(grad_cross_queries, grad_w_cross_q)
@@ -577,7 +1101,11 @@
     grad_w_attn = matmul_tn(attended_rows, grad_attn_rows)
     grad_b_attn = jnp.sum(grad_attn_rows, axis=0)
     grad_attn_rows = after(grad_attn_rows, grad_w_attn)
-    mlp_sum = scatter_tokens(after(mlp_parts, grad_w_attn))
+    mlp_sum, grad_kv_share = mid_way(after(mlp_parts, grad_w_attn), grad_kv)
+    grad_attn_rows = after(grad_attn_rows, mlp_sum)
+    grad_w_cross_kv = matmul_tn(caption_share, grad_kv_share)
+    grad_b_cross_v = jnp.sum(grad_kv_share[:, width:], axis=0)
+    grad_caption_share = matmul_nt(cross_kv_weight, grad_kv_share)
     mlp_branch = (mlp_sum + b_second).reshape(slots, cols, width)
     block_out = to_slots(after_cross + column_mask * gate_two * mlp_branch)
     grad_gate_two = jnp.sum(column_mask * mlp_branch * cotangent, axis=0)
@@ -595,9 +1123,8 @@
     grad_hidden_one = matmul_nt(grad_qkv, w_qkv).reshape(slots, cols, width)
     grad_shift_one = jnp.sum(grad_hidden_one, axis=0)
     grad_scale_one = jnp.sum(grad_hidden_one * normed_one, axis=0)
-    input_grad = to_slots(
-        grad_after_attn
-        + normalize_back(grad_hidden_one * (1.0 + scale_one), normed_one, inverse_one)
+    input_grad = grad_after_attn + normalize_back(
+        grad_hidden_one * (1.0 + scale_one), normed_one, inverse_one
     )
     grad_per_column = jnp.concatenate(
         [
@@ -623,11 +1150,12 @@
         grad_b_cross_o,
         grad_b_second,
     )
-    small_grads = all_sum(
-        all_sum(
-            jnp.concatenate([grad_modulation_part.reshape(-1)] + list(bias_grads)), "patch"
-        ),
-        "frame",
+    small_grads = jnp.concatenate(
+        [grad_modulation_part.reshape(-1)] + list(bias_grads) + [placed(grad_b_first, "patch")]
+    )
+    weights, grad_w_cross_kv, input_grad, small_grads, grad_caption = close_up(
+        (grad_w_qkv, grad_w_attn, grad_w_cross_q, grad_w_cross_o),
+        grad_w_cross_kv, input_grad, small_grads, grad_caption_share,
     )
     place = grad_modulation_part.size
     grad_modulation = small_grads[:place].reshape(grad_modulation_part.shape)
@@ -636,14 +1164,17 @@
         own_biases.append(own_part(small_grads[place : place + b.shape[0]], "patch", 0))
         place += b.shape[0]
     g_query, g_value, g_attn, g_cross_q, g_cross_v, g_cross_o, g_second = own_biases
+    grad_b_first = own_part(small_grads[place:], "patch", 0)
     grad_w_ada = matmul_tn(cond_own, grad_modulation)
     grad_b_ada = own_part(jnp.sum(grad_modulation, axis=0), "patch", 0)
-    grad_cond_act = all_sum(placed(matmul_nt(grad_modulation, ada_weight), "patch"), "patch")
+    grad_cond_own = matmul_nt(grad_modulation, ada_weight)
+    if small_patch():
+        grad_cond_act = jnp.transpose(spread(grad_cond_own), (1, 0, 2)).reshape(cond.shape)
+    else:
+        grad_cond_act = all_sum(placed(grad_cond_own, "patch"), "patch")
     grad_cond = silu_pull(grad_cond_act)[0]
 
-    def finish(whole_grad):
-        return frame_sum(scatter_rows(whole_grad))
-
+    grad_w_qkv, grad_w_attn, grad_w_cross_q, grad_w_cross_o = weights
     return (
         block_out,
         input_grad,
@@ -651,16 +1182,16 @@
         grad_cond,
         grad_w_ada,
         grad_b_ada,
-        finish(grad_w_qkv),
+        grad_w_qkv,
         g_query,
         g_value,
-        finish(grad_w_attn),
+        grad_w_attn,
         g_attn,
-        finish(grad_w_cross_q),
+        grad_w_cross_q,
         g_cross_q,
         grad_w_cross_kv,
         g_cross_v,
-        finish(grad_w_cross_o),
+        grad_w_cross_o,
         g_cross_o,
         grad_w_first,
         grad_b_first,

time: 1670 us -> 1280 us (0.77)
  waiting for transfers between devices: 592 us -> 53.3 us
  Pallas kernels: 231 us -> 570 us
  starting transfers between devices: 145 us -> 58.3 us
  other arithmetic: 133 us -> 59.9 us
  local copies, waits for them, and re-layouts: 182 us -> 150 us
    pallas_call x0 -> x4, Pallas kernels: none -> 433 us  [the longest x1 238 us: finish(): pl.pallas_call(finish_kernel, out_shape=(shape(rows, 3 * width), shape(ro...]
    ppermute x53 -> x8, waiting for transfers between devices: 429 us -> 4.86 us  [swap(): return lax.ppermute(value, axis, [(i, i ^ bit) for i in range(size)])]
    ppermute x21 -> x0, waiting for transfers between devices: 115 us -> none  [the longest x7 94.8 us: frame_sum(): lax.ppermute(value, 'frame', [(1, 0), (2, 3)])]
    pallas_call x2 -> x1, Pallas kernels: 149 us -> 54.2 us  [token_scatter(): pl.pallas_call(token_scatter_kernel, out_shape=jax.ShapeDtypeStruct(block...]
    ppermute x21 -> x0, starting transfers between devices: 65.7 us -> none  [the longest x7 46.3 us: frame_sum(): value = value + lax.ppermute(value, 'frame', [(0, 1), (3, 2)])]
    ppermute x53 -> x8, starting transfers between devices: 68.2 us -> 7.18 us  [swap(): return lax.ppermute(value, axis, [(i, i ^ bit) for i in range(size)])]
    add x38 -> x1, other arithmetic: 45.9 us -> 0.17 us  [on_device(): after_attn = tokens_in + column_mask * gate_one * attn_branch]
    all_to_all x0 -> x1, starting transfers between devices: none -> 37.3 us  [to_slots(): return lax.all_to_all(x, 'frame', split_axis=0, concat_axis=1, tiled=True)]
  transfers between devices with their start and end apart: 83 -> 14, of which waited for: 36 -> 2; matrix products, arithmetic and copies ran while one was open for 22% -> 33% of each run, Pallas kernels for 11% -> 40%
where the time goes in v4:
time: 1280 us
  Pallas kernels  570 us (45%)
  matrix products  368 us (29%)
  local copies, waits for them, and re-layouts  150 us (12%)
  other arithmetic  59.9 us (5%)
  starting transfers between devices  58.3 us (5%)
  waiting for transfers between devices  53.3 us (4%)
  between operations  15.9 us (1%)
    pallas_call x1, Pallas kernels, finish(): pl.pallas_call(finish_kernel, out_shape=(shape(rows, 3 * width), shape(ro...  238 us
    pallas_call x1, Pallas kernels, middle(): pl.pallas_call(middle_kernel, out_shape=(jax.ShapeDtypeStruct(block, f32)...  104 us
    dot_general x12, matrix products, contract(): return jnp.einsum(form, left, right, precision=BEST)  98.4 us
    dot_general x8, matrix products, matmul_tn(): lax.dot_general(left, right, (((0,), (0,)), ((), ())), precision=BEST)  97 us
    dot_general x8, matrix products, matmul_nt(): lax.dot_general(left, right, (((1,), (1,)), ((), ())), precision=BEST)  89.1 us
    pallas_call x1, Pallas kernels, begin(): pl.pallas_call(begin_kernel, out_shape=(jax.ShapeDtypeStruct((4 * count,...  84.6 us
    dot_general x8, matrix products, matmul(): return jnp.dot(left, right, precision=BEST)  83.2 us
    pallas_call x1, Pallas kernels, token_gather(): pl.pallas_call(token_gather_kernel, out_shape=jax.ShapeDtypeStruct((8, le...  80.6 us
  transfers between devices with their start and end apart: 14, of which 2 were waited for; matrix products, arithmetic and copies ran while one was open for 33% of the time, Pallas kernels for 40%

profile of v4, /device:TPU:0, one launch (start us, length us, event | category | flops | bytes accessed | tf_op | source)
XLA Modules:
  0.0 1275.1 jit_solution(13136307874797375839)
XLA Ops:
  17.6 84.6 %shard_map.400 = (f32[20,16,1152]{2,1,0:T(8,128)S(1)}, f32[4,8,128]{2,1,0:T(8,128)S(1)}, f32[336,128]{1,0:T(8,128)S(1)}, f32[480,2304]{1,0:T(8,128)S(1)}) custom-call(f32[5,64,1152]{2,1,0:T(8,128)S(1)} %copy-done.13, f32[8,128]{1,0:T(8,128)S(1)} %pad_bitcast_fusion.2.slots, f32[336,128]{1,0:T(8,128)S(1)} %pad_bitcast_fusion.small, f32[120,2304]{1,0:T(8,128)S(1)} %fusion.76.kv), custom_call_target="tpu_custom_call" | custom-call | bytes 33554432 | tf_op jit(solution)/shard_map/pallas_call | solution.py:359
  110.5 13.0 %all-to-all-start = ((f32[5,64,1152]{2,0,1:T(8,128)}), f32[5,64,1152]{2,0,1:T(8,128)}, u32[]{:S(2)}, u32[]{:S(2)}) async-start(f32[5,64,1152]{2,0,1:T(8,128)} %copy.122), calls=%async_computation | async-start | bytes 4718592 | tf_op jit(solution)/shard_map/all_to_all | solution.py:887
  131.2 47.7 %all-to-all-done = f32[5,64,1152]{2,0,1:T(8,128)} async-done(((f32[5,64,1152]{2,0,1:T(8,128)}), f32[5,64,1152]{2,0,1:T(8,128)}, u32[]{:S(2)}, u32[]{:S(2)}) %all-to-all-start) | async-done | bytes 1474592 | tf_op jit(solution)/shard_map/all_to_all | solution.py:887
  183.2 15.3 %fusion.110 = f32[320,3456]{1,0:T(8,128)} fusion(f32[320,1152]{1,0:T(8,128)} %bitcast.206, f32[1152,3456]{1,0:T(8,128)} %all-gather.4.cloned.1.call-done), kind=kOutput, calls=%fused_computation.233 | convolution fusion | flops 7644119040 | bytes 21823488 | tf_op jit(solution)/shard_map/dot_general | solution.py:21
  231.9 8.4 fusion.57
  255.9 6.8 fusion.46
  265.0 7.3 fusion.49
  276.7 9.7 fusion.4
  291.4 7.9 convolution_bitcast_fusion.1
  321.0 80.6 %shard_map.401 = f32[8,320,1152]{2,1,0:T(8,128)S(1)} custom-call(f32[320,1152]{1,0:T(8,128)S(1)} %bitcast.199), custom_call_target="tpu_custom_call" | custom-call | bytes 23592960 | tf_op jit(solution)/shard_map/pallas_call | solution.py:157
  407.9 16.3 %fusion.111 = f32[2560,576]{0,1:T(8,128)} fusion(f32[2560,1152]{1,0:T(8,128)} %all-gather.8.cloned.1.call-done, f32[576,1152]{1,0:T(8,128)S(1)} %copy-done), kind=kOutput, calls=%fused_computation.234 | convolution fusion | flops 10192158720 | bytes 20348928 | tf_op jit(solution)/shard_map/dot_general | solution.py:29
  424.3 22.8 %fusion.10 = (f32[2560,576]{0,1:T(8,128)S(1)}, f32[2560,576]{0,1:T(8,128)}) fusion(f32[2560,576]{0,1:T(8,128)} %fusion.111, f32[576]{0:T(1024)S(1)} %copy-done.112, f32[2560,1152]{1,0:T(8,128)} %bitcast.196, f32[1152,576]{1,0:T(8,128)S(1)} %copy-done.11), kind=kOutput, calls=%fused_computation.15 | convolution fusion | flops 10223124480 | bytes 32147712 | tf_op jit(solution)/shard_map/dot_general | solution.py:21
  447.0 26.3 %fusion.112 = f32[2560,1152]{1,0:T(8,128)S(1)} fusion(f32[2560,576]{0,1:T(8,128)S(1)} %get-tuple-element.55, f32[1152,576]{1,0:T(8,128)S(1)} %copy-done.11), kind=kOutput, calls=%fused_computation.235 | convolution fusion | flops 10192158720 | bytes 20348928 | tf_op jit(solution)/shard_map/dot_general | solution.py:29
  473.4 54.2 %shard_map.403 = f32[320,1152]{1,0:T(8,128)S(1)} custom-call(f32[8,320,1152]{2,1,0:T(8,128)S(1)} %bitcast.198), custom_call_target="tpu_custom_call" | custom-call | bytes 17694720 | tf_op jit(solution)/shard_map/pallas_call | solution.py:221
  536.1 7.1 fusion.113.cross_o
  543.2 30.8 %fusion.115 = f32[1152,576]{1,0:T(8,128)S(1)} fusion(f32[2560,1152]{1,0:T(8,128)} %bitcast.197, f32[2560,576]{0,1:T(8,128)S(1)} %bitcast.223), kind=kOutput, calls=%fused_computation.238 | convolution fusion | flops 10192158720 | bytes 20348928 | tf_op jit(solution)/shard_map/dot_general | solution.py:33
  576.3 17.5 %fusion.116 = f32[576,1152]{1,0:T(8,128)} fusion(f32[2560,576]{0,1:T(8,128)} %get-tuple-element.54, f32[2560,1152]{1,0:T(8,128)} %all-gather.8.cloned.1.call-done), kind=kOutput, calls=%fused_computation.239 | convolution fusion | flops 10192158720 | bytes 20348928 | tf_op jit(solution)/shard_map/dot_general | solution.py:33
  602.9 18.9 %fusion.114 = f32[2560,1152]{1,0:T(8,128)} fusion(f32[2560,576]{0,1:T(8,128)} %get-tuple-element.54, f32[576,1152]{1,0:T(8,128)S(1)} %copy-done), kind=kOutput, calls=%fused_computation.237 | convolution fusion | flops 10192158720 | bytes 20348928 | tf_op jit(solution)/shard_map/dot_general | solution.py:21
  635.3 7.1 fusion.11
  650.3 13.0 %fusion.27 = f32[16,72,480,1]{2,1,3,0:T(8,128)} fusion(f32[20,16,16,72]{3,2,1,0:T(8,128)S(1)} %reshape.414, f32[16,480,20,16]{1,2,3,0:T(8,128)} %copy-done.18, f32[20,16,16]{0,1,2:T(8,128)S(1)} %copy-done.92, f32[20,16,16]{0,1,2:T(8,128)S(1)} %get-tuple-element.192, pred[16,480]{1,0:T(8,128)(4,1)S(1)} %compare_and_fusion), kind=kOutput, calls=%fused_computation.35 | convolution fusion | flops 1071513600 | bytes 13565440 | tf_op jit(solution)/shard_map/fchk,fchd->khd/dot_general | solution.py:25
  663.3 13.0 %fusion.1 = f32[20,16,16,480]{3,0,1,2:T(8,128)S(1)} fusion(f32[20,16,16]{0,1,2:T(8,128)S(1)} %fusion.44, f32[480,16,72,1]{0,2,3,1:T(8,128)S(1)} %bitcast.228, f32[20,16,16,72]{3,2,1,0:T(8,128)} %copy-done.44, f32[20,16,16]{0,1,2:T(8,128)S(1)} %copy-done.92, f32[20,16,16]{0,1,2:T(8,128)S(1)} %get-tuple-element.192, f32[16,480,20,16]{1,2,3,0:T(8,128)} %copy-done.18, ...), kind=kOutput, calls=%fused_computation.2 | convolution fusion | flops 1078886400 | bytes 23416320 | tf_op jit(solution)/shard_map/fchd,khd->fchk/dot_general | solution.py:25
  676.4 8.0 fusion.30
  684.3 7.1 fusion.109
  705.0 8.5 fusion.117.cross_q
  721.6 7.4 fusion.118.attn
  731.4 104.2 %shard_map.404 = (f32[320,1152]{1,0:T(8,128)S(1)}, f32[120,2304]{1,0:T(8,128)S(1)}) custom-call(f32[8,320,1152]{2,1,0:T(8,128)} %bitcast.218, f32[480,2304]{1,0:T(8,128)} %pad_maximum_fusion.kv), custom_call_target="tpu_custom_call" | custom-call | bytes 67108864 | tf_op jit(solution)/shard_map/pallas_call | solution.py:730
  835.6 7.6 fusion.19
  847.8 7.6 fusion.108
  898.9 19.9 %multiply_reduce_fusion.4 = (f32[320]{0:T(512)S(1)}, f32[320,1152]{1,0:T(8,128)S(1)}) fusion(f32[320,1152]{1,0:T(8,128)S(1)} %bitcast.225, f32[320,3456]{1,0:T(8,128)S(1)} %constant_dynamic-update-slice_fusion.1, f32[1152,3456]{1,0:T(8,128)} %all-gather.4.cloned.1.call-done), kind=kOutput, calls=%fused_computation.88 | convolution fusion | flops 7644856320 | bytes 23299328 | tf_op jit(solution)/shard_map/dot_general | solution.py:29
  928.2 37.3 %all-to-all-start.1 = ((f32[20,16,1152]{2,1,0:T(8,128)}), f32[20,16,1152]{2,1,0:T(8,128)}, u32[]{:S(2)}, u32[]{:S(2)}) async-start(f32[20,16,1152]{2,1,0:T(8,128)} %get-tuple-element.202), calls=%async_computation.1 | async-start | bytes 2949120 | tf_op jit(solution)/shard_map/all_to_all | solution.py:891
  970.5 18.3 %fusion.119.first = f32[1152,3456]{1,0:T(8,128)} fusion(f32[320,1152]{1,0:T(8,128)S(1)} %bitcast.207, f32[320,3456]{1,0:T(8,128)} %copy-done.22), kind=kOutput, calls=%fused_computation.242 | convolution fusion | flops 7644119040 | bytes 21823488 | tf_op jit(solution)/shard_map/dot_general | solution.py:33
  988.8 238.2 %shard_map.405 = (f32[144,3456]{1,0:T(8,128)}, f32[144,1152]{1,0:T(8,128)}, f32[144,1152]{1,0:T(8,128)}, f32[144,1152]{1,0:T(8,128)}, f32[144,2304]{1,0:T(8,128)...) custom-call(f32[1152,3456]{1,0:T(8,128)} %fusion.119.first, f32[1152,1152]{1,0:T(8,128)} %fusion.118.attn, ...), custom_call_target="tpu_custom_call" | custom-call | bytes 268435456 | tf_op jit(solution)/shard_map/pallas_call | solution.py:612
  (466 shorter events, 286.8 us)
Async XLA Ops:
  7.2 400.7 %copy-start = (f32[576,1152]{1,0:T(8,128)S(1)}, f32[576,1152]{1,0:T(8,128)}, u32[]{:S(2)}) copy-start(f32[576,1152]{1,0:T(8,128)} %param.44) | copy-start | bytes 7962628
  7.2 176.0 %all-gather.4.cloned.1.call-start = ((), (), s32[]{:S(2)}) async-start(), calls=%async_computation.2 | async-start | bytes 17915904 | tf_op jit(solution)/shard_map/all_gather | solution.py:804
  8.0 247.9 %all-gather.6.cloned.1.call-start = ((), (), s32[]{:S(2)}) async-start(), calls=%async_computation.3 | async-start | bytes 17915904 | tf_op jit(solution)/shard_map/all_gather | solution.py:804
  15.3 90.1 %copy-start.76 = (f32[144,1152]{1,0:T(8,128)S(1)}, f32[144,1152]{1,0:T(8,128)}, u32[]{:S(2)}) copy-start(f32[144,1152]{1,0:T(8,128)} %param.40) | copy-start | bytes 1990660
  15.3 90.1 %copy-start.77 = (f32[144,1152]{1,0:T(8,128)S(1)}, f32[144,1152]{1,0:T(8,128)}, u32[]{:S(2)}) copy-start(f32[144,1152]{1,0:T(8,128)} %param.36) | copy-start | bytes 1990660
  15.3 90.1 %copy-start.78 = (f32[144,1152]{1,0:T(8,128)S(1)}, f32[144,1152]{1,0:T(8,128)}, u32[]{:S(2)}) copy-start(f32[144,1152]{1,0:T(8,128)} %param.34) | copy-start | bytes 1990660
  110.5 68.3 %all-to-all-start = ((f32[5,64,1152]{2,0,1:T(8,128)}), f32[5,64,1152]{2,0,1:T(8,128)}, u32[]{:S(2)}, u32[]{:S(2)}) async-start(f32[5,64,1152]{2,0,1:T(8,128)} %copy.122), calls=%async_computation | async-start | bytes 4718592 | tf_op jit(solution)/shard_map/all_to_all | solution.py:887
  123.6 284.4 %all-gather.8.cloned.1.call-start = ((), (), s32[]{:S(2)}) async-start(), calls=%async_computation.4 | async-start | bytes 13271040 | tf_op jit(solution)/shard_map/all_gather | solution.py:804
  126.1 84.4 %copy-start.99 = (s32[16]{0:T(128)}, s32[16]{0:T(128)S(1)}, u32[]{:S(2)}) copy-start(s32[16]{0:T(128)S(1)} %dynamic_slice.91) | copy-start | bytes 196
  128.1 52.7 %copy-start.89 = (f32[20,16]{1,0:T(8,128)}, f32[20,16]{1,0:T(8,128)S(1)}, u32[]{:S(2)}) copy-start(f32[20,16]{1,0:T(8,128)S(1)} %add_rsqrt_fusion.1) | copy-start | bytes 3844
  129.2 51.7 %copy-start.71 = (f32[16,1152]{1,0:T(8,128)}, f32[16,1152]{1,0:T(8,128)S(1)}, u32[]{:S(2)}) copy-start(f32[16,1152]{1,0:T(8,128)S(1)} %get-tuple-element.170) | copy-start | bytes 221188
  129.2 133.6 %copy-start.79 = (f32[16,1152]{1,0:T(8,128)}, f32[16,1152]{1,0:T(8,128)S(1)}, u32[]{:S(2)}) copy-start(f32[16,1152]{1,0:T(8,128)S(1)} %get-tuple-element.171) | copy-start | bytes 221188
  198.5 1057.4 %all-reduce.6.cloned.1.call-start = ((), (), s32[]{:S(2)}) async-start(), calls=%async_computation.5 | async-start | bytes 10616832 | tf_op jit(solution)/shard_map/psum | solution.py:1074
  210.5 31.2 %copy-start.103 = (pred[20]{0:T(512)(128)(4,1)}, pred[20]{0:T(512)(128)(4,1)S(1)}, u32[]{:S(2)}) copy-start(pred[20]{0:T(512)(128)(4,1)S(1)} %broadcast_compare_fusion.1) | copy-start | bytes 64
  210.8 31.0 %copy-start.61 = (f32[16,20,20]{1,2,0:T(8,128)}, f32[16,20,20]{1,2,0:T(8,128)S(1)}, u32[]{:S(2)}) copy-start(f32[16,20,20]{1,2,0:T(8,128)S(1)} %broadcast_multiply_fusion.2) | copy-start | bytes 76804
  216.4 98.6 %collective-permute-start = (f32[576,576]{1,0:T(8,128)}, f32[576,576]{1,0:T(8,128)}, u32[]{:S(2)}, u32[]{:S(2)}) collective-permute-start(f32[576,576]{1,0:T(8,128)} %pad_maximum_fusion.3), channel_id=1, source_target_pairs={{0,4},{4,0},{8,12},{12,8},{16,20},{20,16},{24,28},{28,24},{1,5},{5... | collective-permute-start | bytes 3981320 | tf_op jit(solution)/shard_map/ppermute | solution.py:59
  316.9 89.0 %collective-permute-start.3 = (f32[288,576]{1,0:T(8,128)S(1)}, f32[288,576]{1,0:T(8,128)S(1)}, u32[]{:S(2)}, u32[]{:S(2)}) collective-permute-start(f32[288,576]{1,0:T(8,128)S(1)} %pad_maximum_fusion.7), channel_id=1, source_target_pairs={{0,24},{4,28},{8,16},{12,20},{16,8},{20,12},{24,0},{28,4},{1,25},{... | collective-permute-start | bytes 1990664 | tf_op jit(solution)/shard_map/ppermute | solution.py:59
  317.3 88.7 %collective-permute-start.2 = (f32[288,576]{1,0:T(8,128)S(1)}, f32[288,576]{1,0:T(8,128)S(1)}, u32[]{:S(2)}, u32[]{:S(2)}) collective-permute-start(f32[288,576]{1,0:T(8,128)S(1)} %pad_maximum_fusion.6), channel_id=1, source_target_pairs={{0,16},{4,20},{8,24},{12,28},{16,0},{20,4},{24,8},{28,12},{1,17},{... | collective-permute-start | bytes 1990664 | tf_op jit(solution)/shard_map/ppermute | solution.py:59
  318.8 87.2 %collective-permute-start.1 = (f32[288,576]{1,0:T(8,128)S(1)}, f32[288,576]{1,0:T(8,128)S(1)}, u32[]{:S(2)}, u32[]{:S(2)}) collective-permute-start(f32[288,576]{1,0:T(8,128)S(1)} %pad_maximum_fusion.5), channel_id=1, source_target_pairs={{0,8},{4,12},{8,0},{12,4},{16,24},{20,28},{24,16},{28,20},{1,9},{5... | collective-permute-start | bytes 1990664 | tf_op jit(solution)/shard_map/ppermute | solution.py:59
  407.9 16.3 %copy-start.112 = (f32[576]{0:T(1024)S(1)}, f32[576]{0:T(1024)}, u32[]{:S(2)}) copy-start(f32[576]{0:T(1024)} %param.43) | copy-start | bytes 6916
  447.0 26.4 %copy-start.48 = (f32[2560,576]{0,1:T(8,128)}, f32[2560,576]{0,1:T(8,128)S(1)}, u32[]{:S(2)}) copy-start(f32[2560,576]{0,1:T(8,128)S(1)} %get-tuple-element.55) | copy-start | bytes 17694724
  576.3 17.5 %collective-permute-start.4 = (f32[576,576]{1,0:T(8,128)}, f32[576,576]{1,0:T(8,128)}, u32[]{:S(2)}, u32[]{:S(2)}) collective-permute-start(f32[576,576]{1,0:T(8,128)} %pad_maximum_fusion.4), channel_id=1, source_target_pairs={{0,4},{4,0},{8,12},{12,8},{16,20},{20,16},{24,28},{28,24},{1,5},{5... | collective-permute-start | bytes 3981320 | tf_op jit(solution)/shard_map/ppermute | solution.py:59
  597.2 28.7 %collective-permute-start.5 = (f32[144,1152]{1,0:T(8,128)}, f32[144,1152]{1,0:T(8,128)}, u32[]{:S(2)}, u32[]{:S(2)}) collective-permute-start(f32[144,1152]{1,0:T(8,128)} %maximum_select_fusion.1), channel_id=1, source_target_pairs={{0,8},{4,12},{8,0},{12,4},{16,24},{20,28},{24,16},{28,20},{1,9},{5... | collective-permute-start | bytes 1990664 | tf_op jit(solution)/shard_map/ppermute | solution.py:59
  599.2 31.6 %collective-permute-start.6 = (f32[144,1152]{1,0:T(8,128)}, f32[144,1152]{1,0:T(8,128)}, u32[]{:S(2)}, u32[]{:S(2)}) collective-permute-start(f32[144,1152]{1,0:T(8,128)} %maximum_select_fusion.2), channel_id=1, source_target_pairs={{0,16},{4,20},{8,24},{12,28},{16,0},{20,4},{24,8},{28,12},{1,17},{... | collective-permute-start | bytes 1990664 | tf_op jit(solution)/shard_map/ppermute | solution.py:59
  601.4 29.3 %collective-permute-start.7 = (f32[144,1152]{1,0:T(8,128)}, f32[144,1152]{1,0:T(8,128)}, u32[]{:S(2)}, u32[]{:S(2)}) collective-permute-start(f32[144,1152]{1,0:T(8,128)} %maximum_select_fusion.3), channel_id=1, source_target_pairs={{0,24},{4,28},{8,16},{12,20},{16,8},{20,12},{24,0},{28,4},{1,25},{... | collective-permute-start | bytes 1990664 | tf_op jit(solution)/shard_map/ppermute | solution.py:59
  898.8 20.1 %copy-start.22 = (f32[320,3456]{1,0:T(8,128)}, f32[320,3456]{1,0:T(8,128)S(1)}, u32[]{:S(2)}) copy-start(f32[320,3456]{1,0:T(8,128)S(1)} %constant_dynamic-update-slice_fusion.1) | copy-start | bytes 13271044
  898.9 21.1 %copy-start.5 = (f32[20,16,1152]{2,1,0:T(8,128)S(1)}, f32[20,16,1152]{2,1,0:T(8,128)}, u32[]{:S(2)}) copy-start(f32[20,16,1152]{2,1,0:T(8,128)} %copy-done.2) | copy-start | bytes 4423684
  898.9 21.1 %copy-start.84 = (f32[20,16]{1,0:T(8,128)S(1)}, f32[20,16]{1,0:T(8,128)}, u32[]{:S(2)}) copy-start(f32[20,16]{1,0:T(8,128)} %copy-done.83) | copy-start | bytes 3844
  898.9 21.1 %copy-start.90 = (f32[20,16]{1,0:T(8,128)S(1)}, f32[20,16]{1,0:T(8,128)}, u32[]{:S(2)}) copy-start(f32[20,16]{1,0:T(8,128)} %copy-done.89) | copy-start | bytes 3844
  927.4 38.2 %copy-start.98 = (f32[1152]{0:T(1024)S(1)}, f32[1152]{0:T(1024)}, u32[]{:S(2)}) copy-start(f32[1152]{0:T(1024)} %get-tuple-element.123) | copy-start | bytes 13828
  928.2 325.1 %all-to-all-start.1 = ((f32[20,16,1152]{2,1,0:T(8,128)}), f32[20,16,1152]{2,1,0:T(8,128)}, u32[]{:S(2)}, u32[]{:S(2)}) async-start(f32[20,16,1152]{2,1,0:T(8,128)} %get-tuple-element.202), calls=%async_computation.1 | async-start | bytes 2949120 | tf_op jit(solution)/shard_map/all_to_all | solution.py:891
  1230.8 17.2 %copy-start.95 = (f32[4,1152]{1,0:T(4,128)S(1)}, f32[4,1152]{1,0:T(4,128)}, u32[]{:S(2)}) copy-start(f32[4,1152]{1,0:T(4,128)} %param.28) | copy-start | bytes 55300
  (102 other events, 475.3 us)
Sparse Core Ops, SparseCore 0:
  9.9 104.4 all-gather.3
  116.9 86.2 all-gather.5
  205.7 68.7 all-gather.7
  634.1 236.6 all-reduce.5

commit v5 on v4

--- a/solution.py
+++ b/solution.py
@@ -15,14 +15,11 @@
 
 EPSILON = 1e-06
 BEST = lax.Precision.HIGH
+LIGHT = pl.CostEstimate(flops=0, bytes_accessed=1 << 16, transcendentals=0)
 
 
 def matmul(left, right):
     return jnp.dot(left, right, precision=BEST)
-
-
-def contract(form, left, right):
-    return jnp.einsum(form, left, right, precision=BEST)
 
 
 def matmul_nt(left, right):
@@ -45,13 +42,6 @@
     first_mean = jnp.mean(grad_normed, axis=-1, keepdims=True)
     second_mean = jnp.mean(grad_normed * normed, axis=-1, keepdims=True)
     return inverse * (grad_normed - first_mean - normed * second_mean)
-
-
-def softmax_rows(scores, allowed):
-    masked = jnp.where(allowed, scores, -1e30)
-    highest = jnp.max(masked, axis=-1, keepdims=True)
-    exponent = jnp.exp(masked - highest)
-    return exponent / jnp.sum(exponent, axis=-1, keepdims=True)
 
 
 def swap(value, axis, bit):
@@ -161,7 +151,7 @@
         out_specs=pl.BlockSpec(memory_space=pl.ANY),
         scratch_shapes=[pltpu.SemaphoreType.DMA, pltpu.SemaphoreType.DMA((28,)), pltpu.SemaphoreType.DMA((28,))],
         compiler_params=pltpu.CompilerParams(collective_id=0, has_side_effects=True, vmem_limit_bytes=16 << 20),
-        cost_estimate=pl.CostEstimate(flops=0, bytes_accessed=64 * length * width, transcendentals=0),
+        cost_estimate=LIGHT,
     )(rows).reshape(8 * length, width)
 
 
@@ -230,7 +220,7 @@
             pltpu.SemaphoreType.DMA((4,)), pltpu.SemaphoreType.DMA((10,)), pltpu.SemaphoreType.DMA((10,)),
         ],
         compiler_params=pltpu.CompilerParams(collective_id=1, has_side_effects=True, vmem_limit_bytes=32 << 20),
-        cost_estimate=pl.CostEstimate(flops=0, bytes_accessed=48 * length * width, transcendentals=0),
+        cost_estimate=LIGHT,
     )(parts.reshape((8,) + block))
 
 
@@ -271,15 +261,16 @@
 
 
 def begin_kernel(
-    tokens, slots, small, kv,
-    tokens_out, slots_out, small_out, kv_out,
-    small_1, small_2, small_got, kv_1, kv_2, kv_got_core, kv_got_1, kv_got_2,
+    tokens, later, slots, small, kv, weight,
+    tokens_out, later_out, slots_out, small_out, kv_out, weight_out,
+    weight_sem, small_1, small_2, small_got, kv_1, kv_2, kv_got_core, kv_got_1, kv_got_2,
     send_sems, recv_sems,
 ):
     me, z = lax.axis_index("patch"), lax.axis_index("frame")
     core, x, y = ({"patch": me ^ k} for k in (1, 2, 4))
     frames = [None] + [{"frame": z ^ k} for k in (1, 2, 3)]
-    greet_all([core, x, y] + frames[1:])
+    chips = {2: x, 4: y, 6: {"patch": me ^ 6}}
+    greet_all([core, x, y, chips[6]] + frames[1:])
     links = Links(send_sems, recv_sems)
     count, part = tokens.shape[0], tokens.shape[1] // 4
     rows, width = kv_1.shape
@@ -300,6 +291,18 @@
     links.send(kv.at[:, theirs], kv_got_core, at_kv, core)
     token_at = [None] + [links.plan() for _ in range(3)]
     slot_at = [None] + [links.plan() for _ in range(3)]
+    chip_width = weight.shape[1] // 4
+    own_chip = weight_out.at[me]
+    own_copy = pltpu.make_async_copy(
+        weight.at[:, pl.ds(pl.multiple_of(me // 2 * chip_width, 128), chip_width)],
+        own_chip, weight_sem,
+    )
+    own_copy.start()
+    weight_at = {k: links.plan() for k in (2, 4, 6)}
+    pair_at = {k: links.plan() for k in (0, 2, 4, 6)}
+    for k, device in chips.items():
+        start = pl.multiple_of((me ^ k) // 2 * chip_width, 128)
+        links.send(weight.at[:, pl.ds(start, chip_width)], own_chip, weight_at[k], device)
     for k in (1, 2, 3):
         links.send(slots, slots_out.at[z], slot_at[k], frames[k])
         links.send(tokens.at[:, columns(k)], tokens_out.at[of_slots(0)], token_at[k], frames[k])
@@ -340,6 +343,10 @@
     for k in (1, 2, 3):
         links.send(share(0, mine), share(0, mine), kv_at[k], frames[k])
     links.send(share(0, mine), share(0, mine), core_at[0], core)
+    later_at = [None] + [links.plan() for _ in range(3)]
+    for k in (1, 2, 3):
+        links.send(later.at[:, columns(k)], later_out.at[of_slots(0)], later_at[k], frames[k])
+    later_out[of_slots(0)] = later[:, columns(0)]
     for k in (1, 2, 3):
         links.wait(share(k, mine), kv_at[k], frames[k])
         links.send(share(k, mine), share(k, mine), core_at[k], core)
@@ -348,10 +355,19 @@
         links.wait(tokens_out.at[of_slots(k)], token_at[k], frames[k])
     for k in range(4):
         links.wait(share(k, theirs), core_at[k], core)
+    own_copy.wait()
+    for k in (0, 2, 4, 6):
+        if k:
+            links.wait(weight_out.at[me ^ k], weight_at[k], chips[k])
+        links.send(weight_out.at[me ^ k], weight_out.at[me ^ k], pair_at[k], core)
+    for k in (0, 2, 4, 6):
+        links.wait(weight_out.at[me ^ 1 ^ k], pair_at[k], core)
+    for k in (1, 2, 3):
+        links.wait(later_out.at[of_slots(k)], later_at[k], frames[k])
     links.drain()
 
 
-def begin(tokens, slots, small, kv):
+def begin(tokens, later, slots, small, kv, weight):
     count, cols, width = tokens.shape
     rows = kv.shape[0]
     f32, vmem = jnp.float32, pl.BlockSpec(memory_space=pltpu.VMEM)
@@ -360,22 +376,25 @@
         begin_kernel,
         out_shape=(
             jax.ShapeDtypeStruct((4 * count, cols // 4, width), f32),
+            jax.ShapeDtypeStruct((4 * count, cols // 4, width), f32),
             jax.ShapeDtypeStruct((4,) + slots.shape, f32),
             jax.ShapeDtypeStruct(small.shape, f32),
             jax.ShapeDtypeStruct((4 * rows, 2 * width), f32),
+            jax.ShapeDtypeStruct((8, weight.shape[0], weight.shape[1] // 4), f32),
         ),
-        in_specs=[vmem] * 4,
-        out_specs=[vmem] * 4,
+        in_specs=[vmem] * 5 + [pl.BlockSpec(memory_space=pl.ANY)],
+        out_specs=[vmem] * 6,
         scratch_shapes=[
+            pltpu.SemaphoreType.DMA,
             pltpu.VMEM(small.shape, f32), pltpu.VMEM(small.shape, f32),
             pltpu.VMEM((3,) + small.shape, f32), half, half, half, half, half,
-            pltpu.SemaphoreType.DMA((24,)), pltpu.SemaphoreType.DMA((24,)),
+            pltpu.SemaphoreType.DMA((32,)), pltpu.SemaphoreType.DMA((32,)),
         ],
         compiler_params=pltpu.CompilerParams(
-            collective_id=2, has_side_effects=True, vmem_limit_bytes=32 << 20
+            collective_id=2, has_side_effects=True, vmem_limit_bytes=40 << 20
         ),
-        cost_estimate=pl.CostEstimate(flops=0, bytes_accessed=32 << 20, transcendentals=0),
-    )(tokens, slots, small, kv)
+        cost_estimate=LIGHT,
+    )(tokens, later, slots, small, kv, weight)
 
 
 UNITS = 6
@@ -401,14 +420,13 @@
 
     token_at = [None] + [links.plan() for _ in range(3)]
 
-    def send_tokens():
-        for k in (1, 2, 3):
-            links.send(
-                tokens.at[pl.ds((z ^ k) * count, count)],
-                tokens_out.at[:, pl.ds(pl.multiple_of(z * part, part), part)],
-                token_at[k], frames[k],
-            )
-        tokens_out[:, pl.ds(pl.multiple_of(z * part, part), part)] = tokens[pl.ds(z * count, count)]
+    def send_tokens(k):
+        where = pl.ds(pl.multiple_of(z * part, part), part)
+        if k == 0:
+            tokens_out[:, where] = tokens[pl.ds(z * count, count)]
+        else:
+            source = tokens.at[pl.ds((z ^ k) * count, count)]
+            links.send(source, tokens_out.at[:, where], token_at[k], frames[k])
 
     def frame_steps(value, result, near_got, facing_got):
         up, over, down = links.plan(), links.plan(), links.plan()
@@ -559,38 +577,50 @@
     small_sums[1] = small_sums[0] + small_got[1]
     links.send(small_sums.at[1], small_got.at[2], small_at[2], y)
     stage_one(1)
-    steps[6][1]()
-    steps[7][1]()
+    stage_two(0)
     links.wait(small_got.at[2], small_at[2], y)
     small_sums[2] = small_sums[1] + small_got[2]
     small_steps[0]()
-    stage_two(0)
     caption_x()
     stage_one(2)
-    send_tokens()
-    small_steps[1]()
+    steps[6][1]()
+    steps[7][1]()
+    send_tokens(0)
+    send_tokens(1)
+    stage_two(1)
+    stage_three(0)
+    stage_one(3)
     steps[6][2]()
     steps[7][2]()
+    small_steps[1]()
+    send_tokens(2)
+    stage_two(2)
+    stage_three(1)
+    stage_one(4)
+    steps[0][1]()
     small_steps[2]()
-    for u in range(1, UNITS):
-        stage_two(u)
-        if u + 2 < UNITS:
-            stage_one(u + 2)
-        stage_three(u - 1)
-        if u >= 2:
-            steps[u - 2][1]()
-        if u >= 3:
-            steps[u - 3][2]()
-        if u == 2:
-            caption_y()
-        if u == 4:
-            caption_core()
-    stage_three(UNITS - 1)
-    steps[UNITS - 2][1]()
-    steps[UNITS - 3][2]()
-    steps[UNITS - 1][1]()
-    steps[UNITS - 2][2]()
-    steps[UNITS - 1][2]()
+    caption_y()
+    send_tokens(3)
+    stage_two(3)
+    stage_three(2)
+    stage_one(5)
+    steps[1][1]()
+    steps[0][2]()
+    stage_two(4)
+    stage_three(3)
+    stage_two(5)
+    steps[2][1]()
+    steps[1][2]()
+    caption_core()
+    stage_three(4)
+    steps[3][1]()
+    steps[2][2]()
+    stage_three(5)
+    steps[4][1]()
+    steps[3][2]()
+    steps[5][1]()
+    steps[4][2]()
+    steps[5][2]()
     for step in steps + [small_steps]:
         step[3]()
     caption_end()
@@ -631,7 +661,7 @@
         compiler_params=pltpu.CompilerParams(
             collective_id=3, has_side_effects=True, vmem_limit_bytes=60 << 20
         ),
-        cost_estimate=pl.CostEstimate(flops=0, bytes_accessed=256 << 20, transcendentals=0),
+        cost_estimate=LIGHT,
     )(first, attn, cross_q, cross_o, kv, tokens, small, caption)
 
 
@@ -746,7 +776,7 @@
         compiler_params=pltpu.CompilerParams(
             collective_id=4, has_side_effects=True, vmem_limit_bytes=48 << 20
         ),
-        cost_estimate=pl.CostEstimate(flops=0, bytes_accessed=64 << 20, transcendentals=0),
+        cost_estimate=LIGHT,
     )(parts.reshape((8,) + block), kv)
 
 
@@ -776,6 +806,272 @@
     )(block)
 
 
+def halves(x):
+    high = x.astype(jnp.bfloat16)
+    return high, (x - high.astype(jnp.float32)).astype(jnp.bfloat16)
+
+
+NN, NT, TN = (((1,), (0,)), ((), ())), (((1,), (1,)), ((), ())), (((0,), (0,)), ((), ()))
+
+
+def three(left, right, dims):
+    def dot(a, b):
+        return lax.dot_general(a, b, dims, preferred_element_type=jnp.float32)
+
+    return dot(left[0], right[0]) + (dot(left[0], right[1]) + dot(left[1], right[0]))
+
+
+WINDOW = 256
+
+
+def head_window(head, head_dim, width):
+    start = jnp.minimum(head * head_dim // 128 * 128, width - WINDOW)
+    lane = lax.broadcasted_iota(jnp.int32, (1, WINDOW), 1) - (head * head_dim - start)
+    mask = ((lane >= 0) & (lane < head_dim)).astype(jnp.float32)
+    return pl.ds(pl.multiple_of(start, 128), WINDOW), mask
+
+
+def softmax_last(scores):
+    exponent = jnp.exp(scores - jnp.max(scores, axis=-1, keepdims=True))
+    return exponent / jnp.sum(exponent, axis=-1, keepdims=True)
+
+
+GROUP = 8
+
+
+def grouped(ref, group, lanes):
+    slots = ref.shape[0]
+    value = ref[:, group * GROUP : (group + 1) * GROUP, lanes]
+    return value.reshape(slots * GROUP, value.shape[-1])
+
+
+def store_halves(high, low, index, value):
+    high[index], low[index] = halves(value)
+
+
+def frame_attention_kernel(qkv, b_query, b_value, distance, allowed, probs, out, *split):
+    (q_high, q_low, k_high, k_low, v_high, v_low), total = split[:6], split[6]
+    slots, width = qkv.shape[0], out.shape[-1]
+    head_dim = width // H
+    scaling = head_dim**-0.5
+    for g in range(2):
+        store_halves(q_high, q_low, g, grouped(qkv, g, slice(0, width)) + b_query[...])
+        store_halves(k_high, k_low, g, grouped(qkv, g, slice(width, 2 * width)))
+        store_halves(
+            v_high, v_low, g, grouped(qkv, g, slice(2 * width, 3 * width)) + b_value[...]
+        )
+    total[...] = jnp.zeros(total.shape, jnp.float32)
+
+    def step(head, _):
+        at, mask = head_window(head, head_dim, width)
+        mask = mask.astype(jnp.bfloat16)
+        slope = jnp.exp2(-8.0 / H * (jnp.full((1, 1), head, jnp.int32).astype(jnp.float32) + 1.0))
+        for g in range(2):
+            query = (q_high[g, :, at] * mask, q_low[g, :, at] * mask)
+            scores = three(query, (k_high[g, :, at], k_low[g, :, at]), NT)
+            scores = jnp.where(allowed[...] > 0, scores * scaling - slope * distance[...], -1e30)
+            prob = softmax_last(scores)
+            probs[head, g] = prob
+            value = (v_high[g, :, at] * mask, v_low[g, :, at] * mask)
+            total[g, :, at] = total[g, :, at] + three(halves(prob), value, NN)
+        return 0
+
+    lax.fori_loop(0, H, step, 0, unroll=4)
+    for g in range(2):
+        out[:, g * GROUP : (g + 1) * GROUP, :] = total[g].reshape(slots, GROUP, width)
+
+
+def frame_tables(frame_pos):
+    slots = frame_pos.shape[0]
+    position = jnp.repeat(frame_pos, GROUP)
+    column = jnp.tile(jnp.arange(GROUP), slots)
+    distance = jnp.abs(position[:, None] - position[None, :])
+    same = column[:, None] == column[None, :]
+    return distance, (same & (position[None, :] < FRAMES - 0.5)).astype(jnp.float32)
+
+
+VMEM_SPEC = pl.BlockSpec(memory_space=pltpu.VMEM)
+
+
+def frame_attention(qkv, b_query, b_value, distance, allowed):
+    slots, cols, width = qkv.shape[0], qkv.shape[1], qkv.shape[2] // 3
+    rows = slots * GROUP
+    part = pltpu.VMEM((2, rows, width), jnp.bfloat16)
+    return pl.pallas_call(
+        frame_attention_kernel,
+        out_shape=(
+            jax.ShapeDtypeStruct((H, 2, rows, rows), jnp.float32),
+            jax.ShapeDtypeStruct((slots, cols, width), jnp.float32),
+        ),
+        in_specs=[VMEM_SPEC] * 5,
+        out_specs=[VMEM_SPEC] * 2,
+        scratch_shapes=[part] * 6 + [pltpu.VMEM((2, rows, width), jnp.float32)],
+        compiler_params=pltpu.CompilerParams(vmem_limit_bytes=40 << 20),
+        cost_estimate=LIGHT,
+    )(qkv, b_query.reshape(1, width), b_value.reshape(1, width), distance, allowed)
+
+
+def frame_attention_back_kernel(qkv, b_query, b_value, probs, attended, grad, out, *split):
+    width = attended.shape[-1]
+    slots, head_dim = qkv.shape[0], width // H
+    scaling = head_dim**-0.5
+    names = [(split[2 * i], split[2 * i + 1]) for i in range(4)]
+    (q_high, q_low), (k_high, k_low), (v_high, v_low), (g_high, g_low) = names
+    total, product = split[8], split[9]
+    for g in range(2):
+        store_halves(q_high, q_low, g, grouped(qkv, g, slice(0, width)) + b_query[...])
+        store_halves(k_high, k_low, g, grouped(qkv, g, slice(width, 2 * width)))
+        store_halves(
+            v_high, v_low, g, grouped(qkv, g, slice(2 * width, 3 * width)) + b_value[...]
+        )
+        upstream = grouped(grad, g, slice(0, width))
+        store_halves(g_high, g_low, g, upstream)
+        product[g] = upstream * grouped(attended, g, slice(0, width))
+    total[...] = jnp.zeros(total.shape, jnp.float32)
+
+    def step(head, _):
+        at, mask = head_window(head, head_dim, width)
+        small = mask.astype(jnp.bfloat16)
+
+        def masked(high, low, g):
+            return high[g, :, at] * small, low[g, :, at] * small
+
+        for g in range(2):
+            upstream = masked(g_high, g_low, g)
+            prob = probs[head, g]
+            grad_prob = three(upstream, (v_high[g, :, at], v_low[g, :, at]), NT)
+            term = jnp.sum(product[g, :, at] * mask, axis=-1, keepdims=True)
+            score = halves(prob * (grad_prob - term) * scaling)
+            total[0, g, :, at] = total[0, g, :, at] + three(score, masked(k_high, k_low, g), NN)
+            total[1, g, :, at] = total[1, g, :, at] + three(score, masked(q_high, q_low, g), TN)
+            total[2, g, :, at] = total[2, g, :, at] + three(halves(prob), upstream, TN)
+        return 0
+
+    lax.fori_loop(0, H, step, 0, unroll=4)
+    for g in range(2):
+        for i in range(3):
+            out[:, g * GROUP : (g + 1) * GROUP, i * width : (i + 1) * width] = total[
+                i, g
+            ].reshape(slots, GROUP, width)
+
+
+def frame_attention_back(qkv, b_query, b_value, probs, attended, grad):
+    slots, cols, width = attended.shape
+    rows = slots * GROUP
+    part = pltpu.VMEM((2, rows, width), jnp.bfloat16)
+    return pl.pallas_call(
+        frame_attention_back_kernel,
+        out_shape=jax.ShapeDtypeStruct((slots, cols, 3 * width), jnp.float32),
+        in_specs=[VMEM_SPEC] * 6,
+        out_specs=VMEM_SPEC,
+        scratch_shapes=[part] * 8
+        + [pltpu.VMEM((3, 2, rows, width), jnp.float32), pltpu.VMEM((2, rows, width), jnp.float32)],
+        compiler_params=pltpu.CompilerParams(vmem_limit_bytes=48 << 20),
+        cost_estimate=LIGHT,
+    )(qkv, b_query.reshape(1, width), b_value.reshape(1, width), probs, attended, grad)
+
+
+def cross_attention_kernel(queries, b_query, kv, b_value, allowed, probs, out, *split):
+    q_high, q_low, k_high, k_low, v_high, v_low = split
+    width = out.shape[-1]
+    head_dim = width // H
+    scaling = head_dim**-0.5
+    store_halves(q_high, q_low, Ellipsis, queries[...] + b_query[...])
+    store_halves(k_high, k_low, Ellipsis, kv[:, 0:width])
+    store_halves(v_high, v_low, Ellipsis, kv[:, width : 2 * width] + b_value[...])
+    out[...] = jnp.zeros(out.shape, jnp.float32)
+
+    def step(head, _):
+        at, mask = head_window(head, head_dim, width)
+        mask = mask.astype(jnp.bfloat16)
+        query = (q_high[:, at] * mask, q_low[:, at] * mask)
+        scores = three(query, (k_high[:, at], k_low[:, at]), NT)
+        prob = softmax_last(jnp.where(allowed[...] > 0, scores * scaling, -1e30))
+        probs[head] = prob
+        value = (v_high[:, at] * mask, v_low[:, at] * mask)
+        out[:, at] = out[:, at] + three(halves(prob), value, NN)
+        return 0
+
+    lax.fori_loop(0, H, step, 0, unroll=4)
+
+
+def cross_attention(queries, b_query, kv, b_value, allowed):
+    rows, width = queries.shape
+    keys = kv.shape[0]
+    q_part = pltpu.VMEM((rows, width), jnp.bfloat16)
+    k_part = pltpu.VMEM((keys, width), jnp.bfloat16)
+    return pl.pallas_call(
+        cross_attention_kernel,
+        out_shape=(
+            jax.ShapeDtypeStruct((H, rows, keys), jnp.float32),
+            jax.ShapeDtypeStruct((rows, width), jnp.float32),
+        ),
+        in_specs=[VMEM_SPEC] * 5,
+        out_specs=[VMEM_SPEC] * 2,
+        scratch_shapes=[q_part] * 2 + [k_part] * 4,
+        compiler_params=pltpu.CompilerParams(vmem_limit_bytes=48 << 20),
+        cost_estimate=LIGHT,
+    )(queries, b_query.reshape(1, width), kv, b_value.reshape(1, width), allowed)
+
+
+def cross_attention_back_kernel(
+    queries, b_query, kv, b_value, probs, attended, grad, grad_q, grad_kv, *split
+):
+    names = [(split[2 * i], split[2 * i + 1]) for i in range(4)]
+    (q_high, q_low), (g_high, g_low), (k_high, k_low), (v_high, v_low) = names
+    product = split[8]
+    width = grad_q.shape[-1]
+    head_dim = width // H
+    scaling = head_dim**-0.5
+    store_halves(q_high, q_low, Ellipsis, queries[...] + b_query[...])
+    store_halves(k_high, k_low, Ellipsis, kv[:, 0:width])
+    store_halves(v_high, v_low, Ellipsis, kv[:, width : 2 * width] + b_value[...])
+    store_halves(g_high, g_low, Ellipsis, grad[...])
+    product[...] = grad[...] * attended[...]
+    grad_q[...] = jnp.zeros(grad_q.shape, jnp.float32)
+    grad_kv[...] = jnp.zeros(grad_kv.shape, jnp.float32)
+
+    def step(head, _):
+        at, mask = head_window(head, head_dim, width)
+        start = jnp.minimum(head * head_dim // 128 * 128, width - WINDOW)
+        at_value = pl.ds(pl.multiple_of(start + width, 128), WINDOW)
+        small = mask.astype(jnp.bfloat16)
+
+        def masked(high, low):
+            return high[:, at] * small, low[:, at] * small
+
+        upstream = masked(g_high, g_low)
+        prob = probs[head]
+        grad_prob = three(upstream, (v_high[:, at], v_low[:, at]), NT)
+        term = jnp.sum(product[:, at] * mask, axis=-1, keepdims=True)
+        score = halves(prob * (grad_prob - term) * scaling)
+        grad_q[:, at] = grad_q[:, at] + three(score, masked(k_high, k_low), NN)
+        grad_kv[:, at] = grad_kv[:, at] + three(score, masked(q_high, q_low), TN)
+        grad_kv[:, at_value] = grad_kv[:, at_value] + three(halves(prob), upstream, TN)
+        return 0
+
+    lax.fori_loop(0, H, step, 0, unroll=4)
+
+
+def cross_attention_back(queries, b_query, kv, b_value, probs, attended, grad):
+    rows, width = queries.shape
+    keys = kv.shape[0]
+    q_part = pltpu.VMEM((rows, width), jnp.bfloat16)
+    k_part = pltpu.VMEM((keys, width), jnp.bfloat16)
+    return pl.pallas_call(
+        cross_attention_back_kernel,
+        out_shape=(
+            jax.ShapeDtypeStruct((rows, width), jnp.float32),
+            jax.ShapeDtypeStruct(kv.shape, jnp.float32),
+        ),
+        in_specs=[VMEM_SPEC] * 7,
+        out_specs=[VMEM_SPEC] * 2,
+        scratch_shapes=[q_part] * 4 + [k_part] * 4 + [pltpu.VMEM((rows, width), jnp.float32)],
+        compiler_params=pltpu.CompilerParams(vmem_limit_bytes=52 << 20),
+        cost_estimate=LIGHT,
+    )(queries, b_query.reshape(1, width), kv, b_value.reshape(1, width), probs, attended, grad)
+
+
 def assemble_kernel(axis, dim, *refs):
     blocks, whole = refs[:-1], refs[-1]
     own = lax.axis_index(axis)
@@ -796,7 +1092,7 @@
         in_specs=[pl.BlockSpec(memory_space=pltpu.VMEM)] * len(blocks),
         out_specs=pl.BlockSpec(memory_space=pltpu.VMEM),
         compiler_params=pltpu.CompilerParams(vmem_limit_bytes=24 << 20),
-        cost_estimate=pl.CostEstimate(flops=0, bytes_accessed=2 * size, transcendentals=0),
+        cost_estimate=LIGHT,
     )(*blocks)
 
 
@@ -833,22 +1129,6 @@
         swap(blocks[2], "patch", 4),
         swap(blocks[3], "patch", 6),
     ]
-
-
-def to_own_columns(weight):
-    if not small_patch():
-        return lax.all_to_all(weight, "patch", 1, 0, tiled=True)
-    length = weight.shape[0]
-    blocks = [block_of(weight, "patch", k, 1) for k in range(8)]
-    theirs = swap(jnp.concatenate(blocks[1::2], axis=0), "patch", 1)
-    both = [
-        jnp.concatenate([kept, theirs[j * length : (j + 1) * length]], axis=0)
-        for j, kept in enumerate(blocks[::2])
-    ]
-    halves = []
-    for block in over_chips(both):
-        halves += [block[:length], block[length:]]
-    return assemble(halves, "patch", 0)
 
 
 def back_to_rows(grad):
@@ -879,7 +1159,7 @@
         in_specs=[pl.BlockSpec(memory_space=pltpu.VMEM)],
         out_specs=pl.BlockSpec(memory_space=pltpu.VMEM),
         compiler_params=pltpu.CompilerParams(vmem_limit_bytes=24 << 20),
-        cost_estimate=pl.CostEstimate(flops=0, bytes_accessed=8 * stack.size, transcendentals=0),
+        cost_estimate=LIGHT,
     )(stack)
 
 
@@ -895,22 +1175,28 @@
     return token_scatter(parts) if small_patch() else scatter_rows(parts)
 
 
-def open_up(block_input, frame_slot, small, kv_part):
+def open_up(block_input, cotangent, frame_slot, small, kv_part, fc1_weight):
     frame_number = frame_slot.astype(jnp.float32)
     if not small_patch():
         kv = all_sum(kv_part, "patch")
         return (
             to_columns(block_input),
+            to_columns(cotangent),
             all_sum(placed(frame_number, "frame"), "frame"),
             all_sum(small, "patch"),
             lax.all_gather(kv, "frame", axis=0, tiled=True),
+            lax.all_to_all(fc1_weight, "patch", 1, 0, tiled=True),
         )
     count = frame_slot.shape[0]
     rows = -(-small.shape[0] // 1024) * 8
-    tokens, slots, summed, kv = begin(
-        block_input, padded(frame_number, 8), padded(small, rows), kv_part
-    )
-    return tokens, slots[:, 0, :count].reshape(-1), summed.reshape(-1)[: small.shape[0]], kv
+    tokens, later, slots, summed, kv, pairs = begin(
+        block_input, cotangent, padded(frame_number, 8), padded(small, rows), kv_part, fc1_weight
+    )
+    half = pairs.shape[2] // 2
+    weight = jnp.where(lax.axis_index("patch") % 2 == 0, pairs[..., :half], pairs[..., half:])
+    summed = summed.reshape(-1)[: small.shape[0]]
+    slots = slots[:, 0, :count].reshape(-1)
+    return tokens, later, slots, summed, kv, weight.reshape(-1, half)
 
 
 def mid_way(parts, kv):
@@ -965,8 +1251,6 @@
     caption_mask,
 ):
     width = block_input.shape[-1]
-    head_dim = width // H
-    scaling = head_dim ** (-0.5)
     cond_act, silu_pull = jax.vjp(jax.nn.silu, cond)
     cond_own = own_part(cond_act, "patch", 1)
     modulation_part = matmul(cond_own, ada_weight)
@@ -979,10 +1263,14 @@
     )
     caption_rows = caption.reshape(CLIPS * CAP, width)
     caption_share = own_part(own_part(caption_rows, "frame", 0), "patch", 1)
-    tokens_in, frame_pos, small, caption_kv = open_up(
-        block_input, frame_slot, small, matmul(caption_share, cross_kv_weight)
-    )
-    cotangent = to_columns(after(out_cotangent, tokens_in))
+    tokens_in, cotangent, frame_pos, small, caption_kv, w_first = open_up(
+        block_input,
+        out_cotangent,
+        frame_slot,
+        small,
+        matmul(caption_share, cross_kv_weight),
+        fc1_weight,
+    )
     w_qkv = gather_rows(qkv_weight)
     three = jnp.concatenate([attn_out_weight, cross_q_weight, cross_out_weight], axis=1)
     w_three = gather_rows(after(three, tokens_in))
@@ -1008,40 +1296,26 @@
         per_column, 6, axis=1
     )
 
-    cross_keys = caption_kv[:, :width].reshape(CLIPS * CAP, H, head_dim)
-    cross_values = (caption_kv[:, width:] + b_cross_v).reshape(CLIPS * CAP, H, head_dim)
-
     grad_mlp = (column_mask * gate_two * cotangent).reshape(rows, width)
     normed_one, inverse_one = normalize(tokens_in)
     hidden_one = (normed_one * (1.0 + scale_one) + shift_one).reshape(rows, width)
     qkv_rows = matmul(hidden_one, w_qkv)
-    w_first = to_own_columns(after(fc1_weight, qkv_rows))
     grad_mlp_all = gather_rows(after(grad_mlp, qkv_rows))
-    queries = (qkv_rows[:, :width] + b_query).reshape(slots, cols, H, head_dim)
-    keys = qkv_rows[:, width : 2 * width].reshape(slots, cols, H, head_dim)
-    values = (qkv_rows[:, 2 * width :] + b_value).reshape(slots, cols, H, head_dim)
-    slopes = 2.0 ** (-8.0 * (jnp.arange(H).astype(jnp.float32) + 1.0) / H)
-    distance = jnp.abs(frame_pos[:, None] - frame_pos[None, :])
-    bias_table = -slopes[:, None, None] * distance[None]
-    key_valid = (frame_pos < FRAMES - 0.5)[None, None, None, :]
-    scores = contract("fchd,schd->chfs", queries, keys) * scaling + bias_table[None]
-    probs = softmax_rows(scores, key_valid)
-    attended = contract("chfs,schd->fchd", probs, values)
+    qkv = qkv_rows.reshape(slots, cols, 3 * width)
+    probs, attended = frame_attention(qkv, b_query, b_value, *frame_tables(frame_pos))
     attended_rows = attended.reshape(rows, width)
     attn_branch = (matmul(attended_rows, w_attn) + b_attn).reshape(slots, cols, width)
     after_attn = tokens_in + column_mask * gate_one * attn_branch
     after_attn_rows = after_attn.reshape(rows, width)
-    cross_queries = (matmul(after_attn_rows, w_cross_q) + b_cross_q).reshape(
-        slots, cols, H, head_dim
-    )
+    cross_queries = matmul(after_attn_rows, w_cross_q)
     key_clip = jnp.arange(CLIPS * CAP, dtype=jnp.int32) // CAP
-    caption_ok = (
-        (clip_own[:, None] == key_clip[None, :]) & (caption_mask.reshape(CLIPS * CAP)[None, :] > 0)
-    )[None, :, None, :]
-    cross_scores = contract("fchd,khd->fchk", cross_queries, cross_keys) * scaling
-    cross_probs = softmax_rows(cross_scores, caption_ok)
-    cross_att = contract("fchk,khd->fchd", cross_probs, cross_values)
-    cross_rows = cross_att.reshape(rows, width)
+    caption_ok = (clip_own[:, None] == key_clip[None, :]) & (
+        caption_mask.reshape(CLIPS * CAP)[None, :] > 0
+    )
+    caption_ok = jnp.tile(caption_ok.astype(jnp.float32), (slots, 1))
+    cross_probs, cross_rows = cross_attention(
+        cross_queries, b_cross_q, caption_kv, b_cross_v, caption_ok
+    )
     cross_branch = (matmul(cross_rows, w_cross_o) + b_cross_o).reshape(slots, cols, width)
     after_cross = after_attn + column_mask * cross_branch
     normed_two, inverse_two = normalize(after_cross)
@@ -1066,30 +1340,21 @@
     activated, grad_pre = after((activated, grad_pre), grad_w_cross_o)
     grad_w_first = matmul_tn(hidden_all, grad_pre)
     grad_w_second = matmul_tn(activated, grad_mlp_all)
+    grad_cross_branch = after(grad_cross_branch, (grad_w_first, grad_w_second))
     if small_patch():
         grad_w_first = back_to_rows(grad_w_first)
     else:
         grad_w_first = lax.all_to_all(grad_w_first, "patch", 0, 1, tiled=True)
-    grad_cross_branch = after(grad_cross_branch, (grad_w_first, grad_w_second))
+    first_sent = grad_w_first
     grad_w_first, grad_w_second = lax.psum((grad_w_first, grad_w_second), "frame")
     if small_patch():
         grad_w_first = side_by_side(grad_w_first)
     grad_b_first = jnp.sum(grad_pre, axis=0)
     mlp_parts = matmul(activated, fc2_weight)
-    grad_cross_att = matmul_nt(grad_cross_branch, w_cross_o).reshape(slots, cols, H, head_dim)
-    cross_row_terms = jnp.sum(grad_cross_att * cross_att, axis=-1)[..., None]
-    grad_cross_probs = contract("fchd,khd->fchk", grad_cross_att, cross_values)
-    grad_cross_scores = cross_probs * (grad_cross_probs - cross_row_terms) * scaling
-    grad_cross_queries = contract("fchk,khd->fchd", grad_cross_scores, cross_keys).reshape(
-        rows, width
-    )
-    grad_cross_keys = contract("fchk,fchd->khd", grad_cross_scores, cross_queries).reshape(
-        CLIPS * CAP, width
-    )
-    grad_cross_values = contract("fchk,fchd->khd", cross_probs, grad_cross_att).reshape(
-        CLIPS * CAP, width
-    )
-    grad_kv = jnp.concatenate([grad_cross_keys, grad_cross_values], axis=1)
+    grad_cross_rows = matmul_nt(grad_cross_branch, w_cross_o)
+    grad_cross_queries, grad_kv = cross_attention_back(
+        cross_queries, b_cross_q, caption_kv, b_cross_v, cross_probs, cross_rows, grad_cross_rows
+    )
     grad_w_cross_q = matmul_tn(after_attn_rows, grad_cross_queries)
     grad_b_cross_q = jnp.sum(grad_cross_queries, axis=0)
     grad_cross_queries = after(grad_cross_queries, grad_w_cross_q)
@@ -1101,7 +1366,7 @@
     grad_w_attn = matmul_tn(attended_rows, grad_attn_rows)
     grad_b_attn = jnp.sum(grad_attn_rows, axis=0)
     grad_attn_rows = after(grad_attn_rows, grad_w_attn)
-    mlp_sum, grad_kv_share = mid_way(after(mlp_parts, grad_w_attn), grad_kv)
+    mlp_sum, grad_kv_share = mid_way(after(mlp_parts, (grad_w_attn, first_sent)), grad_kv)
     grad_attn_rows = after(grad_attn_rows, mlp_sum)
     grad_w_cross_kv = matmul_tn(caption_share, grad_kv_share)
     grad_b_cross_v = jnp.sum(grad_kv_share[:, width:], axis=0)
@@ -1109,17 +1374,13 @@
     mlp_branch = (mlp_sum + b_second).reshape(slots, cols, width)
     block_out = to_slots(after_cross + column_mask * gate_two * mlp_branch)
     grad_gate_two = jnp.sum(column_mask * mlp_branch * cotangent, axis=0)
-    grad_attended = matmul_nt(grad_attn_rows, w_attn).reshape(slots, cols, H, head_dim)
-    row_terms = jnp.transpose(jnp.sum(grad_attended * attended, axis=-1), (1, 2, 0))[..., None]
-    grad_probs = contract("fchd,schd->chfs", grad_attended, values)
-    grad_scores = probs * (grad_probs - row_terms)
-    grad_queries = (contract("chfs,schd->fchd", grad_scores, keys) * scaling).reshape(rows, width)
-    grad_keys = (contract("chfs,fchd->schd", grad_scores, queries) * scaling).reshape(rows, width)
-    grad_values = contract("chfs,fchd->schd", probs, grad_attended).reshape(rows, width)
-    grad_qkv = jnp.concatenate([grad_queries, grad_keys, grad_values], axis=1)
+    grad_attended = matmul_nt(grad_attn_rows, w_attn).reshape(slots, cols, width)
+    grad_qkv = frame_attention_back(
+        qkv, b_query, b_value, probs, attended, grad_attended
+    ).reshape(rows, 3 * width)
     grad_w_qkv = matmul_tn(hidden_one, grad_qkv)
-    grad_b_query = jnp.sum(grad_queries, axis=0)
-    grad_b_value = jnp.sum(grad_values, axis=0)
+    grad_b_query = jnp.sum(grad_qkv[:, :width], axis=0)
+    grad_b_value = jnp.sum(grad_qkv[:, 2 * width :], axis=0)
     grad_hidden_one = matmul_nt(grad_qkv, w_qkv).reshape(slots, cols, width)
     grad_shift_one = jnp.sum(grad_hidden_one, axis=0)
     grad_scale_one = jnp.sum(grad_hidden_one * normed_one, axis=0)

time: 1280 us -> 1200 us (0.938)
  Pallas kernels: 570 us -> 731 us
  matrix products: 368 us -> 237 us
  local copies, waits for them, and re-layouts: 150 us -> 78.3 us
  other arithmetic: 59.9 us -> 39.3 us
  starting transfers between devices: 58.3 us -> 40.6 us
    dot_general x12 -> x0, matrix products: 98.4 us -> none  [contract(): return jnp.einsum(form, left, right, precision=BEST)]
    pallas_call x1 -> x4, Pallas kernels: 0.21 us -> 87 us  [the longest x1 34.8 us: cross_attention_back(): pl.pallas_call(cross_attention_back_kernel, out_shape=(jax.ShapeDtypeStru...]
    pallas_call x1, Pallas kernels: 84.6 us -> 155 us  [begin(): pl.pallas_call(begin_kernel, out_shape=(jax.ShapeDtypeStruct((4 * count,...]
    reshape x14 -> x0, local copies, waits for them, and re-layouts: 51.3 us -> none  [the longest x1 4.56 us: on_device(): matmul_nt(grad_attn_rows, w_attn).reshape(slots, cols, H, head_dim)]
    all_gather x3, waiting for transfers between devices: 0.01 us -> 48.5 us  [gather_rows(): return lax.all_gather(shard, 'patch', axis=0, tiled=True)]
    all_to_all x1 -> x0, waiting for transfers between devices: 47.7 us -> none  [to_columns(): return lax.all_to_all(x, 'frame', split_axis=1, concat_axis=0, tiled=True)]
    dot_general x8, matrix products: 97 us -> 80.1 us  [matmul_tn(): lax.dot_general(left, right, (((0,), (0,)), ((), ())), precision=BEST)]
    all_to_all x1 -> x0, starting transfers between devices: 13 us -> none  [to_columns(): return lax.all_to_all(x, 'frame', split_axis=1, concat_axis=0, tiled=True)]
  transfers between devices with their start and end apart: 14 -> 9, of which waited for: 2 -> 2; matrix products, arithmetic and copies ran while one was open for 33% -> 17% of each run, Pallas kernels for 40% -> 55%
where the time goes in v5:
time: 1200 us; the launch traced here: 1190 us
  Pallas kernels  731 us (61%)
  matrix products  237 us (20%)
  local copies, waits for them, and re-layouts  78.3 us (7%)
  waiting for transfers between devices  52.8 us (4%)
  starting transfers between devices  40.6 us (3%)
  other arithmetic  39.3 us (3%)
  between operations  15.5 us (1%)
    pallas_call x1, Pallas kernels, finish(): pl.pallas_call(finish_kernel, out_shape=(shape(rows, 3 * width), shape(ro...  233 us
    pallas_call x1, Pallas kernels, begin(): pl.pallas_call(begin_kernel, out_shape=(jax.ShapeDtypeStruct((4 * count,...  155 us
    pallas_call x1, Pallas kernels, middle(): pl.pallas_call(middle_kernel, out_shape=(jax.ShapeDtypeStruct(block, f32)...  104 us
    pallas_call x1, Pallas kernels, token_gather(): pl.pallas_call(token_gather_kernel, out_shape=jax.ShapeDtypeStruct((8, le...  89.1 us
    dot_general x8, matrix products, matmul_nt(): lax.dot_general(left, right, (((1,), (1,)), ((), ())), precision=BEST)  82.6 us
    dot_general x8, matrix products, matmul_tn(): lax.dot_general(left, right, (((0,), (0,)), ((), ())), precision=BEST)  80.1 us
    dot_general x8, matrix products, matmul(): return jnp.dot(left, right, precision=BEST)  73.6 us
    pallas_call x1, Pallas kernels, token_scatter(): pl.pallas_call(token_scatter_kernel, out_shape=jax.ShapeDtypeStruct(block...  55.2 us
  transfers between devices with their start and end apart: 9, of which 2 were waited for; matrix products, arithmetic and copies ran while one was open for 17% of the time, Pallas kernels for 55%

profile of v5, /device:TPU:0, one launch (start us, length us, event | category | flops | bytes accessed | tf_op | source)
XLA Modules:
  0.0 1194.8 jit_solution(9294033205770247569)
XLA Ops:
  19.9 155.5 %shard_map.400 = (f32[20,16,1152]{2,1,0:T(8,128)S(1)}, f32[20,16,1152]{2,1,0:T(8,128)S(1)}, f32[4,8,128]{2,1,0:T(8,128)S(1)}, f32[336,128]{1,0:T(8,128)S(1)}, f3...) custom-call(f32[5,64,1152]{2,1,0:T(8,128)S(1)} %copy-done.25, f32[5,64,1152]{2,1,0:T(8,128)S(1)} %copy-done.26, ...), custom_call_target="tpu_custom_call" | custom-call | bytes 65536 | tf_op jit(solution)/shard_map/pallas_call | solution.py:375
  189.0 15.7 %fusion.48 = f32[320,3456]{1,0:T(8,128)S(1)} fusion(f32[320,1152]{1,0:T(8,128)} %bitcast.170, f32[1152,3456]{1,0:T(8,128)} %all-gather.4.cloned.1.call-done), kind=kOutput, calls=%fused_computation.166 | convolution fusion | flops 7644119040 | bytes 21823488 | tf_op jit(solution)/shard_map/dot_general | solution.py:22
  204.7 9.6 shard_map.401
  219.9 48.5 %all-gather.6.cloned.1.call-done = f32[1152,3456]{1,0:T(8,128)} async-done(((f32[144,3456]{1,0:T(8,128)}), f32[1152,3456]{1,0:T(8,128)}) %all-gather.6.cloned.1.call-update) | async-done | bytes 15925264 | tf_op jit(solution)/shard_map/all_gather | solution.py:1100
  268.4 6.6 fusion.20
  276.1 6.5 fusion.14.queries
  282.7 19.7 %shard_map.402 = (f32[16,320,480]{2,1,0:T(8,128)}, f32[320,1152]{1,0:T(8,128)S(1)}) custom-call(f32[320,1152]{1,0:T(8,128)S(1)} %fusion.14.queries, f32[1,1152]{1,0:T(1,128)S(1)} %bitcast.150, f32[480,2304]{1,0:T(8,128)} %copy-done.9, f32[1,1152]{1,0:T(1,128)S(1)} %bitcast.148, f32[320,480]{1,0:T(8,128)S(1)} %bitcast.143), custom_call_target="tpu_custom_call" | custom-call | bytes 65536 | tf_op jit(solution)/shard_map/pallas_call | solution.py:1003
  302.4 6.6 fusion.23
  315.3 89.1 %shard_map.403 = f32[8,320,1152]{2,1,0:T(8,128)S(1)} custom-call(f32[320,1152]{1,0:T(8,128)S(1)} %bitcast.140), custom_call_target="tpu_custom_call" | custom-call | bytes 65536 | tf_op jit(solution)/shard_map/pallas_call | solution.py:147
  408.7 14.2 %fusion.49 = f32[2560,576]{0,1:T(8,128)} fusion(f32[2560,1152]{1,0:T(8,128)S(1)} %bitcast.138, f32[1152,576]{1,0:T(8,128)S(1)} %bitcast.171), kind=kOutput, calls=%fused_computation.167 | convolution fusion | flops 10192158720 | bytes 20348928 | tf_op jit(solution)/shard_map/dot_general | solution.py:22
  422.9 20.0 %fusion.7 = (f32[2560,576]{0,1:T(8,128)}, f32[2560,576]{0,1:T(8,128)}) fusion(f32[2560,576]{0,1:T(8,128)} %fusion.49, f32[576]{0:T(1024)S(1)} %copy-done.77, f32[2560,1152]{1,0:T(8,128)} %all-gather.8.cloned.1.call-done, f32[576,1152]{1,0:T(8,128)S(1)} %copy-done), kind=kOutput, calls=%fused_computation.11 | convolution fusion | flops 10223124480 | bytes 32147712 | tf_op jit(solution)/shard_map/dot_general | solution.py:26
  442.9 6.6 copy.61
  449.5 18.3 %fusion.50.parts = f32[8,320,1152]{2,1,0:T(8,128)S(1)} fusion(f32[8,320,576]{2,1,0:T(8,128)} %bitcast.163, f32[1152,576,1]{1,0,2:T(8,128)} %bitcast.172), kind=kOutput, calls=%fused_computation.168 | convolution fusion | flops 10192158720 | bytes 20348928 | tf_op jit(solution)/shard_map/dot_general | solution.py:26
  467.8 55.2 %shard_map.404 = f32[320,1152]{1,0:T(8,128)S(1)} custom-call(f32[8,320,1152]{2,1,0:T(8,128)S(1)} %fusion.50.parts), custom_call_target="tpu_custom_call" | custom-call | bytes 65536 | tf_op jit(solution)/shard_map/pallas_call | solution.py:211
  530.2 7.1 fusion.51.cross_o
  537.3 15.3 %fusion.53 = f32[1152,576]{0,1:T(8,128)S(1)} fusion(f32[2560,1152]{1,0:T(8,128)} %bitcast.139, f32[2560,576]{0,1:T(8,128)S(1)} %bitcast.154), kind=kOutput, calls=%fused_computation.171 | convolution fusion | flops 10192158720 | bytes 20348928 | tf_op jit(solution)/shard_map/dot_general | solution.py:30
  571.8 17.7 %fusion.54 = f32[576,1152]{1,0:T(8,128)} fusion(f32[2560,576]{0,1:T(8,128)} %get-tuple-element.62, f32[2560,1152]{1,0:T(8,128)} %all-gather.8.cloned.1.call-done), kind=kOutput, calls=%fused_computation.172 | convolution fusion | flops 10192158720 | bytes 20348928 | tf_op jit(solution)/shard_map/dot_general | solution.py:30
  589.6 7.0 fusion.8.grad
  596.6 34.8 %shard_map.405 = (f32[320,1152]{1,0:T(8,128)S(1)}, f32[480,2304]{1,0:T(8,128)}) custom-call(f32[320,1152]{1,0:T(8,128)} %copy-done.10, f32[1,1152]{1,0:T(1,128)S(1)} %bitcast.151, f32[480,2304]{1,0:T(8,128)} %copy-done.9, f32[1,1152]{1,0:T(1,128)S(1)} %bitcast.149, f32[16,320,480]{2,1,0:T(8,128)} %get-tuple-element.63.probs, f32[320,1152]{1,0:T(8,128)} %copy-done.11, ...), custom_call_target="tpu_custom_call" | custom-call | bytes 65536 | tf_op jit(solution)/shard_map/pallas_call | solution.py:1061
  631.4 7.0 fusion.55.cross_q
  638.4 6.0 fusion.12
  646.2 7.5 convolution_bitcast_fusion.1.attn
  662.1 18.5 %fusion.52 = f32[2560,1152]{1,0:T(8,128)} fusion(f32[2560,576]{0,1:T(8,128)S(1)} %bitcast.179, f32[576,1152]{1,0:T(8,128)S(1)} %copy-done), kind=kOutput, calls=%fused_computation.170 | convolution fusion | flops 10192158720 | bytes 20348928 | tf_op jit(solution)/shard_map/dot_general | solution.py:22
  693.9 104.3 %shard_map.406 = (f32[320,1152]{1,0:T(8,128)S(1)}, f32[120,2304]{1,0:T(8,128)S(1)}) custom-call(f32[8,320,1152]{2,1,0:T(8,128)} %bitcast.161, f32[480,2304]{1,0:T(8,128)} %get-tuple-element.69.kv), custom_call_target="tpu_custom_call" | custom-call | bytes 65536 | tf_op jit(solution)/shard_map/pallas_call | solution.py:760
  798.1 6.0 fusion.16
  804.2 23.0 %shard_map.407 = f32[20,16,3456]{2,1,0:T(8,128)} custom-call(f32[20,16,3456]{2,1,0:T(8,128)} %bitcast.135, f32[1,1152]{1,0:T(1,128)S(1)} %bitcast.147, f32[1,1152]{1,0:T(1,128)S(1)} %bitcast.145, f32[16,2,160,160]{3,2,1,0:T(8,128)} %copy-done.22, f32[20,16,1152]{2,1,0:T(8,128)S(1)} %copy-done.21, f32[20,16,1152]{2,1,0:T(8,128)S(1)} %bitcast.142), custom_call_target="tpu_custom_call" | custom-call | bytes 65536 | tf_op jit(solution)/shard_map/pallas_call | solution.py:962
  827.3 19.5 %multiply_reduce_fusion.3 = (f32[16,1152]{1,0:T(8,128)S(1)}, f32[20,16]{1,0:T(8,128)S(1)}, f32[20,16]{1,0:T(8,128)S(1)}, f32[16,1152]{1,0:T(8,128)S(1)}, f32[20,16,1152]{2,1,0:T(8,128)S(1)}) fusion(f32[20,16,1152]{2,1,0:T(8,128)S(1)} %copy-done.5, f32[20,16]{1,0:T(8,128)S(1)} %copy-done.60, f32[20,16]{1,0:T(8,128)S(1)} %copy-done.58, ...), kind=kOutput, calls=%fused_computation.36 | convolution fusion | flops 7647399424 | bytes 23524352 | tf_op jit(solution)/shard_map/dot_general | solution.py:26
  853.7 36.7 %all-to-all-start = ((f32[20,16,1152]{2,1,0:T(8,128)}), f32[20,16,1152]{2,1,0:T(8,128)}, u32[]{:S(2)}, u32[]{:S(2)}) async-start(f32[20,16,1152]{2,1,0:T(8,128)} %get-tuple-element.138), calls=%async_computation | async-start | bytes 2949120 | tf_op jit(solution)/shard_map/all_to_all | solution.py:1171
  890.5 18.1 %convolution_bitcast_fusion.first = f32[1152,3456]{1,0:T(8,128)} fusion(f32[20,16,1152]{2,1,0:T(8,128)S(1)} %copy-done.39, f32[20,16,3456]{2,1,0:T(8,128)} %shard_map.407), kind=kOutput, calls=%fused_computation | convolution fusion | flops 7644119040 | bytes 21823488 | tf_op jit(solution)/shard_map/dot_general | solution.py:30
  913.4 232.5 %shard_map.408 = (f32[144,3456]{1,0:T(8,128)}, f32[144,1152]{1,0:T(8,128)}, f32[144,1152]{1,0:T(8,128)}, f32[144,1152]{1,0:T(8,128)}, f32[144,2304]{1,0:T(8,128)...) custom-call(f32[1152,3456]{1,0:T(8,128)} %convolution_bitcast_fusion.first, ...), custom_call_target="tpu_custom_call" | custom-call | bytes 65536 | tf_op jit(solution)/shard_map/pallas_call | solution.py:642
  1154.2 6.0 shard_map.409
  1167.0 4.6 fusion.42
  (346 shorter events, 135.6 us)
Async XLA Ops:
  7.2 415.7 %copy-start = (f32[576,1152]{1,0:T(8,128)S(1)}, f32[576,1152]{1,0:T(8,128)}, u32[]{:S(2)}) copy-start(f32[576,1152]{1,0:T(8,128)} %param.44) | copy-start | bytes 7962628
  7.2 181.8 %all-gather.4.cloned.1.call-start = ((), (), s32[]{:S(2)}) async-start(), calls=%async_computation.1 | async-start | bytes 17915904 | tf_op jit(solution)/shard_map/all_gather | solution.py:1100
  8.0 260.4 %all-gather.6.cloned.1.call-start = ((), (), s32[]{:S(2)}) async-start(), calls=%async_computation.2 | async-start | bytes 17915904 | tf_op jit(solution)/shard_map/all_gather | solution.py:1100
  19.9 159.9 %copy-start.54 = (f32[144,1152]{1,0:T(8,128)S(1)}, f32[144,1152]{1,0:T(8,128)}, u32[]{:S(2)}) copy-start(f32[144,1152]{1,0:T(8,128)} %param.40) | copy-start | bytes 1990660
  19.9 159.9 %copy-start.55 = (f32[144,1152]{1,0:T(8,128)S(1)}, f32[144,1152]{1,0:T(8,128)}, u32[]{:S(2)}) copy-start(f32[144,1152]{1,0:T(8,128)} %param.36) | copy-start | bytes 1990660
  19.9 159.9 %copy-start.56 = (f32[144,1152]{1,0:T(8,128)S(1)}, f32[144,1152]{1,0:T(8,128)}, u32[]{:S(2)}) copy-start(f32[144,1152]{1,0:T(8,128)} %param.34) | copy-start | bytes 1990660
  181.2 241.6 %all-gather.8.cloned.1.call-start = ((), (), s32[]{:S(2)}) async-start(), calls=%async_computation.3 | async-start | bytes 13271040 | tf_op jit(solution)/shard_map/all_gather | solution.py:1100
  276.1 32.9 %copy-start.29 = (f32[20,16,1152]{2,1,0:T(8,128)}, f32[20,16,1152]{2,1,0:T(8,128)S(1)}, u32[]{:S(2)}) copy-start(f32[20,16,1152]{2,1,0:T(8,128)S(1)} %multiply_add_fusion.5) | copy-start | bytes 4423684
  282.6 19.8 %copy-start.10 = (f32[320,1152]{1,0:T(8,128)}, f32[320,1152]{1,0:T(8,128)S(1)}, u32[]{:S(2)}) copy-start(f32[320,1152]{1,0:T(8,128)S(1)} %fusion.14.queries) | copy-start | bytes 4423684
  310.9 863.9 %all-reduce.6.cloned.1.call-start = ((), (), s32[]{:S(2)}) async-start(), calls=%async_computation.4 | async-start | bytes 10616832 | tf_op jit(solution)/shard_map/psum | solution.py:1349
  314.7 89.8 %copy-start.41 = (f32[8,144,576]{2,1,0:T(8,128)}, f32[8,144,576]{2,1,0:T(8,128)S(1)}, u32[]{:S(2)}) copy-start(f32[8,144,576]{2,1,0:T(8,128)S(1)} %slice_select_fusion) | copy-start | bytes 7962628
  408.7 14.2 %copy-start.77 = (f32[576]{0:T(1024)S(1)}, f32[576]{0:T(1024)}, u32[]{:S(2)}) copy-start(f32[576]{0:T(1024)} %param.43) | copy-start | bytes 6916
  526.9 10.4 slice-start
  565.8 87.9 %collective-permute-start = (f32[576,576]{1,0:T(8,128)}, f32[576,576]{1,0:T(8,128)}, u32[]{:S(2)}, u32[]{:S(2)}) collective-permute-start(f32[576,576]{1,0:T(8,128)} %pad_maximum_fusion.2), channel_id=1, source_target_pairs={{0,4},{4,0},{8,12},{12,8},{16,20},{20,16},{24,28},{28,24},{1,5},{5... | collective-permute-start | bytes 3981320 | tf_op jit(solution)/shard_map/ppermute | solution.py:49
  571.8 17.7 %copy-start.34 = (f32[20,16,1152]{2,1,0:T(8,128)S(1)}, f32[20,16,1152]{2,1,0:T(8,128)}, u32[]{:S(2)}) copy-start(f32[20,16,1152]{2,1,0:T(8,128)} %copy-done.33) | copy-start | bytes 4423684
  596.6 34.8 %copy-start.30 = (f32[20,16,1152]{2,1,0:T(8,128)S(1)}, f32[20,16,1152]{2,1,0:T(8,128)}, u32[]{:S(2)}) copy-start(f32[20,16,1152]{2,1,0:T(8,128)} %copy-done.29) | copy-start | bytes 4423684
  644.4 17.6 %slice-start.2 = ((s8[5898240]{0:T(1024)(128)(4,1)}), s8[4194304]{0:T(1024)(128)(4,1)S(1)}, s32[]{:S(2)}) async-start(s8[5898240]{0:T(1024)(128)(4,1)} %bitcast.178), calls=%async_computation.7 | async-start | bytes 8388608
  646.2 15.9 %slice-start.3 = ((s8[5898240]{0:T(1024)(128)(4,1)}), s8[1703936]{0:T(1024)(128)(4,1)S(1)}, s32[]{:S(2)}) async-start(s8[5898240]{0:T(1024)(128)(4,1)} %bitcast.178), calls=%async_computation.8 | async-start | bytes 3407872
  656.4 30.8 %collective-permute-start.1 = (f32[144,1152]{1,0:T(8,128)}, f32[144,1152]{1,0:T(8,128)}, u32[]{:S(2)}, u32[]{:S(2)}) collective-permute-start(f32[144,1152]{1,0:T(8,128)} %maximum_select_fusion.1), channel_id=1, source_target_pairs={{0,8},{4,12},{8,0},{12,4},{16,24},{20,28},{24,16},{28,20},{1,9},{5... | collective-permute-start | bytes 1990664 | tf_op jit(solution)/shard_map/ppermute | solution.py:49
  659.1 31.6 %collective-permute-start.2 = (f32[144,1152]{1,0:T(8,128)}, f32[144,1152]{1,0:T(8,128)}, u32[]{:S(2)}, u32[]{:S(2)}) collective-permute-start(f32[144,1152]{1,0:T(8,128)} %maximum_select_fusion.2), channel_id=1, source_target_pairs={{0,16},{4,20},{8,24},{12,28},{16,0},{20,4},{24,8},{28,12},{1,17},{... | collective-permute-start | bytes 1990664 | tf_op jit(solution)/shard_map/ppermute | solution.py:49
  660.6 30.1 %collective-permute-start.3 = (f32[144,1152]{1,0:T(8,128)}, f32[144,1152]{1,0:T(8,128)}, u32[]{:S(2)}, u32[]{:S(2)}) collective-permute-start(f32[144,1152]{1,0:T(8,128)} %maximum_select_fusion.3), channel_id=1, source_target_pairs={{0,24},{4,28},{8,16},{12,20},{16,8},{20,12},{24,0},{28,4},{1,25},{... | collective-permute-start | bytes 1990664 | tf_op jit(solution)/shard_map/ppermute | solution.py:49
  693.9 104.3 %copy-start.37 = (f32[20,16,1152]{2,1,0:T(8,128)S(1)}, f32[20,16,1152]{2,1,0:T(8,128)}, u32[]{:S(2)}) copy-start(f32[20,16,1152]{2,1,0:T(8,128)} %copy-done.36) | copy-start | bytes 4423684
  804.2 23.0 %copy-start.5 = (f32[20,16,1152]{2,1,0:T(8,128)S(1)}, f32[20,16,1152]{2,1,0:T(8,128)}, u32[]{:S(2)}) copy-start(f32[20,16,1152]{2,1,0:T(8,128)} %copy-done.2) | copy-start | bytes 4423684
  804.2 23.0 %copy-start.45 = (f32[16,1152]{1,0:T(8,128)S(1)}, f32[16,1152]{1,0:T(8,128)}, u32[]{:S(2)}) copy-start(f32[16,1152]{1,0:T(8,128)} %copy-done.44) | copy-start | bytes 221188
  804.2 23.0 %copy-start.58 = (f32[20,16]{1,0:T(8,128)S(1)}, f32[20,16]{1,0:T(8,128)}, u32[]{:S(2)}) copy-start(f32[20,16]{1,0:T(8,128)} %copy-done.57) | copy-start | bytes 3844
  804.2 23.0 %copy-start.60 = (f32[20,16]{1,0:T(8,128)S(1)}, f32[20,16]{1,0:T(8,128)}, u32[]{:S(2)}) copy-start(f32[20,16]{1,0:T(8,128)} %copy-done.59) | copy-start | bytes 3844
  827.2 19.6 %copy-start.65 = (f32[1152]{0:T(1024)S(1)}, f32[1152]{0:T(1024)}, u32[]{:S(2)}) copy-start(f32[1152]{0:T(1024)} %get-tuple-element.149) | copy-start | bytes 13828
  827.2 19.7 %copy-start.32 = (f32[320,1152]{1,0:T(8,128)S(1)}, f32[320,1152]{1,0:T(8,128)}, u32[]{:S(2)}) copy-start(f32[320,1152]{1,0:T(8,128)} %copy-done.31) | copy-start | bytes 4423684
  827.2 19.7 %copy-start.35 = (f32[20,16,1152]{2,1,0:T(8,128)S(1)}, f32[20,16,1152]{2,1,0:T(8,128)}, u32[]{:S(2)}) copy-start(f32[20,16,1152]{2,1,0:T(8,128)} %get-tuple-element.124) | copy-start | bytes 4423684
  853.6 36.9 %copy-start.39 = (f32[20,16,1152]{2,1,0:T(8,128)S(1)}, f32[20,16,1152]{2,1,0:T(8,128)}, u32[]{:S(2)}) copy-start(f32[20,16,1152]{2,1,0:T(8,128)} %multiply_add_fusion.6) | copy-start | bytes 4423684
  853.7 318.5 %all-to-all-start = ((f32[20,16,1152]{2,1,0:T(8,128)}), f32[20,16,1152]{2,1,0:T(8,128)}, u32[]{:S(2)}, u32[]{:S(2)}) async-start(f32[20,16,1152]{2,1,0:T(8,128)} %get-tuple-element.138), calls=%async_computation | async-start | bytes 2949120 | tf_op jit(solution)/shard_map/all_to_all | solution.py:1171
  1149.8 17.2 %copy-start.63 = (f32[4,1152]{1,0:T(4,128)S(1)}, f32[4,1152]{1,0:T(4,128)}, u32[]{:S(2)}) copy-start(f32[4,1152]{1,0:T(4,128)} %param.28) | copy-start | bytes 55300
  (62 other events, 197.7 us)
Sparse Core Ops, SparseCore 0:
  9.9 128.4 all-gather.3
  181.3 87.0 all-gather.5
  311.0 104.5 all-gather.7
  694.0 275.7 all-reduce.5

commit v6 on v5

--- a/solution.py
+++ b/solution.py
@@ -269,8 +269,7 @@
     me, z = lax.axis_index("patch"), lax.axis_index("frame")
     core, x, y = ({"patch": me ^ k} for k in (1, 2, 4))
     frames = [None] + [{"frame": z ^ k} for k in (1, 2, 3)]
-    chips = {2: x, 4: y, 6: {"patch": me ^ 6}}
-    greet_all([core, x, y, chips[6]] + frames[1:])
+    greet_all([core, x, y] + frames[1:])
     links = Links(send_sems, recv_sems)
     count, part = tokens.shape[0], tokens.shape[1] // 4
     rows, width = kv_1.shape
@@ -284,30 +283,54 @@
     half = pl.multiple_of((me % 2) * width, 128)
     other = pl.multiple_of((1 - me % 2) * width, 128)
     mine, theirs = pl.ds(half, width), pl.ds(other, width)
+
+    length = weight.shape[0]
+    weight_at = [[links.plan() for _ in range(7)] for _ in range(3)]
+    weight_core = links.plan()
+
+    def piece(k, u, first=0, size=length):
+        start = pl.multiple_of((me ^ k) * length + first, 8)
+        return weight_out.at[pl.ds(start, size), pl.ds(u * width, width)]
+
+    whole = weight_out.at[pl.ds(pl.multiple_of(me * length, 8), length)]
+    sibling = weight_out.at[pl.ds(pl.multiple_of((me ^ 1) * length, 8), length)]
+    own_copy = pltpu.make_async_copy(weight, whole, weight_sem)
+
+    def weight_links(u):
+        source = weight.at[:, pl.ds(u * width, width)]
+        links.send(source, piece(0, u), weight_at[u][0], x)
+        links.send(source, piece(0, u), weight_at[u][1], y)
+
+    def weight_across(u):
+        middle_row = length // 2
+        links.wait(piece(2, u), weight_at[u][0], x)
+        upper = piece(2, u, 0, middle_row)
+        links.send(upper, upper, weight_at[u][2], y)
+        links.send(piece(2, u), piece(2, u), weight_at[u][4], core)
+        links.wait(piece(4, u), weight_at[u][1], y)
+        lower = piece(4, u, middle_row, middle_row)
+        links.send(lower, lower, weight_at[u][3], x)
+        links.send(piece(4, u), piece(4, u), weight_at[u][5], core)
+
+    def weight_last(u):
+        middle_row = length // 2
+        links.wait(piece(6, u, 0, middle_row), weight_at[u][2], y)
+        links.wait(piece(6, u, middle_row, middle_row), weight_at[u][3], x)
+        links.send(piece(6, u), piece(6, u), weight_at[u][6], core)
 
     at = links.plan()
     links.send(small, small_got.at[0], at, core)
     at_kv = links.plan()
     links.send(kv.at[:, theirs], kv_got_core, at_kv, core)
+    own_copy.start()
     token_at = [None] + [links.plan() for _ in range(3)]
     slot_at = [None] + [links.plan() for _ in range(3)]
-    chip_width = weight.shape[1] // 4
-    own_chip = weight_out.at[me]
-    own_copy = pltpu.make_async_copy(
-        weight.at[:, pl.ds(pl.multiple_of(me // 2 * chip_width, 128), chip_width)],
-        own_chip, weight_sem,
-    )
-    own_copy.start()
-    weight_at = {k: links.plan() for k in (2, 4, 6)}
-    pair_at = {k: links.plan() for k in (0, 2, 4, 6)}
-    for k, device in chips.items():
-        start = pl.multiple_of((me ^ k) // 2 * chip_width, 128)
-        links.send(weight.at[:, pl.ds(start, chip_width)], own_chip, weight_at[k], device)
+    later_at = [None] + [links.plan() for _ in range(3)]
     for k in (1, 2, 3):
         links.send(slots, slots_out.at[z], slot_at[k], frames[k])
         links.send(tokens.at[:, columns(k)], tokens_out.at[of_slots(0)], token_at[k], frames[k])
-    slots_out[z] = slots[...]
-    tokens_out[of_slots(0)] = tokens[:, columns(0)]
+    for k in (1, 2, 3):
+        links.send(later.at[:, columns(k)], later_out.at[of_slots(0)], later_at[k], frames[k])
 
     links.wait(small_got.at[0], at, core)
     small_1[...] = small[...] + small_got[0]
@@ -319,6 +342,11 @@
     at_u, at_l = links.plan(), links.plan()
     links.send(kv_1.at[upper], kv_got_1.at[upper], at_u, x)
     links.send(kv_1.at[lower], kv_got_1.at[lower], at_l, y)
+    weight_links(0)
+    links.send(weight, whole, weight_core, core)
+    slots_out[z] = slots[...]
+    tokens_out[of_slots(0)] = tokens[:, columns(0)]
+    later_out[of_slots(0)] = later[:, columns(0)]
     links.wait(small_got.at[1], at, x)
     small_2[...] = small_1[...] + small_got[1]
     at = links.plan()
@@ -329,8 +357,11 @@
     at_u, at_l = links.plan(), links.plan()
     links.send(kv_2.at[upper], kv_got_2.at[upper], at_u, y)
     links.send(kv_2.at[lower], kv_got_2.at[lower], at_l, x)
+    weight_links(1)
     links.wait(small_got.at[2], at, y)
     small_out[...] = small_2[...] + small_got[2]
+    weight_across(0)
+    weight_links(2)
     links.wait(kv_got_2.at[upper], at_u, y)
     links.wait(kv_got_2.at[lower], at_l, x)
 
@@ -343,27 +374,25 @@
     for k in (1, 2, 3):
         links.send(share(0, mine), share(0, mine), kv_at[k], frames[k])
     links.send(share(0, mine), share(0, mine), core_at[0], core)
-    later_at = [None] + [links.plan() for _ in range(3)]
+    weight_across(1)
+    weight_last(0)
+    weight_across(2)
+    weight_last(1)
     for k in (1, 2, 3):
-        links.send(later.at[:, columns(k)], later_out.at[of_slots(0)], later_at[k], frames[k])
-    later_out[of_slots(0)] = later[:, columns(0)]
+        links.wait(slots_out.at[z ^ k], slot_at[k], frames[k])
+        links.wait(tokens_out.at[of_slots(k)], token_at[k], frames[k])
+        links.wait(later_out.at[of_slots(k)], later_at[k], frames[k])
     for k in (1, 2, 3):
         links.wait(share(k, mine), kv_at[k], frames[k])
         links.send(share(k, mine), share(k, mine), core_at[k], core)
-    for k in (1, 2, 3):
-        links.wait(slots_out.at[z ^ k], slot_at[k], frames[k])
-        links.wait(tokens_out.at[of_slots(k)], token_at[k], frames[k])
+    weight_last(2)
     for k in range(4):
         links.wait(share(k, theirs), core_at[k], core)
+    links.wait(sibling, weight_core, core)
+    for u in range(3):
+        for i, k in enumerate((2, 4, 6)):
+            links.wait(piece(k ^ 1, u), weight_at[u][4 + i], core)
     own_copy.wait()
-    for k in (0, 2, 4, 6):
-        if k:
-            links.wait(weight_out.at[me ^ k], weight_at[k], chips[k])
-        links.send(weight_out.at[me ^ k], weight_out.at[me ^ k], pair_at[k], core)
-    for k in (0, 2, 4, 6):
-        links.wait(weight_out.at[me ^ 1 ^ k], pair_at[k], core)
-    for k in (1, 2, 3):
-        links.wait(later_out.at[of_slots(k)], later_at[k], frames[k])
     links.drain()
 
 
@@ -371,6 +400,7 @@
     count, cols, width = tokens.shape
     rows = kv.shape[0]
     f32, vmem = jnp.float32, pl.BlockSpec(memory_space=pltpu.VMEM)
+    hbm = pl.BlockSpec(memory_space=pl.ANY)
     half = pltpu.VMEM((rows, width), f32)
     return pl.pallas_call(
         begin_kernel,
@@ -380,18 +410,18 @@
             jax.ShapeDtypeStruct((4,) + slots.shape, f32),
             jax.ShapeDtypeStruct(small.shape, f32),
             jax.ShapeDtypeStruct((4 * rows, 2 * width), f32),
-            jax.ShapeDtypeStruct((8, weight.shape[0], weight.shape[1] // 4), f32),
+            jax.ShapeDtypeStruct((8 * weight.shape[0], weight.shape[1]), f32),
         ),
-        in_specs=[vmem] * 5 + [pl.BlockSpec(memory_space=pl.ANY)],
-        out_specs=[vmem] * 6,
+        in_specs=[vmem] * 5 + [hbm],
+        out_specs=[vmem] * 5 + [hbm],
         scratch_shapes=[
             pltpu.SemaphoreType.DMA,
             pltpu.VMEM(small.shape, f32), pltpu.VMEM(small.shape, f32),
             pltpu.VMEM((3,) + small.shape, f32), half, half, half, half, half,
-            pltpu.SemaphoreType.DMA((32,)), pltpu.SemaphoreType.DMA((32,)),
+            pltpu.SemaphoreType.DMA((48,)), pltpu.SemaphoreType.DMA((48,)),
         ],
         compiler_params=pltpu.CompilerParams(
-            collective_id=2, has_side_effects=True, vmem_limit_bytes=40 << 20
+            collective_id=2, has_side_effects=True, vmem_limit_bytes=36 << 20
         ),
         cost_estimate=LIGHT,
     )(tokens, later, slots, small, kv, weight)
@@ -401,8 +431,9 @@
 
 
 def finish_kernel(
-    first, attn, cross_q, cross_o, kv, tokens, small, caption,
+    first, attn, cross_q, cross_o, kv, tokens, small, caption, columns,
     first_out, attn_out, cross_q_out, cross_o_out, kv_out, tokens_out, small_out, caption_out,
+    columns_out, columns_got, columns_sem,
     kept, theirs, by_x, by_y, from_x, from_y, along_z, across_z,
     small_sums, small_got, small_z, load_sems, credit, send_sems, recv_sems,
 ):
@@ -412,7 +443,8 @@
     core, x, y = ({"patch": me ^ k} for k in (1, 2, 4))
     frames = [None] + [{"frame": z ^ k} for k in (1, 2, 3)]
     near, facing = frames[1], frames[3]
-    greet_all([core, x, y] + frames[1:])
+    chips = {2: x, 4: y, 6: {"patch": me ^ 6}}
+    greet_all([core, x, y, chips[6]] + frames[1:])
     links = Links(send_sems, recv_sems)
     rows, width = by_x.shape[1] * 2, by_x.shape[2]
     upper, lower = pl.ds(0, rows // 2), pl.ds(rows // 2, rows // 2)
@@ -488,15 +520,15 @@
         return pltpu.make_async_copy(source(u, me, j), kept.at[u, j], load_sems.at[u, j])
 
     def to_core(u):
-        if u >= 3:
-            pl.semaphore_wait(credit.at[u - 3], 1)
+        if u >= 2:
+            pl.semaphore_wait(credit.at[u - 2], 1)
         for j in (3, 2, 1, 0):
-            links.send(source(u, me ^ 1, j), theirs.at[u % 3, j], core_at[u][j], core)
+            links.send(source(u, me ^ 1, j), theirs.at[u % 2, j], core_at[u][j], core)
 
     def add_cores(u, j):
         load(u, j).wait()
-        links.wait(theirs.at[u % 3, j], core_at[u][j], core)
-        kept[u, j] = kept[u, j] + theirs[u % 3, j]
+        links.wait(theirs.at[u % 2, j], core_at[u][j], core)
+        kept[u, j] = kept[u, j] + theirs[u % 2, j]
 
     def stage_one(u):
         at = link_at[u]
@@ -508,11 +540,11 @@
         add_cores(u, 1)
         links.send(kept.at[u, 1, upper], from_x.at[u, upper], at[3], x)
         add_cores(u, 0)
-        if u + 3 < UNITS:
+        if u + 2 < UNITS:
             pl.semaphore_signal(
                 credit.at[u], inc=1, device_id=core, device_id_type=pl.DeviceIdType.MESH
             )
-            to_core(u + 3)
+            to_core(u + 2)
 
     def stage_two(u):
         at = link_at[u]
@@ -532,6 +564,40 @@
         kept[u, 0] = kept[u, 0] + from_x[u] + from_y[u]
         steps[u][0]()
 
+    block = columns_got.shape[1] // 2
+    columns_at = {k: links.plan() for k in (2, 4, 6)}
+    columns_core = {k: links.plan() for k in (0, 2, 4, 6)}
+
+    def chip_rows(k):
+        return columns.at[pl.ds(pl.multiple_of((me ^ k) // 2 * (2 * block), 8), 2 * block)]
+
+    own_rows = pltpu.make_async_copy(chip_rows(0), columns_got.at[0], columns_sem.at[0])
+
+    def own_block(k):
+        core_rows = pl.ds(pl.multiple_of(me % 2 * block, 8), block)
+        return pltpu.make_async_copy(
+            columns_got.at[k // 2, core_rows], columns_out.at[me ^ k], columns_sem.at[1 + k // 2]
+        )
+
+    def send_columns(k):
+        links.send(chip_rows(k), columns_got.at[k // 2], columns_at[k], chips[k])
+
+    def columns_over():
+        other_rows = pl.ds(pl.multiple_of((1 - me % 2) * block, 8), block)
+        own_rows.wait()
+        for k in (0, 2, 4, 6):
+            if k:
+                links.wait(columns_got.at[k // 2], columns_at[k], chips[k])
+            links.send(
+                columns_got.at[k // 2, other_rows], columns_out.at[me ^ k], columns_core[k], core
+            )
+            own_block(k).start()
+
+    def columns_end():
+        for k in (0, 2, 4, 6):
+            links.wait(columns_out.at[me ^ 1 ^ k], columns_core[k], core)
+            own_block(k).wait()
+
     caption_at = [links.plan() for _ in range(10)]
 
     def caption_frames():
@@ -562,12 +628,13 @@
     small_at = [links.plan() for _ in range(3)]
     links.send(small, small_got.at[0], small_at[0], core)
     caption_frames()
+    own_rows.start()
     for u in range(UNITS):
         for j in (3, 2, 1, 0):
             load(u, j).start()
     steps[6][0]()
     steps[7][0]()
-    for u in range(3):
+    for u in range(2):
         to_core(u)
     links.wait(small_got.at[0], small_at[0], core)
     small_sums[0] = small[...] + small_got[0]
@@ -606,6 +673,8 @@
     stage_one(5)
     steps[1][1]()
     steps[0][2]()
+    for k in (2, 4, 6):
+        send_columns(k)
     stage_two(4)
     stage_three(3)
     stage_two(5)
@@ -623,14 +692,16 @@
     steps[5][2]()
     for step in steps + [small_steps]:
         step[3]()
+    columns_over()
     caption_end()
+    columns_end()
     for k in (1, 2, 3):
         where = pl.ds(pl.multiple_of((z ^ k) * part, part), part)
         links.wait(tokens_out.at[:, where], token_at[k], frames[k])
     links.drain()
 
 
-def finish(first, attn, cross_q, cross_o, kv, tokens, small, caption):
+def finish(first, attn, cross_q, cross_o, kv, tokens, small, caption, columns):
     rows, width = first.shape[0] // 8, first.shape[1] // 3
     count, part = tokens.shape[0] // 4, tokens.shape[1]
     f32, vmem = jnp.float32, pl.BlockSpec(memory_space=pltpu.VMEM)
@@ -644,25 +715,27 @@
         out_shape=(
             shape(rows, 3 * width), shape(rows, width), shape(rows, width), shape(rows, width),
             shape(rows, 2 * width), shape(count, 4 * part, tokens.shape[2]), shape(*small.shape),
-            shape(8, 4, *caption.shape),
+            shape(8, 4, *caption.shape), shape(8, columns.shape[0] // 8, columns.shape[1]),
         ),
-        in_specs=[hbm] * 4 + [vmem] * 4,
-        out_specs=[vmem] * 8,
+        in_specs=[hbm] * 4 + [vmem] * 4 + [hbm],
+        out_specs=[vmem] * 8 + [hbm],
         scratch_shapes=[
-            pltpu.VMEM((UNITS, 4, rows, width), f32), pltpu.VMEM((3, 4, rows, width), f32),
+            pltpu.VMEM((4, columns.shape[0] // 4, columns.shape[1]), f32),
+            pltpu.SemaphoreType.DMA((5,)),
+            pltpu.VMEM((UNITS, 4, rows, width), f32), pltpu.VMEM((2, 4, rows, width), f32),
             pltpu.VMEM((UNITS, rows // 2, width), f32), pltpu.VMEM((UNITS, rows // 2, width), f32),
             pltpu.VMEM((UNITS, rows, width), f32), pltpu.VMEM((UNITS, rows, width), f32),
             pltpu.VMEM((UNITS + 2, rows, width), f32), pltpu.VMEM((UNITS + 2, rows, width), f32),
             pltpu.VMEM((3,) + small.shape, f32), pltpu.VMEM((3,) + small.shape, f32),
             pltpu.VMEM((2,) + small.shape, f32),
-            pltpu.SemaphoreType.DMA((UNITS, 4)), pltpu.SemaphoreType.REGULAR((3,)),
+            pltpu.SemaphoreType.DMA((UNITS, 4)), pltpu.SemaphoreType.REGULAR((4,)),
             pltpu.SemaphoreType.DMA((112,)), pltpu.SemaphoreType.DMA((112,)),
         ],
         compiler_params=pltpu.CompilerParams(
-            collective_id=3, has_side_effects=True, vmem_limit_bytes=60 << 20
+            collective_id=3, has_side_effects=True, vmem_limit_bytes=58 << 20
         ),
         cost_estimate=LIGHT,
-    )(first, attn, cross_q, cross_o, kv, tokens, small, caption)
+    )(first, attn, cross_q, cross_o, kv, tokens, small, caption, columns)
 
 
 def middle_kernel(
@@ -1114,14 +1187,6 @@
     return lax.dynamic_slice_in_dim(array, start, length, axis=dim)
 
 
-def pair_up(kept, theirs, core):
-    return jnp.where(
-        core == 0,
-        jnp.concatenate([kept, theirs], axis=-1),
-        jnp.concatenate([theirs, kept], axis=-1),
-    )
-
-
 def over_chips(blocks):
     return [
         blocks[0],
@@ -1131,36 +1196,20 @@
     ]
 
 
-def back_to_rows(grad):
-    core = lax.axis_index("patch") % 2
-    blocks = [block_of(grad, "patch", k, 0) for k in range(8)]
-    length = blocks[0].shape[0]
+def to_own_columns(weight):
+    if not small_patch():
+        return lax.all_to_all(weight, "patch", 1, 0, tiled=True)
+    length = weight.shape[0]
+    blocks = [block_of(weight, "patch", k, 1) for k in range(8)]
     theirs = swap(jnp.concatenate(blocks[1::2], axis=0), "patch", 1)
     both = [
-        pair_up(kept, theirs[j * length : (j + 1) * length], core)
+        jnp.concatenate([kept, theirs[j * length : (j + 1) * length]], axis=0)
         for j, kept in enumerate(blocks[::2])
     ]
-    return jnp.concatenate(over_chips(both), axis=0)
-
-
-def side_by_side_kernel(stack, whole):
-    own = lax.axis_index("patch") // 2
-    length, width = whole.shape[0], stack.shape[1]
-    for j in range(4):
-        start = pl.multiple_of((own ^ j) * width, width)
-        whole[:, pl.ds(start, width)] = stack[j * length : (j + 1) * length, :]
-
-
-def side_by_side(stack):
-    length, width = stack.shape[0] // 4, stack.shape[1]
-    return pl.pallas_call(
-        side_by_side_kernel,
-        out_shape=jax.ShapeDtypeStruct((length, 4 * width), jnp.float32),
-        in_specs=[pl.BlockSpec(memory_space=pltpu.VMEM)],
-        out_specs=pl.BlockSpec(memory_space=pltpu.VMEM),
-        compiler_params=pltpu.CompilerParams(vmem_limit_bytes=24 << 20),
-        cost_estimate=LIGHT,
-    )(stack)
+    halves = []
+    for block in over_chips(both):
+        halves += [block[:length], block[length:]]
+    return assemble(halves, "patch", 0)
 
 
 def to_columns(x):
@@ -1175,7 +1224,7 @@
     return token_scatter(parts) if small_patch() else scatter_rows(parts)
 
 
-def open_up(block_input, cotangent, frame_slot, small, kv_part, fc1_weight):
+def open_up(block_input, cotangent, frame_slot, small, kv_part, weight):
     frame_number = frame_slot.astype(jnp.float32)
     if not small_patch():
         kv = all_sum(kv_part, "patch")
@@ -1185,18 +1234,16 @@
             all_sum(placed(frame_number, "frame"), "frame"),
             all_sum(small, "patch"),
             lax.all_gather(kv, "frame", axis=0, tiled=True),
-            lax.all_to_all(fc1_weight, "patch", 1, 0, tiled=True),
+            gather_rows(weight),
         )
     count = frame_slot.shape[0]
     rows = -(-small.shape[0] // 1024) * 8
-    tokens, later, slots, summed, kv, pairs = begin(
-        block_input, cotangent, padded(frame_number, 8), padded(small, rows), kv_part, fc1_weight
-    )
-    half = pairs.shape[2] // 2
-    weight = jnp.where(lax.axis_index("patch") % 2 == 0, pairs[..., :half], pairs[..., half:])
+    tokens, later, slots, summed, kv, whole = begin(
+        block_input, cotangent, padded(frame_number, 8), padded(small, rows), kv_part, weight
+    )
     summed = summed.reshape(-1)[: small.shape[0]]
     slots = slots[:, 0, :count].reshape(-1)
-    return tokens, later, slots, summed, kv, weight.reshape(-1, half)
+    return tokens, later, slots, summed, kv, whole
 
 
 def mid_way(parts, kv):
@@ -1206,7 +1253,7 @@
     return middle(parts, kv)
 
 
-def close_up(weights, kv, tokens, small, caption):
+def close_up(weights, kv, tokens, small, caption, columns):
     clips, length = lax.axis_size("frame"), caption.shape[1]
     if not small_patch():
         weights = [lax.psum(scatter_rows(w), "frame") for w in weights]
@@ -1214,13 +1261,15 @@
         whole = lax.all_gather(whole, "frame", axis=0)
         whole = jnp.transpose(whole, (0, 2, 1))
         small = all_sum(all_sum(small, "patch"), "frame")
-        return weights, lax.psum(kv, "frame"), to_slots(tokens), small, whole
+        columns = lax.all_to_all(columns, "patch", 0, 1, tiled=True)
+        return weights, lax.psum(kv, "frame"), to_slots(tokens), small, whole, columns
     rows = -(-small.shape[0] // 1024) * 8
-    *weights, kv, tokens, summed, whole = finish(
-        *weights, kv, tokens, padded(small, rows), caption
-    )
+    *weights, kv, tokens, summed, whole, blocks = finish(
+        *weights, kv, tokens, padded(small, rows), caption, columns
+    )
+    columns = jnp.transpose(blocks, (1, 0, 2)).reshape(blocks.shape[1], -1)
     whole = jnp.transpose(whole, (1, 3, 0, 2)).reshape(clips, length, -1)
-    return weights, kv, tokens, summed.reshape(-1)[: small.shape[0]], whole
+    return weights, kv, tokens, summed.reshape(-1)[: small.shape[0]], whole, columns
 
 
 def on_device(
@@ -1263,18 +1312,17 @@
     )
     caption_rows = caption.reshape(CLIPS * CAP, width)
     caption_share = own_part(own_part(caption_rows, "frame", 0), "patch", 1)
-    tokens_in, cotangent, frame_pos, small, caption_kv, w_first = open_up(
+    tokens_in, cotangent, frame_pos, small, caption_kv, w_qkv = open_up(
         block_input,
         out_cotangent,
         frame_slot,
         small,
         matmul(caption_share, cross_kv_weight),
-        fc1_weight,
-    )
-    w_qkv = gather_rows(qkv_weight)
-    three = jnp.concatenate([attn_out_weight, cross_q_weight, cross_out_weight], axis=1)
-    w_three = gather_rows(after(three, tokens_in))
-    w_attn, w_cross_q, w_cross_o = jnp.split(w_three, 3, axis=1)
+        qkv_weight,
+    )
+    w_two = gather_rows(jnp.concatenate([attn_out_weight, cross_q_weight], axis=1))
+    w_attn, w_cross_q = jnp.split(w_two, 2, axis=1)
+    w_cross_o = gather_rows(cross_out_weight)
     slots, cols, _ = tokens_in.shape
     rows = slots * cols
     clip_own = own_part(clip_id, "frame", 0)
@@ -1300,6 +1348,7 @@
     normed_one, inverse_one = normalize(tokens_in)
     hidden_one = (normed_one * (1.0 + scale_one) + shift_one).reshape(rows, width)
     qkv_rows = matmul(hidden_one, w_qkv)
+    w_first = to_own_columns(after(fc1_weight, qkv_rows))
     grad_mlp_all = gather_rows(after(grad_mlp, qkv_rows))
     qkv = qkv_rows.reshape(slots, cols, 3 * width)
     probs, attended = frame_attention(qkv, b_query, b_value, *frame_tables(frame_pos))
@@ -1307,6 +1356,7 @@
     attn_branch = (matmul(attended_rows, w_attn) + b_attn).reshape(slots, cols, width)
     after_attn = tokens_in + column_mask * gate_one * attn_branch
     after_attn_rows = after_attn.reshape(rows, width)
+    after_attn_rows = after(after_attn_rows, w_first)
     cross_queries = matmul(after_attn_rows, w_cross_q)
     key_clip = jnp.arange(CLIPS * CAP, dtype=jnp.int32) // CAP
     caption_ok = (clip_own[:, None] == key_clip[None, :]) & (
@@ -1341,14 +1391,7 @@
     grad_w_first = matmul_tn(hidden_all, grad_pre)
     grad_w_second = matmul_tn(activated, grad_mlp_all)
     grad_cross_branch = after(grad_cross_branch, (grad_w_first, grad_w_second))
-    if small_patch():
-        grad_w_first = back_to_rows(grad_w_first)
-    else:
-        grad_w_first = lax.all_to_all(grad_w_first, "patch", 0, 1, tiled=True)
-    first_sent = grad_w_first
     grad_w_first, grad_w_second = lax.psum((grad_w_first, grad_w_second), "frame")
-    if small_patch():
-        grad_w_first = side_by_side(grad_w_first)
     grad_b_first = jnp.sum(grad_pre, axis=0)
     mlp_parts = matmul(activated, fc2_weight)
     grad_cross_rows = matmul_nt(grad_cross_branch, w_cross_o)
@@ -1366,7 +1409,7 @@
     grad_w_attn = matmul_tn(attended_rows, grad_attn_rows)
     grad_b_attn = jnp.sum(grad_attn_rows, axis=0)
     grad_attn_rows = after(grad_attn_rows, grad_w_attn)
-    mlp_sum, grad_kv_share = mid_way(after(mlp_parts, (grad_w_attn, first_sent)), grad_kv)
+    mlp_sum, grad_kv_share = mid_way(after(mlp_parts, grad_w_attn), grad_kv)
     grad_attn_rows = after(grad_attn_rows, mlp_sum)
     grad_w_cross_kv = matmul_tn(caption_share, grad_kv_share)
     grad_b_cross_v = jnp.sum(grad_kv_share[:, width:], axis=0)
@@ -1414,9 +1457,9 @@
     small_grads = jnp.concatenate(
         [grad_modulation_part.reshape(-1)] + list(bias_grads) + [placed(grad_b_first, "patch")]
     )
-    weights, grad_w_cross_kv, input_grad, small_grads, grad_caption = close_up(
+    weights, grad_w_cross_kv, input_grad, small_grads, grad_caption, grad_w_first = close_up(
         (grad_w_qkv, grad_w_attn, grad_w_cross_q, grad_w_cross_o),
-        grad_w_cross_kv, input_grad, small_grads, grad_caption_share,
+        grad_w_cross_kv, input_grad, small_grads, grad_caption_share, grad_w_first,
     )
     place = grad_modulation_part.size
     grad_modulation = small_grads[:place].reshape(grad_modulation_part.shape)

time: 1200 us -> 1200 us (level)
  matrix products: 237 us -> 270 us
  waiting for transfers between devices: 52.8 us -> 34.5 us
  Pallas kernels: 731 us -> 714 us
    all_gather x3, waiting for transfers between devices: 48.5 us -> 8.3 us  [gather_rows(): return lax.all_gather(shard, 'patch', axis=0, tiled=True)]
    pallas_call x1, Pallas kernels: 155 us -> 139 us  [begin(): pl.pallas_call(begin_kernel, out_shape=(jax.ShapeDtypeStruct((4 * count,...]
    dot_general x8, matrix products: 73.6 us -> 89.2 us  [matmul(): return jnp.dot(left, right, precision=BEST)]
    pallas_call x1, Pallas kernels: 233 us -> 247 us  [finish(): pl.pallas_call(finish_kernel, out_shape=(shape(rows, 3 * width), shape(ro...]
    ppermute x4, waiting for transfers between devices: 3.56 us -> 16.7 us  [swap(): return lax.ppermute(value, axis, [(i, i ^ bit) for i in range(size)])]
    dot_general x8, matrix products: 80.1 us -> 92.6 us  [matmul_tn(): lax.dot_general(left, right, (((0,), (0,)), ((), ())), precision=BEST)]
    unnamed x210 -> x230, local copies, waits for them, and re-layouts: 50.6 us -> 45 us
  transfers between devices with their start and end apart: 9 -> 9, of which waited for: 2 -> 5; matrix products, arithmetic and copies ran while one was open for 17% -> 13% of each run, Pallas kernels for 55% -> 34%
where the time goes in v6:
time: 1200 us
  Pallas kernels  714 us (60%)
  matrix products  270 us (22%)
  local copies, waits for them, and re-layouts  81.5 us (7%)
  starting transfers between devices  50.1 us (4%)
  waiting for transfers between devices  34.5 us (3%)
  other arithmetic  31.2 us (3%)
  between operations  15.3 us (1%)
    pallas_call x1, Pallas kernels, finish(): pl.pallas_call(finish_kernel, out_shape=(shape(rows, 3 * width), shape(ro...  247 us
    pallas_call x1, Pallas kernels, begin(): pl.pallas_call(begin_kernel, out_shape=(jax.ShapeDtypeStruct((4 * count,...  139 us
    pallas_call x1, Pallas kernels, middle(): pl.pallas_call(middle_kernel, out_shape=(jax.ShapeDtypeStruct(block, f32)...  94.7 us
    dot_general x8, matrix products, matmul_tn(): lax.dot_general(left, right, (((0,), (0,)), ((), ())), precision=BEST)  92.6 us
    dot_general x8, matrix products, matmul(): return jnp.dot(left, right, precision=BEST)  89.2 us
    dot_general x8, matrix products, matmul_nt(): lax.dot_general(left, right, (((1,), (1,)), ((), ())), precision=BEST)  87.4 us
    pallas_call x1, Pallas kernels, token_gather(): pl.pallas_call(token_gather_kernel, out_shape=jax.ShapeDtypeStruct((8, le...  86.6 us
    pallas_call x1, Pallas kernels, token_scatter(): pl.pallas_call(token_scatter_kernel, out_shape=jax.ShapeDtypeStruct(block...  54.2 us
  transfers between devices with their start and end apart: 9, of which 5 were waited for; matrix products, arithmetic and copies ran while one was open for 13% of the time, Pallas kernels for 34%

profile of v6, /device:TPU:0, one launch (start us, length us, event | category | flops | bytes accessed | tf_op | source)
XLA Modules:
  0.0 1196.8 jit_solution(1698003971325510363)
XLA Ops:
  22.1 138.9 %shard_map.400 = (f32[20,16,1152]{2,1,0:T(8,128)S(1)}, f32[20,16,1152]{2,1,0:T(8,128)S(1)}, f32[4,8,128]{2,1,0:T(8,128)S(1)}, f32[336,128]{1,0:T(8,128)S(1)}, f3...) custom-call(f32[5,64,1152]{2,1,0:T(8,128)S(1)} %copy-done.26, f32[5,64,1152]{2,1,0:T(8,128)S(1)} %copy-done.27, ...), custom_call_target="tpu_custom_call" | custom-call | bytes 65536 | tf_op jit(solution)/shard_map/pallas_call | solution.py:405
  171.9 25.8 %fusion.44 = f32[320,3456]{1,0:T(8,128)} fusion(f32[320,1152]{1,0:T(8,128)S(1)} %bitcast.171, f32[1152,3456]{1,0:T(8,128)} %get-tuple-element.56), kind=kOutput, calls=%fused_computation.162 | convolution fusion | flops 7644119040 | bytes 21823488 | tf_op jit(solution)/shard_map/dot_general | solution.py:22
  222.5 9.2 shard_map.401
  236.0 8.9 collective-permute-done.2
  246.1 6.1 collective-permute-done.1
  254.0 6.7 fusion.16
  265.6 19.3 %shard_map.403 = (f32[16,320,480]{2,1,0:T(8,128)}, f32[320,1152]{1,0:T(8,128)S(1)}) custom-call(f32[320,1152]{1,0:T(8,128)S(1)} %fusion.10.queries, f32[1,1152]{1,0:T(1,128)S(1)} %bitcast.151, f32[480,2304]{1,0:T(8,128)} %copy-done.9, f32[1,1152]{1,0:T(1,128)S(1)} %bitcast.149, f32[320,480]{1,0:T(8,128)S(1)} %bitcast.144), custom_call_target="tpu_custom_call" | custom-call | bytes 65536 | tf_op jit(solution)/shard_map/pallas_call | solution.py:1076
  287.2 6.7 convolution_add_fusion
  297.9 86.6 %shard_map.404 = f32[8,320,1152]{2,1,0:T(8,128)S(1)} custom-call(f32[320,1152]{1,0:T(8,128)S(1)} %bitcast.141), custom_call_target="tpu_custom_call" | custom-call | bytes 65536 | tf_op jit(solution)/shard_map/pallas_call | solution.py:147
  388.9 8.3 all-gather.8.cloned.1.call-done
  397.2 16.3 %fusion.45 = f32[2560,576]{0,1:T(8,128)} fusion(f32[2560,1152]{1,0:T(8,128)} %all-gather.8.cloned.1.call-done, f32[576,1152]{1,0:T(8,128)S(1)} %copy-done), kind=kOutput, calls=%fused_computation.163 | convolution fusion | flops 10192158720 | bytes 20348928 | tf_op jit(solution)/shard_map/dot_general | solution.py:26
  413.5 22.1 %fusion.7 = (f32[2560,576]{0,1:T(8,128)}, f32[2560,576]{0,1:T(8,128)}) fusion(f32[2560,576]{0,1:T(8,128)} %fusion.45, f32[576]{0:T(1024)S(1)} %copy-done.93, f32[2560,1152]{1,0:T(8,128)S(1)} %bitcast.139, f32[1152,576]{1,0:T(8,128)} %copy-done.24), kind=kOutput, calls=%fused_computation.11 | convolution fusion | flops 10223124480 | bytes 32147712 | tf_op jit(solution)/shard_map/dot_general | solution.py:22
  435.6 28.9 %fusion.46 = f32[2560,1152]{1,0:T(8,128)S(1)} fusion(f32[2560,576]{0,1:T(8,128)} %get-tuple-element.67, f32[1152,576]{1,0:T(8,128)} %copy-done.24), kind=kOutput, calls=%fused_computation.164 | convolution fusion | flops 10192158720 | bytes 20348928 | tf_op jit(solution)/shard_map/dot_general | solution.py:26
  464.5 54.2 %shard_map.405 = f32[320,1152]{1,0:T(8,128)S(1)} custom-call(f32[8,320,1152]{2,1,0:T(8,128)S(1)} %bitcast.140), custom_call_target="tpu_custom_call" | custom-call | bytes 65536 | tf_op jit(solution)/shard_map/pallas_call | solution.py:211
  525.9 7.2 fusion.47.cross_o
  533.1 16.9 %fusion.49 = f32[1152,576]{0,1:T(8,128)} fusion(f32[2560,1152]{1,0:T(8,128)} %bitcast.138, f32[2560,576]{0,1:T(8,128)S(1)} %bitcast.164), kind=kOutput, calls=%fused_computation.167 | convolution fusion | flops 10192158720 | bytes 20348928 | tf_op jit(solution)/shard_map/dot_general | solution.py:30
  553.4 18.9 %fusion.48 = f32[2560,1152]{1,0:T(8,128)} fusion(f32[2560,576]{0,1:T(8,128)} %get-tuple-element.65, f32[576,1152]{1,0:T(8,128)S(1)} %copy-done), kind=kOutput, calls=%fused_computation.166 | convolution fusion | flops 10192158720 | bytes 20348928 | tf_op jit(solution)/shard_map/dot_general | solution.py:22
  572.3 28.6 %fusion.50 = f32[576,1152]{1,0:T(8,128)} fusion(f32[2560,576]{0,1:T(8,128)} %get-tuple-element.65, f32[2560,1152]{1,0:T(8,128)} %all-gather.8.cloned.1.call-done), kind=kOutput, calls=%fused_computation.168 | convolution fusion | flops 10192158720 | bytes 20348928 | tf_op jit(solution)/shard_map/dot_general | solution.py:30
  602.3 7.1 fusion.51.grad
  609.3 35.0 %shard_map.406 = (f32[320,1152]{1,0:T(8,128)S(1)}, f32[480,2304]{1,0:T(8,128)}) custom-call(f32[320,1152]{1,0:T(8,128)} %copy-done.10, f32[1,1152]{1,0:T(1,128)S(1)} %bitcast.152, f32[480,2304]{1,0:T(8,128)} %copy-done.9, f32[1,1152]{1,0:T(1,128)S(1)} %bitcast.150, f32[16,320,480]{2,1,0:T(8,128)} %get-tuple-element.66.probs, f32[320,1152]{1,0:T(8,128)} %copy-done.11, ...), custom_call_target="tpu_custom_call" | custom-call | bytes 65536 | tf_op jit(solution)/shard_map/pallas_call | solution.py:1134
  644.3 7.0 fusion.52.cross_q
  651.3 6.2 fusion.8
  658.9 7.2 convolution_bitcast_fusion.1.attn
  666.1 94.7 %shard_map.407 = (f32[320,1152]{1,0:T(8,128)S(1)}, f32[120,2304]{1,0:T(8,128)S(1)}) custom-call(f32[8,320,1152]{2,1,0:T(8,128)} %bitcast.160, f32[480,2304]{1,0:T(8,128)} %get-tuple-element.72.kv), custom_call_target="tpu_custom_call" | custom-call | bytes 65536 | tf_op jit(solution)/shard_map/pallas_call | solution.py:833
  760.8 5.9 fusion.12
  766.8 23.1 %shard_map.408 = f32[20,16,3456]{2,1,0:T(8,128)} custom-call(f32[20,16,3456]{2,1,0:T(8,128)} %bitcast.134, f32[1,1152]{1,0:T(1,128)S(1)} %bitcast.148, f32[1,1152]{1,0:T(1,128)S(1)} %bitcast.146, f32[16,2,160,160]{3,2,1,0:T(8,128)} %copy-done.23, f32[20,16,1152]{2,1,0:T(8,128)S(1)} %copy-done.22, f32[20,16,1152]{2,1,0:T(8,128)S(1)} %bitcast.143), custom_call_target="tpu_custom_call" | custom-call | bytes 65536 | tf_op jit(solution)/shard_map/pallas_call | solution.py:1035
  790.0 19.4 %multiply_reduce_fusion.3 = (f32[16,1152]{1,0:T(8,128)S(1)}, f32[20,16]{1,0:T(8,128)S(1)}, f32[20,16]{1,0:T(8,128)S(1)}, f32[16,1152]{1,0:T(8,128)S(1)}, f32[20,16,1152]{2,1,0:T(8,128)S(1)}) fusion(f32[20,16,1152]{2,1,0:T(8,128)S(1)} %copy-done.5, f32[20,16]{1,0:T(8,128)S(1)} %copy-done.70, f32[20,16]{1,0:T(8,128)S(1)} %copy-done.68, ...), kind=kOutput, calls=%fused_computation.29 | convolution fusion | flops 7647399424 | bytes 23524352 | tf_op jit(solution)/shard_map/dot_general | solution.py:26
  816.7 46.3 %all-to-all-start = ((f32[20,16,1152]{2,1,0:T(8,128)}), f32[20,16,1152]{2,1,0:T(8,128)S(1)}, u32[]{:S(2)}, u32[]{:S(2)}) async-start(f32[20,16,1152]{2,1,0:T(8,128)} %get-tuple-element.142), calls=%async_computation | async-start | bytes 2949120 | tf_op jit(solution)/shard_map/all_to_all | solution.py:1220
  871.4 18.3 %convolution_bitcast_fusion.first = f32[1152,3456]{1,0:T(8,128)} fusion(f32[20,16,1152]{2,1,0:T(8,128)S(1)} %copy-done.48, f32[20,16,3456]{2,1,0:T(8,128)} %shard_map.408), kind=kOutput, calls=%fused_computation | convolution fusion | flops 7644119040 | bytes 21823488 | tf_op jit(solution)/shard_map/dot_general | solution.py:30
  889.6 8.8 all-to-all-done
  899.6 246.9 %shard_map.409 = (f32[144,3456]{1,0:T(8,128)}, f32[144,1152]{1,0:T(8,128)}, f32[144,1152]{1,0:T(8,128)}, f32[144,1152]{1,0:T(8,128)}, f32[144,2304]{1,0:T(8,128)...) custom-call(f32[1152,3456]{1,0:T(8,128)} %convolution_bitcast_fusion.first,, ...), custom_call_target="tpu_custom_call" | custom-call | bytes 65536 | tf_op jit(solution)/shard_map/pallas_call | solution.py:713
  1166.5 6.2 shard_map.410
  (367 shorter events, 140.1 us)
Async XLA Ops:
  7.2 390.0 %copy-start = (f32[576,1152]{1,0:T(8,128)S(1)}, f32[576,1152]{1,0:T(8,128)}, u32[]{:S(2)}) copy-start(f32[576,1152]{1,0:T(8,128)} %param.44) | copy-start | bytes 7962628
  7.2 246.8 %all-gather.4.cloned.1.call-start = ((), (), s32[]{:S(2)}) async-start(), calls=%async_computation.1 | async-start | bytes 11943936 | tf_op jit(solution)/shard_map/all_gather | solution.py:1173
  9.9 277.3 %all-gather.6.cloned.1.call-start = ((), (), s32[]{:S(2)}) async-start(), calls=%async_computation.2 | async-start | bytes 5971968 | tf_op jit(solution)/shard_map/all_gather | solution.py:1173
  10.6 386.6 %all-gather.8.cloned.1.call-start = ((), (), s32[]{:S(2)}) async-start(), calls=%async_computation.3 | async-start | bytes 13271040 | tf_op jit(solution)/shard_map/all_gather | solution.py:1173
  202.7 3.6 collective-permute-start
  209.4 25.5 %collective-permute-start.3 = (f32[288,576]{1,0:T(8,128)}, f32[288,576]{1,0:T(8,128)}, u32[]{:S(2)}, u32[]{:S(2)}) collective-permute-start(f32[288,576]{1,0:T(8,128)} %pad_maximum_fusion.4), channel_id=1, source_target_pairs={{0,24},{4,28},{8,16},{12,20},{16,8},{20,12},{24,0},{28,4},{1,25},{... | collective-permute-start | bytes 1990664 | tf_op jit(solution)/shard_map/ppermute | solution.py:49
  212.3 32.6 %collective-permute-start.2 = (f32[288,576]{1,0:T(8,128)}, f32[288,576]{1,0:T(8,128)}, u32[]{:S(2)}, u32[]{:S(2)}) collective-permute-start(f32[288,576]{1,0:T(8,128)} %pad_maximum_fusion.3), channel_id=1, source_target_pairs={{0,16},{4,20},{8,24},{12,28},{16,0},{20,4},{24,8},{28,12},{1,17},{... | collective-permute-start | bytes 1990664 | tf_op jit(solution)/shard_map/ppermute | solution.py:49
  222.5 11.5 copy-start.56
  222.5 11.5 copy-start.59
  234.1 18.0 %collective-permute-start.1 = (f32[288,576]{1,0:T(8,128)S(1)}, f32[288,576]{1,0:T(8,128)S(1)}, u32[]{:S(2)}, u32[]{:S(2)}) collective-permute-start(f32[288,576]{1,0:T(8,128)S(1)} %pad_maximum_fusion.2), channel_id=1, source_target_pairs={{0,8},{4,12},{8,0},{12,4},{16,24},{20,28},{24,16},{28,20},{1,9},{5... | collective-permute-start | bytes 1990664 | tf_op jit(solution)/shard_map/ppermute | solution.py:49
  252.2 8.5 copy-start.64
  254.0 7.8 copy-start.37
  265.6 21.6 %copy-start.76 = (f32[1152]{0:T(1024)S(1)}, f32[1152]{0:T(1024)}, u32[]{:S(2)}) copy-start(f32[1152]{0:T(1024)} %get-tuple-element.160) | copy-start | bytes 13828
  287.1 6.7 copy-start.39
  287.1 6.7 copy-start.65
  287.1 6.7 copy-start.80
  295.7 603.9 %all-reduce.6.cloned.1.call-start = ((), (), s32[]{:S(2)}) async-start(), calls=%async_computation.4 | async-start | bytes 11206656 | tf_op jit(solution)/shard_map/psum | solution.py:1394
  388.9 24.6 %copy-start.93 = (f32[576]{0:T(1024)S(1)}, f32[576]{0:T(1024)}, u32[]{:S(2)}) copy-start(f32[576]{0:T(1024)} %param.43) | copy-start | bytes 6916
  397.2 16.3 %copy-start.20 = (f32[8,320,1152]{2,1,0:T(8,128)S(1)}, f32[8,320,1152]{2,1,0:T(8,128)}, u32[]{:S(2)}) copy-start(f32[8,320,1152]{2,1,0:T(8,128)} %copy-done.19) | copy-start | bytes 35389444
  522.6 10.5 slice-start
  525.8 7.2 copy-start.44
  525.9 7.2 slice-start.1
  609.3 35.0 %copy-start.40 = (f32[20,16,1152]{2,1,0:T(8,128)S(1)}, f32[20,16,1152]{2,1,0:T(8,128)}, u32[]{:S(2)}) copy-start(f32[20,16,1152]{2,1,0:T(8,128)} %copy-done.38) | copy-start | bytes 4423684
  644.3 7.0 copy-start.13
  766.8 23.2 %copy-start.5 = (f32[20,16,1152]{2,1,0:T(8,128)S(1)}, f32[20,16,1152]{2,1,0:T(8,128)}, u32[]{:S(2)}) copy-start(f32[20,16,1152]{2,1,0:T(8,128)} %copy-done.2) | copy-start | bytes 4423684
  766.8 23.1 %copy-start.54 = (f32[16,1152]{1,0:T(8,128)S(1)}, f32[16,1152]{1,0:T(8,128)}, u32[]{:S(2)}) copy-start(f32[16,1152]{1,0:T(8,128)} %copy-done.53) | copy-start | bytes 221188
  766.8 23.1 %copy-start.68 = (f32[20,16]{1,0:T(8,128)S(1)}, f32[20,16]{1,0:T(8,128)}, u32[]{:S(2)}) copy-start(f32[20,16]{1,0:T(8,128)} %copy-done.67) | copy-start | bytes 3844
  766.8 23.1 %copy-start.70 = (f32[20,16]{1,0:T(8,128)S(1)}, f32[20,16]{1,0:T(8,128)}, u32[]{:S(2)}) copy-start(f32[20,16]{1,0:T(8,128)} %copy-done.69) | copy-start | bytes 3844
  789.9 19.5 %copy-start.75 = (f32[1152]{0:T(1024)S(1)}, f32[1152]{0:T(1024)}, u32[]{:S(2)}) copy-start(f32[1152]{0:T(1024)} %get-tuple-element.159) | copy-start | bytes 13828
  790.0 19.7 %copy-start.43 = (f32[320,1152]{1,0:T(8,128)S(1)}, f32[320,1152]{1,0:T(8,128)}, u32[]{:S(2)}) copy-start(f32[320,1152]{1,0:T(8,128)} %copy-done.42) | copy-start | bytes 4423684
  816.7 81.7 %all-to-all-start = ((f32[20,16,1152]{2,1,0:T(8,128)}), f32[20,16,1152]{2,1,0:T(8,128)S(1)}, u32[]{:S(2)}, u32[]{:S(2)}) async-start(f32[20,16,1152]{2,1,0:T(8,128)} %get-tuple-element.142), calls=%async_computation | async-start | bytes 2949120 | tf_op jit(solution)/shard_map/all_to_all | solution.py:1220
  899.6 247.9 %copy-start.73 = (f32[4,1152]{1,0:T(4,128)S(1)}, f32[4,1152]{1,0:T(4,128)}, u32[]{:S(2)}) copy-start(f32[4,1152]{1,0:T(4,128)} %param.28) | copy-start | bytes 55300
  (76 other events, 199.8 us)
Sparse Core Ops, SparseCore 0:
  10.5 104.9 all-gather.3
  117.4 52.4 all-gather.5
  295.9 101.3 all-gather.7
  601.0 237.4 all-reduce.5

commit v7 on v6

--- a/solution.py
+++ b/solution.py
@@ -648,7 +648,6 @@
     links.wait(small_got.at[2], small_at[2], y)
     small_sums[2] = small_sums[1] + small_got[2]
     small_steps[0]()
-    caption_x()
     stage_one(2)
     steps[6][1]()
     steps[7][1]()
@@ -666,25 +665,26 @@
     stage_one(4)
     steps[0][1]()
     small_steps[2]()
-    caption_y()
     send_tokens(3)
     stage_two(3)
     stage_three(2)
     stage_one(5)
     steps[1][1]()
     steps[0][2]()
-    for k in (2, 4, 6):
-        send_columns(k)
     stage_two(4)
     stage_three(3)
     stage_two(5)
+    caption_x()
+    for k in (2, 4, 6):
+        send_columns(k)
     steps[2][1]()
     steps[1][2]()
-    caption_core()
     stage_three(4)
+    caption_y()
     steps[3][1]()
     steps[2][2]()
     stage_three(5)
+    caption_core()
     steps[4][1]()
     steps[3][2]()
     steps[5][1]()
@@ -739,9 +739,9 @@
 
 
 def middle_kernel(
-    parts, kv,
-    total, kv_out,
-    kept, theirs, by_x, by_y, from_x, from_y,
+    parts, kv, residual, gate, bias,
+    total, kv_out, block_out,
+    block, kept, theirs, by_x, by_y, from_x, from_y,
     kv_half, kv_core, kv_got, kv_1, kv_2, kv_got_1, kv_got_2,
     load_sems, send_sems, recv_sems,
 ):
@@ -810,6 +810,14 @@
     links.wait(from_y.at[upper], at[4], y)
     links.wait(from_x.at[lower], at[5], x)
     total[...] = kept[0] + from_x[...] + from_y[...]
+    slots, part = residual.shape[0] // 4, residual.shape[1]
+    block[...] = residual[...] + gate[...] * (total[...] + bias[...]).reshape(residual.shape)
+    block_at = [None] + [links.plan() for _ in range(3)]
+    place = pl.ds(pl.multiple_of(z * part, part), part)
+    for k in (1, 2, 3):
+        source = block.at[pl.ds((z ^ k) * slots, slots)]
+        links.send(source, block_out.at[:, place], block_at[k], frames[k])
+    block_out[:, place] = block[pl.ds(z * slots, slots)]
     links.wait(kv_got_1.at[top], at_u, x)
     links.wait(kv_got_1.at[bottom], at_l, y)
     kv_2[...] = kv_1[...] + kv_got_1[...]
@@ -822,10 +830,14 @@
     at_core = links.plan()
     links.send(kv_out.at[:, mine], kv_out.at[:, mine], at_core, core)
     links.wait(kv_out.at[:, others], at_core, core)
+    for k in (1, 2, 3):
+        there = pl.ds(pl.multiple_of((z ^ k) * part, part), part)
+        links.wait(block_out.at[:, there], block_at[k], frames[k])
     links.drain()
 
 
-def middle(parts, kv):
+def middle(parts, kv, residual, gate, bias):
+    slots, cols, _ = residual.shape
     length, width = parts.shape[0] // 8, parts.shape[1]
     rows = kv.shape[0] // 4
     f32, vmem = jnp.float32, pl.BlockSpec(memory_space=pltpu.VMEM)
@@ -834,10 +846,12 @@
         middle_kernel,
         out_shape=(
             jax.ShapeDtypeStruct(block, f32), jax.ShapeDtypeStruct((rows, 2 * width), f32),
+            jax.ShapeDtypeStruct((slots // 4, 4 * cols, width), f32),
         ),
-        in_specs=[pl.BlockSpec(memory_space=pl.ANY), vmem],
-        out_specs=[vmem] * 2,
+        in_specs=[pl.BlockSpec(memory_space=pl.ANY)] + [vmem] * 4,
+        out_specs=[vmem] * 3,
         scratch_shapes=[
+            pltpu.VMEM((slots, cols, width), f32),
             pltpu.VMEM((4,) + block, f32), pltpu.VMEM((4,) + block, f32),
             pltpu.VMEM((length // 2, width), f32), pltpu.VMEM((length // 2, width), f32),
             pltpu.VMEM(block, f32), pltpu.VMEM(block, f32),
@@ -850,7 +864,7 @@
             collective_id=4, has_side_effects=True, vmem_limit_bytes=48 << 20
         ),
         cost_estimate=LIGHT,
-    )(parts.reshape((8,) + block), kv)
+    )(parts.reshape((8,) + block), kv, residual, gate[None], bias[None])
 
 
 def spread_kernel(block, whole, send_sems, recv_sems):
@@ -1246,11 +1260,13 @@
     return tokens, later, slots, summed, kv, whole
 
 
-def mid_way(parts, kv):
+def mid_way(parts, kv, residual, gate, bias):
     if not small_patch():
         kv = lax.psum_scatter(all_sum(kv, "patch"), "frame", scatter_dimension=0, tiled=True)
-        return scatter_rows(parts), kv
-    return middle(parts, kv)
+        total = scatter_rows(parts)
+        block = residual + gate * (total + bias).reshape(residual.shape)
+        return total, kv, to_slots(block)
+    return middle(parts, kv, residual, gate, bias)
 
 
 def close_up(weights, kv, tokens, small, caption, columns):
@@ -1348,7 +1364,6 @@
     normed_one, inverse_one = normalize(tokens_in)
     hidden_one = (normed_one * (1.0 + scale_one) + shift_one).reshape(rows, width)
     qkv_rows = matmul(hidden_one, w_qkv)
-    w_first = to_own_columns(after(fc1_weight, qkv_rows))
     grad_mlp_all = gather_rows(after(grad_mlp, qkv_rows))
     qkv = qkv_rows.reshape(slots, cols, 3 * width)
     probs, attended = frame_attention(qkv, b_query, b_value, *frame_tables(frame_pos))
@@ -1356,8 +1371,9 @@
     attn_branch = (matmul(attended_rows, w_attn) + b_attn).reshape(slots, cols, width)
     after_attn = tokens_in + column_mask * gate_one * attn_branch
     after_attn_rows = after_attn.reshape(rows, width)
-    after_attn_rows = after(after_attn_rows, w_first)
     cross_queries = matmul(after_attn_rows, w_cross_q)
+    w_first = to_own_columns(after(fc1_weight, cross_queries))
+    cross_queries = after(cross_queries, grad_mlp_all)
     key_clip = jnp.arange(CLIPS * CAP, dtype=jnp.int32) // CAP
     caption_ok = (clip_own[:, None] == key_clip[None, :]) & (
         caption_mask.reshape(CLIPS * CAP)[None, :] > 0
@@ -1371,7 +1387,7 @@
     normed_two, inverse_two = normalize(after_cross)
     hidden_two = (normed_two * (1.0 + scale_two) + shift_two).reshape(rows, width)
 
-    hidden_all = gather_tokens(hidden_two)
+    hidden_all = gather_tokens(after(hidden_two, w_first))
     pre_act = matmul(hidden_all, w_first) + fc1_bias
     activated, gelu_pull = jax.vjp(partial(jax.nn.gelu, approximate=True), pre_act)
     grad_pre = gelu_pull(matmul_nt(grad_mlp_all, fc2_weight))[0]
@@ -1409,13 +1425,14 @@
     grad_w_attn = matmul_tn(attended_rows, grad_attn_rows)
     grad_b_attn = jnp.sum(grad_attn_rows, axis=0)
     grad_attn_rows = after(grad_attn_rows, grad_w_attn)
-    mlp_sum, grad_kv_share = mid_way(after(mlp_parts, grad_w_attn), grad_kv)
+    mlp_sum, grad_kv_share, block_out = mid_way(
+        after(mlp_parts, grad_w_attn), grad_kv, after_cross, column_mask * gate_two, b_second
+    )
     grad_attn_rows = after(grad_attn_rows, mlp_sum)
     grad_w_cross_kv = matmul_tn(caption_share, grad_kv_share)
     grad_b_cross_v = jnp.sum(grad_kv_share[:, width:], axis=0)
     grad_caption_share = matmul_nt(cross_kv_weight, grad_kv_share)
     mlp_branch = (mlp_sum + b_second).reshape(slots, cols, width)
-    block_out = to_slots(after_cross + column_mask * gate_two * mlp_branch)
     grad_gate_two = jnp.sum(column_mask * mlp_branch * cotangent, axis=0)
     grad_attended = matmul_nt(grad_attn_rows, w_attn).reshape(slots, cols, width)
     grad_qkv = frame_attention_back(

time: 1200 us -> 1220 us (1.017)
  starting transfers between devices: 50.1 us -> 4.65 us
  waiting for transfers between devices: 34.5 us -> 78.3 us
  Pallas kernels: 714 us -> 752 us
  matrix products: 270 us -> 256 us
    pallas_call x1, Pallas kernels: 94.7 us -> 161 us  [middle(): pl.pallas_call(middle_kernel, out_shape=(jax.ShapeDtypeStruct(block, f32)...]
    all_to_all x1 -> x0, starting transfers between devices: 46.3 us -> none  [to_slots(): return lax.all_to_all(x, 'frame', split_axis=0, concat_axis=1, tiled=True)]
    ppermute x4, waiting for transfers between devices: 16.7 us -> 55.9 us  [swap(): return lax.ppermute(value, axis, [(i, i ^ bit) for i in range(size)])]
    pallas_call x1, Pallas kernels: 86.6 us -> 53 us  [token_gather(): pl.pallas_call(token_gather_kernel, out_shape=jax.ShapeDtypeStruct((8, le...]
    pallas_call x1, Pallas kernels: 247 us -> 263 us  [finish(): pl.pallas_call(finish_kernel, out_shape=(shape(rows, 3 * width), shape(ro...]
    all_gather x3, waiting for transfers between devices: 8.3 us -> 21.6 us  [gather_rows(): return lax.all_gather(shard, 'patch', axis=0, tiled=True)]
    unnamed x230 -> x220, local copies, waits for them, and re-layouts: 45 us -> 39.8 us
  transfers between devices with their start and end apart: 9 -> 8, of which waited for: 5 -> 6; matrix products, arithmetic and copies ran while one was open for 13% -> 11% of each run, Pallas kernels for 34% -> 31%
where the time goes in v7:
time: 1220 us; the launch traced here: 1210 us
  Pallas kernels  752 us (62%)
  matrix products  256 us (21%)
  waiting for transfers between devices  78.3 us (6%)
  local copies, waits for them, and re-layouts  71.1 us (6%)
  other arithmetic  27.6 us (2%)
  between operations  15.3 us (1%)
    pallas_call x1, Pallas kernels, finish(): pl.pallas_call(finish_kernel, out_shape=(shape(rows, 3 * width), shape(ro...  263 us
    pallas_call x1, Pallas kernels, middle(): pl.pallas_call(middle_kernel, out_shape=(jax.ShapeDtypeStruct(block, f32)...  161 us
    pallas_call x1, Pallas kernels, begin(): pl.pallas_call(begin_kernel, out_shape=(jax.ShapeDtypeStruct((4 * count,...  128 us
    dot_general x8, matrix products, matmul_nt(): lax.dot_general(left, right, (((1,), (1,)), ((), ())), precision=BEST)  92.6 us
    dot_general x8, matrix products, matmul_tn(): lax.dot_general(left, right, (((0,), (0,)), ((), ())), precision=BEST)  82.1 us
    dot_general x8, matrix products, matmul(): return jnp.dot(left, right, precision=BEST)  80.1 us
    ppermute x4, waiting for transfers between devices, swap(): return lax.ppermute(value, axis, [(i, i ^ bit) for i in range(size)])  55.9 us
    pallas_call x1, Pallas kernels, token_scatter(): pl.pallas_call(token_scatter_kernel, out_shape=jax.ShapeDtypeStruct(block...  54.2 us
  transfers between devices with their start and end apart: 8, of which 6 were waited for; matrix products, arithmetic and copies ran while one was open for 11% of the time, Pallas kernels for 31%

profile of v7, /device:TPU:0, one launch (start us, length us, event | category | flops | bytes accessed | tf_op | source)
XLA Modules:
  0.0 1205.4 jit_solution(5837049353938815073)
XLA Ops:
  21.9 127.9 %shard_map.400 = (f32[20,16,1152]{2,1,0:T(8,128)S(1)}, f32[20,16,1152]{2,1,0:T(8,128)S(1)}, f32[4,8,128]{2,1,0:T(8,128)S(1)}, f32[336,128]{1,0:T(8,128)S(1)}, f3...) custom-call(f32[5,64,1152]{2,1,0:T(8,128)S(1)} %copy-done.29, f32[5,64,1152]{2,1,0:T(8,128)S(1)} %copy-done.30, ...), custom_call_target="tpu_custom_call" | custom-call | bytes 65536 | tf_op jit(solution)/shard_map/pallas_call | solution.py:405
  162.6 15.4 %fusion.44 = f32[320,3456]{1,0:T(8,128)} fusion(f32[320,1152]{1,0:T(8,128)S(1)} %bitcast.163, f32[1152,3456]{1,0:T(8,128)} %get-tuple-element.58), kind=kOutput, calls=%fused_computation.163 | convolution fusion | flops 7644119040 | bytes 21823488 | tf_op jit(solution)/shard_map/dot_general | solution.py:22
  182.9 9.2 shard_map.401
  195.5 6.7 fusion.16
  203.3 5.0 fusion.10.queries
  223.0 30.5 %collective-permute-done.3 = f32[288,576]{1,0:T(8,128)} collective-permute-done((f32[288,576]{1,0:T(8,128)}, f32[288,576]{1,0:T(8,128)}, u32[]{:S(2)}, u32[]{:S(2)}) %collective-permute-start.3) | collective-permute-done | bytes 663584 | tf_op jit(solution)/shard_map/ppermute | solution.py:49
  254.8 14.2 %collective-permute-done.2 = f32[288,576]{1,0:T(8,128)} collective-permute-done((f32[288,576]{1,0:T(8,128)}, f32[288,576]{1,0:T(8,128)}, u32[]{:S(2)}, u32[]{:S(2)}) %collective-permute-start.2) | collective-permute-done | bytes 663584 | tf_op jit(solution)/shard_map/ppermute | solution.py:49
  270.2 6.4 collective-permute-done.1
  280.2 19.5 %shard_map.402 = (f32[16,320,480]{2,1,0:T(8,128)}, f32[320,1152]{1,0:T(8,128)S(1)}) custom-call(f32[320,1152]{1,0:T(8,128)S(1)} %copy-done.16, f32[1,1152]{1,0:T(1,128)S(1)} %get-tuple-element.182.b_query, f32[480,2304]{1,0:T(8,128)} %copy-done.12, f32[1,1152]{1,0:T(1,128)S(1)} %get-tuple-element.181.b_value, f32[320,480]{1,0:T(8,128)S(1)} %bitcast.143), custom_call_target="tpu_custom_call" | custom-call | bytes 65536 | tf_op jit(solution)/shard_map/pallas_call | solution.py:1090
  300.8 21.2 %all-gather.8.cloned.1.call-done = f32[1152,1152]{1,0:T(8,128)} async-done(((f32[144,1152]{1,0:T(8,128)}), f32[1152,1152]{1,0:T(8,128)}) %all-gather.8.cloned.1.call-update) | async-done | bytes 5308432 | tf_op jit(solution)/shard_map/all_gather | solution.py:1187
  322.1 6.6 convolution_add_fusion
  330.4 53.0 %shard_map.404 = f32[8,320,1152]{2,1,0:T(8,128)S(1)} custom-call(f32[320,1152]{1,0:T(8,128)S(1)} %bitcast.140), custom_call_target="tpu_custom_call" | custom-call | bytes 65536 | tf_op jit(solution)/shard_map/pallas_call | solution.py:147
  383.5 20.4 %fusion.45 = f32[2560,576]{0,1:T(8,128)} fusion(f32[2560,1152]{1,0:T(8,128)} %all-gather.6.cloned.1.call-done, f32[576,1152]{1,0:T(8,128)S(1)} %copy-done), kind=kOutput, calls=%fused_computation.164 | convolution fusion | flops 10192158720 | bytes 20348928 | tf_op jit(solution)/shard_map/dot_general | solution.py:26
  403.8 22.0 %fusion.7 = (f32[2560,576]{0,1:T(8,128)}, f32[2560,576]{0,1:T(8,128)}) fusion(f32[2560,576]{0,1:T(8,128)} %fusion.45, f32[576]{0:T(1024)S(1)} %copy-done.89, f32[2560,1152]{1,0:T(8,128)S(1)} %bitcast.137, f32[1152,576]{1,0:T(8,128)} %copy-done.27), kind=kOutput, calls=%fused_computation.11 | convolution fusion | flops 10223124480 | bytes 32147712 | tf_op jit(solution)/shard_map/dot_general | solution.py:22
  425.8 29.2 %fusion.46 = f32[2560,1152]{1,0:T(8,128)S(1)} fusion(f32[2560,576]{0,1:T(8,128)} %get-tuple-element.70, f32[1152,576]{1,0:T(8,128)} %copy-done.27), kind=kOutput, calls=%fused_computation.165 | convolution fusion | flops 10192158720 | bytes 20348928 | tf_op jit(solution)/shard_map/dot_general | solution.py:26
  455.0 54.2 %shard_map.405 = f32[320,1152]{1,0:T(8,128)S(1)} custom-call(f32[8,320,1152]{2,1,0:T(8,128)S(1)} %bitcast.139), custom_call_target="tpu_custom_call" | custom-call | bytes 65536 | tf_op jit(solution)/shard_map/pallas_call | solution.py:211
  516.4 7.1 fusion.47.cross_o
  523.5 16.8 %fusion.49 = f32[1152,576]{0,1:T(8,128)} fusion(f32[2560,1152]{1,0:T(8,128)} %bitcast.138, f32[2560,576]{0,1:T(8,128)S(1)} %bitcast.158), kind=kOutput, calls=%fused_computation.168 | convolution fusion | flops 10192158720 | bytes 20348928 | tf_op jit(solution)/shard_map/dot_general | solution.py:30
  543.8 18.9 %fusion.48 = f32[2560,1152]{1,0:T(8,128)} fusion(f32[2560,576]{0,1:T(8,128)} %get-tuple-element.68, f32[576,1152]{1,0:T(8,128)S(1)} %copy-done), kind=kOutput, calls=%fused_computation.167 | convolution fusion | flops 10192158720 | bytes 20348928 | tf_op jit(solution)/shard_map/dot_general | solution.py:22
  562.7 17.7 %fusion.50 = f32[576,1152]{1,0:T(8,128)} fusion(f32[2560,576]{0,1:T(8,128)} %get-tuple-element.68, f32[2560,1152]{1,0:T(8,128)} %all-gather.6.cloned.1.call-done), kind=kOutput, calls=%fused_computation.169 | convolution fusion | flops 10192158720 | bytes 20348928 | tf_op jit(solution)/shard_map/dot_general | solution.py:30
  581.8 7.1 fusion.51.grad
  588.8 34.9 %shard_map.406 = (f32[320,1152]{1,0:T(8,128)S(1)}, f32[480,2304]{1,0:T(8,128)}) custom-call(f32[320,1152]{1,0:T(8,128)} %fusion.10.queries, f32[1,1152]{1,0:T(1,128)S(1)} %get-tuple-element.182.b_query, f32[480,2304]{1,0:T(8,128)} %copy-done.12, f32[1,1152]{1,0:T(1,128)S(1)} %get-tuple-element.181.b_value, f32[16,320,480]{2,1,0:T(8,128)} %get-tuple-element.69.probs, ...), custom_call_target="tpu_custom_call" | custom-call | bytes 65536 | tf_op jit(solution)/shard_map/pallas_call | solution.py:1148
  623.7 7.0 fusion.52.cross_q
  630.8 6.2 fusion.8
  638.4 7.5 convolution_bitcast_fusion.1.attn
  645.9 161.3 %shard_map.407 = (f32[320,1152]{1,0:T(8,128)S(1)}, f32[120,2304]{1,0:T(8,128)S(1)}, f32[5,64,1152]{2,1,0:T(8,128)S(1)}) custom-call(f32[8,320,1152]{2,1,0:T(8,128)} %bitcast.153, f32[480,2304]{1,0:T(8,128)} %get-tuple-element.75.kv, f32[20,16,1152]{2,1,0:T(8,128)S(1)} %copy-done.8, f32[1,16,1152]{2,1,0:T(8,128)S(1)} %bitcast.144, f32[1,1152]{1,0:T(1,128)S(1)} %bitcast.145), custom_call_target="tpu_custom_call" | custom-call | bytes 65536 | tf_op jit(solution)/shard_map/pallas_call | solution.py:845
  807.2 6.9 fusion.12
  814.2 23.0 %shard_map.408 = f32[20,16,3456]{2,1,0:T(8,128)} custom-call(f32[20,16,3456]{2,1,0:T(8,128)} %bitcast.133, f32[1,1152]{1,0:T(1,128)S(1)} %get-tuple-element.184.b_query, f32[1,1152]{1,0:T(1,128)S(1)} %get-tuple-element.183.b_value, f32[16,2,160,160]{3,2,1,0:T(8,128)} %copy-done.26, f32[20,16,1152]{2,1,0:T(8,128)S(1)} %copy-done.25, f32[20,16,1152]{2,1,0:T(8,128)S(1)} %bitcast.142), custom_call_target="tpu_custom_call" | custom-call | bytes 65536 | tf_op jit(solution)/shard_map/pallas_call | solution.py:1049
  837.2 19.3 %multiply_reduce_fusion.3 = (f32[16,1152]{1,0:T(8,128)S(1)}, f32[20,16]{1,0:T(8,128)S(1)}, f32[20,16]{1,0:T(8,128)S(1)}, f32[16,1152]{1,0:T(8,128)S(1)}, f32[20,16,1152]{2,1,0:T(8,128)S(1)}) fusion(f32[20,16,1152]{2,1,0:T(8,128)S(1)} %copy-done.5, f32[20,16]{1,0:T(8,128)S(1)} %copy-done.65, f32[20,16]{1,0:T(8,128)S(1)} %copy-done.63, ...), kind=kOutput, calls=%fused_computation.29 | convolution fusion | flops 7647399424 | bytes 23524352 | tf_op jit(solution)/shard_map/dot_general | solution.py:26
  871.6 18.4 %convolution_bitcast_fusion.first = f32[1152,3456]{1,0:T(8,128)} fusion(f32[20,16,1152]{2,1,0:T(8,128)S(1)} %copy-done.44, f32[20,16,3456]{2,1,0:T(8,128)} %shard_map.408), kind=kOutput, calls=%fused_computation | convolution fusion | flops 7644119040 | bytes 21823488 | tf_op jit(solution)/shard_map/dot_general | solution.py:30
  890.0 262.6 %shard_map.409 = (f32[144,3456]{1,0:T(8,128)}, f32[144,1152]{1,0:T(8,128)}, f32[144,1152]{1,0:T(8,128)}, f32[144,1152]{1,0:T(8,128)}, f32[144,2304]{1,0:T(8,128)...) custom-call(f32[1152,3456]{1,0:T(8,128)} %convolution_bitcast_fusion.first,, ...), custom_call_target="tpu_custom_call" | custom-call | bytes 65536 | tf_op jit(solution)/shard_map/pallas_call | solution.py:713
  1173.7 6.4 shard_map.410
  (356 shorter events, 127.8 us)
Async XLA Ops:
  7.2 376.2 %copy-start = (f32[576,1152]{1,0:T(8,128)S(1)}, f32[576,1152]{1,0:T(8,128)}, u32[]{:S(2)}) copy-start(f32[576,1152]{1,0:T(8,128)} %param.44) | copy-start | bytes 7962628
  7.2 188.3 %all-gather.4.cloned.1.call-start = ((), (), s32[]{:S(2)}) async-start(), calls=%async_computation | async-start | bytes 11943936 | tf_op jit(solution)/shard_map/all_gather | solution.py:1187
  9.9 268.9 %all-gather.6.cloned.1.call-start = ((), (), s32[]{:S(2)}) async-start(), calls=%async_computation.1 | async-start | bytes 13271040 | tf_op jit(solution)/shard_map/all_gather | solution.py:1187
  160.5 41.7 %copy-start.60 = (f32[16,1152]{1,0:T(8,128)}, f32[16,1152]{1,0:T(8,128)S(1)}, u32[]{:S(2)}) copy-start(f32[16,1152]{1,0:T(8,128)S(1)} %get-tuple-element.160) | copy-start | bytes 221188
  162.6 15.4 %copy-start.43 = (f32[20,16,1152]{2,1,0:T(8,128)}, f32[20,16,1152]{2,1,0:T(8,128)S(1)}, u32[]{:S(2)}) copy-start(f32[20,16,1152]{2,1,0:T(8,128)S(1)} %get-tuple-element.180) | copy-start | bytes 4423684
  178.1 144.0 %all-gather.8.cloned.1.call-start = ((), (), s32[]{:S(2)}) async-start(), calls=%async_computation.2 | async-start | bytes 5971968 | tf_op jit(solution)/shard_map/all_gather | solution.py:1187
  178.8 711.2 %all-reduce.6.cloned.1.call-start = ((), (), s32[]{:S(2)}) async-start(), calls=%async_computation.3 | async-start | bytes 11206656 | tf_op jit(solution)/shard_map/psum | solution.py:1410
  195.5 6.7 copy-start.4
  195.5 7.8 copy-start.33
  210.0 5.5 collective-permute-start
  217.2 36.4 %collective-permute-start.3 = (f32[288,576]{1,0:T(8,128)}, f32[288,576]{1,0:T(8,128)}, u32[]{:S(2)}, u32[]{:S(2)}) collective-permute-start(f32[288,576]{1,0:T(8,128)} %pad_maximum_fusion.4), channel_id=1, source_target_pairs={{0,24},{4,28},{8,16},{12,20},{16,8},{20,12},{24,0},{28,4},{1,25},{... | collective-permute-start | bytes 1990664 | tf_op jit(solution)/shard_map/ppermute | solution.py:49
  218.1 50.9 %collective-permute-start.2 = (f32[288,576]{1,0:T(8,128)}, f32[288,576]{1,0:T(8,128)}, u32[]{:S(2)}, u32[]{:S(2)}) collective-permute-start(f32[288,576]{1,0:T(8,128)} %pad_maximum_fusion.3), channel_id=1, source_target_pairs={{0,16},{4,20},{8,24},{12,28},{16,0},{20,4},{24,8},{28,12},{1,17},{... | collective-permute-start | bytes 1990664 | tf_op jit(solution)/shard_map/ppermute | solution.py:49
  220.2 56.3 %collective-permute-start.1 = (f32[288,576]{1,0:T(8,128)S(1)}, f32[288,576]{1,0:T(8,128)S(1)}, u32[]{:S(2)}, u32[]{:S(2)}) collective-permute-start(f32[288,576]{1,0:T(8,128)S(1)} %pad_maximum_fusion.2), channel_id=1, source_target_pairs={{0,8},{4,12},{8,0},{12,4},{16,24},{20,28},{24,16},{28,20},{1,9},{5... | collective-permute-start | bytes 1990664 | tf_op jit(solution)/shard_map/ppermute | solution.py:49
  280.2 41.9 %copy-start.72 = (f32[1152]{0:T(1024)S(1)}, f32[1152]{0:T(1024)}, u32[]{:S(2)}) copy-start(f32[1152]{0:T(1024)} %get-tuple-element.166) | copy-start | bytes 13828
  383.4 20.4 %copy-start.21 = (f32[8,320,1152]{2,1,0:T(8,128)}, f32[8,320,1152]{2,1,0:T(8,128)S(1)}, u32[]{:S(2)}) copy-start(f32[8,320,1152]{2,1,0:T(8,128)S(1)} %shard_map.404) | copy-start | bytes 35389444
  383.4 20.4 %copy-start.89 = (f32[576]{0:T(1024)S(1)}, f32[576]{0:T(1024)}, u32[]{:S(2)}) copy-start(f32[576]{0:T(1024)} %param.43) | copy-start | bytes 6916
  455.0 54.2 %copy-start.54 = (f32[16,1152]{1,0:T(8,128)S(1)}, f32[16,1152]{1,0:T(8,128)}, u32[]{:S(2)}) copy-start(f32[16,1152]{1,0:T(8,128)} %get-tuple-element.158) | copy-start | bytes 221188
  513.1 10.4 slice-start
  516.4 7.1 copy-start.40
  516.4 7.1 slice-start.1
  588.8 34.9 %copy-start.36 = (f32[20,16,1152]{2,1,0:T(8,128)S(1)}, f32[20,16,1152]{2,1,0:T(8,128)}, u32[]{:S(2)}) copy-start(f32[20,16,1152]{2,1,0:T(8,128)} %copy-done.34) | copy-start | bytes 4423684
  623.7 7.0 copy-start.17
  638.4 7.5 copy-start.8
  807.2 6.9 copy-start.22
  807.2 6.9 copy-start.31
  814.1 23.1 %copy-start.5 = (f32[20,16,1152]{2,1,0:T(8,128)S(1)}, f32[20,16,1152]{2,1,0:T(8,128)}, u32[]{:S(2)}) copy-start(f32[20,16,1152]{2,1,0:T(8,128)} %copy-done.2) | copy-start | bytes 4423684
  814.1 23.0 %copy-start.52 = (f32[16,1152]{1,0:T(8,128)S(1)}, f32[16,1152]{1,0:T(8,128)}, u32[]{:S(2)}) copy-start(f32[16,1152]{1,0:T(8,128)} %copy-done.51) | copy-start | bytes 221188
  814.1 23.0 %copy-start.63 = (f32[20,16]{1,0:T(8,128)S(1)}, f32[20,16]{1,0:T(8,128)}, u32[]{:S(2)}) copy-start(f32[20,16]{1,0:T(8,128)} %copy-done.62) | copy-start | bytes 3844
  814.1 23.0 %copy-start.65 = (f32[20,16]{1,0:T(8,128)S(1)}, f32[20,16]{1,0:T(8,128)}, u32[]{:S(2)}) copy-start(f32[20,16]{1,0:T(8,128)} %copy-done.64) | copy-start | bytes 3844
  837.2 19.3 %copy-start.71 = (f32[1152]{0:T(1024)S(1)}, f32[1152]{0:T(1024)}, u32[]{:S(2)}) copy-start(f32[1152]{0:T(1024)} %get-tuple-element.164) | copy-start | bytes 13828
  890.0 263.5 %copy-start.68 = (f32[4,1152]{1,0:T(4,128)S(1)}, f32[4,1152]{1,0:T(4,128)}, u32[]{:S(2)}) copy-start(f32[4,1152]{1,0:T(4,128)} %param.28) | copy-start | bytes 55300
  1170.5 16.8 %copy-start.32 = (f32[5,64,1152]{2,1,0:T(8,128)S(1)}, f32[5,64,1152]{2,1,0:T(8,128)}, u32[]{:S(2)}) copy-start(f32[5,64,1152]{2,1,0:T(8,128)} %copy-done.31) | copy-start | bytes 4423684
  (71 other events, 201.1 us)
Sparse Core Ops, SparseCore 0:
  10.5 105.3 all-gather.3
  178.2 100.5 all-gather.5
  280.6 41.3 all-gather.7
  580.6 268.7 all-reduce.5

commit v8 on v7

--- a/solution.py
+++ b/solution.py
@@ -1,3 +1,4 @@
+import math
 from functools import partial
 
 import jax
@@ -1159,6 +1160,67 @@
     )(queries, b_query.reshape(1, width), kv, b_value.reshape(1, width), probs, attended, grad)
 
 
+MLP_ROWS = 256
+
+
+def mlp_kernel(
+    hidden, cotangent, w_first, b_first, w_second,
+    grad_hidden, out, grad_first, grad_second, grad_bias,
+    first_high, first_low, second_high, second_low,
+):
+    @pl.when(pl.program_id(0) == 0)
+    def _():
+        first_high[...], first_low[...] = halves(w_first[...])
+        second_high[...], second_low[...] = halves(w_second[...])
+        grad_first[...] = jnp.zeros(grad_first.shape, jnp.float32)
+        grad_second[...] = jnp.zeros(grad_second.shape, jnp.float32)
+        grad_bias[...] = jnp.zeros(grad_bias.shape, jnp.float32)
+
+    first = (first_high[...], first_low[...])
+    second = (second_high[...], second_low[...])
+    tokens, upstream = halves(hidden[...]), halves(cotangent[...])
+    u = three(tokens, first, NN) + b_first[...]
+    slope = math.sqrt(2.0 / math.pi)
+    t = jnp.tanh(slope * (u + 0.044715 * (u * u * u)))
+    active = halves(0.5 * u * (1.0 + t))
+    derivative = 0.5 * (1.0 + t) + 0.5 * u * (1.0 - t * t) * slope * (1.0 + 0.134145 * (u * u))
+    grad_pre = three(upstream, second, NT) * derivative
+    grad_bias[...] = grad_bias[...] + jnp.sum(grad_pre, axis=0, keepdims=True)
+    grad_pre = halves(grad_pre)
+    grad_hidden[...] = three(grad_pre, first, NT)
+    out[...] = three(active, second, NN)
+    grad_first[...] = grad_first[...] + three(tokens, grad_pre, TN)
+    grad_second[...] = grad_second[...] + three(active, upstream, TN)
+
+
+def mlp(hidden, cotangent, w_first, b_first, w_second):
+    rows, width = hidden.shape
+    units = w_first.shape[1]
+    f32 = jnp.float32
+    tile = pl.BlockSpec((MLP_ROWS, width), lambda i: (i, 0))
+
+    def fixed(*shape):
+        return pl.BlockSpec(shape, lambda i: (0, 0))
+
+    return pl.pallas_call(
+        mlp_kernel,
+        grid=(rows // MLP_ROWS,),
+        out_shape=(
+            jax.ShapeDtypeStruct((rows, width), f32), jax.ShapeDtypeStruct((rows, width), f32),
+            jax.ShapeDtypeStruct((width, units), f32), jax.ShapeDtypeStruct((units, width), f32),
+            jax.ShapeDtypeStruct((1, units), f32),
+        ),
+        in_specs=[tile, tile, fixed(width, units), fixed(1, units), fixed(units, width)],
+        out_specs=[tile, tile, fixed(width, units), fixed(units, width), fixed(1, units)],
+        scratch_shapes=[
+            pltpu.VMEM((width, units), jnp.bfloat16), pltpu.VMEM((width, units), jnp.bfloat16),
+            pltpu.VMEM((units, width), jnp.bfloat16), pltpu.VMEM((units, width), jnp.bfloat16),
+        ],
+        compiler_params=pltpu.CompilerParams(vmem_limit_bytes=50 << 20),
+        cost_estimate=LIGHT,
+    )(hidden, cotangent, w_first, b_first.reshape(1, units), w_second)
+
+
 def assemble_kernel(axis, dim, *refs):
     blocks, whole = refs[:-1], refs[-1]
     own = lax.axis_index(axis)
@@ -1258,6 +1320,22 @@
     summed = summed.reshape(-1)[: small.shape[0]]
     slots = slots[:, 0, :count].reshape(-1)
     return tokens, later, slots, summed, kv, whole
+
+
+def mlp_part(hidden, cotangent, w_first, b_first, w_second):
+    if small_patch():
+        *parts, grad_bias = mlp(hidden, cotangent, w_first, b_first, w_second)
+        return (*parts, grad_bias[0])
+    pre = matmul(hidden, w_first) + b_first
+    active, pull = jax.vjp(partial(jax.nn.gelu, approximate=True), pre)
+    grad_pre = pull(matmul_nt(cotangent, w_second))[0]
+    return (
+        matmul_nt(grad_pre, w_first),
+        matmul(active, w_second),
+        matmul_tn(hidden, grad_pre),
+        matmul_tn(active, cotangent),
+        jnp.sum(grad_pre, axis=0),
+    )
 
 
 def mid_way(parts, kv, residual, gate, bias):
@@ -1388,10 +1466,10 @@
     hidden_two = (normed_two * (1.0 + scale_two) + shift_two).reshape(rows, width)
 
     hidden_all = gather_tokens(after(hidden_two, w_first))
-    pre_act = matmul(hidden_all, w_first) + fc1_bias
-    activated, gelu_pull = jax.vjp(partial(jax.nn.gelu, approximate=True), pre_act)
-    grad_pre = gelu_pull(matmul_nt(grad_mlp_all, fc2_weight))[0]
-    grad_hidden_two = scatter_tokens(matmul_nt(grad_pre, w_first))
+    grad_parts, mlp_parts, grad_w_first, grad_w_second, grad_b_first = mlp_part(
+        hidden_all, grad_mlp_all, w_first, fc1_bias, fc2_weight
+    )
+    grad_hidden_two = scatter_tokens(grad_parts)
     grad_hidden_two = grad_hidden_two.reshape(slots, cols, width)
     grad_b_second = jnp.sum(grad_mlp, axis=0)
 
@@ -1403,17 +1481,13 @@
     grad_cross_branch = (column_mask * grad_after_cross).reshape(rows, width)
     grad_w_cross_o = matmul_tn(cross_rows, grad_cross_branch)
     grad_b_cross_o = jnp.sum(grad_cross_branch, axis=0)
-    activated, grad_pre = after((activated, grad_pre), grad_w_cross_o)
-    grad_w_first = matmul_tn(hidden_all, grad_pre)
-    grad_w_second = matmul_tn(activated, grad_mlp_all)
-    grad_cross_branch = after(grad_cross_branch, (grad_w_first, grad_w_second))
-    grad_w_first, grad_w_second = lax.psum((grad_w_first, grad_w_second), "frame")
-    grad_b_first = jnp.sum(grad_pre, axis=0)
-    mlp_parts = matmul(activated, fc2_weight)
+    grad_w_first = lax.psum(grad_w_first, "frame")
+    grad_w_second = lax.psum(after(grad_w_second, grad_w_first), "frame")
     grad_cross_rows = matmul_nt(grad_cross_branch, w_cross_o)
     grad_cross_queries, grad_kv = cross_attention_back(
         cross_queries, b_cross_q, caption_kv, b_cross_v, cross_probs, cross_rows, grad_cross_rows
     )
+    grad_cross_queries = after(grad_cross_queries, grad_w_first)
     grad_w_cross_q = matmul_tn(after_attn_rows, grad_cross_queries)
     grad_b_cross_q = jnp.sum(grad_cross_queries, axis=0)
     grad_cross_queries = after(grad_cross_queries, grad_w_cross_q)
@@ -1425,20 +1499,19 @@
     grad_w_attn = matmul_tn(attended_rows, grad_attn_rows)
     grad_b_attn = jnp.sum(grad_attn_rows, axis=0)
     grad_attn_rows = after(grad_attn_rows, grad_w_attn)
+    grad_attended = matmul_nt(grad_attn_rows, w_attn).reshape(slots, cols, width)
+    grad_qkv = frame_attention_back(
+        qkv, b_query, b_value, probs, attended, grad_attended
+    ).reshape(rows, 3 * width)
+    grad_w_qkv = matmul_tn(hidden_one, grad_qkv)
     mlp_sum, grad_kv_share, block_out = mid_way(
-        after(mlp_parts, grad_w_attn), grad_kv, after_cross, column_mask * gate_two, b_second
-    )
-    grad_attn_rows = after(grad_attn_rows, mlp_sum)
+        after(mlp_parts, grad_w_qkv), grad_kv, after_cross, column_mask * gate_two, b_second
+    )
     grad_w_cross_kv = matmul_tn(caption_share, grad_kv_share)
     grad_b_cross_v = jnp.sum(grad_kv_share[:, width:], axis=0)
     grad_caption_share = matmul_nt(cross_kv_weight, grad_kv_share)
     mlp_branch = (mlp_sum + b_second).reshape(slots, cols, width)
     grad_gate_two = jnp.sum(column_mask * mlp_branch * cotangent, axis=0)
-    grad_attended = matmul_nt(grad_attn_rows, w_attn).reshape(slots, cols, width)
-    grad_qkv = frame_attention_back(
-        qkv, b_query, b_value, probs, attended, grad_attended
-    ).reshape(rows, 3 * width)
-    grad_w_qkv = matmul_tn(hidden_one, grad_qkv)
     grad_b_query = jnp.sum(grad_qkv[:, :width], axis=0)
     grad_b_value = jnp.sum(grad_qkv[:, 2 * width :], axis=0)
     grad_hidden_one = matmul_nt(grad_qkv, w_qkv).reshape(slots, cols, width)

time: 1220 us -> 1180 us (0.967)
  matrix products: 256 us -> 126 us
  Pallas kernels: 752 us -> 822 us
  local copies, waits for them, and re-layouts: 71.1 us -> 98.8 us
    pallas_call x0 -> x1, Pallas kernels: none -> 95.7 us  [mlp(): pl.pallas_call(mlp_kernel, grid=(rows // MLP_ROWS,), out_shape=(jax.Shape...]
    dot_general x8 -> x6, matrix products: 92.6 us -> 38.8 us  [matmul_nt(): lax.dot_general(left, right, (((1,), (1,)), ((), ())), precision=BEST)]
    dot_general x8 -> x6, matrix products: 80.1 us -> 38.4 us  [matmul(): return jnp.dot(left, right, precision=BEST)]
    dot_general x8 -> x6, matrix products: 82.1 us -> 47.8 us  [matmul_tn(): lax.dot_general(left, right, (((0,), (0,)), ((), ())), precision=BEST)]
    unnamed x220 -> x166, local copies, waits for them, and re-layouts: 39.8 us -> 56.3 us
  transfers between devices with their start and end apart: 8 -> 9, of which waited for: 6 -> 6; matrix products, arithmetic and copies ran while one was open for 11% -> 12% of each run, Pallas kernels for 31% -> 55%
where the time goes in v8:
time: 1180 us; the launch traced here: 1170 us
  Pallas kernels  822 us (70%)
  matrix products  126 us (11%)
  local copies, waits for them, and re-layouts  98.8 us (8%)
  waiting for transfers between devices  81.6 us (7%)
  other arithmetic  27.4 us (2%)
  between operations  14.9 us (1%)
    pallas_call x1, Pallas kernels, finish(): pl.pallas_call(finish_kernel, out_shape=(shape(rows, 3 * width), shape(ro...  257 us
    pallas_call x1, Pallas kernels, middle(): pl.pallas_call(middle_kernel, out_shape=(jax.ShapeDtypeStruct(block, f32)...  151 us
    pallas_call x1, Pallas kernels, begin(): pl.pallas_call(begin_kernel, out_shape=(jax.ShapeDtypeStruct((4 * count,...  118 us
    pallas_call x1, Pallas kernels, mlp(): pl.pallas_call(mlp_kernel, grid=(rows // MLP_ROWS,), out_shape=(jax.Shape...  95.7 us
    ppermute x4, waiting for transfers between devices, swap(): return lax.ppermute(value, axis, [(i, i ^ bit) for i in range(size)])  59.3 us
    unnamed x166, local copies, waits for them, and re-layouts  56.3 us
    pallas_call x1, Pallas kernels, token_scatter(): pl.pallas_call(token_scatter_kernel, out_shape=jax.ShapeDtypeStruct(block...  54.1 us
    pallas_call x1, Pallas kernels, token_gather(): pl.pallas_call(token_gather_kernel, out_shape=jax.ShapeDtypeStruct((8, le...  52.9 us
  transfers between devices with their start and end apart: 9, of which 6 were waited for; matrix products, arithmetic and copies ran while one was open for 12% of the time, Pallas kernels for 55%

profile of v8, /device:TPU:0, one launch (start us, length us, event | category | flops | bytes accessed | tf_op | source)
XLA Modules:
  0.0 1174.8 jit_solution(2244360114572221475)
XLA Ops:
  39.6 117.8 %shard_map.400 = (f32[20,16,1152]{2,1,0:T(8,128)S(1)}, f32[20,16,1152]{2,1,0:T(8,128)S(1)}, f32[4,8,128]{2,1,0:T(8,128)S(1)}, f32[336,128]{1,0:T(8,128)S(1)}, f3...) custom-call(f32[5,64,1152]{2,1,0:T(8,128)S(1)} %copy-done.28, f32[5,64,1152]{2,1,0:T(8,128)S(1)} %copy-done.29, ...), custom_call_target="tpu_custom_call" | custom-call | bytes 65536 | tf_op jit(solution)/shard_map/pallas_call | solution.py:406
  167.3 15.4 %fusion.38 = f32[320,3456]{1,0:T(8,128)} fusion(f32[320,1152]{1,0:T(8,128)S(1)} %bitcast.152, f32[1152,3456]{1,0:T(8,128)} %get-tuple-element.61), kind=kOutput, calls=%fused_computation.154 | convolution fusion | flops 7644119040 | bytes 21823488 | tf_op jit(solution)/shard_map/dot_general | solution.py:23
  186.7 9.2 shard_map.401
  199.3 6.7 fusion.10
  207.1 5.0 fusion.4.queries
  224.7 30.5 %collective-permute-done.3 = f32[288,576]{1,0:T(8,128)} collective-permute-done((f32[288,576]{1,0:T(8,128)}, f32[288,576]{1,0:T(8,128)}, u32[]{:S(2)}, u32[]{:S(2)}) %collective-permute-start.3) | collective-permute-done | bytes 663584 | tf_op jit(solution)/shard_map/ppermute | solution.py:50
  256.3 15.0 %collective-permute-done.2 = f32[288,576]{1,0:T(8,128)} collective-permute-done((f32[288,576]{1,0:T(8,128)}, f32[288,576]{1,0:T(8,128)}, u32[]{:S(2)}, u32[]{:S(2)}) %collective-permute-start.2) | collective-permute-done | bytes 663584 | tf_op jit(solution)/shard_map/ppermute | solution.py:50
  272.5 10.9 collective-permute-done.1
  287.1 19.6 %shard_map.402 = (f32[16,320,480]{2,1,0:T(8,128)}, f32[320,1152]{1,0:T(8,128)S(1)}) custom-call(f32[320,1152]{1,0:T(8,128)S(1)} %copy-done.17, f32[1,1152]{1,0:T(1,128)S(1)} %get-tuple-element.184.b_query, f32[480,2304]{1,0:T(8,128)} %copy-done.13, f32[1,1152]{1,0:T(1,128)S(1)} %get-tuple-element.183.b_value, f32[320,480]{1,0:T(8,128)S(1)} %bitcast.132), custom_call_target="tpu_custom_call" | custom-call | bytes 65536 | tf_op jit(solution)/shard_map/pallas_call | solution.py:1091
  307.7 21.2 %all-gather.8.cloned.1.call-done = f32[1152,1152]{1,0:T(8,128)} async-done(((f32[144,1152]{1,0:T(8,128)}), f32[1152,1152]{1,0:T(8,128)}) %all-gather.8.cloned.1.call-update) | async-done | bytes 5308432 | tf_op jit(solution)/shard_map/all_gather | solution.py:1249
  328.9 6.6 convolution_add_fusion
  337.0 52.9 %shard_map.404 = f32[8,320,1152]{2,1,0:T(8,128)S(1)} custom-call(f32[320,1152]{1,0:T(8,128)S(1)} %bitcast.129), custom_call_target="tpu_custom_call" | custom-call | bytes 65536 | tf_op jit(solution)/shard_map/pallas_call | solution.py:148
  389.9 4.2 copy-done.9
  394.2 95.7 %shard_map.405 = (f32[2560,1152]{1,0:T(8,128)}, f32[2560,1152]{1,0:T(8,128)}, f32[1152,576]{1,0:T(8,128)}, f32[576,1152]{1,0:T(8,128)S(1)}, f32[1,576]{1,0:T(1,128)S(1)}) custom-call(f32[2560,1152]{1,0:T(8,128)} %bitcast.123, f32[2560,1152]{1,0:T(8,128)} %all-gather.6.cloned.1.call-done.cotangent, f32[1152,576]{1,0:T(8,128)} %copy-done.21, ...), custom_call_target="tpu_custom_call" | custom-call | bytes 65536 | tf_op jit(solution)/shard_map/pallas_call | solution.py:1205
  491.5 4.3 copy-done.22
  495.9 54.1 %shard_map.406 = f32[320,1152]{1,0:T(8,128)S(1)} custom-call(f32[8,320,1152]{2,1,0:T(8,128)S(1)} %bitcast.128), custom_call_target="tpu_custom_call" | custom-call | bytes 65536 | tf_op jit(solution)/shard_map/pallas_call | solution.py:212
  558.2 7.6 fusion.39.grad
  565.9 34.6 %shard_map.407 = (f32[320,1152]{1,0:T(8,128)S(1)}, f32[480,2304]{1,0:T(8,128)}) custom-call(f32[320,1152]{1,0:T(8,128)} %fusion.4.queries, f32[1,1152]{1,0:T(1,128)S(1)} %get-tuple-element.184.b_query, f32[480,2304]{1,0:T(8,128)} %copy-done.13, f32[1,1152]{1,0:T(1,128)S(1)} %get-tuple-element.183.b_value, f32[16,320,480]{2,1,0:T(8,128)} %get-tuple-element.74.probs, ...), custom_call_target="tpu_custom_call" | custom-call | bytes 65536 | tf_op jit(solution)/shard_map/pallas_call | solution.py:1149
  602.3 8.8 fusion.41.cross_o
  611.1 8.9 fusion.40.cross_q
  620.0 6.2 fusion.2
  628.1 7.1 convolution_bitcast_fusion.1.attn
  638.9 23.3 %shard_map.408 = f32[20,16,3456]{2,1,0:T(8,128)} custom-call(f32[20,16,3456]{2,1,0:T(8,128)} %bitcast.124, f32[1,1152]{1,0:T(1,128)S(1)} %get-tuple-element.186.b_query, f32[1,1152]{1,0:T(1,128)S(1)} %get-tuple-element.185.b_value, f32[16,2,160,160]{3,2,1,0:T(8,128)} %copy-done.25, f32[20,16,1152]{2,1,0:T(8,128)S(1)} %copy-done.24, f32[20,16,1152]{2,1,0:T(8,128)S(1)} %bitcast.131), custom_call_target="tpu_custom_call" | custom-call | bytes 65536 | tf_op jit(solution)/shard_map/pallas_call | solution.py:1050
  662.1 15.6 %multiply_reduce_fusion.3 = (f32[16,1152]{1,0:T(8,128)S(1)}, f32[20,16]{1,0:T(8,128)S(1)}, f32[20,16]{1,0:T(8,128)S(1)}, f32[16,1152]{1,0:T(8,128)S(1)}, f32[20,16,1152]{2,1,0:T(8,128)}) fusion(f32[20,16,1152]{2,1,0:T(8,128)S(1)} %copy-done.4, f32[20,16]{1,0:T(8,128)S(1)} %add_rsqrt_fusion.1, f32[20,16]{1,0:T(8,128)S(1)} %broadcast_multiply_fusion.7, ...), kind=kOutput, calls=%fused_computation.20 | convolution fusion | flops 7647399424 | bytes 23524352 | tf_op jit(solution)/shard_map/dot_general | solution.py:27
  677.7 16.7 %convolution_bitcast_fusion.first = f32[1152,3456]{1,0:T(8,128)} fusion(f32[20,16,1152]{2,1,0:T(8,128)S(1)} %copy-done.42, f32[20,16,3456]{2,1,0:T(8,128)S(1)} %copy-done.32), kind=kOutput, calls=%fused_computation | convolution fusion | flops 7644119040 | bytes 21823488 | tf_op jit(solution)/shard_map/dot_general | solution.py:31
  695.9 150.9 %shard_map.409 = (f32[320,1152]{1,0:T(8,128)S(1)}, f32[120,2304]{1,0:T(8,128)S(1)}, f32[5,64,1152]{2,1,0:T(8,128)S(1)}) custom-call(f32[8,320,1152]{2,1,0:T(8,128)} %bitcast.144, f32[480,2304]{1,0:T(8,128)} %get-tuple-element.81.kv, f32[20,16,1152]{2,1,0:T(8,128)S(1)} %copy-done.8, f32[1,16,1152]{2,1,0:T(8,128)S(1)} %bitcast.133, f32[1,1152]{1,0:T(1,128)S(1)} %bitcast.134), custom_call_target="tpu_custom_call" | custom-call | bytes 65536 | tf_op jit(solution)/shard_map/pallas_call | solution.py:846
  861.2 257.3 %shard_map.410 = (f32[144,3456]{1,0:T(8,128)}, f32[144,1152]{1,0:T(8,128)}, f32[144,1152]{1,0:T(8,128)}, f32[144,1152]{1,0:T(8,128)}, f32[144,2304]{1,0:T(8,128)...) custom-call(f32[1152,3456]{1,0:T(8,128)} %convolution_bitcast_fusion.first,, ...), custom_call_target="tpu_custom_call" | custom-call | bytes 65536 | tf_op jit(solution)/shard_map/pallas_call | solution.py:714
  1118.6 4.4 copy.56
  1123.0 4.1 reshape.352
  1133.4 4.4 fusion.42.block
  1137.8 6.3 shard_map.411
  1150.9 4.6 fusion.29
  (300 shorter events, 130.1 us)
Async XLA Ops:
  7.2 29.0 %copy-start = (f32[4,120,1152]{2,1,0:T(8,128)S(1)}, f32[4,120,1152]{2,1,0:T(8,128)}, u32[]{:S(2)}) copy-start(f32[4,120,1152]{2,1,0:T(8,128)} %param.27) | copy-start | bytes 6635524
  7.2 192.0 %all-gather.4.cloned.1.call-start = ((), (), s32[]{:S(2)}) async-start(), calls=%async_computation | async-start | bytes 11943936 | tf_op jit(solution)/shard_map/all_gather | solution.py:1249
  9.9 275.7 %all-gather.6.cloned.1.call-start = ((), (), s32[]{:S(2)}) async-start(), calls=%async_computation.1 | async-start | bytes 13271040 | tf_op jit(solution)/shard_map/all_gather | solution.py:1249
  10.6 5.6 copy-start.62
  10.6 6.1 copy-start.61
  10.6 25.6 %copy-start.43 = (f32[144,2304]{1,0:T(8,128)S(1)}, f32[144,2304]{1,0:T(8,128)}, u32[]{:S(2)}) copy-start(f32[144,2304]{1,0:T(8,128)} %param.38) | copy-start | bytes 3981316
  167.3 15.4 %copy-start.41 = (f32[20,16,1152]{2,1,0:T(8,128)}, f32[20,16,1152]{2,1,0:T(8,128)S(1)}, u32[]{:S(2)}) copy-start(f32[20,16,1152]{2,1,0:T(8,128)S(1)} %get-tuple-element.182) | copy-start | bytes 4423684
  182.8 146.2 %all-gather.8.cloned.1.call-start = ((), (), s32[]{:S(2)}) async-start(), calls=%async_computation.2 | async-start | bytes 5971968 | tf_op jit(solution)/shard_map/all_gather | solution.py:1249
  183.5 427.6 %all-reduce.6.cloned.1.call-start = ((), (), s32[]{:S(2)}) async-start(), calls=%async_computation.3 | async-start | bytes 5898240 | tf_op jit(solution)/shard_map/psum | solution.py:1484
  199.3 6.7 copy-start.3
  199.3 7.8 copy-start.31
  207.1 5.0 copy-start.33
  207.1 5.0 copy-start.45
  213.7 3.4 collective-permute-start
  218.8 36.4 %collective-permute-start.3 = (f32[288,576]{1,0:T(8,128)}, f32[288,576]{1,0:T(8,128)}, u32[]{:S(2)}, u32[]{:S(2)}) collective-permute-start(f32[288,576]{1,0:T(8,128)} %pad_maximum_fusion.4), channel_id=1, source_target_pairs={{0,24},{4,28},{8,16},{12,20},{16,8},{20,12},{24,0},{28,4},{1,25},{... | collective-permute-start | bytes 1990664 | tf_op jit(solution)/shard_map/ppermute | solution.py:50
  221.2 50.1 %collective-permute-start.2 = (f32[288,576]{1,0:T(8,128)}, f32[288,576]{1,0:T(8,128)}, u32[]{:S(2)}, u32[]{:S(2)}) collective-permute-start(f32[288,576]{1,0:T(8,128)} %pad_maximum_fusion.3), channel_id=1, source_target_pairs={{0,16},{4,20},{8,24},{12,28},{16,0},{20,4},{24,8},{28,12},{1,17},{... | collective-permute-start | bytes 1990664 | tf_op jit(solution)/shard_map/ppermute | solution.py:50
  224.0 59.4 %collective-permute-start.1 = (f32[288,576]{1,0:T(8,128)S(1)}, f32[288,576]{1,0:T(8,128)S(1)}, u32[]{:S(2)}, u32[]{:S(2)}) collective-permute-start(f32[288,576]{1,0:T(8,128)S(1)} %pad_maximum_fusion.2), channel_id=1, source_target_pairs={{0,8},{4,12},{8,0},{12,4},{16,24},{20,28},{24,16},{28,20},{1,9},{5... | collective-permute-start | bytes 1990664 | tf_op jit(solution)/shard_map/ppermute | solution.py:50
  328.9 6.6 copy-start.34
  491.5 664.6 %all-reduce.8.cloned.1.call-start = ((), (), s32[]{:S(2)}) async-start(), calls=%async_computation.4 | async-start | bytes 5308416 | tf_op jit(solution)/shard_map/psum | solution.py:1485
  558.2 7.6 copy-start.37
  611.1 8.9 copy-start.19
  620.0 6.2 copy-start.40
  626.3 8.9 slice-start
  628.1 7.1 slice-start.1
  628.1 7.1 slice-start.2
  638.9 23.3 %copy-start.4 = (f32[20,16,1152]{2,1,0:T(8,128)S(1)}, f32[20,16,1152]{2,1,0:T(8,128)}, u32[]{:S(2)}) copy-start(f32[20,16,1152]{2,1,0:T(8,128)} %copy-done.1) | copy-start | bytes 4423684
  662.1 15.6 %copy-start.32 = (f32[20,16,3456]{2,1,0:T(8,128)S(1)}, f32[20,16,3456]{2,1,0:T(8,128)}, u32[]{:S(2)}) copy-start(f32[20,16,3456]{2,1,0:T(8,128)} %shard_map.408) | copy-start | bytes 13271044
  662.1 15.6 %copy-start.42 = (f32[20,16,1152]{2,1,0:T(8,128)S(1)}, f32[20,16,1152]{2,1,0:T(8,128)}, u32[]{:S(2)}) copy-start(f32[20,16,1152]{2,1,0:T(8,128)} %copy-done.41) | copy-start | bytes 4423684
  695.9 152.0 %copy-start.36 = (f32[320,1152]{1,0:T(8,128)S(1)}, f32[320,1152]{1,0:T(8,128)}, u32[]{:S(2)}) copy-start(f32[320,1152]{1,0:T(8,128)} %copy-done.35) | copy-start | bytes 4423684
  695.9 152.0 %copy-start.38 = (f32[20,16,1152]{2,1,0:T(8,128)S(1)}, f32[20,16,1152]{2,1,0:T(8,128)}, u32[]{:S(2)}) copy-start(f32[20,16,1152]{2,1,0:T(8,128)} %get-tuple-element.181) | copy-start | bytes 4423684
  695.9 152.0 %copy-start.39 = (f32[20,16,1152]{2,1,0:T(8,128)S(1)}, f32[20,16,1152]{2,1,0:T(8,128)}, u32[]{:S(2)}) copy-start(f32[20,16,1152]{2,1,0:T(8,128)} %get-tuple-element.136) | copy-start | bytes 4423684
  1133.4 17.4 %copy-start.57 = (f32[4,1152]{1,0:T(4,128)S(1)}, f32[4,1152]{1,0:T(4,128)}, u32[]{:S(2)}) copy-start(f32[4,1152]{1,0:T(4,128)} %param.28) | copy-start | bytes 55300
  (45 other events, 92.0 us)
Sparse Core Ops, SparseCore 0:
  10.5 92.7 all-gather.3
  182.9 102.6 all-gather.5
  287.5 41.3 all-gather.7
  491.6 114.7 all-reduce.5
  694.6 173.3 all-reduce.7

commit v9 on v8

--- a/solution.py
+++ b/solution.py
@@ -428,7 +428,7 @@
     )(tokens, later, slots, small, kv, weight)
 
 
-UNITS = 6
+UNITS = 3
 
 
 def finish_kernel(
@@ -500,12 +500,12 @@
     def piece(ref, u):
         return ref.at[:, pl.ds(u * width, width)]
 
-    outs = [piece(first_out, u) for u in range(3)] + [attn_out, cross_q_out, cross_o_out]
+    pairs = [(kept.at[u, 0], piece(first_out, u)) for u in range(UNITS)]
+    pairs += [(attn, attn_out), (cross_q, cross_q_out), (cross_o, cross_o_out)]
+    pairs += [(piece(kv, u), piece(kv_out, u)) for u in range(2)]
     steps = [
-        frame_steps(kept.at[u, 0], outs[u], along_z.at[u], across_z.at[u]) for u in range(UNITS)
-    ] + [
-        frame_steps(piece(kv, u), piece(kv_out, u), along_z.at[UNITS + u], across_z.at[UNITS + u])
-        for u in range(2)
+        frame_steps(value, result, along_z.at[i], across_z.at[i])
+        for i, (value, result) in enumerate(pairs)
     ]
     small_steps = frame_steps(small_sums.at[2], small_out, small_z.at[0], small_z.at[1])
 
@@ -514,8 +514,7 @@
 
     def source(u, device, j):
         start = pl.multiple_of((device ^ (2 * j)) * rows, rows)
-        ref = first if u < 3 else (attn, cross_q, cross_o)[u - 3]
-        return ref.at[pl.ds(start, rows), pl.ds((u % 3) * width if u < 3 else 0, width)]
+        return first.at[pl.ds(start, rows), pl.ds(u * width, width)]
 
     def load(u, j):
         return pltpu.make_async_copy(source(u, me, j), kept.at[u, j], load_sems.at[u, j])
@@ -633,8 +632,8 @@
     for u in range(UNITS):
         for j in (3, 2, 1, 0):
             load(u, j).start()
-    steps[6][0]()
-    steps[7][0]()
+    for i in (6, 7, 3, 4, 5):
+        steps[i][0]()
     for u in range(2):
         to_core(u)
     links.wait(small_got.at[0], small_at[0], core)
@@ -649,48 +648,37 @@
     links.wait(small_got.at[2], small_at[2], y)
     small_sums[2] = small_sums[1] + small_got[2]
     small_steps[0]()
-    stage_one(2)
     steps[6][1]()
     steps[7][1]()
-    send_tokens(0)
-    send_tokens(1)
+    stage_one(2)
+    stage_three(0)
+    steps[3][1]()
     stage_two(1)
-    stage_three(0)
-    stage_one(3)
     steps[6][2]()
     steps[7][2]()
-    small_steps[1]()
-    send_tokens(2)
+    steps[4][1]()
     stage_two(2)
     stage_three(1)
-    stage_one(4)
-    steps[0][1]()
-    small_steps[2]()
-    send_tokens(3)
-    stage_two(3)
-    stage_three(2)
-    stage_one(5)
-    steps[1][1]()
-    steps[0][2]()
-    stage_two(4)
-    stage_three(3)
-    stage_two(5)
     caption_x()
     for k in (2, 4, 6):
         send_columns(k)
+    steps[3][2]()
+    steps[5][1]()
+    small_steps[1]()
+    stage_three(2)
+    for k in range(4):
+        send_tokens(k)
+    steps[4][2]()
+    small_steps[2]()
+    steps[0][1]()
+    caption_y()
+    steps[5][2]()
+    steps[1][1]()
+    steps[0][2]()
+    caption_core()
     steps[2][1]()
     steps[1][2]()
-    stage_three(4)
-    caption_y()
-    steps[3][1]()
     steps[2][2]()
-    stage_three(5)
-    caption_core()
-    steps[4][1]()
-    steps[3][2]()
-    steps[5][1]()
-    steps[4][2]()
-    steps[5][2]()
     for step in steps + [small_steps]:
         step[3]()
     columns_over()
@@ -703,7 +691,7 @@
 
 
 def finish(first, attn, cross_q, cross_o, kv, tokens, small, caption, columns):
-    rows, width = first.shape[0] // 8, first.shape[1] // 3
+    rows, width = attn.shape
     count, part = tokens.shape[0] // 4, tokens.shape[1]
     f32, vmem = jnp.float32, pl.BlockSpec(memory_space=pltpu.VMEM)
     hbm = pl.BlockSpec(memory_space=pl.ANY)
@@ -718,7 +706,7 @@
             shape(rows, 2 * width), shape(count, 4 * part, tokens.shape[2]), shape(*small.shape),
             shape(8, 4, *caption.shape), shape(8, columns.shape[0] // 8, columns.shape[1]),
         ),
-        in_specs=[hbm] * 4 + [vmem] * 4 + [hbm],
+        in_specs=[hbm] + [vmem] * 7 + [hbm],
         out_specs=[vmem] * 8 + [hbm],
         scratch_shapes=[
             pltpu.VMEM((4, columns.shape[0] // 4, columns.shape[1]), f32),
@@ -726,10 +714,10 @@
             pltpu.VMEM((UNITS, 4, rows, width), f32), pltpu.VMEM((2, 4, rows, width), f32),
             pltpu.VMEM((UNITS, rows // 2, width), f32), pltpu.VMEM((UNITS, rows // 2, width), f32),
             pltpu.VMEM((UNITS, rows, width), f32), pltpu.VMEM((UNITS, rows, width), f32),
-            pltpu.VMEM((UNITS + 2, rows, width), f32), pltpu.VMEM((UNITS + 2, rows, width), f32),
+            pltpu.VMEM((8, rows, width), f32), pltpu.VMEM((8, rows, width), f32),
             pltpu.VMEM((3,) + small.shape, f32), pltpu.VMEM((3,) + small.shape, f32),
             pltpu.VMEM((2,) + small.shape, f32),
-            pltpu.SemaphoreType.DMA((UNITS, 4)), pltpu.SemaphoreType.REGULAR((4,)),
+            pltpu.SemaphoreType.DMA((UNITS, 4)), pltpu.SemaphoreType.REGULAR((1,)),
             pltpu.SemaphoreType.DMA((112,)), pltpu.SemaphoreType.DMA((112,)),
         ],
         compiler_params=pltpu.CompilerParams(
@@ -740,8 +728,9 @@
 
 
 def middle_kernel(
-    parts, kv, residual, gate, bias,
-    total, kv_out, block_out,
+    parts, kv, residual, gate, bias, attn, cross_q, cross_o,
+    total, kv_out, block_out, attn_out, cross_q_out, cross_o_out,
+    w_kept, w_theirs, w_by_x, w_by_y, w_from_x, w_from_y, w_loads, credit, kv_sem,
     block, kept, theirs, by_x, by_y, from_x, from_y,
     kv_half, kv_core, kv_got, kv_1, kv_2, kv_got_1, kv_got_2,
     load_sems, send_sems, recv_sems,
@@ -759,8 +748,64 @@
     def share(ref, k):
         return ref.at[pl.ds(pl.multiple_of((z ^ k) * rows, rows), rows)]
 
+    grads, sums = (attn, cross_q, cross_o), (attn_out, cross_q_out, cross_o_out)
+    length = attn_out.shape[0]
+    top_rows, low_rows = pl.ds(0, length // 2), pl.ds(length // 2, length // 2)
+    w_core_at = [[links.plan() for _ in range(4)] for _ in grads]
+    w_at = [[links.plan() for _ in range(6)] for _ in grads]
+
+    def w_source(u, device, j):
+        start = pl.multiple_of((device ^ (2 * j)) * length, length)
+        return grads[u].at[pl.ds(start, length)]
+
+    def w_load(u, j):
+        return pltpu.make_async_copy(w_source(u, me, j), w_kept.at[u, j], w_loads.at[u, j])
+
+    def w_to_core(u):
+        if u >= 2:
+            pl.semaphore_wait(credit.at[u - 2], 1)
+        for j in (3, 2, 1, 0):
+            links.send(w_source(u, me ^ 1, j), w_theirs.at[u % 2, j], w_core_at[u][j], core)
+
+    def w_add(u, j):
+        w_load(u, j).wait()
+        links.wait(w_theirs.at[u % 2, j], w_core_at[u][j], core)
+        w_kept[u, j] = w_kept[u, j] + w_theirs[u % 2, j]
+
+    def w_one(u):
+        w_add(u, 3)
+        links.send(w_kept.at[u, 3, top_rows], w_by_x.at[u], w_at[u][0], x)
+        links.send(w_kept.at[u, 3, low_rows], w_by_y.at[u], w_at[u][1], y)
+        w_add(u, 2)
+        links.send(w_kept.at[u, 2, low_rows], w_from_y.at[u, low_rows], w_at[u][2], y)
+        w_add(u, 1)
+        links.send(w_kept.at[u, 1, top_rows], w_from_x.at[u, top_rows], w_at[u][3], x)
+        w_add(u, 0)
+        if u == 0:
+            pl.semaphore_signal(
+                credit.at[u], inc=1, device_id=core, device_id_type=pl.DeviceIdType.MESH
+            )
+            w_to_core(2)
+
+    def w_two(u):
+        links.wait(w_by_x.at[u], w_at[u][0], x)
+        w_kept[u, 2, top_rows] = w_kept[u, 2, top_rows] + w_by_x[u]
+        links.send(w_kept.at[u, 2, top_rows], w_from_y.at[u, top_rows], w_at[u][4], y)
+        links.wait(w_by_y.at[u], w_at[u][1], y)
+        w_kept[u, 1, low_rows] = w_kept[u, 1, low_rows] + w_by_y[u]
+        links.send(w_kept.at[u, 1, low_rows], w_from_x.at[u, low_rows], w_at[u][5], x)
+
+    def w_three(u):
+        links.wait(w_from_y.at[u, low_rows], w_at[u][2], y)
+        links.wait(w_from_x.at[u, top_rows], w_at[u][3], x)
+        links.wait(w_from_y.at[u, top_rows], w_at[u][4], y)
+        links.wait(w_from_x.at[u, low_rows], w_at[u][5], x)
+        sums[u][...] = w_kept[u, 0] + w_from_x[u] + w_from_y[u]
+
     at_kv = links.plan()
     links.send(kv.at[:, others], kv_core, at_kv, core)
+    kv_load = pltpu.make_async_copy(kv.at[:, mine], kv_half, kv_sem)
+    kv_load.start()
     core_at = [links.plan() for _ in range(4)]
     loads = [
         pltpu.make_async_copy(parts.at[me ^ (2 * j)], kept.at[j], load_sems.at[j])
@@ -769,8 +814,14 @@
     for j in (3, 2, 1, 0):
         links.send(parts.at[me ^ 1 ^ (2 * j)], theirs.at[j], core_at[j], core)
         loads[j].start()
+    for u in range(3):
+        for j in (3, 2, 1, 0):
+            w_load(u, j).start()
+    for u in range(2):
+        w_to_core(u)
+    kv_load.wait()
     links.wait(kv_core, at_kv, core)
-    kv_half[...] = kv[:, mine] + kv_core[...]
+    kv_half[...] = kv_half[...] + kv_core[...]
     kv_at = [None] + [links.plan() for _ in range(3)]
     for k in (1, 2, 3):
         links.send(share(kv_half, k), kv_got.at[k - 1], kv_at[k], frames[k])
@@ -799,13 +850,7 @@
     kept[1, lower] = kept[1, lower] + by_y[...]
     links.send(kept.at[1, lower], from_x.at[lower], at[5], x)
 
-    for k in (1, 2, 3):
-        links.wait(kv_got.at[k - 1], kv_at[k], frames[k])
-    kv_1[...] = share(kv_half, 0)[...] + kv_got[0] + (kv_got[1] + kv_got[2])
-    top, bottom = pl.ds(0, 64), pl.ds(64, rows - 64)
-    at_u, at_l = links.plan(), links.plan()
-    links.send(kv_1.at[top], kv_got_1.at[top], at_u, x)
-    links.send(kv_1.at[bottom], kv_got_1.at[bottom], at_l, y)
+    w_one(0)
     links.wait(from_y.at[lower], at[2], y)
     links.wait(from_x.at[upper], at[3], x)
     links.wait(from_y.at[upper], at[4], y)
@@ -819,6 +864,18 @@
         source = block.at[pl.ds((z ^ k) * slots, slots)]
         links.send(source, block_out.at[:, place], block_at[k], frames[k])
     block_out[:, place] = block[pl.ds(z * slots, slots)]
+    w_one(1)
+    w_two(0)
+    for k in (1, 2, 3):
+        links.wait(kv_got.at[k - 1], kv_at[k], frames[k])
+    kv_1[...] = share(kv_half, 0)[...] + kv_got[0] + (kv_got[1] + kv_got[2])
+    top, bottom = pl.ds(0, 64), pl.ds(64, rows - 64)
+    at_u, at_l = links.plan(), links.plan()
+    links.send(kv_1.at[top], kv_got_1.at[top], at_u, x)
+    links.send(kv_1.at[bottom], kv_got_1.at[bottom], at_l, y)
+    w_one(2)
+    w_two(1)
+    w_three(0)
     links.wait(kv_got_1.at[top], at_u, x)
     links.wait(kv_got_1.at[bottom], at_l, y)
     kv_2[...] = kv_1[...] + kv_got_1[...]
@@ -830,6 +887,9 @@
     kv_out[:, mine] = kv_2[...] + kv_got_2[...]
     at_core = links.plan()
     links.send(kv_out.at[:, mine], kv_out.at[:, mine], at_core, core)
+    w_two(2)
+    w_three(1)
+    w_three(2)
     links.wait(kv_out.at[:, others], at_core, core)
     for k in (1, 2, 3):
         there = pl.ds(pl.multiple_of((z ^ k) * part, part), part)
@@ -837,35 +897,43 @@
     links.drain()
 
 
-def middle(parts, kv, residual, gate, bias):
+def middle(parts, kv, residual, gate, bias, attn, cross_q, cross_o):
     slots, cols, _ = residual.shape
+    count = attn.shape[0] // 8
     length, width = parts.shape[0] // 8, parts.shape[1]
     rows = kv.shape[0] // 4
     f32, vmem = jnp.float32, pl.BlockSpec(memory_space=pltpu.VMEM)
+    hbm = pl.BlockSpec(memory_space=pl.ANY)
     block, half = (length, width), pltpu.VMEM((rows, width), f32)
     return pl.pallas_call(
         middle_kernel,
         out_shape=(
             jax.ShapeDtypeStruct(block, f32), jax.ShapeDtypeStruct((rows, 2 * width), f32),
             jax.ShapeDtypeStruct((slots // 4, 4 * cols, width), f32),
+            *[jax.ShapeDtypeStruct((count, width), f32)] * 3,
         ),
-        in_specs=[pl.BlockSpec(memory_space=pl.ANY)] + [vmem] * 4,
-        out_specs=[vmem] * 3,
+        in_specs=[hbm] * 2 + [vmem] * 3 + [hbm] * 3,
+        out_specs=[vmem] * 6,
         scratch_shapes=[
+            pltpu.VMEM((3, 4, count, width), f32), pltpu.VMEM((2, 4, count, width), f32),
+            pltpu.VMEM((3, count // 2, width), f32), pltpu.VMEM((3, count // 2, width), f32),
+            pltpu.VMEM((3, count, width), f32), pltpu.VMEM((3, count, width), f32),
+            pltpu.SemaphoreType.DMA((3, 4)), pltpu.SemaphoreType.REGULAR((1,)),
+            pltpu.SemaphoreType.DMA,
             pltpu.VMEM((slots, cols, width), f32),
             pltpu.VMEM((4,) + block, f32), pltpu.VMEM((4,) + block, f32),
             pltpu.VMEM((length // 2, width), f32), pltpu.VMEM((length // 2, width), f32),
             pltpu.VMEM(block, f32), pltpu.VMEM(block, f32),
             pltpu.VMEM((4 * rows, width), f32), pltpu.VMEM((4 * rows, width), f32),
             pltpu.VMEM((3, rows, width), f32), half, half, half, half,
-            pltpu.SemaphoreType.DMA((4,)), pltpu.SemaphoreType.DMA((24,)),
-            pltpu.SemaphoreType.DMA((24,)),
+            pltpu.SemaphoreType.DMA((4,)), pltpu.SemaphoreType.DMA((56,)),
+            pltpu.SemaphoreType.DMA((56,)),
         ],
         compiler_params=pltpu.CompilerParams(
-            collective_id=4, has_side_effects=True, vmem_limit_bytes=48 << 20
+            collective_id=4, has_side_effects=True, vmem_limit_bytes=58 << 20
         ),
         cost_estimate=LIGHT,
-    )(parts.reshape((8,) + block), kv, residual, gate[None], bias[None])
+    )(parts.reshape((8,) + block), kv, residual, gate[None], bias[None], attn, cross_q, cross_o)
 
 
 def spread_kernel(block, whole, send_sems, recv_sems):
@@ -1338,19 +1406,21 @@
     )
 
 
-def mid_way(parts, kv, residual, gate, bias):
+def mid_way(parts, kv, residual, gate, bias, weights):
     if not small_patch():
         kv = lax.psum_scatter(all_sum(kv, "patch"), "frame", scatter_dimension=0, tiled=True)
         total = scatter_rows(parts)
         block = residual + gate * (total + bias).reshape(residual.shape)
-        return total, kv, to_slots(block)
-    return middle(parts, kv, residual, gate, bias)
+        return total, kv, to_slots(block), [scatter_rows(w) for w in weights]
+    total, kv, block, *weights = middle(parts, kv, residual, gate, bias, *weights)
+    return total, kv, block, weights
 
 
 def close_up(weights, kv, tokens, small, caption, columns):
     clips, length = lax.axis_size("frame"), caption.shape[1]
     if not small_patch():
-        weights = [lax.psum(scatter_rows(w), "frame") for w in weights]
+        weights = [scatter_rows(weights[0]), *weights[1:]]
+        weights = [lax.psum(w, "frame") for w in weights]
         whole = lax.all_gather(caption, "patch", axis=0, tiled=True)
         whole = lax.all_gather(whole, "frame", axis=0)
         whole = jnp.transpose(whole, (0, 2, 1))
@@ -1504,8 +1574,13 @@
         qkv, b_query, b_value, probs, attended, grad_attended
     ).reshape(rows, 3 * width)
     grad_w_qkv = matmul_tn(hidden_one, grad_qkv)
-    mlp_sum, grad_kv_share, block_out = mid_way(
-        after(mlp_parts, grad_w_qkv), grad_kv, after_cross, column_mask * gate_two, b_second
+    mlp_sum, grad_kv_share, block_out, shares = mid_way(
+        after(mlp_parts, grad_w_qkv),
+        grad_kv,
+        after_cross,
+        column_mask * gate_two,
+        b_second,
+        (grad_w_attn, grad_w_cross_q, grad_w_cross_o),
     )
     grad_w_cross_kv = matmul_tn(caption_share, grad_kv_share)
     grad_b_cross_v = jnp.sum(grad_kv_share[:, width:], axis=0)
@@ -1548,7 +1623,7 @@
         [grad_modulation_part.reshape(-1)] + list(bias_grads) + [placed(grad_b_first, "patch")]
     )
     weights, grad_w_cross_kv, input_grad, small_grads, grad_caption, grad_w_first = close_up(
-        (grad_w_qkv, grad_w_attn, grad_w_cross_q, grad_w_cross_o),
+        (grad_w_qkv, *shares),
         grad_w_cross_kv, input_grad, small_grads, grad_caption_share, grad_w_first,
     )
     place = grad_modulation_part.size

time: 1180 us -> 1140 us (0.966)
  Pallas kernels: 822 us -> 779 us
    pallas_call x1, Pallas kernels: 257 us -> 223 us  [finish(): pl.pallas_call(finish_kernel, out_shape=(shape(rows, 3 * width), shape(ro...]
    unnamed x166 -> x178, local copies, waits for them, and re-layouts: 56.3 us -> 54.5 us
  transfers between devices with their start and end apart: 9 -> 9, of which waited for: 6 -> 6; matrix products, arithmetic and copies ran while one was open for 12% -> 12% of each run, Pallas kernels for 55% -> 54%
where the time goes in v9:
time: 1140 us; the launch traced here: 1130 us
  Pallas kernels  779 us (68%)
  matrix products  126 us (11%)
  local copies, waits for them, and re-layouts  97.5 us (9%)
  waiting for transfers between devices  79.6 us (7%)
  other arithmetic  31.3 us (3%)
  between operations  15 us (1%)
    pallas_call x1, Pallas kernels, finish(): pl.pallas_call(finish_kernel, out_shape=(shape(rows, 3 * width), shape(ro...  223 us
    pallas_call x1, Pallas kernels, middle(): pl.pallas_call(middle_kernel, out_shape=(jax.ShapeDtypeStruct(block, f32)...  142 us
    pallas_call x1, Pallas kernels, begin(): pl.pallas_call(begin_kernel, out_shape=(jax.ShapeDtypeStruct((4 * count,...  118 us
    pallas_call x1, Pallas kernels, mlp(): pl.pallas_call(mlp_kernel, grid=(rows // MLP_ROWS,), out_shape=(jax.Shape...  95.5 us
    ppermute x4, waiting for transfers between devices, swap(): return lax.ppermute(value, axis, [(i, i ^ bit) for i in range(size)])  57.5 us
    unnamed x178, local copies, waits for them, and re-layouts  54.5 us
    pallas_call x1, Pallas kernels, token_scatter(): pl.pallas_call(token_scatter_kernel, out_shape=jax.ShapeDtypeStruct(block...  54.1 us
    pallas_call x1, Pallas kernels, token_gather(): pl.pallas_call(token_gather_kernel, out_shape=jax.ShapeDtypeStruct((8, le...  53 us
  transfers between devices with their start and end apart: 9, of which 6 were waited for; matrix products, arithmetic and copies ran while one was open for 12% of the time, Pallas kernels for 54%

profile of v9, /device:TPU:0, one launch (start us, length us, event | category | flops | bytes accessed | tf_op | source)
XLA Modules:
  0.0 1132.3 jit_solution(10435602072184108112)
XLA Ops:
  39.7 117.8 %shard_map.400 = (f32[20,16,1152]{2,1,0:T(8,128)S(1)}, f32[20,16,1152]{2,1,0:T(8,128)S(1)}, f32[4,8,128]{2,1,0:T(8,128)S(1)}, f32[336,128]{1,0:T(8,128)S(1)}, f3...) custom-call(f32[5,64,1152]{2,1,0:T(8,128)S(1)} %copy-done.26, f32[5,64,1152]{2,1,0:T(8,128)S(1)} %copy-done.27, ...), custom_call_target="tpu_custom_call" | custom-call | bytes 65536 | tf_op jit(solution)/shard_map/pallas_call | solution.py:406
  168.5 15.4 %fusion.38 = f32[320,3456]{1,0:T(8,128)} fusion(f32[320,1152]{1,0:T(8,128)S(1)} %bitcast.150, f32[1152,3456]{1,0:T(8,128)} %get-tuple-element.64), kind=kOutput, calls=%fused_computation.154 | convolution fusion | flops 7644119040 | bytes 21823488 | tf_op jit(solution)/shard_map/dot_general | solution.py:23
  188.5 9.2 shard_map.401
  201.1 6.7 fusion.10
  208.9 5.0 fusion.4.queries
  227.4 28.9 %collective-permute-done.3 = f32[288,576]{1,0:T(8,128)} collective-permute-done((f32[288,576]{1,0:T(8,128)}, f32[288,576]{1,0:T(8,128)}, u32[]{:S(2)}, u32[]{:S(2)}) %collective-permute-start.3) | collective-permute-done | bytes 663584 | tf_op jit(solution)/shard_map/ppermute | solution.py:50
  257.4 15.3 %collective-permute-done.2 = f32[288,576]{1,0:T(8,128)} collective-permute-done((f32[288,576]{1,0:T(8,128)}, f32[288,576]{1,0:T(8,128)}, u32[]{:S(2)}, u32[]{:S(2)}) %collective-permute-start.2) | collective-permute-done | bytes 663584 | tf_op jit(solution)/shard_map/ppermute | solution.py:50
  273.9 10.6 collective-permute-done.1
  288.2 19.8 %shard_map.402 = (f32[16,320,480]{2,1,0:T(8,128)}, f32[320,1152]{1,0:T(8,128)S(1)}) custom-call(f32[320,1152]{1,0:T(8,128)S(1)} %copy-done.15, f32[1,1152]{1,0:T(1,128)S(1)} %get-tuple-element.190.b_query, f32[480,2304]{1,0:T(8,128)} %copy-done.10, f32[1,1152]{1,0:T(1,128)S(1)} %get-tuple-element.189.b_value, f32[320,480]{1,0:T(8,128)S(1)} %bitcast.132), custom_call_target="tpu_custom_call" | custom-call | bytes 65536 | tf_op jit(solution)/shard_map/pallas_call | solution.py:1159
  309.0 21.0 %all-gather.8.cloned.1.call-done = f32[1152,1152]{1,0:T(8,128)} async-done(((f32[144,1152]{1,0:T(8,128)}), f32[1152,1152]{1,0:T(8,128)}) %all-gather.8.cloned.1.call-update) | async-done | bytes 5308432 | tf_op jit(solution)/shard_map/all_gather | solution.py:1317
  330.0 6.6 convolution_add_fusion
  338.3 53.0 %shard_map.404 = f32[8,320,1152]{2,1,0:T(8,128)S(1)} custom-call(f32[320,1152]{1,0:T(8,128)S(1)} %bitcast.129), custom_call_target="tpu_custom_call" | custom-call | bytes 65536 | tf_op jit(solution)/shard_map/pallas_call | solution.py:148
  391.2 4.3 copy-done.6
  395.5 95.5 %shard_map.405 = (f32[2560,1152]{1,0:T(8,128)}, f32[2560,1152]{1,0:T(8,128)}, f32[1152,576]{1,0:T(8,128)}, f32[576,1152]{1,0:T(8,128)S(1)}, f32[1,576]{1,0:T(1,128)S(1)}) custom-call(f32[2560,1152]{1,0:T(8,128)} %bitcast.123, f32[2560,1152]{1,0:T(8,128)} %all-gather.6.cloned.1.call-done.cotangent, f32[1152,576]{1,0:T(8,128)} %copy-done.19, ...), custom_call_target="tpu_custom_call" | custom-call | bytes 65536 | tf_op jit(solution)/shard_map/pallas_call | solution.py:1273
  493.9 4.4 copy-done.20
  498.2 54.1 %shard_map.406 = f32[320,1152]{1,0:T(8,128)S(1)} custom-call(f32[8,320,1152]{2,1,0:T(8,128)S(1)} %bitcast.128), custom_call_target="tpu_custom_call" | custom-call | bytes 65536 | tf_op jit(solution)/shard_map/pallas_call | solution.py:212
  560.4 7.6 fusion.39.grad
  568.0 34.6 %shard_map.407 = (f32[320,1152]{1,0:T(8,128)S(1)}, f32[480,2304]{1,0:T(8,128)}) custom-call(f32[320,1152]{1,0:T(8,128)} %fusion.4.queries, f32[1,1152]{1,0:T(1,128)S(1)} %get-tuple-element.190.b_query, f32[480,2304]{1,0:T(8,128)} %copy-done.10, f32[1,1152]{1,0:T(1,128)S(1)} %get-tuple-element.189.b_value, f32[16,320,480]{2,1,0:T(8,128)} %get-tuple-element.77.probs, ...), custom_call_target="tpu_custom_call" | custom-call | bytes 65536 | tf_op jit(solution)/shard_map/pallas_call | solution.py:1217
  604.6 8.8 fusion.41.cross_o
  613.3 9.0 fusion.40.cross_q
  622.3 6.2 fusion.2
  630.4 7.0 convolution_bitcast_fusion.1.attn
  641.1 23.2 %shard_map.408 = f32[20,16,3456]{2,1,0:T(8,128)} custom-call(f32[20,16,3456]{2,1,0:T(8,128)} %bitcast.124, f32[1,1152]{1,0:T(1,128)S(1)} %get-tuple-element.192.b_query, f32[1,1152]{1,0:T(1,128)S(1)} %get-tuple-element.191.b_value, f32[16,2,160,160]{3,2,1,0:T(8,128)} %copy-done.23, f32[20,16,1152]{2,1,0:T(8,128)S(1)} %copy-done.22, f32[20,16,1152]{2,1,0:T(8,128)S(1)} %bitcast.131), custom_call_target="tpu_custom_call" | custom-call | bytes 65536 | tf_op jit(solution)/shard_map/pallas_call | solution.py:1118
  664.4 15.6 %multiply_reduce_fusion.3 = (f32[16,1152]{1,0:T(8,128)S(1)}, f32[20,16]{1,0:T(8,128)S(1)}, f32[20,16]{1,0:T(8,128)S(1)}, f32[16,1152]{1,0:T(8,128)S(1)}, f32[20,16,1152]{2,1,0:T(8,128)}) fusion(f32[20,16,1152]{2,1,0:T(8,128)S(1)} %copy-done.4, f32[20,16]{1,0:T(8,128)S(1)} %add_rsqrt_fusion.1, f32[20,16]{1,0:T(8,128)S(1)} %broadcast_multiply_fusion.7, ...), kind=kOutput, calls=%fused_computation.20 | convolution fusion | flops 7647399424 | bytes 23524352 | tf_op jit(solution)/shard_map/dot_general | solution.py:27
  680.0 16.7 %convolution_bitcast_fusion.first = f32[1152,3456]{1,0:T(8,128)} fusion(f32[20,16,1152]{2,1,0:T(8,128)S(1)} %copy-done.40, f32[20,16,3456]{2,1,0:T(8,128)S(1)} %copy-done.30), kind=kOutput, calls=%fused_computation | convolution fusion | flops 7644119040 | bytes 21823488 | tf_op jit(solution)/shard_map/dot_general | solution.py:31
  696.8 142.5 %shard_map.409 = (f32[320,1152]{1,0:T(8,128)}, f32[120,2304]{1,0:T(8,128)}, f32[5,64,1152]{2,1,0:T(8,128)}, f32[144,1152]{1,0:T(8,128)}, f32[144,1152]{1,0:T(8,128)}, /*index=5*/f32[144,1152]{1,0:T(8,128)}) custom-call(f32[8,320,1152]{2,1,0:T(8,128)} %bitcast.142, f32[480,2304]{1,0:T(8,128)} %get-tuple-element.84.kv, f32[20,16,1152]{2,1,0:T(8,128)} %copy-done.28, ...), custom_call_target="tpu_custom_call" | custom-call | bytes 65536 | tf_op jit(solution)/shard_map/pallas_call | solution.py:908
  853.7 222.5 %shard_map.410 = (f32[144,3456]{1,0:T(8,128)}, f32[144,1152]{1,0:T(8,128)}, f32[144,1152]{1,0:T(8,128)}, f32[144,1152]{1,0:T(8,128)}, f32[144,2304]{1,0:T(8,128)...) custom-call(f32[1152,3456]{1,0:T(8,128)} %convolution_bitcast_fusion.first,, ...), custom_call_target="tpu_custom_call" | custom-call | bytes 65536 | tf_op jit(solution)/shard_map/pallas_call | solution.py:702
  1076.2 4.4 copy.56
  1080.6 4.1 reshape.352
  1091.1 4.4 fusion.42.block
  1095.5 6.1 shard_map.411
  1108.4 4.6 fusion.29
  (312 shorter events, 132.6 us)
Async XLA Ops:
  7.2 29.0 %copy-start = (f32[4,120,1152]{2,1,0:T(8,128)S(1)}, f32[4,120,1152]{2,1,0:T(8,128)}, u32[]{:S(2)}) copy-start(f32[4,120,1152]{2,1,0:T(8,128)} %param.27) | copy-start | bytes 6635524
  7.2 193.8 %all-gather.4.cloned.1.call-start = ((), (), s32[]{:S(2)}) async-start(), calls=%async_computation | async-start | bytes 11943936 | tf_op jit(solution)/shard_map/all_gather | solution.py:1317
  9.9 276.8 %all-gather.6.cloned.1.call-start = ((), (), s32[]{:S(2)}) async-start(), calls=%async_computation.1 | async-start | bytes 13271040 | tf_op jit(solution)/shard_map/all_gather | solution.py:1317
  10.6 5.6 copy-start.68
  10.6 6.1 copy-start.65
  10.6 25.6 %copy-start.41 = (f32[144,2304]{1,0:T(8,128)S(1)}, f32[144,2304]{1,0:T(8,128)}, u32[]{:S(2)}) copy-start(f32[144,2304]{1,0:T(8,128)} %param.38) | copy-start | bytes 3981316
  166.3 41.4 %copy-start.51 = (f32[16,1152]{1,0:T(8,128)}, f32[16,1152]{1,0:T(8,128)S(1)}, u32[]{:S(2)}) copy-start(f32[16,1152]{1,0:T(8,128)S(1)} %get-tuple-element.168) | copy-start | bytes 221188
  168.5 15.4 %copy-start.39 = (f32[20,16,1152]{2,1,0:T(8,128)}, f32[20,16,1152]{2,1,0:T(8,128)S(1)}, u32[]{:S(2)}) copy-start(f32[20,16,1152]{2,1,0:T(8,128)S(1)} %get-tuple-element.188) | copy-start | bytes 4423684
  183.9 146.1 %all-gather.8.cloned.1.call-start = ((), (), s32[]{:S(2)}) async-start(), calls=%async_computation.2 | async-start | bytes 5971968 | tf_op jit(solution)/shard_map/all_gather | solution.py:1317
  184.7 428.7 %all-reduce.6.cloned.1.call-start = ((), (), s32[]{:S(2)}) async-start(), calls=%async_computation.3 | async-start | bytes 5898240 | tf_op jit(solution)/shard_map/psum | solution.py:1554
  201.0 6.7 copy-start.3
  201.0 7.8 copy-start.29
  214.8 3.4 collective-permute-start
  220.0 36.3 %collective-permute-start.3 = (f32[288,576]{1,0:T(8,128)}, f32[288,576]{1,0:T(8,128)}, u32[]{:S(2)}, u32[]{:S(2)}) collective-permute-start(f32[288,576]{1,0:T(8,128)} %pad_maximum_fusion.4), channel_id=1, source_target_pairs={{0,24},{4,28},{8,16},{12,20},{16,8},{20,12},{24,0},{28,4},{1,25},{... | collective-permute-start | bytes 1990664 | tf_op jit(solution)/shard_map/ppermute | solution.py:50
  222.0 5.3 copy-start.63
  222.9 49.8 %collective-permute-start.2 = (f32[288,576]{1,0:T(8,128)}, f32[288,576]{1,0:T(8,128)}, u32[]{:S(2)}, u32[]{:S(2)}) collective-permute-start(f32[288,576]{1,0:T(8,128)} %pad_maximum_fusion.3), channel_id=1, source_target_pairs={{0,16},{4,20},{8,24},{12,28},{16,0},{20,4},{24,8},{28,12},{1,17},{... | collective-permute-start | bytes 1990664 | tf_op jit(solution)/shard_map/ppermute | solution.py:50
  226.7 57.8 %collective-permute-start.1 = (f32[288,576]{1,0:T(8,128)S(1)}, f32[288,576]{1,0:T(8,128)S(1)}, u32[]{:S(2)}, u32[]{:S(2)}) collective-permute-start(f32[288,576]{1,0:T(8,128)S(1)} %pad_maximum_fusion.2), channel_id=1, source_target_pairs={{0,8},{4,12},{8,0},{12,4},{16,24},{20,28},{24,16},{28,20},{1,9},{5... | collective-permute-start | bytes 1990664 | tf_op jit(solution)/shard_map/ppermute | solution.py:50
  330.0 6.6 copy-start.32
  492.6 621.0 %all-reduce.8.cloned.1.call-start = ((), (), s32[]{:S(2)}) async-start(), calls=%async_computation.4 | async-start | bytes 5308416 | tf_op jit(solution)/shard_map/psum | solution.py:1555
  560.4 7.6 copy-start.35
  613.3 9.0 copy-start.17
  622.3 6.3 copy-start.38
  622.3 6.3 copy-start.52
  628.6 8.8 slice-start
  630.4 7.0 slice-start.1
  630.4 7.0 slice-start.2
  641.1 23.3 %copy-start.4 = (f32[20,16,1152]{2,1,0:T(8,128)S(1)}, f32[20,16,1152]{2,1,0:T(8,128)}, u32[]{:S(2)}) copy-start(f32[20,16,1152]{2,1,0:T(8,128)} %copy-done.1) | copy-start | bytes 4423684
  664.4 15.6 %copy-start.30 = (f32[20,16,3456]{2,1,0:T(8,128)S(1)}, f32[20,16,3456]{2,1,0:T(8,128)}, u32[]{:S(2)}) copy-start(f32[20,16,3456]{2,1,0:T(8,128)} %shard_map.408) | copy-start | bytes 13271044
  664.4 15.6 %copy-start.40 = (f32[20,16,1152]{2,1,0:T(8,128)S(1)}, f32[20,16,1152]{2,1,0:T(8,128)}, u32[]{:S(2)}) copy-start(f32[20,16,1152]{2,1,0:T(8,128)} %copy-done.39) | copy-start | bytes 4423684
  696.7 144.1 %copy-start.34 = (f32[320,1152]{1,0:T(8,128)S(1)}, f32[320,1152]{1,0:T(8,128)}, u32[]{:S(2)}) copy-start(f32[320,1152]{1,0:T(8,128)} %copy-done.33) | copy-start | bytes 4423684
  696.7 144.1 %copy-start.36 = (f32[20,16,1152]{2,1,0:T(8,128)S(1)}, f32[20,16,1152]{2,1,0:T(8,128)}, u32[]{:S(2)}) copy-start(f32[20,16,1152]{2,1,0:T(8,128)} %get-tuple-element.187) | copy-start | bytes 4423684
  1091.1 17.3 %copy-start.57 = (f32[4,1152]{1,0:T(4,128)S(1)}, f32[4,1152]{1,0:T(4,128)}, u32[]{:S(2)}) copy-start(f32[4,1152]{1,0:T(4,128)} %param.28) | copy-start | bytes 55300
  (51 other events, 107.9 us)
Sparse Core Ops, SparseCore 0:
  10.5 92.7 all-gather.3
  184.0 102.6 all-gather.5
  288.6 41.3 all-gather.7
  492.7 114.8 all-reduce.5
  696.8 173.0 all-reduce.7

commit v10 on v9

--- a/solution.py
+++ b/solution.py
@@ -1472,7 +1472,7 @@
         fc2_bias,
     )
     small = jnp.concatenate(
-        [modulation_part.reshape(-1)] + [placed(b, "patch") for b in biases]
+        [modulation_part.reshape(-1), placed(jnp.concatenate(biases), "patch")]
     )
     caption_rows = caption.reshape(CLIPS * CAP, width)
     caption_share = own_part(own_part(caption_rows, "frame", 0), "patch", 1)
@@ -1493,11 +1493,11 @@
     column_mask = own_part(patch_mask, "frame", 0).astype(jnp.float32)[:, None]
     place = modulation_part.size
     modulation = small[:place].reshape(modulation_part.shape)
-    whole = []
+    table = small[place:].reshape(lax.axis_size("patch"), -1)
+    whole, place = [], 0
     for b in biases:
-        length = b.shape[0] * lax.axis_size("patch")
-        whole.append(small[place : place + length])
-        place += length
+        whole.append(table[:, place : place + b.shape[0]].reshape(-1))
+        place += b.shape[0]
     b_ada, b_query, b_value, b_attn, b_cross_q, b_cross_v, b_cross_o, b_second = whole
     modulation = modulation + b_ada
     clip_onehot = (clip_own[:, None] == jnp.arange(CLIPS, dtype=jnp.int32)[None, :]).astype(
@@ -1619,21 +1619,24 @@
         grad_b_cross_o,
         grad_b_second,
     )
-    small_grads = jnp.concatenate(
-        [grad_modulation_part.reshape(-1)] + list(bias_grads) + [placed(grad_b_first, "patch")]
-    )
+    bias_rows = jnp.concatenate(
+        [b.reshape(lax.axis_size("patch"), -1) for b in bias_grads]
+        + [placed(grad_b_first, "patch").reshape(lax.axis_size("patch"), -1)],
+        axis=1,
+    )
+    small_grads = jnp.concatenate([grad_modulation_part.reshape(-1), bias_rows.reshape(-1)])
     weights, grad_w_cross_kv, input_grad, small_grads, grad_caption, grad_w_first = close_up(
         (grad_w_qkv, *shares),
         grad_w_cross_kv, input_grad, small_grads, grad_caption_share, grad_w_first,
     )
     place = grad_modulation_part.size
     grad_modulation = small_grads[:place].reshape(grad_modulation_part.shape)
-    own_biases = []
-    for b in bias_grads:
-        own_biases.append(own_part(small_grads[place : place + b.shape[0]], "patch", 0))
-        place += b.shape[0]
-    g_query, g_value, g_attn, g_cross_q, g_cross_v, g_cross_o, g_second = own_biases
-    grad_b_first = own_part(small_grads[place:], "patch", 0)
+    own_row = own_part(small_grads[place:], "patch", 0)
+    length = bias_grads[0].shape[0] // lax.axis_size("patch")
+    g_query, g_value, g_attn, g_cross_q, g_cross_v, g_cross_o, g_second = (
+        own_row[i * length : (i + 1) * length] for i in range(7)
+    )
+    grad_b_first = own_row[7 * length :]
     grad_w_ada = matmul_tn(cond_own, grad_modulation)
     grad_b_ada = own_part(jnp.sum(grad_modulation, axis=0), "patch", 0)
     grad_cond_own = matmul_nt(grad_modulation, ada_weight)

time: 1140 us -> 1130 us (level)
  local copies, waits for them, and re-layouts: 97.5 us -> 84.4 us
    unnamed x178 -> x176, local copies, waits for them, and re-layouts: 54.5 us -> 49.4 us
  transfers between devices with their start and end apart: 9 -> 9, of which waited for: 6 -> 6; matrix products, arithmetic and copies ran while one was open for 12% -> 11% of each run, Pallas kernels for 54% -> 55%
where the time goes in v10:
time: 1130 us; the launch traced here: 1120 us
  Pallas kernels  785 us (69%)
  matrix products  124 us (11%)
  local copies, waits for them, and re-layouts  84.4 us (7%)
  waiting for transfers between devices  75.2 us (7%)
  other arithmetic  34.3 us (3%)
  between operations  15 us (1%)
    pallas_call x1, Pallas kernels, finish(): pl.pallas_call(finish_kernel, out_shape=(shape(rows, 3 * width), shape(ro...  222 us
    pallas_call x1, Pallas kernels, middle(): pl.pallas_call(middle_kernel, out_shape=(jax.ShapeDtypeStruct(block, f32)...  142 us
    pallas_call x1, Pallas kernels, begin(): pl.pallas_call(begin_kernel, out_shape=(jax.ShapeDtypeStruct((4 * count,...  124 us
    pallas_call x1, Pallas kernels, mlp(): pl.pallas_call(mlp_kernel, grid=(rows // MLP_ROWS,), out_shape=(jax.Shape...  95.5 us
    pallas_call x1, Pallas kernels, token_scatter(): pl.pallas_call(token_scatter_kernel, out_shape=jax.ShapeDtypeStruct(block...  54.1 us
    ppermute x4, waiting for transfers between devices, swap(): return lax.ppermute(value, axis, [(i, i ^ bit) for i in range(size)])  53.1 us
    pallas_call x1, Pallas kernels, token_gather(): pl.pallas_call(token_gather_kernel, out_shape=jax.ShapeDtypeStruct((8, le...  53 us
    unnamed x176, local copies, waits for them, and re-layouts  49.4 us
  transfers between devices with their start and end apart: 9, of which 6 were waited for; matrix products, arithmetic and copies ran while one was open for 11% of the time, Pallas kernels for 55%

profile of v10, /device:TPU:0, one launch (start us, length us, event | category | flops | bytes accessed | tf_op | source)
XLA Modules:
  0.0 1122.2 jit_solution(2469591724007801968)
XLA Ops:
  25.3 124.5 %shard_map.400 = (f32[20,16,1152]{2,1,0:T(8,128)S(1)}, f32[20,16,1152]{2,1,0:T(8,128)S(1)}, f32[4,8,128]{2,1,0:T(8,128)S(1)}, f32[336,128]{1,0:T(8,128)S(1)}, f3...) custom-call(f32[5,64,1152]{2,1,0:T(8,128)S(1)} %copy-done.27, f32[5,64,1152]{2,1,0:T(8,128)S(1)} %copy-done.28, ...), custom_call_target="tpu_custom_call" | custom-call | bytes 65536 | tf_op jit(solution)/shard_map/pallas_call | solution.py:406
  160.5 15.5 %fusion.42 = f32[320,3456]{1,0:T(8,128)} fusion(f32[320,1152]{1,0:T(8,128)S(1)} %bitcast.102, f32[1152,3456]{1,0:T(8,128)} %get-tuple-element.64), kind=kOutput, calls=%fused_computation.122 | convolution fusion | flops 7644119040 | bytes 21823488 | tf_op jit(solution)/shard_map/dot_general | solution.py:23
  180.9 9.2 shard_map.401
  193.5 6.7 fusion.10
  201.3 5.0 fusion.4.queries
  222.1 26.6 %collective-permute-done.3 = f32[288,576]{1,0:T(8,128)} collective-permute-done((f32[288,576]{1,0:T(8,128)}, f32[288,576]{1,0:T(8,128)}, u32[]{:S(2)}, u32[]{:S(2)}) %collective-permute-start.3) | collective-permute-done | bytes 663584 | tf_op jit(solution)/shard_map/ppermute | solution.py:50
  249.8 15.3 %collective-permute-done.2 = f32[288,576]{1,0:T(8,128)} collective-permute-done((f32[288,576]{1,0:T(8,128)}, f32[288,576]{1,0:T(8,128)}, u32[]{:S(2)}, u32[]{:S(2)}) %collective-permute-start.2) | collective-permute-done | bytes 663584 | tf_op jit(solution)/shard_map/ppermute | solution.py:50
  266.3 8.2 collective-permute-done.1
  278.2 19.7 %shard_map.402 = (f32[16,320,480]{2,1,0:T(8,128)}, f32[320,1152]{1,0:T(8,128)S(1)}) custom-call(f32[320,1152]{1,0:T(8,128)S(1)} %copy-done.15, f32[1,1152]{1,0:T(1,128)S(1)} %reshape_reshape.18.b_query, f32[480,2304]{1,0:T(8,128)} %copy-done.10, f32[1,1152]{1,0:T(1,128)S(1)} %reshape_reshape.19.b_value, f32[320,480]{1,0:T(8,128)S(1)} %bitcast.84), custom_call_target="tpu_custom_call" | custom-call | bytes 65536 | tf_op jit(solution)/shard_map/pallas_call | solution.py:1159
  299.1 21.0 %all-gather.8.cloned.1.call-done = f32[1152,1152]{1,0:T(8,128)} async-done(((f32[144,1152]{1,0:T(8,128)}), f32[1152,1152]{1,0:T(8,128)}) %all-gather.8.cloned.1.call-update) | async-done | bytes 5308432 | tf_op jit(solution)/shard_map/all_gather | solution.py:1317
  320.1 6.6 convolution_add_fusion
  328.3 53.0 %shard_map.404 = f32[8,320,1152]{2,1,0:T(8,128)S(1)} custom-call(f32[320,1152]{1,0:T(8,128)S(1)} %bitcast.81), custom_call_target="tpu_custom_call" | custom-call | bytes 65536 | tf_op jit(solution)/shard_map/pallas_call | solution.py:148
  381.3 4.3 copy-done.6
  385.6 95.5 %shard_map.405 = (f32[2560,1152]{1,0:T(8,128)}, f32[2560,1152]{1,0:T(8,128)}, f32[1152,576]{1,0:T(8,128)}, f32[576,1152]{1,0:T(8,128)S(1)}, f32[1,576]{1,0:T(1,128)S(1)}) custom-call(f32[2560,1152]{1,0:T(8,128)} %bitcast.75, f32[2560,1152]{1,0:T(8,128)} %all-gather.6.cloned.1.call-done.cotangent, f32[1152,576]{1,0:T(8,128)} %copy-done.20, ...), custom_call_target="tpu_custom_call" | custom-call | bytes 65536 | tf_op jit(solution)/shard_map/pallas_call | solution.py:1273
  484.2 4.6 copy-done.21
  488.7 54.1 %shard_map.406 = f32[320,1152]{1,0:T(8,128)S(1)} custom-call(f32[8,320,1152]{2,1,0:T(8,128)S(1)} %bitcast.80), custom_call_target="tpu_custom_call" | custom-call | bytes 65536 | tf_op jit(solution)/shard_map/pallas_call | solution.py:212
  552.8 7.5 fusion.43.grad
  560.3 35.2 %shard_map.407 = (f32[320,1152]{1,0:T(8,128)S(1)}, f32[480,2304]{1,0:T(8,128)}) custom-call(f32[320,1152]{1,0:T(8,128)} %fusion.4.queries, f32[1,1152]{1,0:T(1,128)S(1)} %reshape_reshape.18.b_query, f32[480,2304]{1,0:T(8,128)} %copy-done.10, f32[1,1152]{1,0:T(1,128)S(1)} %reshape_reshape.19.b_value, f32[16,320,480]{2,1,0:T(8,128)} %get-tuple-element.77.probs, ...), custom_call_target="tpu_custom_call" | custom-call | bytes 65536 | tf_op jit(solution)/shard_map/pallas_call | solution.py:1217
  596.6 7.0 fusion.45.cross_o
  603.6 9.0 fusion.44.cross_q
  612.6 6.2 fusion.2
  620.7 7.0 convolution_bitcast_fusion.1.attn
  631.4 23.3 %shard_map.408 = f32[20,16,3456]{2,1,0:T(8,128)} custom-call(f32[20,16,3456]{2,1,0:T(8,128)} %bitcast.76, f32[1,1152]{1,0:T(1,128)S(1)} %reshape_reshape.16.b_query, f32[1,1152]{1,0:T(1,128)S(1)} %reshape_reshape.17.b_value, f32[16,2,160,160]{3,2,1,0:T(8,128)} %copy-done.24, f32[20,16,1152]{2,1,0:T(8,128)S(1)} %copy-done.23, f32[20,16,1152]{2,1,0:T(8,128)S(1)} %bitcast.83), custom_call_target="tpu_custom_call" | custom-call | bytes 65536 | tf_op jit(solution)/shard_map/pallas_call | solution.py:1118
  654.7 15.6 %multiply_reduce_fusion.3 = (f32[16,1152]{1,0:T(8,128)S(1)}, f32[20,16]{1,0:T(8,128)S(1)}, f32[20,16]{1,0:T(8,128)S(1)}, f32[16,1152]{1,0:T(8,128)S(1)}, f32[20,16,1152]{2,1,0:T(8,128)}) fusion(f32[20,16,1152]{2,1,0:T(8,128)S(1)} %copy-done.4, f32[20,16]{1,0:T(8,128)S(1)} %add_rsqrt_fusion.1, f32[20,16]{1,0:T(8,128)S(1)} %broadcast_multiply_fusion.7, ...), kind=kOutput, calls=%fused_computation.20 | convolution fusion | flops 7647399424 | bytes 23524352 | tf_op jit(solution)/shard_map/dot_general | solution.py:27
  670.3 16.7 %convolution_bitcast_fusion.first = f32[1152,3456]{1,0:T(8,128)} fusion(f32[20,16,1152]{2,1,0:T(8,128)S(1)} %copy-done.41, f32[20,16,3456]{2,1,0:T(8,128)S(1)} %copy-done.31), kind=kOutput, calls=%fused_computation | convolution fusion | flops 7644119040 | bytes 21823488 | tf_op jit(solution)/shard_map/dot_general | solution.py:31
  687.8 142.4 %shard_map.409 = (f32[320,1152]{1,0:T(8,128)}, f32[120,2304]{1,0:T(8,128)}, f32[5,64,1152]{2,1,0:T(8,128)}, f32[144,1152]{1,0:T(8,128)}, f32[144,1152]{1,0:T(8,128)}, /*index=5*/f32[144,1152]{1,0:T(8,128)}) custom-call(f32[8,320,1152]{2,1,0:T(8,128)} %bitcast.94, f32[480,2304]{1,0:T(8,128)} %get-tuple-element.84.kv, f32[20,16,1152]{2,1,0:T(8,128)} %copy-done.29, ...), custom_call_target="tpu_custom_call" | custom-call | bytes 65536 | tf_op jit(solution)/shard_map/pallas_call | solution.py:908
  848.4 221.5 %shard_map.410 = (f32[144,3456]{1,0:T(8,128)}, f32[144,1152]{1,0:T(8,128)}, f32[144,1152]{1,0:T(8,128)}, f32[144,1152]{1,0:T(8,128)}, f32[144,2304]{1,0:T(8,128)...) custom-call(f32[1152,3456]{1,0:T(8,128)} %convolution_bitcast_fusion.first,, ...), custom_call_target="tpu_custom_call" | custom-call | bytes 65536 | tf_op jit(solution)/shard_map/pallas_call | solution.py:702
  1069.9 4.4 copy.56
  1074.3 4.1 reshape.351
  1084.8 4.4 fusion.46.block
  1089.2 6.1 shard_map.411
  1098.3 4.6 fusion.31
  (307 shorter events, 122.4 us)
Async XLA Ops:
  7.2 14.4 %copy-start = (f32[4,120,1152]{2,1,0:T(8,128)S(1)}, f32[4,120,1152]{2,1,0:T(8,128)}, u32[]{:S(2)}) copy-start(f32[4,120,1152]{2,1,0:T(8,128)} %param.27) | copy-start | bytes 6635524
  7.2 186.2 %all-gather.4.cloned.1.call-start = ((), (), s32[]{:S(2)}) async-start(), calls=%async_computation | async-start | bytes 11943936 | tf_op jit(solution)/shard_map/all_gather | solution.py:1317
  9.9 266.9 %all-gather.6.cloned.1.call-start = ((), (), s32[]{:S(2)}) async-start(), calls=%async_computation.1 | async-start | bytes 13271040 | tf_op jit(solution)/shard_map/all_gather | solution.py:1317
  10.6 6.1 copy-start.73
  10.6 11.0 copy-start.42
  158.9 41.2 %copy-start.52 = (f32[16,1152]{1,0:T(8,128)}, f32[16,1152]{1,0:T(8,128)S(1)}, u32[]{:S(2)}) copy-start(f32[16,1152]{1,0:T(8,128)S(1)} %get-tuple-element.168) | copy-start | bytes 221188
  160.5 15.5 %copy-start.40 = (f32[20,16,1152]{2,1,0:T(8,128)}, f32[20,16,1152]{2,1,0:T(8,128)S(1)}, u32[]{:S(2)}) copy-start(f32[20,16,1152]{2,1,0:T(8,128)S(1)} %get-tuple-element.187) | copy-start | bytes 4423684
  176.0 144.0 %all-gather.8.cloned.1.call-start = ((), (), s32[]{:S(2)}) async-start(), calls=%async_computation.2 | async-start | bytes 5971968 | tf_op jit(solution)/shard_map/all_gather | solution.py:1317
  176.8 426.9 %all-reduce.6.cloned.1.call-start = ((), (), s32[]{:S(2)}) async-start(), calls=%async_computation.3 | async-start | bytes 5898240 | tf_op jit(solution)/shard_map/psum | solution.py:1554
  193.5 6.7 copy-start.3
  193.5 7.8 copy-start.30
  207.2 3.4 collective-permute-start
  212.3 36.3 %collective-permute-start.3 = (f32[288,576]{1,0:T(8,128)}, f32[288,576]{1,0:T(8,128)}, u32[]{:S(2)}, u32[]{:S(2)}) collective-permute-start(f32[288,576]{1,0:T(8,128)} %pad_maximum_fusion.4), channel_id=1, source_target_pairs={{0,24},{4,28},{8,16},{12,20},{16,8},{20,12},{24,0},{28,4},{1,25},{... | collective-permute-start | bytes 1990664 | tf_op jit(solution)/shard_map/ppermute | solution.py:50
  215.3 49.9 %collective-permute-start.2 = (f32[288,576]{1,0:T(8,128)}, f32[288,576]{1,0:T(8,128)}, u32[]{:S(2)}, u32[]{:S(2)}) collective-permute-start(f32[288,576]{1,0:T(8,128)} %pad_maximum_fusion.3), channel_id=1, source_target_pairs={{0,16},{4,20},{8,24},{12,28},{16,0},{20,4},{24,8},{28,12},{1,17},{... | collective-permute-start | bytes 1990664 | tf_op jit(solution)/shard_map/ppermute | solution.py:50
  220.7 53.8 %collective-permute-start.1 = (f32[288,576]{1,0:T(8,128)S(1)}, f32[288,576]{1,0:T(8,128)S(1)}, u32[]{:S(2)}, u32[]{:S(2)}) collective-permute-start(f32[288,576]{1,0:T(8,128)S(1)} %pad_maximum_fusion.2), channel_id=1, source_target_pairs={{0,8},{4,12},{8,0},{12,4},{16,24},{20,28},{24,16},{28,20},{1,9},{5... | collective-permute-start | bytes 1990664 | tf_op jit(solution)/shard_map/ppermute | solution.py:50
  320.1 6.6 copy-start.33
  320.1 6.6 copy-start.68
  482.7 620.8 %all-reduce.8.cloned.1.call-start = ((), (), s32[]{:S(2)}) async-start(), calls=%async_computation.4 | async-start | bytes 5308416 | tf_op jit(solution)/shard_map/psum | solution.py:1555
  560.3 36.4 %copy-start.17 = (f32[320,1152]{1,0:T(8,128)S(1)}, f32[320,1152]{1,0:T(8,128)}, u32[]{:S(2)}) copy-start(f32[320,1152]{1,0:T(8,128)} %copy-done.16) | copy-start | bytes 4423684
  560.3 36.4 %copy-start.36 = (f32[20,16,1152]{2,1,0:T(8,128)S(1)}, f32[20,16,1152]{2,1,0:T(8,128)}, u32[]{:S(2)}) copy-start(f32[20,16,1152]{2,1,0:T(8,128)} %get-tuple-element.138) | copy-start | bytes 4423684
  603.6 9.0 copy-start.19
  612.6 6.2 copy-start.39
  612.6 6.3 copy-start.53
  618.9 8.8 slice-start
  620.7 7.0 slice-start.1
  620.7 7.0 slice-start.2
  631.4 23.3 %copy-start.4 = (f32[20,16,1152]{2,1,0:T(8,128)S(1)}, f32[20,16,1152]{2,1,0:T(8,128)}, u32[]{:S(2)}) copy-start(f32[20,16,1152]{2,1,0:T(8,128)} %copy-done.1) | copy-start | bytes 4423684
  654.7 15.6 %copy-start.31 = (f32[20,16,3456]{2,1,0:T(8,128)S(1)}, f32[20,16,3456]{2,1,0:T(8,128)}, u32[]{:S(2)}) copy-start(f32[20,16,3456]{2,1,0:T(8,128)} %shard_map.408) | copy-start | bytes 13271044
  654.7 15.6 %copy-start.41 = (f32[20,16,1152]{2,1,0:T(8,128)S(1)}, f32[20,16,1152]{2,1,0:T(8,128)}, u32[]{:S(2)}) copy-start(f32[20,16,1152]{2,1,0:T(8,128)} %copy-done.40) | copy-start | bytes 4423684
  687.8 144.1 %copy-start.35 = (f32[320,1152]{1,0:T(8,128)S(1)}, f32[320,1152]{1,0:T(8,128)}, u32[]{:S(2)}) copy-start(f32[320,1152]{1,0:T(8,128)} %copy-done.34) | copy-start | bytes 4423684
  687.8 144.1 %copy-start.37 = (f32[20,16,1152]{2,1,0:T(8,128)S(1)}, f32[20,16,1152]{2,1,0:T(8,128)}, u32[]{:S(2)}) copy-start(f32[20,16,1152]{2,1,0:T(8,128)} %get-tuple-element.186) | copy-start | bytes 4423684
  1084.8 13.4 %copy-start.62 = (f32[4,1152]{1,0:T(4,128)S(1)}, f32[4,1152]{1,0:T(4,128)}, u32[]{:S(2)}) copy-start(f32[4,1152]{1,0:T(4,128)} %param.28) | copy-start | bytes 55300
  (58 other events, 138.7 us)
Sparse Core Ops, SparseCore 0:
  10.5 103.5 all-gather.3
  176.1 100.5 all-gather.5
  278.6 41.3 all-gather.7
  482.8 114.7 all-reduce.5
  687.1 172.9 all-reduce.7

commit v11 on v10

--- a/solution.py
+++ b/solution.py
@@ -1484,9 +1484,10 @@
         matmul(caption_share, cross_kv_weight),
         qkv_weight,
     )
-    w_two = gather_rows(jnp.concatenate([attn_out_weight, cross_q_weight], axis=1))
-    w_attn, w_cross_q = jnp.split(w_two, 2, axis=1)
-    w_cross_o = gather_rows(cross_out_weight)
+    w_three = gather_rows(
+        jnp.concatenate([attn_out_weight, cross_q_weight, cross_out_weight], axis=1)
+    )
+    w_attn, w_cross_q, w_cross_o = jnp.split(w_three, 3, axis=1)
     slots, cols, _ = tokens_in.shape
     rows = slots * cols
     clip_own = own_part(clip_id, "frame", 0)

time: 1130 us -> 1150 us (1.018)
  Pallas kernels: 785 us -> 806 us
    pallas_call x1, Pallas kernels: 124 us -> 145 us  [begin(): pl.pallas_call(begin_kernel, out_shape=(jax.ShapeDtypeStruct((4 * count,...]
    ppermute x4, waiting for transfers between devices: 53.1 us -> 38.7 us  [swap(): return lax.ppermute(value, axis, [(i, i ^ bit) for i in range(size)])]
    all_gather x3 -> x2, waiting for transfers between devices: 21.4 us -> 31.5 us  [gather_rows(): return lax.all_gather(shard, 'patch', axis=0, tiled=True)]
    unnamed x176 -> x172, local copies, waits for them, and re-layouts: 49.4 us -> 47.9 us
  transfers between devices with their start and end apart: 9 -> 8, of which waited for: 6 -> 4; matrix products, arithmetic and copies ran while one was open for 11% -> 10% of each run, Pallas kernels for 55% -> 54%
where the time goes in v11:
time: 1150 us; the launch traced here: 1140 us
  Pallas kernels  806 us (70%)
  matrix products  128 us (11%)
  local copies, waits for them, and re-layouts  81.6 us (7%)
  waiting for transfers between devices  70.3 us (6%)
  other arithmetic  36 us (3%)
  between operations  15 us (1%)
    pallas_call x1, Pallas kernels, finish(): pl.pallas_call(finish_kernel, out_shape=(shape(rows, 3 * width), shape(ro...  221 us
    pallas_call x1, Pallas kernels, begin(): pl.pallas_call(begin_kernel, out_shape=(jax.ShapeDtypeStruct((4 * count,...  145 us
    pallas_call x1, Pallas kernels, middle(): pl.pallas_call(middle_kernel, out_shape=(jax.ShapeDtypeStruct(block, f32)...  142 us
    pallas_call x1, Pallas kernels, mlp(): pl.pallas_call(mlp_kernel, grid=(rows // MLP_ROWS,), out_shape=(jax.Shape...  95.5 us
    pallas_call x1, Pallas kernels, token_scatter(): pl.pallas_call(token_scatter_kernel, out_shape=jax.ShapeDtypeStruct(block...  54.1 us
    pallas_call x1, Pallas kernels, token_gather(): pl.pallas_call(token_gather_kernel, out_shape=jax.ShapeDtypeStruct((8, le...  53 us
    unnamed x172, local copies, waits for them, and re-layouts  47.9 us
    dot_general x6, matrix products, matmul_tn(): lax.dot_general(left, right, (((0,), (0,)), ((), ())), precision=BEST)  46 us
  transfers between devices with their start and end apart: 8, of which 4 were waited for; matrix products, arithmetic and copies ran while one was open for 10% of the time, Pallas kernels for 54%

profile of v11, /device:TPU:0, one launch (start us, length us, event | category | flops | bytes accessed | tf_op | source)
XLA Modules:
  0.0 1140.7 jit_solution(12124413436458951454)
XLA Ops:
  26.5 145.5 %shard_map.400 = (f32[20,16,1152]{2,1,0:T(8,128)S(1)}, f32[20,16,1152]{2,1,0:T(8,128)S(1)}, f32[4,8,128]{2,1,0:T(8,128)S(1)}, f32[336,128]{1,0:T(8,128)S(1)}, f3...) custom-call(f32[5,64,1152]{2,1,0:T(8,128)S(1)} %copy-done.27, f32[5,64,1152]{2,1,0:T(8,128)S(1)} %copy-done.28, ...), custom_call_target="tpu_custom_call" | custom-call | bytes 65536 | tf_op jit(solution)/shard_map/pallas_call | solution.py:406
  182.8 14.5 %fusion.49 = f32[320,3456]{1,0:T(8,128)S(1)} fusion(f32[320,1152]{1,0:T(8,128)S(1)} %bitcast.98, f32[1152,3456]{1,0:T(8,128)} %get-tuple-element.64), kind=kOutput, calls=%fused_computation.126 | convolution fusion | flops 7644119040 | bytes 21823488 | tf_op jit(solution)/shard_map/dot_general | solution.py:23
  197.3 9.4 shard_map.401
  212.4 6.7 fusion.14
  221.9 7.7 fusion.8.queries
  244.0 21.8 %collective-permute-done.3 = f32[288,576]{1,0:T(8,128)} collective-permute-done((f32[288,576]{1,0:T(8,128)}, f32[288,576]{1,0:T(8,128)}, u32[]{:S(2)}, u32[]{:S(2)}) %collective-permute-start.3) | collective-permute-done | bytes 663584 | tf_op jit(solution)/shard_map/ppermute | solution.py:50
  266.9 14.1 %collective-permute-done.2 = f32[288,576]{1,0:T(8,128)} collective-permute-done((f32[288,576]{1,0:T(8,128)}, f32[288,576]{1,0:T(8,128)}, u32[]{:S(2)}, u32[]{:S(2)}) %collective-permute-start.2) | collective-permute-done | bytes 663584 | tf_op jit(solution)/shard_map/ppermute | solution.py:50
  284.1 31.5 %all-gather.5.cloned.1.call-done.cotangent = f32[2560,1152]{1,0:T(8,128)} async-done(((f32[320,1152]{1,0:T(8,128)}), f32[2560,1152]{1,0:T(8,128)}) %all-gather.5.cloned.1.call-update) | async-done | bytes 11796496 | tf_op jit(solution)/shard_map/all_gather | solution.py:1317
  317.0 19.7 %shard_map.402 = (f32[16,320,480]{2,1,0:T(8,128)}, f32[320,1152]{1,0:T(8,128)S(1)}) custom-call(f32[320,1152]{1,0:T(8,128)S(1)} %copy-done.15, f32[1,1152]{1,0:T(1,128)S(1)} %reshape_reshape.18.b_query, f32[480,2304]{1,0:T(8,128)} %copy-done.10, f32[1,1152]{1,0:T(1,128)S(1)} %reshape_reshape.19.b_value, f32[320,480]{1,0:T(8,128)S(1)} %bitcast.82), custom_call_target="tpu_custom_call" | custom-call | bytes 65536 | tf_op jit(solution)/shard_map/pallas_call | solution.py:1159
  336.7 6.6 fusion.17
  344.9 53.0 %shard_map.404 = f32[8,320,1152]{2,1,0:T(8,128)S(1)} custom-call(f32[320,1152]{1,0:T(8,128)S(1)} %bitcast.79), custom_call_target="tpu_custom_call" | custom-call | bytes 65536 | tf_op jit(solution)/shard_map/pallas_call | solution.py:148
  397.9 4.2 copy-done.6
  402.1 95.5 %shard_map.405 = (f32[2560,1152]{1,0:T(8,128)}, f32[2560,1152]{1,0:T(8,128)}, f32[1152,576]{1,0:T(8,128)}, f32[576,1152]{1,0:T(8,128)S(1)}, f32[1,576]{1,0:T(1,128)S(1)}) custom-call(f32[2560,1152]{1,0:T(8,128)} %bitcast.73, f32[2560,1152]{1,0:T(8,128)} %all-gather.5.cloned.1.call-done.cotangent, f32[1152,576]{1,0:T(8,128)} %copy-done.20, ...), custom_call_target="tpu_custom_call" | custom-call | bytes 65536 | tf_op jit(solution)/shard_map/pallas_call | solution.py:1273
  500.7 4.6 copy-done.21
  505.3 54.1 %shard_map.406 = f32[320,1152]{1,0:T(8,128)S(1)} custom-call(f32[8,320,1152]{2,1,0:T(8,128)S(1)} %bitcast.78), custom_call_target="tpu_custom_call" | custom-call | bytes 65536 | tf_op jit(solution)/shard_map/pallas_call | solution.py:212
  569.3 7.5 fusion.2.grad
  576.8 35.2 %shard_map.407 = (f32[320,1152]{1,0:T(8,128)S(1)}, f32[480,2304]{1,0:T(8,128)}) custom-call(f32[320,1152]{1,0:T(8,128)} %fusion.8.queries, f32[1,1152]{1,0:T(1,128)S(1)} %reshape_reshape.18.b_query, f32[480,2304]{1,0:T(8,128)} %copy-done.10, f32[1,1152]{1,0:T(1,128)S(1)} %reshape_reshape.19.b_value, f32[16,320,480]{2,1,0:T(8,128)} %get-tuple-element.77.probs, ...), custom_call_target="tpu_custom_call" | custom-call | bytes 65536 | tf_op jit(solution)/shard_map/pallas_call | solution.py:1217
  613.2 7.0 fusion.51.cross_o
  620.2 9.0 fusion.50.cross_q
  629.2 6.2 fusion.6
  637.3 7.0 convolution_bitcast_fusion.1.attn
  644.3 5.9 fusion.10
  650.2 23.1 %shard_map.408 = f32[20,16,3456]{2,1,0:T(8,128)} custom-call(f32[20,16,3456]{2,1,0:T(8,128)} %bitcast.75, f32[1,1152]{1,0:T(1,128)S(1)} %reshape_reshape.16.b_query, f32[1,1152]{1,0:T(1,128)S(1)} %reshape_reshape.17.b_value, f32[16,2,160,160]{3,2,1,0:T(8,128)} %copy-done.24, f32[20,16,1152]{2,1,0:T(8,128)S(1)} %copy-done.23, f32[20,16,1152]{2,1,0:T(8,128)S(1)} %bitcast.81), custom_call_target="tpu_custom_call" | custom-call | bytes 65536 | tf_op jit(solution)/shard_map/pallas_call | solution.py:1118
  673.3 15.6 %multiply_reduce_fusion.3 = (f32[16,1152]{1,0:T(8,128)S(1)}, f32[20,16]{1,0:T(8,128)S(1)}, f32[20,16]{1,0:T(8,128)S(1)}, f32[16,1152]{1,0:T(8,128)S(1)}, f32[20,16,1152]{2,1,0:T(8,128)}) fusion(f32[20,16,1152]{2,1,0:T(8,128)S(1)} %copy-done.4, f32[20,16]{1,0:T(8,128)S(1)} %add_rsqrt_fusion.1, f32[20,16]{1,0:T(8,128)S(1)} %broadcast_multiply_fusion.7, ...), kind=kOutput, calls=%fused_computation.25 | convolution fusion | flops 7647399424 | bytes 23524352 | tf_op jit(solution)/shard_map/dot_general | solution.py:27
  688.9 16.7 %convolution_bitcast_fusion.first = f32[1152,3456]{1,0:T(8,128)} fusion(f32[20,16,1152]{2,1,0:T(8,128)S(1)} %copy-done.39, f32[20,16,3456]{2,1,0:T(8,128)S(1)} %copy-done.30), kind=kOutput, calls=%fused_computation | convolution fusion | flops 7644119040 | bytes 21823488 | tf_op jit(solution)/shard_map/dot_general | solution.py:31
  706.5 142.4 %shard_map.409 = (f32[320,1152]{1,0:T(8,128)}, f32[120,2304]{1,0:T(8,128)}, f32[5,64,1152]{2,1,0:T(8,128)}, f32[144,1152]{1,0:T(8,128)}, f32[144,1152]{1,0:T(8,128)}, /*index=5*/f32[144,1152]{1,0:T(8,128)}) custom-call(f32[8,320,1152]{2,1,0:T(8,128)} %bitcast.90, f32[480,2304]{1,0:T(8,128)} %get-tuple-element.84.kv, f32[20,16,1152]{2,1,0:T(8,128)} %copy-done.29, ...), custom_call_target="tpu_custom_call" | custom-call | bytes 65536 | tf_op jit(solution)/shard_map/pallas_call | solution.py:908
  867.0 221.4 %shard_map.410 = (f32[144,3456]{1,0:T(8,128)}, f32[144,1152]{1,0:T(8,128)}, f32[144,1152]{1,0:T(8,128)}, f32[144,1152]{1,0:T(8,128)}, f32[144,2304]{1,0:T(8,128)...) custom-call(f32[1152,3456]{1,0:T(8,128)} %convolution_bitcast_fusion.first,, ...), custom_call_target="tpu_custom_call" | custom-call | bytes 65536 | tf_op jit(solution)/shard_map/pallas_call | solution.py:702
  1088.4 4.4 copy.56
  1092.8 4.1 reshape.351
  1103.3 4.4 fusion.52.block
  1107.7 6.2 shard_map.411
  1116.8 4.6 fusion.38
  (299 shorter events, 116.3 us)
Async XLA Ops:
  7.2 15.5 %copy-start = (f32[4,120,1152]{2,1,0:T(8,128)S(1)}, f32[4,120,1152]{2,1,0:T(8,128)}, u32[]{:S(2)}) copy-start(f32[4,120,1152]{2,1,0:T(8,128)} %param.27) | copy-start | bytes 6635524
  7.2 205.2 %all-gather.3.cloned.1.call-start = ((), (), s32[]{:S(2)}) async-start(), calls=%async_computation | async-start | bytes 17915904 | tf_op jit(solution)/shard_map/all_gather | solution.py:1317
  10.3 305.2 %all-gather.5.cloned.1.call-start = ((), (), s32[]{:S(2)}) async-start(), calls=%async_computation.1 | async-start | bytes 13271040 | tf_op jit(solution)/shard_map/all_gather | solution.py:1317
  11.7 6.1 copy-start.71
  11.7 6.1 copy-start.73
  11.7 11.0 copy-start.40
  182.5 36.6 %copy-start.50 = (f32[16,1152]{1,0:T(8,128)}, f32[16,1152]{1,0:T(8,128)S(1)}, u32[]{:S(2)}) copy-start(f32[16,1152]{1,0:T(8,128)S(1)} %get-tuple-element.168) | copy-start | bytes 221188
  182.5 36.6 %copy-start.52 = (f32[16,1152]{1,0:T(8,128)}, f32[16,1152]{1,0:T(8,128)S(1)}, u32[]{:S(2)}) copy-start(f32[16,1152]{1,0:T(8,128)S(1)} %get-tuple-element.169) | copy-start | bytes 221188
  182.8 14.5 %copy-start.38 = (f32[20,16,1152]{2,1,0:T(8,128)}, f32[20,16,1152]{2,1,0:T(8,128)S(1)}, u32[]{:S(2)}) copy-start(f32[20,16,1152]{2,1,0:T(8,128)S(1)} %multiply_add_fusion.5) | copy-start | bytes 4423684
  212.4 6.7 copy-start.3
  212.4 6.7 copy-start.12
  221.8 398.5 %all-reduce.6.cloned.1.call-start = ((), (), s32[]{:S(2)}) async-start(), calls=%async_computation.2 | async-start | bytes 5898240 | tf_op jit(solution)/shard_map/psum | solution.py:1555
  221.9 7.7 copy-start.42
  230.6 3.4 collective-permute-start
  235.7 30.1 %collective-permute-start.3 = (f32[288,576]{1,0:T(8,128)}, f32[288,576]{1,0:T(8,128)}, u32[]{:S(2)}, u32[]{:S(2)}) collective-permute-start(f32[288,576]{1,0:T(8,128)} %pad_maximum_fusion.4), channel_id=1, source_target_pairs={{0,24},{4,28},{8,16},{12,20},{16,8},{20,12},{24,0},{28,4},{1,25},{... | collective-permute-start | bytes 1990664 | tf_op jit(solution)/shard_map/ppermute | solution.py:50
  238.6 42.4 %collective-permute-start.2 = (f32[288,576]{1,0:T(8,128)}, f32[288,576]{1,0:T(8,128)}, u32[]{:S(2)}, u32[]{:S(2)}) collective-permute-start(f32[288,576]{1,0:T(8,128)} %pad_maximum_fusion.3), channel_id=1, source_target_pairs={{0,16},{4,20},{8,24},{12,28},{16,0},{20,4},{24,8},{28,12},{1,17},{... | collective-permute-start | bytes 1990664 | tf_op jit(solution)/shard_map/ppermute | solution.py:50
  242.7 39.5 %collective-permute-start.1 = (f32[288,576]{1,0:T(8,128)S(1)}, f32[288,576]{1,0:T(8,128)S(1)}, u32[]{:S(2)}, u32[]{:S(2)}) collective-permute-start(f32[288,576]{1,0:T(8,128)S(1)} %pad_maximum_fusion.2), channel_id=1, source_target_pairs={{0,8},{4,12},{8,0},{12,4},{16,24},{20,28},{24,16},{28,20},{1,9},{5... | collective-permute-start | bytes 1990664 | tf_op jit(solution)/shard_map/ppermute | solution.py:50
  336.7 6.6 copy-start.16
  336.7 6.6 copy-start.31
  336.7 6.6 copy-start.68
  499.2 622.8 %all-reduce.8.cloned.1.call-start = ((), (), s32[]{:S(2)}) async-start(), calls=%async_computation.3 | async-start | bytes 5308416 | tf_op jit(solution)/shard_map/psum | solution.py:1556
  576.8 36.4 %copy-start.17 = (f32[320,1152]{1,0:T(8,128)S(1)}, f32[320,1152]{1,0:T(8,128)}, u32[]{:S(2)}) copy-start(f32[320,1152]{1,0:T(8,128)} %copy-done.16) | copy-start | bytes 4423684
  576.8 36.4 %copy-start.34 = (f32[20,16,1152]{2,1,0:T(8,128)S(1)}, f32[20,16,1152]{2,1,0:T(8,128)}, u32[]{:S(2)}) copy-start(f32[20,16,1152]{2,1,0:T(8,128)} %get-tuple-element.138) | copy-start | bytes 4423684
  620.2 9.0 copy-start.19
  629.2 6.3 copy-start.37
  629.2 6.3 copy-start.51
  650.2 23.1 %copy-start.4 = (f32[20,16,1152]{2,1,0:T(8,128)S(1)}, f32[20,16,1152]{2,1,0:T(8,128)}, u32[]{:S(2)}) copy-start(f32[20,16,1152]{2,1,0:T(8,128)} %copy-done.1) | copy-start | bytes 4423684
  673.3 15.6 %copy-start.30 = (f32[20,16,3456]{2,1,0:T(8,128)S(1)}, f32[20,16,3456]{2,1,0:T(8,128)}, u32[]{:S(2)}) copy-start(f32[20,16,3456]{2,1,0:T(8,128)} %shard_map.408) | copy-start | bytes 13271044
  673.3 15.6 %copy-start.39 = (f32[20,16,1152]{2,1,0:T(8,128)S(1)}, f32[20,16,1152]{2,1,0:T(8,128)}, u32[]{:S(2)}) copy-start(f32[20,16,1152]{2,1,0:T(8,128)} %copy-done.38) | copy-start | bytes 4423684
  706.5 144.1 %copy-start.33 = (f32[320,1152]{1,0:T(8,128)S(1)}, f32[320,1152]{1,0:T(8,128)}, u32[]{:S(2)}) copy-start(f32[320,1152]{1,0:T(8,128)} %copy-done.32) | copy-start | bytes 4423684
  706.5 144.1 %copy-start.35 = (f32[20,16,1152]{2,1,0:T(8,128)S(1)}, f32[20,16,1152]{2,1,0:T(8,128)}, u32[]{:S(2)}) copy-start(f32[20,16,1152]{2,1,0:T(8,128)} %get-tuple-element.186) | copy-start | bytes 4423684
  1103.3 13.4 %copy-start.60 = (f32[4,1152]{1,0:T(4,128)S(1)}, f32[4,1152]{1,0:T(4,128)}, u32[]{:S(2)}) copy-start(f32[4,1152]{1,0:T(4,128)} %param.28) | copy-start | bytes 55300
  (55 other events, 128.3 us)
Sparse Core Ops, SparseCore 0:
  10.5 146.6 all-gather.2
  221.9 93.6 all-gather.4
  499.3 114.7 all-reduce.5
  705.8 172.9 all-reduce.7
